TPU v7x, 32 devices: a whole 2x2x4 slice. The times are simulated.
32 devices in a mesh: stream: 4 (over y, x), seq: 8 (over z, core).
Axes of the slice: x: 2, y: 2, z: 4, core: 2. Of those that a mesh axis runs over, the one named last changes fastest.
Arguments:
- frame_rows: bfloat16 [16384, 512], P(('stream', 'seq')), as said below
- row_frame: int32 [16384], P(('stream', 'seq')), may hold values from -1 to 16383, as said below
- frame_owner: int32 [4, 4096], P('stream', 'seq'), may hold values from -1 to 31, as said below
- lengths: int32 [4], P('stream'), may hold values from 1024 to 4096, as said below
- query_weight: bfloat16 [512, 512], replicated
- key_weight: bfloat16 [512, 512], replicated
- value_weight: bfloat16 [512, 512], replicated, may hold values from -0.25 to 0.25
- out_weight: bfloat16 [512, 512], replicated, may hold values from -0.25 to 0.25
- cotangent: bfloat16 [4, 4096, 512], P('stream', 'seq'), may hold values from -6 to 6
Outputs:
- out_frames: bfloat16 [4, 4096, 512], P('stream', 'seq')
- frame_grads: bfloat16 [16384, 512], P(('stream', 'seq'))
- weight_grads: float32 [512, 2048], P(('stream', 'seq'))
Inputs may be any that keep to these rules, and one draw needn't show every extreme that they name: Frames at and beyond lengths[s] are padding. The last stream has 4096 valid frames and some other stream 4096 // 4. `frame_owner`: the backbone device (index over stream and seq together, stream slowest) holding each valid frame; -1 exactly at padding frames. At most 16 frames of one time shard of 512 frames lie on one backbone device, and a shard whose frames are all valid puts exactly 16 on each. `row_frame`: the frame s * 4096 + t held by each backbone row, or -1 for an empty row. Every valid frame is held by exactly one row, on the device that frame_owner names; a device's used rows come first, in increasing frame index. `frame_rows`: empty backbone rows are zero.
All inputs are finite; a program needn't handle non-finite values.
Results may differ from a plain program's by a relative error of at most 0.015.
Values may be sent and summed in bfloat16 or wider, within the bound.
No kernel may reach another device: no remote copies, remote signals or barrier semaphores. Data moves between devices by JAX's collectives and lax.ppermute only.
A program may use at most 128 MiB of HBM per device.

v0:
```python
import math

import jax
import jax.numpy as jnp
from jax import lax
from jax.experimental import pallas as pl
from jax.experimental.pallas import tpu as pltpu
from jax.sharding import PartitionSpec as P

H = 8
WIN = 512
NEG = -1e30
EPS_NORM = 1e-06
AXES = ("stream", "seq")
BF = jnp.bfloat16
F32 = jnp.float32

NN = (((1,), (0,)), ((), ()))
NT = (((1,), (1,)), ((), ()))


def mm(a, b, dims=NN):
    return lax.dot_general(a, b, dims, preferred_element_type=F32)


def iota2(shape, dim):
    return lax.broadcasted_iota(jnp.int32, shape, dim)


def vmem_call(body, outs, args, smem=(), scratch=(), flops=0, limit=32):
    specs = [
        pl.BlockSpec(memory_space=pltpu.SMEM if i in smem else pltpu.VMEM)
        for i in range(len(args))
    ]
    size = sum(math.prod(a.shape) * a.dtype.itemsize for a in list(args) + list(outs))
    return pl.pallas_call(
        body,
        out_shape=tuple(outs),
        in_specs=specs,
        out_specs=tuple(pl.BlockSpec(memory_space=pltpu.VMEM) for _ in outs),
        scratch_shapes=list(scratch),
        compiler_params=pltpu.CompilerParams(vmem_limit_bytes=limit * 2**20),
        cost_estimate=pl.CostEstimate(flops=flops, bytes_accessed=size, transcendentals=0),
    )(*args)


def sds(shape, dtype=BF):
    return jax.ShapeDtypeStruct(shape, dtype)


def outgoing_body(span, slots, rf_ref, rows_ref, out_ref, placing_ref):
    count = rf_ref.shape[1]
    total = out_ref.shape[0]
    rf = rf_ref[...]
    target = jnp.where(rf >= 0, lax.div(rf, span), 1 << 20)
    slot = iota2((total, count), 0)
    owner = lax.div(slot, slots)
    rank = slot - owner * slots
    start = jnp.sum(jnp.where(target < owner, 1.0, 0.0), axis=1, keepdims=True)
    here = iota2((total, count), 1) - start.astype(jnp.int32)
    placing = jnp.where((target == owner) & (here == rank), 1.0, 0.0).astype(BF)
    placing_ref[...] = placing
    out_ref[...] = mm(placing, rows_ref[...]).astype(BF)


def early_body(
    slots, owner_ref, placing_ref, cot_ref, wo_ref, pick_ref, pick_t_ref, placing_t_ref, do_ref, dot_ref
):
    span, lanes = owner_ref.shape[0], 128
    total = pick_ref.shape[1]
    owner = owner_ref[...]
    device = iota2((span, lanes), 1)
    hot = jnp.where(owner == device, 1.0, 0.0)
    strict = jnp.where(iota2((span, span), 1) < iota2((span, span), 0), 1.0, 0.0).astype(BF)
    before = mm(strict, hot.astype(BF))
    slot = jnp.sum(hot * (before + (device * slots).astype(F32)), axis=1, keepdims=True)
    slot = jnp.where(owner >= 0, slot.astype(jnp.int32), -1)
    pick = jnp.where(iota2((span, total), 1) == slot, 1.0, 0.0)
    pick_ref[...] = pick.astype(BF)
    pick_t_ref[...] = pick.T.astype(BF)
    placing_t_ref[...] = placing_ref[...].T
    grad = mm(cot_ref[...], wo_ref[...], NT).astype(BF)
    do_ref[...] = grad
    dot_ref[...] = grad.T


def unit_frames(frames):
    frames32 = frames.astype(F32)
    inverse = lax.rsqrt(jnp.mean(frames32 * frames32, axis=1, keepdims=True) + EPS_NORM)
    return frames32, inverse, frames32 * inverse


def frames_body(pick_ref, in_ref, frames_ref, normed_ref):
    frames = mm(pick_ref[...], in_ref[...]).astype(BF)
    frames_ref[...] = frames
    normed_ref[...] = unit_frames(frames)[2].astype(BF)


def project_body(
    query_scale, normed_ref, wq_ref, wk_ref, wv_ref, q_ref, qt_ref, k_ref, kt_ref, v_ref, vt_ref
):
    normed = normed_ref[...]
    q = (mm(normed, wq_ref[...]) * query_scale).astype(BF)
    q_ref[...] = q
    qt_ref[...] = q.T
    k = mm(normed, wk_ref[...]).astype(BF)
    k_ref[...] = k
    kt_ref[...] = k.T
    v = mm(normed, wv_ref[...]).astype(BF)
    v_ref[...] = v
    vt_ref[...] = v.T


def attend_body(
    head_size, meta_ref, halo_ref, wk_ref, wv_ref,
    q_ref, qt_ref, k_ref, kt_ref, v_ref, vt_ref, do_ref, dot_ref,
    ot_ref, dqt_ref, dk_ref, dv_ref, dkh_ref, dvh_ref, back_ref,
    kx, vx, ktx, vtx,
):
    span, width = q_ref.shape
    begin, length = meta_ref[0], meta_ref[1]
    halo = halo_ref[...]
    kh = mm(halo, wk_ref[...]).astype(BF)
    kx[:WIN] = kh
    ktx[:, :WIN] = kh.T
    vh = mm(halo, wv_ref[...]).astype(BF)
    vx[:WIN] = vh
    vtx[:, :WIN] = vh.T
    kx[WIN:] = k_ref[...]
    vx[WIN:] = v_ref[...]
    ktx[:, WIN:] = kt_ref[...]
    vtx[:, WIN:] = vt_ref[...]

    block, tile, pair = 256, 128, 2 * head_size
    reach = WIN + block
    row = iota2((tile, tile), 0)
    col = iota2((tile, tile), 1)
    halo_bias = jnp.where(begin == 0, NEG, 0.0)
    lane = iota2((block, pair), 1)
    zeros_half = jnp.zeros((head_size, block), BF)
    zero_tile = jnp.zeros((tile, tile), BF)

    def one_pair(p, carry):
        cols = pl.ds(pl.multiple_of(p * pair, pair), pair)
        dks, dvs = [], []
        for b in range(span // block):
            first = b * block
            keys = kx[first : first + reach, cols]
            vals = vx[first : first + reach, cols]
            queries = q_ref[first : first + block, cols]
            grads = do_ref[first : first + block, cols]
            dk_block = dv_block = None
            for h in range(2):
                feats = pl.ds(pl.multiple_of(p * pair + h * head_size, head_size), head_size)
                halves = [zeros_half, zeros_half]
                halves[h] = qt_ref[feats, first : first + block]
                scores = mm(keys, jnp.concatenate(halves, axis=0))
                halves[h] = dot_ref[feats, first : first + block]
                slopes = mm(vals, jnp.concatenate(halves, axis=0))
                prob_cols, grad_cols = [], []
                for a in range(block // tile):
                    at = slice(a * tile, (a + 1) * tile)
                    count = WIN // tile + 1
                    parts = []
                    for n in range(count):
                        low = a * tile + n * tile
                        part = scores[low : low + tile, at]
                        if n == 0:
                            part = jnp.where(row > col, part, NEG)
                        if n == count - 1:
                            part = jnp.where(row <= col, part, NEG)
                        elif first + low < WIN:
                            part = part + halo_bias
                        parts.append(part)
                    peak = parts[0]
                    for part in parts[1:]:
                        peak = jnp.maximum(peak, part)
                    peak = jnp.max(peak, axis=0, keepdims=True)
                    parts = [jnp.exp2(part - peak) for part in parts]
                    denom = parts[0]
                    for part in parts[1:]:
                        denom = denom + part
                    denom = jnp.sum(denom, axis=0, keepdims=True)
                    time = begin + first + a * tile + iota2((1, tile), 1)
                    scale = jnp.where(time < length, 1.0 / denom, 0.0)
                    parts = [part * scale for part in parts]
                    moved = [
                        part * slopes[(a + n) * tile : (a + n + 1) * tile, at]
                        for n, part in enumerate(parts)
                    ]
                    centre = moved[0]
                    for part in moved[1:]:
                        centre = centre + part
                    centre = jnp.sum(centre, axis=0, keepdims=True)
                    low_parts = [part.astype(BF) for part in parts]
                    grad_parts = [
                        (move - part * centre).astype(BF) for part, move in zip(parts, moved)
                    ]
                    before = [zero_tile] * a
                    after = [zero_tile] * (block // tile - 1 - a)
                    prob_cols.append(jnp.concatenate(before + low_parts + after, axis=0))
                    grad_cols.append(jnp.concatenate(before + grad_parts + after, axis=0))
                probs = jnp.concatenate(prob_cols, axis=1)
                score_grad = jnp.concatenate(grad_cols, axis=1)
                span_keys = slice(first, first + reach)
                ot_ref[feats, first : first + block] = mm(vtx[feats, span_keys], probs).astype(BF)
                dqt_ref[feats, first : first + block] = (
                    mm(ktx[feats, span_keys], score_grad) * head_size ** (-0.5)
                ).astype(BF)
                mine = (lane >= h * head_size) & (lane < (h + 1) * head_size)
                zero = jnp.zeros((), BF)
                dk_part = mm(score_grad, jnp.where(mine, queries, zero))
                dv_part = mm(probs, jnp.where(mine, grads, zero))
                dk_block = dk_part if dk_block is None else dk_block + dk_part
                dv_block = dv_part if dv_block is None else dv_block + dv_part
            dks.append(dk_block)
            dvs.append(dv_block)
        for parts, scale, far_ref, near_ref in (
            (dks, math.log(2.0), dkh_ref, dk_ref),
            (dvs, 1.0, dvh_ref, dv_ref),
        ):
            for low in range(0, WIN + span, block):
                total = None
                for b, part in enumerate(parts):
                    at = low - b * block
                    if 0 <= at < reach:
                        piece = part[at : at + block]
                        total = piece if total is None else total + piece
                total = (total * scale).astype(BF)
                if low < WIN:
                    far_ref[low : low + block, cols] = total
                else:
                    near_ref[low - WIN : low - WIN + block, cols] = total
        return carry

    lax.fori_loop(0, width // pair, one_pair, 0)
    back_ref[...] = (mm(dkh_ref[...], wk_ref[...], NT) + mm(dvh_ref[...], wv_ref[...], NT)).astype(BF)


def weights_body(
    scale, normed_ref, halo_ref, frames_ref, cot_ref, wq_ref, wk_ref, wv_ref, wo_ref,
    ot_ref, dqt_ref, dk_ref, dv_ref, dkh_ref, dvh_ref,
    sums_ref, out_ref, slope_ref,
):
    width = wq_ref.shape[0]
    normed_t = normed_ref[...].T
    halo_t = halo_ref[...].T
    sums_ref[:, :width] = (mm(normed_t, dqt_ref[...], NT) * scale).astype(BF)
    own = mm(normed_t, dk_ref[...]) + mm(halo_t, dkh_ref[...])
    sums_ref[:, width : 2 * width] = (own * scale).astype(BF)
    own = mm(normed_t, dv_ref[...]) + mm(halo_t, dvh_ref[...])
    sums_ref[:, 2 * width : 3 * width] = (own * scale).astype(BF)
    sums_ref[:, 3 * width :] = (mm(ot_ref[...], cot_ref[...]) * scale).astype(BF)
    slope = mm(dqt_ref[...].T, wq_ref[...], NT)
    slope = slope + mm(dk_ref[...], wk_ref[...], NT)
    slope_ref[...] = slope + mm(dv_ref[...], wv_ref[...], NT)
    out = mm(ot_ref[...].T, wo_ref[...]) + frames_ref[...].astype(F32)
    out_ref[...] = out.astype(BF)


def returning_body(frames_ref, slope_ref, extra_ref, cot_ref, pick_t_ref, out_ref):
    _, inverse, normed32 = unit_frames(frames_ref[...])
    slope = slope_ref[...] + extra_ref[...].astype(F32)
    centre = jnp.mean(slope * normed32, axis=1, keepdims=True)
    grad = inverse * (slope - normed32 * centre) + cot_ref[...].astype(F32)
    out_ref[...] = mm(pick_t_ref[...], grad.astype(BF)).astype(BF)


def arrived_body(placing_t_ref, in_ref, out_ref):
    out_ref[...] = mm(placing_t_ref[...], in_ref[...]).astype(BF)


def passed_along(shard, by):
    devices = lax.axis_size("seq")
    pairs = [(i, i + by) for i in range(devices) if 0 <= i + by < devices]
    return lax.ppermute(shard, "seq", pairs)


def swap(shard, bit):
    devices = lax.axis_size(AXES)
    return lax.ppermute(shard, AXES, [(i, i ^ bit) for i in range(devices)])


def halve(sums, place, bits, bit):
    dim = bits.index(bit)
    mine = (place >> (bit.bit_length() - 1)) & 1
    keep = lax.dynamic_index_in_dim(sums, mine, dim, keepdims=False)
    send = lax.dynamic_index_in_dim(sums, 1 - mine, dim, keepdims=False)
    return keep, swap(send, bit), bits[:dim] + bits[dim + 1 :]


def scatter_sums(sums):
    devices = lax.axis_size(AXES)
    place = lax.axis_index(AXES)
    rows, columns = sums.shape
    bits = [1 << n for n in reversed(range(devices.bit_length() - 1))]
    sums = sums.reshape([2] * len(bits) + [rows // devices, columns])
    keep, got, left = halve(sums, place, bits, 1)
    half = columns // 2
    lanes = []
    for lane in range(2):
        at = slice(lane * half, (lane + 1) * half)
        order = list(left)
        if lane:
            order[0], order[1] = order[1], order[0]
        lanes.append([keep[..., at], got[..., at], left, order])
    while lanes[0][3]:
        for lane in lanes:
            keep, got, left, order = lane
            total = (keep.astype(F32) + got.astype(F32)).astype(BF)
            lane[:3] = halve(total, place, left, order[0])
            lane[3] = order[1:]
    parts = [keep.astype(F32) + got.astype(F32) for keep, got, _, _ in lanes]
    return jnp.concatenate(parts, axis=1)


def shards(
    frame_rows, row_frame, frame_owner, lengths,
    query_weight, key_weight, value_weight, out_weight, cotangent,
):
    devices = lax.axis_size(AXES)
    row_count, width = frame_rows.shape
    span = frame_owner.shape[1]
    slots = row_count // devices
    slab = span * lax.axis_size("seq")
    head_size = width // H
    cube = 2 * span * width * width
    square = sds((span, width))
    begin = (lax.axis_index("seq") * span).astype(jnp.int32)
    meta = jnp.stack([begin, lengths[0]])
    cot = cotangent[0]

    def exchanged(shard):
        got = lax.all_to_all(
            shard.reshape(devices, slots, width), AXES, split_axis=0, concat_axis=0, tiled=True
        )
        return got.reshape(devices * slots, width)

    outgoing, placing = vmem_call(
        lambda *refs: outgoing_body(span, slots, *refs),
        [square, sds((devices * slots, row_count))],
        [row_frame.reshape(1, row_count), frame_rows],
        flops=cube,
    )
    incoming = exchanged(outgoing)
    pick, pick_t, placing_t, do, dot = vmem_call(
        lambda *refs: early_body(slots, *refs),
        [square, square, square, square, sds((width, span))],
        [frame_owner.reshape(span, 1), placing, cot, out_weight],
        flops=2 * cube,
    )
    frames, normed = vmem_call(frames_body, [square, square], [pick, incoming], flops=cube)
    halo = passed_along(normed, 1)
    query_scale = head_size ** (-0.5) * math.log2(math.e)
    q, qt, k, kt, v, vt = vmem_call(
        lambda *refs: project_body(query_scale, *refs),
        [square] * 6,
        [normed, query_weight, key_weight, value_weight],
        flops=3 * cube,
    )
    ot, dqt, dk, dv, dkh, dvh, back = vmem_call(
        lambda *refs: attend_body(head_size, *refs),
        [square] * 7,
        [meta, halo, key_weight, value_weight, q, qt, k, kt, v, vt, do, dot],
        smem=(0,),
        scratch=[
            pltpu.VMEM((WIN + span, width), BF),
            pltpu.VMEM((WIN + span, width), BF),
            pltpu.VMEM((width, WIN + span), BF),
            pltpu.VMEM((width, WIN + span), BF),
        ],
        flops=20 * cube,
        limit=40,
    )
    extra = passed_along(back, -1)
    sums, out_frames, slope = vmem_call(
        lambda *refs: weights_body(slab ** (-0.5), *refs),
        [sds((width, 4 * width)), square, sds((span, width), F32)],
        [normed, halo, frames, cot, query_weight, key_weight, value_weight, out_weight,
         ot, dqt, dk, dv, dkh, dvh],
        flops=10 * cube,
    )
    returning, = vmem_call(
        returning_body, [square], [frames, slope, extra, cot, pick_t], flops=cube
    )
    arrived = exchanged(returning)
    frame_grads, = vmem_call(arrived_body, [square], [placing_t, arrived], flops=cube)
    weight_grads = scatter_sums(sums)
    return (out_frames[None], frame_grads, weight_grads)


def solution(mesh):
    return jax.shard_map(
        shards,
        mesh=mesh,
        in_specs=(
            P(AXES, None), P(AXES), P("stream", "seq"), P("stream"),
            P(), P(), P(), P(), P("stream", "seq", None),
        ),
        out_specs=(P("stream", "seq", None), P(AXES, None), P(AXES, None)),
        check_vma=False,
    )
```

profile of v0, /device:TPU:0, one launch (start us, length us, event | category | flops | bytes accessed | tf_op | source)
XLA Modules:
  0.0 114.3 jit_solution(11503424074259479088)
XLA Ops:
  2.4 1.4 %shard_map.112 = (bf16[512,512]{1,0:T(8,128)(2,1)}, bf16[512,512]{1,0:T(8,128)(2,1)S(1)}) custom-call(s32[1,512]{1,0:T(1,128)S(1)} %bitcast.62, bf16[512,512]{1,0:T(8,128)(2,1)S(1)} %copy-done.1), custom_call_target="tpu_custom_call" | custom-call | flops 268435456 | bytes 1574912 | tf_op jit(solution)/shard_map/pallas_call | solution.py:36
  3.8 7.3 %all-to-all-start = ((bf16[32,16,512]{2,1,0:T(8,128)(2,1)}), bf16[32,16,512]{2,1,0:T(8,128)(2,1)S(1)}, u32[]{:S(2)}, u32[]{:S(2)}) async-start(bf16[32,16,512]{2,1,0:T(8,128)(2,1)} %bitcast.3), calls=%async_computation | async-start | bytes 1048576 | tf_op jit(solution)/shard_map/all_to_all | solution.py:334
  13.0 1.3 %shard_map.113 = (bf16[512,512]{1,0:T(8,128)(2,1)S(1)}, bf16[512,512]{1,0:T(8,128)(2,1)S(1)}, bf16[512,512]{1,0:T(8,128)(2,1)S(1)}, bf16[512,512]{1,0:T(8,128)(2,1)S(1)}, bf16[512,512]{1,0:T(8,128)(2,1)S(1)}) custom-call(s32[512,1]{1,0:T(8,128)S(1)} %copy.14.refs_0_, bf16[512,512]{1,0:T(8,128)(2,1)S(1)} %copy-done.18, bf16[512,512]{1,0:T(8,128)(2,1)S(1)} %bitcast.59, ...), custom_call_target="tpu_custom_call" | custom-call | flops 536870912 | bytes 4196352 | tf_op jit(solution)/shard_map/pallas_call | solution.py:36
  15.9 11.5 %all-to-all-done = bf16[32,16,512]{2,1,0:T(8,128)(2,1)S(1)} async-done(((bf16[32,16,512]{2,1,0:T(8,128)(2,1)}), bf16[32,16,512]{2,1,0:T(8,128)(2,1)S(1)}, u32[]{:S(2)}, u32[]{:S(2)}) %all-to-all-start) | async-done | bytes 524320 | tf_op jit(solution)/shard_map/all_to_all | solution.py:334
  27.5 1.4 %shard_map.114 = (bf16[512,512]{1,0:T(8,128)(2,1)S(1)}, bf16[512,512]{1,0:T(8,128)(2,1)}) custom-call(bf16[512,512]{1,0:T(8,128)(2,1)S(1)} %get-tuple-element.29.pick_ref, bf16[512,512]{1,0:T(8,128)(2,1)S(1)} %bitcast.58), custom_call_target="tpu_custom_call" | custom-call | flops 268435456 | bytes 2097152 | tf_op jit(solution)/shard_map/pallas_call | solution.py:36
  28.9 1.9 %collective-permute-start = (bf16[512,512]{1,0:T(8,128)(2,1)}, bf16[512,512]{1,0:T(8,128)(2,1)S(1)}, u32[]{:S(2)}, u32[]{:S(2)}) collective-permute-start(bf16[512,512]{1,0:T(8,128)(2,1)} %get-tuple-element.31.refs_0_), channel_id=1, source_target_pairs={{0,1},{1,2},{2,3},{3,4},{4,5},{5,6},{6,7},{8,9},{9,10},{10,11},{11... | collective-permute-start | bytes 1572872 | tf_op jit(solution)/shard_map/ppermute | solution.py:276
  34.7 2.2 %shard_map.115 = (bf16[512,512]{1,0:T(8,128)(2,1)S(1)}, bf16[512,512]{1,0:T(8,128)(2,1)S(1)}, bf16[512,512]{1,0:T(8,128)(2,1)S(1)}, bf16[512,512]{1,0:T(8,128)(2...) custom-call(bf16[512,512]{1,0:T(8,128)(2,1)} %get-tuple-element.31.refs_0_, ...), custom_call_target="tpu_custom_call" | custom-call | flops 805306368 | bytes 5242880 | tf_op jit(solution)/shard_map/pallas_call | solution.py:36
  39.2 17.2 %shard_map.116 = (bf16[512,512]{1,0:T(8,128)(2,1)S(1)}, bf16[512,512]{1,0:T(8,128)(2,1)S(1)}, bf16[512,512]{1,0:T(8,128)(2,1)S(1)}, bf16[512,512]{1,0:T(8,128)(2...) custom-call(s32[2]{0:T(128)S(1)} %pad_add_fusion.refs_0_, ...), custom_call_target="tpu_custom_call" | custom-call | flops 5368709120 | bytes 9437192 | tf_op jit(solution)/shard_map/pallas_call | solution.py:36
  57.4 4.8 %shard_map.117 = (bf16[512,2048]{1,0:T(8,128)(2,1)S(1)}, bf16[512,512]{1,0:T(8,128)(2,1)}, f32[512,512]{1,0:T(8,128)S(1)}) custom-call(bf16[512,512]{1,0:T(8,128)(2,1)} %get-tuple-element.31.refs_0_, bf16[512,512]{1,0:T(8,128)(2,1)S(1)} %copy-done.11, bf16[512,512]{1,0:T(8,128)(2,1)S(1)} %get-tuple-element.32.refs_2_.frames_ref, ...), custom_call_target="tpu_custom_call" | custom-call | flops 2684354560 | bytes 11010048 | tf_op jit(solution)/shard_map/pallas_call | solution.py:36
  64.9 1.3 %collective-permute-start.1 = (bf16[512,512]{1,0:T(8,128)(2,1)}, bf16[512,512]{1,0:T(8,128)(2,1)}, u32[]{:S(2)}, u32[]{:S(2)}) collective-permute-start(bf16[512,512]{1,0:T(8,128)(2,1)} %get-tuple-element.50), channel_id=1, source_target_pairs={{1,0},{2,1},{3,2},{4,3},{5,4},{6,5},{7,6},{9,8},{10,9},{11,10},{12... | collective-permute-start | bytes 1572872 | tf_op jit(solution)/shard_map/ppermute | solution.py:276
  66.2 1.3 %copy.20 = bf16[2,2,2,2,1,16,2048]{6,5,3,2,0,1,4:T(8,128)(2,1)S(1)} copy(bf16[2,2,2,2,1,16,2048]{6,5,4,3,2,1,0:T(8,128)(2,1)} %get-tuple-element.55) | data formatting | bytes 2097152 | tf_op jit(solution)/shard_map/jit(dynamic_index_in_dim)/dynamic_slice | solution.py:287
  67.5 2.4 %add_convert_fusion.1 = (bf16[2,2,2,2,16,1024]{5,4,3,2,0,1:T(8,128)(2,1)}, bf16[2,2,2,2,16,1024]{5,4,3,2,0,1:T(8,128)(2,1)S(1)}) fusion(bf16[2,2,2,2,16,2048]{5,4,3,2,0,1:T(8,128)(2,1)} %collective-permute-done.2, bf16[2,2,2,2,16,2048]{5,4,3,2,0,1:T(8,128)(2,1)S(1)} %bitcast.63), kind=kLoop, calls=%fused_computation.3 | loop fusion | flops 2097152 | bytes 3145728 | tf_op jit(solution)/shard_map/convert_element_type | solution.py:310
  71.6 2.6 %shard_map.118 = bf16[512,512]{1,0:T(8,128)(2,1)} custom-call(bf16[512,512]{1,0:T(8,128)(2,1)S(1)} %get-tuple-element.32.refs_2_.frames_ref, f32[512,512]{1,0:T(8,128)S(1)} %get-tuple-element.49.slope_ref, bf16[512,512]{1,0:T(8,128)(2,1)} %collective-permute-done.1.extra_ref, bf16[512,512]{1,0:T(8,128)(2,1)S(1)} %bitcast.61, ...), custom_call_target="tpu_custom_call" | custom-call | flops 268435456 | bytes 3670016 | tf_op jit(solution)/shard_map/pallas_call | solution.py:36
  74.3 7.4 %all-to-all-start.1 = ((bf16[32,16,512]{2,1,0:T(8,128)(2,1)}), bf16[32,16,512]{2,1,0:T(8,128)(2,1)S(1)}, u32[]{:S(2)}, u32[]{:S(2)}) async-start(bf16[32,16,512]{2,1,0:T(8,128)(2,1)} %bitcast.7), calls=%async_computation.1 | async-start | bytes 1048576 | tf_op jit(solution)/shard_map/all_to_all | solution.py:334
  82.7 1.8 %collective-permute-start.3 = (bf16[2,2,2,16,1024]{4,3,2,1,0:T(8,128)(2,1)S(1)}, bf16[2,2,2,16,1024]{4,3,2,1,0:T(8,128)(2,1)S(1)}, u32[]{:S(2)}, u32[]{:S(2)}) collective-permute-start(bf16[2,2,2,16,1024]{4,3,2,1,0:T(8,128)(2,1)S(1)} %dynamic-slice_bitcast_fusion.1), channel_id=1, source_target_pairs={{0,16},{1,17},{2,18},{3,19},{4,20},{5,21},{6,22},{7,23},{8,24},{9,... | collective-permute-start | bytes 786440 | tf_op jit(solution)/shard_map/ppermute | solution.py:281
  85.9 9.7 %collective-permute-done.3 = bf16[2,2,2,16,1024]{4,3,2,1,0:T(8,128)(2,1)S(1)} collective-permute-done((bf16[2,2,2,16,1024]{4,3,2,1,0:T(8,128)(2,1)S(1)}, bf16[2,2,2,16,1024]{4,3,2,1,0:T(8,128)(2,1)S(1)}, u32[]{:S(2)}, u32[]{:S(2)}) %collective-permute-start.3) | collective-permute-done | bytes 262176 | tf_op jit(solution)/shard_map/ppermute | solution.py:281
  95.7 1.5 %collective-permute-start.4 = (bf16[2,2,16,1024]{3,2,1,0:T(8,128)(2,1)S(1)}, bf16[2,2,16,1024]{3,2,1,0:T(8,128)(2,1)S(1)}, u32[]{:S(2)}, u32[]{:S(2)}) collective-permute-start(bf16[2,2,16,1024]{3,2,1,0:T(8,128)(2,1)S(1)} %dynamic-slice_bitcast_fusion.3), channel_id=1, source_target_pairs={{0,8},{1,9},{2,10},{3,11},{4,12},{5,13},{6,14},{7,15},{8,0},{9,1},... | collective-permute-start | bytes 393224 | tf_op jit(solution)/shard_map/ppermute | solution.py:281
  97.2 1.7 %collective-permute-done.8 = bf16[2,2,16,1024]{3,2,1,0:T(8,128)(2,1)S(1)} collective-permute-done((bf16[2,2,16,1024]{3,2,1,0:T(8,128)(2,1)S(1)}, bf16[2,2,16,1024]{3,2,1,0:T(8,128)(2,1)S(1)}, u32[]{:S(2)}, u32[]{:S(2)}) %collective-permute-start.8) | collective-permute-done | bytes 131104 | tf_op jit(solution)/shard_map/ppermute | solution.py:281
  99.0 2.3 %collective-permute-start.9 = (bf16[2,16,1024]{2,1,0:T(8,128)(2,1)S(1)}, bf16[2,16,1024]{2,1,0:T(8,128)(2,1)S(1)}, u32[]{:S(2)}, u32[]{:S(2)}) collective-permute-start(bf16[2,16,1024]{2,1,0:T(8,128)(2,1)S(1)} %dynamic-slice_bitcast_fusion.4), channel_id=1, source_target_pairs={{0,4},{1,5},{2,6},{3,7},{4,0},{5,1},{6,2},{7,3},{8,12},{9,13},{10,... | collective-permute-start | bytes 196616 | tf_op jit(solution)/shard_map/ppermute | solution.py:281
  101.4 2.8 %collective-permute-start.5 = (bf16[2,16,1024]{2,1,0:T(8,128)(2,1)S(1)}, bf16[2,16,1024]{2,1,0:T(8,128)(2,1)S(1)}, u32[]{:S(2)}, u32[]{:S(2)}) collective-permute-start(bf16[2,16,1024]{2,1,0:T(8,128)(2,1)S(1)} %dynamic-slice_bitcast_fusion.5), channel_id=1, source_target_pairs={{0,4},{1,5},{2,6},{3,7},{4,0},{5,1},{6,2},{7,3},{8,12},{9,13},{10,... | collective-permute-start | bytes 196616 | tf_op jit(solution)/shard_map/ppermute | solution.py:281
  104.1 2.6 %collective-permute-done.9 = bf16[2,16,1024]{2,1,0:T(8,128)(2,1)S(1)} collective-permute-done((bf16[2,16,1024]{2,1,0:T(8,128)(2,1)S(1)}, bf16[2,16,1024]{2,1,0:T(8,128)(2,1)S(1)}, u32[]{:S(2)}, u32[]{:S(2)}) %collective-permute-start.9) | collective-permute-done | bytes 65568 | tf_op jit(solution)/shard_map/ppermute | solution.py:281
  106.9 1.5 %collective-permute-done.5 = bf16[2,16,1024]{2,1,0:T(8,128)(2,1)S(1)} collective-permute-done((bf16[2,16,1024]{2,1,0:T(8,128)(2,1)S(1)}, bf16[2,16,1024]{2,1,0:T(8,128)(2,1)S(1)}, u32[]{:S(2)}, u32[]{:S(2)}) %collective-permute-start.5) | collective-permute-done | bytes 65568 | tf_op jit(solution)/shard_map/ppermute | solution.py:281
  109.0 1.8 %collective-permute-done.10 = bf16[16,1024]{1,0:T(8,128)(2,1)S(1)} collective-permute-done((bf16[16,1024]{1,0:T(8,128)(2,1)S(1)}, bf16[16,1024]{1,0:T(8,128)(2,1)S(1)}, u32[]{:S(2)}, u32[]{:S(2)}) %collective-permute-start.10) | collective-permute-done | bytes 32800 | tf_op jit(solution)/shard_map/ppermute | solution.py:281
  110.9 1.6 %collective-permute-done.6 = bf16[16,1024]{1,0:T(8,128)(2,1)S(1)} collective-permute-done((bf16[16,1024]{1,0:T(8,128)(2,1)S(1)}, bf16[16,1024]{1,0:T(8,128)(2,1)S(1)}, u32[]{:S(2)}, u32[]{:S(2)}) %collective-permute-start.6) | collective-permute-done | bytes 32800 | tf_op jit(solution)/shard_map/ppermute | solution.py:281
  (75 shorter events, 21.4 us)
Async XLA Ops:
  0.6 11.3 %copy-start = (bf16[1,512,512]{2,1,0:T(8,128)(2,1)S(1)}, bf16[1,512,512]{2,1,0:T(8,128)(2,1)}, u32[]{:S(2)}) copy-start(bf16[1,512,512]{2,1,0:T(8,128)(2,1)} %param.17) | copy-start | bytes 1572868
  0.6 1.1 copy-start.1
  2.4 9.5 %copy-start.2 = (bf16[512,512]{1,0:T(8,128)(2,1)S(1)}, bf16[512,512]{1,0:T(8,128)(2,1)}, u32[]{:S(2)}) copy-start(bf16[512,512]{1,0:T(8,128)(2,1)} %refs_7_.1) | copy-start | bytes 1572868
  3.8 8.1 %copy-start.17 = (bf16[512,512]{1,0:T(8,128)(2,1)}, bf16[512,512]{1,0:T(8,128)(2,1)S(1)}, u32[]{:S(2)}) copy-start(bf16[512,512]{1,0:T(8,128)(2,1)S(1)} %get-tuple-element.28.refs_1_) | copy-start | bytes 1572868
  3.8 23.7 %all-to-all-start = ((bf16[32,16,512]{2,1,0:T(8,128)(2,1)}), bf16[32,16,512]{2,1,0:T(8,128)(2,1)S(1)}, u32[]{:S(2)}, u32[]{:S(2)}) async-start(bf16[32,16,512]{2,1,0:T(8,128)(2,1)} %bitcast.3), calls=%async_computation | async-start | bytes 1048576 | tf_op jit(solution)/shard_map/all_to_all | solution.py:334
  28.9 8.0 %collective-permute-start = (bf16[512,512]{1,0:T(8,128)(2,1)}, bf16[512,512]{1,0:T(8,128)(2,1)S(1)}, u32[]{:S(2)}, u32[]{:S(2)}) collective-permute-start(bf16[512,512]{1,0:T(8,128)(2,1)} %get-tuple-element.31.refs_0_), channel_id=1, source_target_pairs={{0,1},{1,2},{2,3},{3,4},{4,5},{5,6},{6,7},{8,9},{9,10},{10,11},{11... | collective-permute-start | bytes 1572872 | tf_op jit(solution)/shard_map/ppermute | solution.py:276
  34.7 2.2 %copy-start.14 = (bf16[512,512]{1,0:T(8,128)(2,1)S(1)}, bf16[512,512]{1,0:T(8,128)(2,1)}, u32[]{:S(2)}) copy-start(bf16[512,512]{1,0:T(8,128)(2,1)} %copy-done.13) | copy-start | bytes 1572868
  34.7 2.2 %copy-start.16 = (bf16[512,512]{1,0:T(8,128)(2,1)S(1)}, bf16[512,512]{1,0:T(8,128)(2,1)}, u32[]{:S(2)}) copy-start(bf16[512,512]{1,0:T(8,128)(2,1)} %copy-done.15) | copy-start | bytes 1572868
  36.9 19.5 %copy-start.10 = (bf16[512,512]{1,0:T(8,128)(2,1)}, bf16[512,512]{1,0:T(8,128)(2,1)S(1)}, u32[]{:S(2)}) copy-start(bf16[512,512]{1,0:T(8,128)(2,1)S(1)} %collective-permute-done.refs_1_) | copy-start | bytes 1572868
  36.9 1.2 %copy-start.7 = (bf16[512,512]{1,0:T(8,128)(2,1)S(1)}, bf16[512,512]{1,0:T(8,128)(2,1)}, u32[]{:S(2)}) copy-start(bf16[512,512]{1,0:T(8,128)(2,1)} %refs_5_.1) | copy-start | bytes 1572868
  39.2 17.2 %copy-start.3 = (bf16[512,512]{1,0:T(8,128)(2,1)S(1)}, bf16[512,512]{1,0:T(8,128)(2,1)}, u32[]{:S(2)}) copy-start(bf16[512,512]{1,0:T(8,128)(2,1)} %refs_7_.1) | copy-start | bytes 1572868
  39.2 17.2 %copy-start.5 = (bf16[512,512]{1,0:T(8,128)(2,1)S(1)}, bf16[512,512]{1,0:T(8,128)(2,1)}, u32[]{:S(2)}) copy-start(bf16[512,512]{1,0:T(8,128)(2,1)} %refs_4_.1) | copy-start | bytes 1572868
  64.5 3.0 %collective-permute-start.2 = (bf16[2,2,2,2,16,2048]{5,4,3,2,0,1:T(8,128)(2,1)}, bf16[2,2,2,2,16,2048]{5,4,3,2,0,1:T(8,128)(2,1)}, u32[]{:S(2)}, u32[]{:S(2)}) collective-permute-start(bf16[2,2,2,2,16,2048]{5,4,3,2,0,1:T(8,128)(2,1)} %bitcast.54), channel_id=1, source_target_pairs={{0,1},{1,0},{2,3},{3,2},{4,5},{5,4},{6,7},{7,6},{8,9},{9,8},{10,11... | collective-permute-start | bytes 3145736 | tf_op jit(solution)/shard_map/ppermute | solution.py:281
  64.9 6.8 %collective-permute-start.1 = (bf16[512,512]{1,0:T(8,128)(2,1)}, bf16[512,512]{1,0:T(8,128)(2,1)}, u32[]{:S(2)}, u32[]{:S(2)}) collective-permute-start(bf16[512,512]{1,0:T(8,128)(2,1)} %get-tuple-element.50), channel_id=1, source_target_pairs={{1,0},{2,1},{3,2},{4,3},{5,4},{6,5},{7,6},{9,8},{10,9},{11,10},{12... | collective-permute-start | bytes 1572872 | tf_op jit(solution)/shard_map/ppermute | solution.py:276
  70.7 13.8 %collective-permute-start.7 = (bf16[2,2,2,16,1024]{4,3,2,1,0:T(8,128)(2,1)S(1)}, bf16[2,2,2,16,1024]{4,3,2,1,0:T(8,128)(2,1)}, u32[]{:S(2)}, u32[]{:S(2)}) collective-permute-start(bf16[2,2,2,16,1024]{4,3,2,1,0:T(8,128)(2,1)S(1)} %dynamic-slice_bitcast_fusion), channel_id=1, source_target_pairs={{0,8},{1,9},{2,10},{3,11},{4,12},{5,13},{6,14},{7,15},{8,0},{9,1},... | collective-permute-start | bytes 786440 | tf_op jit(solution)/shard_map/ppermute | solution.py:281
  74.3 21.4 %copy-start.19 = (bf16[2,2,2,2,16,1024]{5,4,3,2,0,1:T(8,128)(2,1)S(1)}, bf16[2,2,2,2,16,1024]{5,4,3,2,0,1:T(8,128)(2,1)}, u32[]{:S(2)}) copy-start(bf16[2,2,2,2,16,1024]{5,4,3,2,0,1:T(8,128)(2,1)} %get-tuple-element.53) | copy-start | bytes 1572868
  74.3 38.9 %all-to-all-start.1 = ((bf16[32,16,512]{2,1,0:T(8,128)(2,1)}), bf16[32,16,512]{2,1,0:T(8,128)(2,1)S(1)}, u32[]{:S(2)}, u32[]{:S(2)}) async-start(bf16[32,16,512]{2,1,0:T(8,128)(2,1)} %bitcast.7), calls=%async_computation.1 | async-start | bytes 1048576 | tf_op jit(solution)/shard_map/all_to_all | solution.py:334
  82.7 13.0 %collective-permute-start.3 = (bf16[2,2,2,16,1024]{4,3,2,1,0:T(8,128)(2,1)S(1)}, bf16[2,2,2,16,1024]{4,3,2,1,0:T(8,128)(2,1)S(1)}, u32[]{:S(2)}, u32[]{:S(2)}) collective-permute-start(bf16[2,2,2,16,1024]{4,3,2,1,0:T(8,128)(2,1)S(1)} %dynamic-slice_bitcast_fusion.1), channel_id=1, source_target_pairs={{0,16},{1,17},{2,18},{3,19},{4,20},{5,21},{6,22},{7,23},{8,24},{9,... | collective-permute-start | bytes 786440 | tf_op jit(solution)/shard_map/ppermute | solution.py:281
  85.6 13.3 %collective-permute-start.8 = (bf16[2,2,16,1024]{3,2,1,0:T(8,128)(2,1)S(1)}, bf16[2,2,16,1024]{3,2,1,0:T(8,128)(2,1)S(1)}, u32[]{:S(2)}, u32[]{:S(2)}) collective-permute-start(bf16[2,2,16,1024]{3,2,1,0:T(8,128)(2,1)S(1)} %dynamic-slice_bitcast_fusion.2), channel_id=1, source_target_pairs={{0,16},{1,17},{2,18},{3,19},{4,20},{5,21},{6,22},{7,23},{8,24},{9,... | collective-permute-start | bytes 393224 | tf_op jit(solution)/shard_map/ppermute | solution.py:281
  95.7 5.6 %collective-permute-start.4 = (bf16[2,2,16,1024]{3,2,1,0:T(8,128)(2,1)S(1)}, bf16[2,2,16,1024]{3,2,1,0:T(8,128)(2,1)S(1)}, u32[]{:S(2)}, u32[]{:S(2)}) collective-permute-start(bf16[2,2,16,1024]{3,2,1,0:T(8,128)(2,1)S(1)} %dynamic-slice_bitcast_fusion.3), channel_id=1, source_target_pairs={{0,8},{1,9},{2,10},{3,11},{4,12},{5,13},{6,14},{7,15},{8,0},{9,1},... | collective-permute-start | bytes 393224 | tf_op jit(solution)/shard_map/ppermute | solution.py:281
  99.0 7.8 %collective-permute-start.9 = (bf16[2,16,1024]{2,1,0:T(8,128)(2,1)S(1)}, bf16[2,16,1024]{2,1,0:T(8,128)(2,1)S(1)}, u32[]{:S(2)}, u32[]{:S(2)}) collective-permute-start(bf16[2,16,1024]{2,1,0:T(8,128)(2,1)S(1)} %dynamic-slice_bitcast_fusion.4), channel_id=1, source_target_pairs={{0,4},{1,5},{2,6},{3,7},{4,0},{5,1},{6,2},{7,3},{8,12},{9,13},{10,... | collective-permute-start | bytes 196616 | tf_op jit(solution)/shard_map/ppermute | solution.py:281
  101.4 7.0 %collective-permute-start.5 = (bf16[2,16,1024]{2,1,0:T(8,128)(2,1)S(1)}, bf16[2,16,1024]{2,1,0:T(8,128)(2,1)S(1)}, u32[]{:S(2)}, u32[]{:S(2)}) collective-permute-start(bf16[2,16,1024]{2,1,0:T(8,128)(2,1)S(1)} %dynamic-slice_bitcast_fusion.5), channel_id=1, source_target_pairs={{0,4},{1,5},{2,6},{3,7},{4,0},{5,1},{6,2},{7,3},{8,12},{9,13},{10,... | collective-permute-start | bytes 196616 | tf_op jit(solution)/shard_map/ppermute | solution.py:281
  106.8 4.0 %collective-permute-start.10 = (bf16[16,1024]{1,0:T(8,128)(2,1)S(1)}, bf16[16,1024]{1,0:T(8,128)(2,1)S(1)}, u32[]{:S(2)}, u32[]{:S(2)}) collective-permute-start(bf16[16,1024]{1,0:T(8,128)(2,1)S(1)} %dynamic-slice_bitcast_fusion.6), channel_id=1, source_target_pairs={{0,2},{1,3},{2,0},{3,1},{4,6},{5,7},{6,4},{7,5},{8,10},{9,11},{10,... | collective-permute-start | bytes 98312 | tf_op jit(solution)/shard_map/ppermute | solution.py:281
  108.5 4.0 %collective-permute-start.6 = (bf16[16,1024]{1,0:T(8,128)(2,1)S(1)}, bf16[16,1024]{1,0:T(8,128)(2,1)S(1)}, u32[]{:S(2)}, u32[]{:S(2)}) collective-permute-start(bf16[16,1024]{1,0:T(8,128)(2,1)S(1)} %dynamic-slice_bitcast_fusion.7), channel_id=1, source_target_pairs={{0,2},{1,3},{2,0},{3,1},{4,6},{5,7},{6,4},{7,5},{8,10},{9,11},{10,... | collective-permute-start | bytes 98312 | tf_op jit(solution)/shard_map/ppermute | solution.py:281
  (10 other events, 9.3 us)
where the time goes:
time: 115 us; the launch traced here: 114 us
  Pallas kernels  32.1 us (28%)
  waiting for transfers between devices  30.5 us (27%)
  starting transfers between devices  28.5 us (25%)
  local copies, waits for them, and re-layouts  17.2 us (15%)
  other arithmetic  4.41 us (4%)
  between operations  1.58 us (1%)
    pallas_call x8, Pallas kernels, vmem_call(): pl.pallas_call(body, out_shape=tuple(outs), in_specs=specs, out_specs=tup...  32.1 us
    ppermute x9, waiting for transfers between devices, swap(): return lax.ppermute(shard, AXES, [(i, i ^ bit) for i in range(devices)])  19 us
    all_to_all x2, starting transfers between devices, exchanged(): lax.all_to_all(shard.reshape(devices, slots, width), AXES, split_axis=0,...  14.7 us
    unnamed x42, local copies, waits for them, and re-layouts  11.6 us
    all_to_all x2, waiting for transfers between devices, exchanged(): lax.all_to_all(shard.reshape(devices, slots, width), AXES, split_axis=0,...  11.5 us
    ppermute x9, starting transfers between devices, swap(): return lax.ppermute(shard, AXES, [(i, i ^ bit) for i in range(devices)])  10.6 us
    convert_element_type x7, other arithmetic, scatter_sums(): total = (keep.astype(F32) + got.astype(F32)).astype(BF)  3.65 us
    ppermute x2, starting transfers between devices, passed_along(): return lax.ppermute(shard, 'seq', pairs)  3.21 us
  transfers between devices with their start and end apart: 13, of which 8 were waited for; matrix products, arithmetic and copies ran while one was open for 7% of the time, Pallas kernels for 5%

commit v1 on v0

--- a/solution.py
+++ b/solution.py
@@ -27,7 +27,7 @@
     return lax.broadcasted_iota(jnp.int32, shape, dim)
 
 
-def vmem_call(body, outs, args, smem=(), scratch=(), flops=0, limit=32):
+def vmem_call(body, outs, args, smem=(), scratch=(), flops=0, limit=12):
     specs = [
         pl.BlockSpec(memory_space=pltpu.SMEM if i in smem else pltpu.VMEM)
         for i in range(len(args))
@@ -238,19 +238,29 @@
 
 
 def weights_body(
-    scale, normed_ref, halo_ref, frames_ref, cot_ref, wq_ref, wk_ref, wv_ref, wo_ref,
+    scale, rows, meta_ref, normed_ref, halo_ref, frames_ref, cot_ref, wq_ref, wk_ref, wv_ref, wo_ref,
     ot_ref, dqt_ref, dk_ref, dv_ref, dkh_ref, dvh_ref,
-    sums_ref, out_ref, slope_ref,
+    keep_ref, send_ref, out_ref, slope_ref,
+    normed_t, halo_t, mixed_t,
 ):
-    width = wq_ref.shape[0]
-    normed_t = normed_ref[...].T
-    halo_t = halo_ref[...].T
-    sums_ref[:, :width] = (mm(normed_t, dqt_ref[...], NT) * scale).astype(BF)
-    own = mm(normed_t, dk_ref[...]) + mm(halo_t, dkh_ref[...])
-    sums_ref[:, width : 2 * width] = (own * scale).astype(BF)
-    own = mm(normed_t, dv_ref[...]) + mm(halo_t, dvh_ref[...])
-    sums_ref[:, 2 * width : 3 * width] = (own * scale).astype(BF)
-    sums_ref[:, 3 * width :] = (mm(ot_ref[...], cot_ref[...]) * scale).astype(BF)
+    width, span = ot_ref.shape
+    chunks = width // (2 * rows)
+    split = (chunks, 2, rows, span)
+    normed_t[...] = normed_ref[...].T.reshape(split)
+    halo_t[...] = halo_ref[...].T.reshape(split)
+    mixed_t[...] = ot_ref[...].reshape(split)
+    mine = meta_ref[2]
+    for side, out in ((1 - mine, send_ref), (mine, keep_ref)):
+        own = normed_t[:, side].reshape(width // 2, span)
+        far = halo_t[:, side].reshape(width // 2, span)
+        mixed = mixed_t[:, side].reshape(width // 2, span)
+        for n, total in enumerate((
+            mm(own, dqt_ref[...], NT),
+            mm(own, dk_ref[...]) + mm(far, dkh_ref[...]),
+            mm(own, dv_ref[...]) + mm(far, dvh_ref[...]),
+            mm(mixed, cot_ref[...]),
+        )):
+            out[:, n * width : (n + 1) * width] = (total * scale).astype(BF)
     slope = mm(dqt_ref[...].T, wq_ref[...], NT)
     slope = slope + mm(dk_ref[...], wk_ref[...], NT)
     slope_ref[...] = slope + mm(dv_ref[...], wv_ref[...], NT)
@@ -276,42 +286,23 @@
     return lax.ppermute(shard, "seq", pairs)
 
 
-def swap(shard, bit):
-    devices = lax.axis_size(AXES)
-    return lax.ppermute(shard, AXES, [(i, i ^ bit) for i in range(devices)])
-
-
-def halve(sums, place, bits, bit):
-    dim = bits.index(bit)
-    mine = (place >> (bit.bit_length() - 1)) & 1
-    keep = lax.dynamic_index_in_dim(sums, mine, dim, keepdims=False)
-    send = lax.dynamic_index_in_dim(sums, 1 - mine, dim, keepdims=False)
-    return keep, swap(send, bit), bits[:dim] + bits[dim + 1 :]
-
-
-def scatter_sums(sums):
-    devices = lax.axis_size(AXES)
-    place = lax.axis_index(AXES)
-    rows, columns = sums.shape
-    bits = [1 << n for n in reversed(range(devices.bit_length() - 1))]
-    sums = sums.reshape([2] * len(bits) + [rows // devices, columns])
-    keep, got, left = halve(sums, place, bits, 1)
-    half = columns // 2
-    lanes = []
-    for lane in range(2):
-        at = slice(lane * half, (lane + 1) * half)
-        order = list(left)
-        if lane:
-            order[0], order[1] = order[1], order[0]
-        lanes.append([keep[..., at], got[..., at], left, order])
-    while lanes[0][3]:
-        for lane in lanes:
-            keep, got, left, order = lane
-            total = (keep.astype(F32) + got.astype(F32)).astype(BF)
-            lane[:3] = halve(total, place, left, order[0])
-            lane[3] = order[1:]
-    parts = [keep.astype(F32) + got.astype(F32) for keep, got, _, _ in lanes]
-    return jnp.concatenate(parts, axis=1)
+def summed(shard, axis, groups=None):
+    got = lax.all_to_all(
+        shard, axis, split_axis=0, concat_axis=0, axis_index_groups=groups, tiled=True
+    )
+    return jnp.sum(got.astype(F32), axis=0)
+
+
+def scatter_sums(keep, send):
+    devices, seqs = lax.axis_size(AXES), lax.axis_size("seq")
+    streams, chips = devices // seqs, seqs // 2
+    columns = keep.shape[1]
+    rows = keep.shape[0] // (streams * chips)
+    got = lax.ppermute(send, "seq", [(i, i ^ 1) for i in range(seqs)])
+    total = (keep.astype(F32) + got.astype(F32)).astype(BF)
+    total = summed(total.reshape(streams, chips * rows, columns), "stream").astype(BF)
+    groups = [list(range(core, seqs, 2)) for core in range(2)]
+    return summed(total.reshape(chips, rows, columns), "seq", groups)
 
 
 def shards(
@@ -327,7 +318,10 @@
     cube = 2 * span * width * width
     square = sds((span, width))
     begin = (lax.axis_index("seq") * span).astype(jnp.int32)
-    meta = jnp.stack([begin, lengths[0]])
+    rows = width // devices
+    in_kernel = rows % 16 == 0
+    core = (lax.axis_index("seq") & 1).astype(jnp.int32)
+    meta = jnp.stack([begin, lengths[0], core if in_kernel else jnp.zeros((), jnp.int32)])
     cot = cotangent[0]
 
     def exchanged(shard):
@@ -370,22 +364,33 @@
             pltpu.VMEM((width, WIN + span), BF),
         ],
         flops=20 * cube,
-        limit=40,
+        limit=22,
     )
     extra = passed_along(back, -1)
-    sums, out_frames, slope = vmem_call(
-        lambda *refs: weights_body(slab ** (-0.5), *refs),
-        [sds((width, 4 * width)), square, sds((span, width), F32)],
-        [normed, halo, frames, cot, query_weight, key_weight, value_weight, out_weight,
+    chunk = rows if in_kernel else width // 2
+    split = pltpu.VMEM((width // (2 * chunk), 2, chunk, span), BF)
+    half = sds((width // 2, 4 * width))
+    keep, send, out_frames, slope = vmem_call(
+        lambda *refs: weights_body(slab ** (-0.5), chunk, *refs),
+        [half, half, square, sds((span, width), F32)],
+        [meta, normed, halo, frames, cot, query_weight, key_weight, value_weight, out_weight,
          ot, dqt, dk, dv, dkh, dvh],
+        smem=(0,),
+        scratch=[split, split, split],
         flops=10 * cube,
-    )
+        limit=20,
+    )
+    send, extra = lax.optimization_barrier((send, extra))
+    if not in_kernel:
+        sums = jnp.concatenate([keep, send], axis=0).reshape(-1, 2, rows, 4 * width)
+        keep = lax.dynamic_index_in_dim(sums, core, 1, keepdims=False).reshape(half.shape)
+        send = lax.dynamic_index_in_dim(sums, 1 - core, 1, keepdims=False).reshape(half.shape)
     returning, = vmem_call(
         returning_body, [square], [frames, slope, extra, cot, pick_t], flops=cube
     )
     arrived = exchanged(returning)
     frame_grads, = vmem_call(arrived_body, [square], [placing_t, arrived], flops=cube)
-    weight_grads = scatter_sums(sums)
+    weight_grads = scatter_sums(keep, send)
     return (out_frames[None], frame_grads, weight_grads)
 
 

time: 115 us -> 120 us (1.043)
  waiting for transfers between devices: 30.5 us -> 48.6 us
  local copies, waits for them, and re-layouts: 17.2 us -> 9.74 us
  starting transfers between devices: 28.5 us -> 24.9 us
  Pallas kernels: 32.1 us -> 30.5 us
    all_to_all x0 -> x2, waiting for transfers between devices: none -> 19.9 us  [summed(): lax.all_to_all(shard, axis, split_axis=0, concat_axis=0, axis_index_group...]
    ppermute x9 -> x1, waiting for transfers between devices: 19 us -> 2.29 us  [scatter_sums(): got = lax.ppermute(send, 'seq', [(i, i ^ 1) for i in range(seqs)])]
    all_to_all x2, waiting for transfers between devices: 11.5 us -> 26.4 us  [exchanged(): lax.all_to_all(shard.reshape(devices, slots, width), AXES, split_axis=0,...]
    all_to_all x0 -> x2, starting transfers between devices: none -> 7.64 us  [summed(): lax.all_to_all(shard, axis, split_axis=0, concat_axis=0, axis_index_group...]
    ppermute x9 -> x1, starting transfers between devices: 10.6 us -> 4.1 us  [scatter_sums(): got = lax.ppermute(send, 'seq', [(i, i ^ 1) for i in range(seqs)])]
    all_to_all x2, starting transfers between devices: 14.7 us -> 9.9 us  [exchanged(): lax.all_to_all(shard.reshape(devices, slots, width), AXES, split_axis=0,...]
    dynamic_slice x3 -> x0, local copies, waits for them, and re-layouts: 3.65 us -> none  [the longest x2 2.54 us: halve(): keep = lax.dynamic_index_in_dim(sums, mine, dim, keepdims=False)]
    reduce_sum x0 -> x2, other arithmetic: none -> 2.85 us  [summed(): return jnp.sum(got.astype(F32), axis=0)]
  transfers between devices with their start and end apart: 13 -> 7, of which waited for: 8 -> 5; matrix products, arithmetic and copies ran while one was open for 7% -> 2% of each run, Pallas kernels for 5% -> 9%
where the time goes in v1:
time: 120 us
  waiting for transfers between devices  48.6 us (40%)
  Pallas kernels  30.5 us (25%)
  starting transfers between devices  24.9 us (21%)
  local copies, waits for them, and re-layouts  9.74 us (8%)
  other arithmetic  4.29 us (4%)
  between operations  1.54 us (1%)
    pallas_call x8, Pallas kernels, vmem_call(): pl.pallas_call(body, out_shape=tuple(outs), in_specs=specs, out_specs=tup...  30.5 us
    all_to_all x2, waiting for transfers between devices, exchanged(): lax.all_to_all(shard.reshape(devices, slots, width), AXES, split_axis=0,...  26.4 us
    all_to_all x2, waiting for transfers between devices, summed(): lax.all_to_all(shard, axis, split_axis=0, concat_axis=0, axis_index_group...  19.9 us
    all_to_all x2, starting transfers between devices, exchanged(): lax.all_to_all(shard.reshape(devices, slots, width), AXES, split_axis=0,...  9.9 us
    unnamed x44, local copies, waits for them, and re-layouts  9.59 us
    all_to_all x2, starting transfers between devices, summed(): lax.all_to_all(shard, axis, split_axis=0, concat_axis=0, axis_index_group...  7.64 us
    ppermute x1, starting transfers between devices, scatter_sums(): got = lax.ppermute(send, 'seq', [(i, i ^ 1) for i in range(seqs)])  4.1 us
    ppermute x2, starting transfers between devices, passed_along(): return lax.ppermute(shard, 'seq', pairs)  3.23 us
  transfers between devices with their start and end apart: 7, of which 5 were waited for; matrix products, arithmetic and copies ran while one was open for 2% of the time, Pallas kernels for 9%

profile of v1, /device:TPU:0, one launch (start us, length us, event | category | flops | bytes accessed | tf_op | source)
XLA Modules:
  0.0 119.6 jit_solution(12252832450364595204)
XLA Ops:
  2.4 1.4 %shard_map.112 = (bf16[512,512]{1,0:T(8,128)(2,1)}, bf16[512,512]{1,0:T(8,128)(2,1)S(1)}) custom-call(s32[1,512]{1,0:T(1,128)S(1)} %bitcast.17, bf16[512,512]{1,0:T(8,128)(2,1)S(1)} %copy-done.3), custom_call_target="tpu_custom_call" | custom-call | flops 268435456 | bytes 1574912 | tf_op jit(solution)/shard_map/pallas_call | solution.py:36
  3.7 7.3 %all-to-all-start = ((bf16[32,16,512]{2,1,0:T(8,128)(2,1)}), bf16[32,16,512]{2,1,0:T(8,128)(2,1)S(1)}, u32[]{:S(2)}, u32[]{:S(2)}) async-start(bf16[32,16,512]{2,1,0:T(8,128)(2,1)} %bitcast.5), calls=%async_computation | async-start | bytes 1048576 | tf_op jit(solution)/shard_map/all_to_all | solution.py:328
  12.3 1.3 %shard_map.113 = (bf16[512,512]{1,0:T(8,128)(2,1)S(1)}, bf16[512,512]{1,0:T(8,128)(2,1)S(1)}, bf16[512,512]{1,0:T(8,128)(2,1)S(1)}, bf16[512,512]{1,0:T(8,128)(2,1)S(1)}, bf16[512,512]{1,0:T(8,128)(2,1)S(1)}) custom-call(s32[512,1]{1,0:T(8,128)S(1)} %copy.13.refs_0_, bf16[512,512]{1,0:T(8,128)(2,1)S(1)} %copy-done.20, bf16[512,512]{1,0:T(8,128)(2,1)S(1)} %bitcast.14, ...), custom_call_target="tpu_custom_call" | custom-call | flops 536870912 | bytes 4196352 | tf_op jit(solution)/shard_map/pallas_call | solution.py:36
  15.2 12.2 %all-to-all-done = bf16[32,16,512]{2,1,0:T(8,128)(2,1)S(1)} async-done(((bf16[32,16,512]{2,1,0:T(8,128)(2,1)}), bf16[32,16,512]{2,1,0:T(8,128)(2,1)S(1)}, u32[]{:S(2)}, u32[]{:S(2)}) %all-to-all-start) | async-done | bytes 524320 | tf_op jit(solution)/shard_map/all_to_all | solution.py:328
  27.4 1.4 %shard_map.114 = (bf16[512,512]{1,0:T(8,128)(2,1)S(1)}, bf16[512,512]{1,0:T(8,128)(2,1)}) custom-call(bf16[512,512]{1,0:T(8,128)(2,1)S(1)} %get-tuple-element.32.pick_ref, bf16[512,512]{1,0:T(8,128)(2,1)S(1)} %bitcast.13), custom_call_target="tpu_custom_call" | custom-call | flops 268435456 | bytes 2097152 | tf_op jit(solution)/shard_map/pallas_call | solution.py:36
  28.8 1.9 %collective-permute-start = (bf16[512,512]{1,0:T(8,128)(2,1)}, bf16[512,512]{1,0:T(8,128)(2,1)S(1)}, u32[]{:S(2)}, u32[]{:S(2)}) collective-permute-start(bf16[512,512]{1,0:T(8,128)(2,1)} %get-tuple-element.34.refs_0_.refs_1_), channel_id=1, source_target_pairs={{0,1},{1,2},{2,3},{3,4},{4,5},{5,6},{6,7},{8,9},{9,10},{10,11},{11... | collective-permute-start | bytes 1572872 | tf_op jit(solution)/shard_map/ppermute | solution.py:286
  31.5 1.0 copy-done.6
  32.5 1.0 copy-done.8
  34.6 2.2 %shard_map.115 = (bf16[512,512]{1,0:T(8,128)(2,1)S(1)}, bf16[512,512]{1,0:T(8,128)(2,1)S(1)}, bf16[512,512]{1,0:T(8,128)(2,1)S(1)}, bf16[512,512]{1,0:T(8,128)(2...) custom-call(bf16[512,512]{1,0:T(8,128)(2,1)} %get-tuple-element.34.refs_0_.refs_1_, ...), custom_call_target="tpu_custom_call" | custom-call | flops 805306368 | bytes 5242880 | tf_op jit(solution)/shard_map/pallas_call | solution.py:36
  37.0 16.4 %shard_map.116 = (bf16[512,512]{1,0:T(8,128)(2,1)S(1)}, bf16[512,512]{1,0:T(8,128)(2,1)S(1)}, bf16[512,512]{1,0:T(8,128)(2,1)S(1)}, bf16[512,512]{1,0:T(8,128)(2...) custom-call(s32[3]{0:T(128)S(1)} %pad_add_fusion.refs_0_, ...), custom_call_target="tpu_custom_call" | custom-call | flops 5368709120 | bytes 9437196 | tf_op jit(solution)/shard_map/pallas_call | solution.py:36
  53.4 1.3 %collective-permute-start.1 = (bf16[512,512]{1,0:T(8,128)(2,1)S(1)}, bf16[512,512]{1,0:T(8,128)(2,1)S(1)}, u32[]{:S(2)}, u32[]{:S(2)}) collective-permute-start(bf16[512,512]{1,0:T(8,128)(2,1)S(1)} %get-tuple-element.54), channel_id=1, source_target_pairs={{1,0},{2,1},{3,2},{4,3},{5,4},{6,5},{7,6},{9,8},{10,9},{11,10},{12... | collective-permute-start | bytes 1572872 | tf_op jit(solution)/shard_map/ppermute | solution.py:286
  55.8 4.9 %shard_map.117 = (bf16[256,2048]{1,0:T(8,128)(2,1)S(1)}, bf16[256,2048]{1,0:T(8,128)(2,1)S(1)}, bf16[512,512]{1,0:T(8,128)(2,1)}, f32[512,512]{1,0:T(8,128)S(1)}) custom-call(s32[3]{0:T(128)S(1)} %pad_add_fusion.refs_0_, bf16[512,512]{1,0:T(8,128)(2,1)} %get-tuple-element.34.refs_0_.refs_1_, bf16[512,512]{1,0:T(8,128)(2,1)S(1)} %copy-done.13, ...), custom_call_target="tpu_custom_call" | custom-call | flops 2684354560 | bytes 11010060 | tf_op jit(solution)/shard_map/pallas_call | solution.py:36
  60.7 4.1 %collective-permute-start.2 = (bf16[256,2048]{1,0:T(8,128)(2,1)S(1)}, bf16[256,2048]{1,0:T(8,128)(2,1)S(1)}, u32[]{:S(2)}, u32[]{:S(2)}) collective-permute-start(bf16[256,2048]{1,0:T(8,128)(2,1)S(1)} %get-tuple-element.58), channel_id=1, source_target_pairs={{0,1},{1,0},{2,3},{3,2},{4,5},{5,4},{6,7},{7,6},{8,9},{9,8},{10,11... | collective-permute-start | bytes 3145736 | tf_op jit(solution)/shard_map/ppermute | solution.py:301
  64.8 2.3 %collective-permute-done.2 = bf16[256,2048]{1,0:T(8,128)(2,1)S(1)} collective-permute-done((bf16[256,2048]{1,0:T(8,128)(2,1)S(1)}, bf16[256,2048]{1,0:T(8,128)(2,1)S(1)}, u32[]{:S(2)}, u32[]{:S(2)}) %collective-permute-start.2) | collective-permute-done | bytes 1048608 | tf_op jit(solution)/shard_map/ppermute | solution.py:301
  67.1 1.4 %add_convert_fusion = bf16[256,2048]{1,0:T(8,128)(2,1)} fusion(bf16[256,2048]{1,0:T(8,128)(2,1)S(1)} %collective-permute-done.2, bf16[256,2048]{1,0:T(8,128)(2,1)S(1)} %get-tuple-element.57), kind=kLoop, calls=%fused_computation | loop fusion | flops 2097152 | bytes 3145728 | tf_op jit(solution)/shard_map/convert_element_type | solution.py:302
  68.4 4.2 %all-to-all-start.2 = ((bf16[4,64,2048]{2,1,0:T(8,128)(2,1)}), bf16[4,64,2048]{2,1,0:T(8,128)(2,1)}, u32[]{:S(2)}, u32[]{:S(2)}) async-start(bf16[4,64,2048]{2,1,0:T(8,128)(2,1)} %bitcast.18), calls=%async_computation.2 | async-start | bytes 2097152 | tf_op jit(solution)/shard_map/all_to_all | solution.py:290
  73.7 1.6 %shard_map.118 = bf16[512,512]{1,0:T(8,128)(2,1)} custom-call(bf16[512,512]{1,0:T(8,128)(2,1)S(1)} %get-tuple-element.35.refs_3_.frames_ref, f32[512,512]{1,0:T(8,128)S(1)} %get-tuple-element.52.slope_ref, bf16[512,512]{1,0:T(8,128)(2,1)S(1)} %copy-done.2, bf16[512,512]{1,0:T(8,128)(2,1)S(1)} %bitcast.16, bf16[512,512]{1,0:T(8,128)(2,1)S(1)} %get-tuple-element.56.pick_t_ref), custom_call_target="tpu_custom_call" | custom-call | flops 268435456 | bytes 3670016 | tf_op jit(solution)/shard_map/pallas_call | solution.py:36
  75.3 11.9 %all-to-all-done.2 = bf16[4,64,2048]{2,1,0:T(8,128)(2,1)} async-done(((bf16[4,64,2048]{2,1,0:T(8,128)(2,1)}), bf16[4,64,2048]{2,1,0:T(8,128)(2,1)}, u32[]{:S(2)}, u32[]{:S(2)}) %all-to-all-start.2) | async-done | bytes 1048608 | tf_op jit(solution)/shard_map/all_to_all | solution.py:290
  87.2 2.6 %all-to-all-start.1 = ((bf16[32,16,512]{2,1,0:T(8,128)(2,1)}), bf16[32,16,512]{2,1,0:T(8,128)(2,1)S(1)}, u32[]{:S(2)}, u32[]{:S(2)}) async-start(bf16[32,16,512]{2,1,0:T(8,128)(2,1)} %bitcast.8), calls=%async_computation.1 | async-start | bytes 1048576 | tf_op jit(solution)/shard_map/all_to_all | solution.py:328
  89.8 2.2 %reduce_sum.21 = bf16[64,2048]{1,0:T(8,128)(2,1)} reduce(bf16[4,64,2048]{2,1,0:T(8,128)(2,1)} %all-to-all-done.2, bf16[]{:T(256)} %constant.10.clone.1), dimensions={0}, to_apply=%region_0.0 | reduce | flops 393216 | bytes 1310722 | tf_op jit(solution)/shard_map/reduce_sum | solution.py:293
  92.0 14.2 %all-to-all-done.1 = bf16[32,16,512]{2,1,0:T(8,128)(2,1)S(1)} async-done(((bf16[32,16,512]{2,1,0:T(8,128)(2,1)}), bf16[32,16,512]{2,1,0:T(8,128)(2,1)S(1)}, u32[]{:S(2)}, u32[]{:S(2)}) %all-to-all-start.1) | async-done | bytes 524320 | tf_op jit(solution)/shard_map/all_to_all | solution.py:328
  106.2 3.4 %all-to-all-start.3 = ((bf16[4,16,2048]{2,1,0:T(8,128)(2,1)}), bf16[4,16,2048]{2,1,0:T(8,128)(2,1)S(1)}, u32[]{:S(2)}, u32[]{:S(2)}) async-start(bf16[4,16,2048]{2,1,0:T(8,128)(2,1)} %bitcast.11), calls=%async_computation.3 | async-start | bytes 524288 | tf_op jit(solution)/shard_map/all_to_all | solution.py:290
  109.6 1.2 %shard_map.119 = bf16[512,512]{1,0:T(8,128)(2,1)} custom-call(bf16[512,512]{1,0:T(8,128)(2,1)S(1)} %get-tuple-element.51.placing_t_ref, bf16[512,512]{1,0:T(8,128)(2,1)S(1)} %bitcast.12), custom_call_target="tpu_custom_call" | custom-call | flops 268435456 | bytes 1572864 | tf_op jit(solution)/shard_map/pallas_call | solution.py:36
  110.8 8.1 %all-to-all-done.3 = bf16[4,16,2048]{2,1,0:T(8,128)(2,1)S(1)} async-done(((bf16[4,16,2048]{2,1,0:T(8,128)(2,1)}), bf16[4,16,2048]{2,1,0:T(8,128)(2,1)S(1)}, u32[]{:S(2)}, u32[]{:S(2)}) %all-to-all-start.3) | async-done | bytes 262176 | tf_op jit(solution)/shard_map/all_to_all | solution.py:290
  (47 shorter events, 8.4 us)
Async XLA Ops:
  0.6 1.0 copy-start.3
  2.4 8.7 %copy-start.21 = (s32[1,512]{1,0:T(1,128)S(1)}, s32[1,512]{1,0:T(1,128)}, u32[]{:S(2)}) copy-start(s32[1,512]{1,0:T(1,128)} %param.11) | copy-start | bytes 6148
  2.4 8.9 %copy-start = (bf16[1,512,512]{2,1,0:T(8,128)(2,1)S(1)}, bf16[1,512,512]{2,1,0:T(8,128)(2,1)}, u32[]{:S(2)}) copy-start(bf16[1,512,512]{2,1,0:T(8,128)(2,1)} %param.17) | copy-start | bytes 1572868
  2.4 8.9 %copy-start.4 = (bf16[512,512]{1,0:T(8,128)(2,1)S(1)}, bf16[512,512]{1,0:T(8,128)(2,1)}, u32[]{:S(2)}) copy-start(bf16[512,512]{1,0:T(8,128)(2,1)} %refs_8_.1) | copy-start | bytes 1572868
  3.7 7.5 %copy-start.19 = (bf16[512,512]{1,0:T(8,128)(2,1)}, bf16[512,512]{1,0:T(8,128)(2,1)S(1)}, u32[]{:S(2)}) copy-start(bf16[512,512]{1,0:T(8,128)(2,1)S(1)} %get-tuple-element.31.refs_1_) | copy-start | bytes 1572868
  3.7 23.7 %all-to-all-start = ((bf16[32,16,512]{2,1,0:T(8,128)(2,1)}), bf16[32,16,512]{2,1,0:T(8,128)(2,1)S(1)}, u32[]{:S(2)}, u32[]{:S(2)}) async-start(bf16[32,16,512]{2,1,0:T(8,128)(2,1)} %bitcast.5), calls=%async_computation | async-start | bytes 1048576 | tf_op jit(solution)/shard_map/all_to_all | solution.py:328
  11.2 1.0 copy-start.20
  28.8 8.1 %collective-permute-start = (bf16[512,512]{1,0:T(8,128)(2,1)}, bf16[512,512]{1,0:T(8,128)(2,1)S(1)}, u32[]{:S(2)}, u32[]{:S(2)}) collective-permute-start(bf16[512,512]{1,0:T(8,128)(2,1)} %get-tuple-element.34.refs_0_.refs_1_), channel_id=1, source_target_pairs={{0,1},{1,2},{2,3},{3,4},{4,5},{5,6},{6,7},{8,9},{9,10},{10,11},{11... | collective-permute-start | bytes 1572872 | tf_op jit(solution)/shard_map/ppermute | solution.py:286
  31.5 1.0 copy-start.6
  34.6 2.3 %copy-start.9 = (bf16[512,512]{1,0:T(8,128)(2,1)S(1)}, bf16[512,512]{1,0:T(8,128)(2,1)}, u32[]{:S(2)}) copy-start(bf16[512,512]{1,0:T(8,128)(2,1)} %refs_6_.1) | copy-start | bytes 1572868
  34.6 2.3 %copy-start.11 = (bf16[512,512]{1,0:T(8,128)(2,1)S(1)}, bf16[512,512]{1,0:T(8,128)(2,1)}, u32[]{:S(2)}) copy-start(bf16[512,512]{1,0:T(8,128)(2,1)} %refs_7_.1) | copy-start | bytes 1572868
  34.6 2.3 %copy-start.16 = (bf16[512,512]{1,0:T(8,128)(2,1)S(1)}, bf16[512,512]{1,0:T(8,128)(2,1)}, u32[]{:S(2)}) copy-start(bf16[512,512]{1,0:T(8,128)(2,1)} %copy-done.15) | copy-start | bytes 1572868
  34.6 2.3 %copy-start.18 = (bf16[512,512]{1,0:T(8,128)(2,1)S(1)}, bf16[512,512]{1,0:T(8,128)(2,1)}, u32[]{:S(2)}) copy-start(bf16[512,512]{1,0:T(8,128)(2,1)} %copy-done.17) | copy-start | bytes 1572868
  36.9 16.5 %copy-start.12 = (bf16[512,512]{1,0:T(8,128)(2,1)}, bf16[512,512]{1,0:T(8,128)(2,1)S(1)}, u32[]{:S(2)}) copy-start(bf16[512,512]{1,0:T(8,128)(2,1)S(1)} %collective-permute-done.refs_1_.refs_2_) | copy-start | bytes 1572868
  36.9 17.8 %copy-start.5 = (bf16[512,512]{1,0:T(8,128)(2,1)S(1)}, bf16[512,512]{1,0:T(8,128)(2,1)}, u32[]{:S(2)}) copy-start(bf16[512,512]{1,0:T(8,128)(2,1)} %refs_8_.1) | copy-start | bytes 1572868
  36.9 17.8 %copy-start.7 = (bf16[512,512]{1,0:T(8,128)(2,1)S(1)}, bf16[512,512]{1,0:T(8,128)(2,1)}, u32[]{:S(2)}) copy-start(bf16[512,512]{1,0:T(8,128)(2,1)} %refs_5_.1) | copy-start | bytes 1572868
  53.4 7.3 %collective-permute-start.1 = (bf16[512,512]{1,0:T(8,128)(2,1)S(1)}, bf16[512,512]{1,0:T(8,128)(2,1)S(1)}, u32[]{:S(2)}, u32[]{:S(2)}) collective-permute-start(bf16[512,512]{1,0:T(8,128)(2,1)S(1)} %get-tuple-element.54), channel_id=1, source_target_pairs={{1,0},{2,1},{3,2},{4,3},{5,4},{6,5},{7,6},{9,8},{10,9},{11,10},{12... | collective-permute-start | bytes 1572872 | tf_op jit(solution)/shard_map/ppermute | solution.py:286
  54.7 1.0 copy-start.13
  60.7 7.8 %copy-start.1 = (bf16[512,512]{1,0:T(8,128)(2,1)}, bf16[512,512]{1,0:T(8,128)(2,1)S(1)}, u32[]{:S(2)}) copy-start(bf16[512,512]{1,0:T(8,128)(2,1)S(1)} %collective-permute-done.1.extra_ref) | copy-start | bytes 1572868
  60.7 6.4 %collective-permute-start.2 = (bf16[256,2048]{1,0:T(8,128)(2,1)S(1)}, bf16[256,2048]{1,0:T(8,128)(2,1)S(1)}, u32[]{:S(2)}, u32[]{:S(2)}) collective-permute-start(bf16[256,2048]{1,0:T(8,128)(2,1)S(1)} %get-tuple-element.58), channel_id=1, source_target_pairs={{0,1},{1,0},{2,3},{3,2},{4,5},{5,4},{6,7},{7,6},{8,9},{9,8},{10,11... | collective-permute-start | bytes 3145736 | tf_op jit(solution)/shard_map/ppermute | solution.py:301
  68.4 18.8 %all-to-all-start.2 = ((bf16[4,64,2048]{2,1,0:T(8,128)(2,1)}), bf16[4,64,2048]{2,1,0:T(8,128)(2,1)}, u32[]{:S(2)}, u32[]{:S(2)}) async-start(bf16[4,64,2048]{2,1,0:T(8,128)(2,1)} %bitcast.18), calls=%async_computation.2 | async-start | bytes 2097152 | tf_op jit(solution)/shard_map/all_to_all | solution.py:290
  72.7 1.0 copy-start.2
  87.2 19.0 %all-to-all-start.1 = ((bf16[32,16,512]{2,1,0:T(8,128)(2,1)}), bf16[32,16,512]{2,1,0:T(8,128)(2,1)S(1)}, u32[]{:S(2)}, u32[]{:S(2)}) async-start(bf16[32,16,512]{2,1,0:T(8,128)(2,1)} %bitcast.8), calls=%async_computation.1 | async-start | bytes 1048576 | tf_op jit(solution)/shard_map/all_to_all | solution.py:328
  106.2 12.7 %all-to-all-start.3 = ((bf16[4,16,2048]{2,1,0:T(8,128)(2,1)}), bf16[4,16,2048]{2,1,0:T(8,128)(2,1)S(1)}, u32[]{:S(2)}, u32[]{:S(2)}) async-start(bf16[4,16,2048]{2,1,0:T(8,128)(2,1)} %bitcast.11), calls=%async_computation.3 | async-start | bytes 524288 | tf_op jit(solution)/shard_map/all_to_all | solution.py:290
  (5 other events, 4.4 us)

commit v2 on v1

v2 whole, which is shorter than its diff:
```python
import math

import jax
import jax.numpy as jnp
from jax import lax
from jax.experimental import pallas as pl
from jax.experimental.pallas import tpu as pltpu
from jax.sharding import PartitionSpec as P

H = 8
WIN = 512
NEG = -1e30
EPS_NORM = 1e-06
AXES = ("stream", "seq")
BF = jnp.bfloat16
F32 = jnp.float32

NN = (((1,), (0,)), ((), ()))
NT = (((1,), (1,)), ((), ()))


def mm(a, b, dims=NN):
    return lax.dot_general(a, b, dims, preferred_element_type=F32)


def iota2(shape, dim):
    return lax.broadcasted_iota(jnp.int32, shape, dim)


def vmem_call(body, outs, args, smem=(), hbm=(), scratch=(), flops=0, limit=12):
    spaces = [pltpu.SMEM if i in smem else pltpu.HBM if i in hbm else pltpu.VMEM for i in range(len(args))]
    size = sum(math.prod(a.shape) * a.dtype.itemsize for a in list(args) + list(outs))
    return pl.pallas_call(
        body,
        out_shape=tuple(outs),
        in_specs=[pl.BlockSpec(memory_space=space) for space in spaces],
        out_specs=tuple(pl.BlockSpec(memory_space=pltpu.VMEM) for _ in outs),
        scratch_shapes=list(scratch),
        compiler_params=pltpu.CompilerParams(vmem_limit_bytes=limit * 2**20),
        cost_estimate=pl.CostEstimate(flops=flops, bytes_accessed=size, transcendentals=0),
    )(*args)


def fetch(sources, targets, sems):
    copies = [
        pltpu.make_async_copy(source, target, sems.at[n])
        for n, (source, target) in enumerate(zip(sources, targets))
    ]
    for copy in copies:
        copy.start()
    return copies


def sds(shape, dtype=BF):
    return jax.ShapeDtypeStruct(shape, dtype)


def outgoing_body(span, slots, rf_ref, rows_hbm, out_ref, placing_ref, rows_ref, sems):
    (rows_copy,) = fetch([rows_hbm], [rows_ref], sems)
    count = rf_ref.shape[1]
    total = out_ref.shape[0]
    rf = rf_ref[...]
    target = jnp.where(rf >= 0, lax.div(rf, span), 1 << 20)
    slot = iota2((total, count), 0)
    owner = lax.div(slot, slots)
    rank = slot - owner * slots
    start = jnp.sum(jnp.where(target < owner, 1.0, 0.0), axis=1, keepdims=True)
    here = iota2((total, count), 1) - start.astype(jnp.int32)
    placing = jnp.where((target == owner) & (here == rank), 1.0, 0.0).astype(BF)
    placing_ref[...] = placing
    rows_copy.wait()
    out_ref[...] = mm(placing, rows_ref[...]).astype(BF)


def early_body(
    slots, owner_ref, placing_ref, cot_ref, wo_ref, pick_ref, pick_t_ref, placing_t_ref, do_ref, dot_ref
):
    span, lanes = owner_ref.shape[0], 128
    total = pick_ref.shape[1]
    owner = owner_ref[...]
    device = iota2((span, lanes), 1)
    hot = jnp.where(owner == device, 1.0, 0.0)
    strict = jnp.where(iota2((span, span), 1) < iota2((span, span), 0), 1.0, 0.0).astype(BF)
    before = mm(strict, hot.astype(BF))
    slot = jnp.sum(hot * (before + (device * slots).astype(F32)), axis=1, keepdims=True)
    slot = jnp.where(owner >= 0, slot.astype(jnp.int32), -1)
    pick = jnp.where(iota2((span, total), 1) == slot, 1.0, 0.0)
    pick_ref[...] = pick.astype(BF)
    pick_t_ref[...] = pick.T.astype(BF)
    placing_t_ref[...] = placing_ref[...].T
    grad = mm(cot_ref[...], wo_ref[...], NT).astype(BF)
    do_ref[...] = grad
    dot_ref[...] = grad.T


def unit_frames(frames):
    frames32 = frames.astype(F32)
    inverse = lax.rsqrt(jnp.mean(frames32 * frames32, axis=1, keepdims=True) + EPS_NORM)
    return frames32, inverse, frames32 * inverse


def frames_body(pick_ref, in_ref, frames_ref, normed_ref):
    frames = mm(pick_ref[...], in_ref[...]).astype(BF)
    frames_ref[...] = frames
    normed_ref[...] = unit_frames(frames)[2].astype(BF)


def project_body(
    query_scale, normed_ref, wq_hbm, wk_hbm, wv_hbm,
    q_ref, qt_ref, k_ref, kt_ref, v_ref, vt_ref, wk_ref, wv_ref, wq_ref, sems,
):
    copies = fetch([wq_hbm, wk_hbm, wv_hbm], [wq_ref, wk_ref, wv_ref], sems)
    normed = normed_ref[...]
    copies[0].wait()
    q = (mm(normed, wq_ref[...]) * query_scale).astype(BF)
    q_ref[...] = q
    qt_ref[...] = q.T
    copies[1].wait()
    k = mm(normed, wk_ref[...]).astype(BF)
    k_ref[...] = k
    kt_ref[...] = k.T
    copies[2].wait()
    v = mm(normed, wv_ref[...]).astype(BF)
    v_ref[...] = v
    vt_ref[...] = v.T


BLOCK = 256
TILE = 128


def softmax_parts(scores, slopes, first, begin, length):
    row = iota2((TILE, TILE), 0)
    col = iota2((TILE, TILE), 1)
    halo_bias = jnp.where(begin == 0, NEG, 0.0)
    zero_tile = jnp.zeros((TILE, TILE), BF)
    count = WIN // TILE + 1
    prob_cols, grad_cols = [], []
    for a in range(BLOCK // TILE):
        at = slice(a * TILE, (a + 1) * TILE)
        parts = []
        for n in range(count):
            low = (a + n) * TILE
            part = scores[low : low + TILE, at]
            if n == 0:
                part = jnp.where(row > col, part, NEG)
            if n == count - 1:
                part = jnp.where(row <= col, part, NEG)
            elif first + low < WIN:
                part = part + halo_bias
            parts.append(part)
        peak = parts[0]
        for part in parts[1:]:
            peak = jnp.maximum(peak, part)
        peak = jnp.max(peak, axis=0, keepdims=True)
        parts = [jnp.exp2(part - peak) for part in parts]
        denom = parts[0]
        for part in parts[1:]:
            denom = denom + part
        denom = jnp.sum(denom, axis=0, keepdims=True)
        time = begin + first + a * TILE + iota2((1, TILE), 1)
        scale = jnp.where(time < length, 1.0 / denom, 0.0)
        parts = [part * scale for part in parts]
        moved = [part * slopes[(a + n) * TILE : (a + n + 1) * TILE, at] for n, part in enumerate(parts)]
        centre = moved[0]
        for part in moved[1:]:
            centre = centre + part
        centre = jnp.sum(centre, axis=0, keepdims=True)
        grads = [(move - part * centre).astype(BF) for part, move in zip(parts, moved)]
        before = [zero_tile] * a
        after = [zero_tile] * (BLOCK // TILE - 1 - a)
        prob_cols.append(jnp.concatenate(before + [part.astype(BF) for part in parts] + after, axis=0))
        grad_cols.append(jnp.concatenate(before + grads + after, axis=0))
    return jnp.concatenate(prob_cols, axis=1), jnp.concatenate(grad_cols, axis=1)


def one_head(value, h, head_size):
    lane = iota2(value.shape, 1)
    mine = (lane >= h * head_size) & (lane < (h + 1) * head_size)
    return jnp.where(mine, value, jnp.zeros((), value.dtype))


def scores_body(
    head_size, meta_ref, halo_ref, wk_ref, wv_ref, q_ref, qt_ref, k_ref, v_ref, do_ref, dot_ref,
    probs_ref, grads_ref, dkh_ref, dvh_ref, khalo_t_ref, vhalo_t_ref, back_ref,
    kx, vx,
):
    span, width = q_ref.shape
    begin, length = meta_ref[0], meta_ref[1]
    halo = halo_ref[...]
    kh = mm(halo, wk_ref[...]).astype(BF)
    kx[:WIN] = kh
    khalo_t_ref[...] = kh.T
    vh = mm(halo, wv_ref[...]).astype(BF)
    vx[:WIN] = vh
    vhalo_t_ref[...] = vh.T
    kx[WIN:] = k_ref[...]
    vx[WIN:] = v_ref[...]

    pair = 2 * head_size
    reach = WIN + BLOCK
    blocks = span // BLOCK
    zeros_half = jnp.zeros((head_size, BLOCK), BF)
    units = [(b, h) for b in range(blocks) for h in range(2)]

    def one_pair(p, carry):
        cols = pl.ds(pl.multiple_of(p * pair, pair), pair)

        def multiply(b, h):
            first = b * BLOCK
            feats = pl.ds(pl.multiple_of(p * pair + h * head_size, head_size), head_size)
            halves = [zeros_half, zeros_half]
            halves[h] = qt_ref[feats, first : first + BLOCK]
            scores = mm(kx[first : first + reach, cols], jnp.concatenate(halves, axis=0))
            halves[h] = dot_ref[feats, first : first + BLOCK]
            slopes = mm(vx[first : first + reach, cols], jnp.concatenate(halves, axis=0))
            return scores, slopes

        totals = {}

        def finish(b, h, probs, grads):
            first = b * BLOCK
            at = (p * 2 + h) * blocks + b
            probs_ref[at] = probs
            grads_ref[at] = grads
            far = WIN - first
            queries = one_head(q_ref[first : first + BLOCK, cols], h, head_size)
            slopes = one_head(do_ref[first : first + BLOCK, cols], h, head_size)
            for name, part in (("k", mm(grads[:far], queries)), ("v", mm(probs[:far], slopes))):
                totals[name, b] = totals[name, b] + part if (name, b) in totals else part

        products = {0: multiply(*units[0])}
        for n, (b, h) in enumerate(units):
            if n + 1 < len(units):
                products[n + 1] = multiply(*units[n + 1])
            probs, grads = softmax_parts(*products.pop(n), b * BLOCK, begin, length)
            finish(b, h, probs, grads)

        for name, scale, out in (("k", math.log(2.0), dkh_ref), ("v", 1.0, dvh_ref)):
            for low in range(0, WIN, BLOCK):
                total = None
                for b in range(blocks):
                    at = low - b * BLOCK
                    if 0 <= at:
                        piece = totals[name, b][at : at + BLOCK]
                        total = piece if total is None else total + piece
                out[low : low + BLOCK, cols] = (total * scale).astype(BF)
        return carry

    lax.fori_loop(0, width // pair, one_pair, 0)
    back_ref[...] = (mm(dkh_ref[...], wk_ref[...], NT) + mm(dvh_ref[...], wv_ref[...], NT)).astype(BF)


def weights_body(
    scale, rows, head_size, meta_ref, normed_ref, halo_ref, frames_ref, cot_ref,
    wq_hbm, wk_hbm, wv_hbm, wo_hbm,
    q_ref, kt_ref, vt_ref, khalo_t_ref, vhalo_t_ref, do_ref, probs_ref, grads_ref, dkh_ref, dvh_ref,
    keep_ref, send_ref, out_ref, slope_ref,
    normed_t, halo_t, mixed_t, ktx, vtx, ot, dqt, dk, dv, wq, wk, wv, wo, sems,
):
    span, width = q_ref.shape
    copies = fetch([wq_hbm, wk_hbm, wv_hbm, wo_hbm], [wq, wk, wv, wo], sems)
    ktx[:, :WIN] = khalo_t_ref[...]
    ktx[:, WIN:] = kt_ref[...]
    vtx[:, :WIN] = vhalo_t_ref[...]
    vtx[:, WIN:] = vt_ref[...]
    pair = 2 * head_size
    reach = WIN + BLOCK
    blocks = span // BLOCK

    def one_pair(p, carry):
        cols = pl.ds(pl.multiple_of(p * pair, pair), pair)
        totals = {}
        for b in range(blocks):
            first = b * BLOCK
            span_keys = slice(first, first + reach)
            for h in range(2):
                feats = pl.ds(pl.multiple_of(p * pair + h * head_size, head_size), head_size)
                at = (p * 2 + h) * blocks + b
                ot[feats, first : first + BLOCK] = mm(vtx[feats, span_keys], probs_ref[at]).astype(BF)
                dqt[feats, first : first + BLOCK] = (
                    mm(ktx[feats, span_keys], grads_ref[at]) * head_size ** (-0.5)
                ).astype(BF)
                queries = one_head(q_ref[first : first + BLOCK, cols], h, head_size)
                slopes = one_head(do_ref[first : first + BLOCK, cols], h, head_size)
                near = slice(WIN - first, reach)
                for name, part in (
                    ("k", mm(grads_ref[at, near], queries)),
                    ("v", mm(probs_ref[at, near], slopes)),
                ):
                    totals[name, b] = totals[name, b] + part if (name, b) in totals else part
        for name, factor, out in (("k", math.log(2.0), dk), ("v", 1.0, dv)):
            for low in range(0, span, BLOCK):
                total = None
                for b in range(blocks):
                    piece = totals[name, b]
                    if low + BLOCK <= piece.shape[0]:
                        piece = piece[low : low + BLOCK]
                        total = piece if total is None else total + piece
                out[low : low + BLOCK, cols] = (total * factor).astype(BF)
        return carry

    lax.fori_loop(0, width // pair, one_pair, 0)

    chunks = width // (2 * rows)
    split = (chunks, 2, rows, span)
    normed_t[...] = normed_ref[...].T.reshape(split)
    halo_t[...] = halo_ref[...].T.reshape(split)
    mixed_t[...] = ot[...].reshape(split)
    mine = meta_ref[2]
    for side, out in ((1 - mine, send_ref), (mine, keep_ref)):
        own = normed_t[:, side].reshape(width // 2, span)
        far = halo_t[:, side].reshape(width // 2, span)
        mixed = mixed_t[:, side].reshape(width // 2, span)
        for n, total in enumerate((
            mm(own, dqt[...], NT),
            mm(own, dk[...]) + mm(far, dkh_ref[...]),
            mm(own, dv[...]) + mm(far, dvh_ref[...]),
            mm(mixed, cot_ref[...]),
        )):
            out[:, n * width : (n + 1) * width] = (total * scale).astype(BF)
    for copy in copies:
        copy.wait()
    slope = mm(dqt[...].T, wq[...], NT)
    slope = slope + mm(dk[...], wk[...], NT)
    slope_ref[...] = slope + mm(dv[...], wv[...], NT)
    out = mm(ot[...].T, wo[...]) + frames_ref[...].astype(F32)
    out_ref[...] = out.astype(BF)


def returning_body(frames_ref, slope_ref, extra_ref, cot_ref, pick_t_ref, out_ref):
    _, inverse, normed32 = unit_frames(frames_ref[...])
    slope = slope_ref[...] + extra_ref[...].astype(F32)
    centre = jnp.mean(slope * normed32, axis=1, keepdims=True)
    grad = inverse * (slope - normed32 * centre) + cot_ref[...].astype(F32)
    out_ref[...] = mm(pick_t_ref[...], grad.astype(BF)).astype(BF)


def arrived_body(placing_t_ref, in_ref, out_ref):
    out_ref[...] = mm(placing_t_ref[...], in_ref[...]).astype(BF)


def passed_along(shard, by):
    devices = lax.axis_size("seq")
    pairs = [(i, i + by) for i in range(devices) if 0 <= i + by < devices]
    return lax.ppermute(shard, "seq", pairs)


def spread_body(place_ref, *refs):
    parts = refs[0].shape[0]
    inputs, outs = refs[:-parts], refs[-parts:]
    for k, out in enumerate(outs):
        at = place_ref[0] ^ k
        total = inputs[0][at].astype(F32)
        for ref in inputs[1:]:
            total = total + ref[at].astype(F32)
        out[...] = total.astype(BF)


def scattered(inputs, place, axis, parts, step):
    columns = inputs[0].shape[-1]
    inputs = [shard.reshape(parts, -1, columns) for shard in inputs]
    piece = sds(inputs[0].shape[1:])
    pieces = vmem_call(
        spread_body, [piece] * parts, [place.reshape(1)] + inputs, smem=(0,)
    )
    count = lax.axis_size(axis)
    return [pieces[0]] + [
        lax.ppermute(pieces[k], axis, [(i, i ^ (k * step)) for i in range(count)])
        for k in range(1, parts)
    ]


def scatter_sums(keep, got):
    seqs, streams = lax.axis_size("seq"), lax.axis_size("stream")
    pieces = scattered([keep, got], lax.axis_index("stream"), "stream", streams, 1)
    pieces = scattered(pieces, lax.axis_index("seq") >> 1, "seq", seqs // 2, 2)
    total = pieces[0].astype(F32)
    for piece in pieces[1:]:
        total = total + piece.astype(F32)
    return total


def shards(
    frame_rows, row_frame, frame_owner, lengths,
    query_weight, key_weight, value_weight, out_weight, cotangent,
):
    devices = lax.axis_size(AXES)
    row_count, width = frame_rows.shape
    span = frame_owner.shape[1]
    slots = row_count // devices
    slab = span * lax.axis_size("seq")
    head_size = width // H
    cube = 2 * span * width * width
    square = sds((span, width))
    begin = (lax.axis_index("seq") * span).astype(jnp.int32)
    rows = width // devices
    in_kernel = rows % 16 == 0
    core = (lax.axis_index("seq") & 1).astype(jnp.int32)
    meta = jnp.stack([begin, lengths[0], core if in_kernel else jnp.zeros((), jnp.int32)])
    cot = cotangent[0]

    def exchanged(shard):
        got = lax.all_to_all(
            shard.reshape(devices, slots, width), AXES, split_axis=0, concat_axis=0, tiled=True
        )
        return got.reshape(devices * slots, width)

    outgoing, placing = vmem_call(
        lambda *refs: outgoing_body(span, slots, *refs),
        [square, sds((devices * slots, row_count))],
        [row_frame.reshape(1, row_count), frame_rows],
        hbm=(1,),
        scratch=[pltpu.VMEM((row_count, width), BF), pltpu.SemaphoreType.DMA((1,))],
        flops=cube,
    )
    incoming = exchanged(outgoing)
    pick, pick_t, placing_t, do, dot = vmem_call(
        lambda *refs: early_body(slots, *refs),
        [square, square, square, square, sds((width, span))],
        [frame_owner.reshape(span, 1), placing, cot, out_weight],
        flops=2 * cube,
    )
    frames, normed = vmem_call(frames_body, [square, square], [pick, incoming], flops=cube)
    halo = passed_along(normed, 1)
    query_scale = head_size ** (-0.5) * math.log2(math.e)
    q, qt, k, kt, v, vt, wk, wv = vmem_call(
        lambda *refs: project_body(query_scale, *refs),
        [square] * 8,
        [normed, query_weight, key_weight, value_weight],
        hbm=(1, 2, 3),
        scratch=[pltpu.VMEM((width, width), BF), pltpu.SemaphoreType.DMA((3,))],
        flops=3 * cube,
    )
    saved = sds((H * (span // BLOCK), WIN + BLOCK, BLOCK))
    probs, grads, dkh, dvh, khalo_t, vhalo_t, back = vmem_call(
        lambda *refs: scores_body(head_size, *refs),
        [saved, saved] + [square] * 5,
        [meta, halo, wk, wv, q, qt, k, v, do, dot],
        smem=(0,),
        scratch=[pltpu.VMEM((WIN + span, width), BF)] * 2,
        flops=12 * cube,
        limit=24,
    )
    extra = passed_along(back, -1)
    chunk = rows if in_kernel else width // 2
    split = pltpu.VMEM((width // (2 * chunk), 2, chunk, span), BF)
    whole = pltpu.VMEM((width, width), BF)
    half = sds((width // 2, 4 * width))
    keep, send, out_frames, slope = vmem_call(
        lambda *refs: weights_body(slab ** (-0.5), chunk, head_size, *refs),
        [half, half, square, sds((span, width), F32)],
        [meta, normed, halo, frames, cot, query_weight, key_weight, value_weight, out_weight,
         q, kt, vt, khalo_t, vhalo_t, do, probs, grads, dkh, dvh],
        smem=(0,),
        hbm=(5, 6, 7, 8),
        scratch=[split] * 3 + [pltpu.VMEM((width, WIN + span), BF)] * 2 + [whole] * 8
        + [pltpu.SemaphoreType.DMA((4,))],
        flops=18 * cube,
        limit=26,
    )
    send, extra = lax.optimization_barrier((send, extra))
    if not in_kernel:
        sums = jnp.concatenate([keep, send], axis=0).reshape(-1, 2, rows, 4 * width)
        keep = lax.dynamic_index_in_dim(sums, core, 1, keepdims=False).reshape(half.shape)
        send = lax.dynamic_index_in_dim(sums, 1 - core, 1, keepdims=False).reshape(half.shape)
    seqs = lax.axis_size("seq")
    got = lax.ppermute(send, "seq", [(i, i ^ 1) for i in range(seqs)])
    returning, = vmem_call(
        returning_body, [square], [frames, slope, extra, cot, pick_t], flops=cube
    )
    got, _ = lax.optimization_barrier((got, returning))
    arrived = exchanged(returning)
    frame_grads, = vmem_call(arrived_body, [square], [placing_t, arrived], flops=cube)
    weight_grads = scatter_sums(keep, got)
    return (out_frames[None], frame_grads, weight_grads)


def solution(mesh):
    return jax.shard_map(
        shards,
        mesh=mesh,
        in_specs=(
            P(AXES, None), P(AXES), P("stream", "seq"), P("stream"),
            P(), P(), P(), P(), P("stream", "seq", None),
        ),
        out_specs=(P("stream", "seq", None), P(AXES, None), P(AXES, None)),
        check_vma=False,
    )
```

time: 120 us -> 102 us (0.85)
  waiting for transfers between devices: 48.6 us -> 31 us
  other arithmetic: 4.29 us -> 0.76 us
  local copies, waits for them, and re-layouts: 9.74 us -> 11.7 us
    all_to_all x2 -> x0, waiting for transfers between devices: 19.9 us -> none  [summed(): lax.all_to_all(shard, axis, split_axis=0, concat_axis=0, axis_index_group...]
    ppermute x1 -> x7, waiting for transfers between devices: 2.29 us -> 20.5 us  [the longest x6 20.5 us: scattered(): lax.ppermute(pieces[k], axis, [(i, i ^ k * step) for i in range(count)])]
    all_to_all x2, waiting for transfers between devices: 26.4 us -> 10.5 us  [exchanged(): lax.all_to_all(shard.reshape(devices, slots, width), AXES, split_axis=0,...]
    all_to_all x2 -> x0, starting transfers between devices: 7.64 us -> none  [summed(): lax.all_to_all(shard, axis, split_axis=0, concat_axis=0, axis_index_group...]
    ppermute x1 -> x7, starting transfers between devices: 4.1 us -> 9.28 us  [the longest x6 7.94 us: scattered(): lax.ppermute(pieces[k], axis, [(i, i ^ k * step) for i in range(count)])]
    reduce_sum x2 -> x0, other arithmetic: 2.85 us -> none  [summed(): return jnp.sum(got.astype(F32), axis=0)]
    all_to_all x2, starting transfers between devices: 9.9 us -> 12.3 us  [exchanged(): lax.all_to_all(shard.reshape(devices, slots, width), AXES, split_axis=0,...]
    convert_element_type x1 -> x0, other arithmetic: 1.36 us -> none  [scatter_sums(): total = (keep.astype(F32) + got.astype(F32)).astype(BF)]
  transfers between devices with their start and end apart: 7 -> 11, of which waited for: 5 -> 6; matrix products, arithmetic and copies ran while one was open for 2% -> 1% of each run, Pallas kernels for 9% -> 16%
where the time goes in v2:
time: 102 us; the launch traced here: 101 us
  Pallas kernels  31.2 us (31%)
  waiting for transfers between devices  31 us (30%)
  starting transfers between devices  24.8 us (24%)
  local copies, waits for them, and re-layouts  11.7 us (11%)
  between operations  1.55 us (2%)
    pallas_call x10, Pallas kernels, vmem_call(): pl.pallas_call(body, out_shape=tuple(outs), in_specs=[pl.BlockSpec(memory...  31.2 us
    ppermute x6, waiting for transfers between devices, scattered(): lax.ppermute(pieces[k], axis, [(i, i ^ k * step) for i in range(count)])  20.5 us
    all_to_all x2, starting transfers between devices, exchanged(): lax.all_to_all(shard.reshape(devices, slots, width), AXES, split_axis=0,...  12.3 us
    unnamed x36, local copies, waits for them, and re-layouts  10.9 us
    all_to_all x2, waiting for transfers between devices, exchanged(): lax.all_to_all(shard.reshape(devices, slots, width), AXES, split_axis=0,...  10.5 us
    ppermute x6, starting transfers between devices, scattered(): lax.ppermute(pieces[k], axis, [(i, i ^ k * step) for i in range(count)])  7.94 us
    ppermute x2, starting transfers between devices, passed_along(): return lax.ppermute(shard, 'seq', pairs)  3.24 us
  transfers between devices with their start and end apart: 11, of which 6 were waited for; matrix products, arithmetic and copies ran while one was open for 1% of the time, Pallas kernels for 16%

profile of v2, /device:TPU:0, one launch (start us, length us, event | category | flops | bytes accessed | tf_op | source)
XLA Modules:
  0.0 101.0 jit_solution(11794826325383056305)
XLA Ops:
  2.4 1.6 %shard_map.112 = (bf16[512,512]{1,0:T(8,128)(2,1)}, bf16[512,512]{1,0:T(8,128)(2,1)S(1)}) custom-call(s32[1,512]{1,0:T(1,128)S(1)} %bitcast.29, bf16[512,512]{1,0:T(8,128)(2,1)S(1)} %copy-done.14), custom_call_target="tpu_custom_call" | custom-call | flops 268435456 | bytes 1574912 | tf_op jit(solution)/shard_map/pallas_call | solution.py:33
  4.0 7.3 %all-to-all-start = ((bf16[32,16,512]{2,1,0:T(8,128)(2,1)}), bf16[32,16,512]{2,1,0:T(8,128)(2,1)S(1)}, u32[]{:S(2)}, u32[]{:S(2)}) async-start(bf16[32,16,512]{2,1,0:T(8,128)(2,1)} %bitcast.5), calls=%async_computation | async-start | bytes 1048576 | tf_op jit(solution)/shard_map/all_to_all | solution.py:404
  14.2 1.3 %shard_map.113 = (bf16[512,512]{1,0:T(8,128)(2,1)S(1)}, bf16[512,512]{1,0:T(8,128)(2,1)S(1)}, bf16[512,512]{1,0:T(8,128)(2,1)S(1)}, bf16[512,512]{1,0:T(8,128)(2,1)S(1)}, bf16[512,512]{1,0:T(8,128)(2,1)S(1)}) custom-call(s32[512,1]{1,0:T(8,128)S(1)} %copy.12.refs_0_, bf16[512,512]{1,0:T(8,128)(2,1)S(1)} %get-tuple-element.42.refs_1_, ...), custom_call_target="tpu_custom_call" | custom-call | flops 536870912 | bytes 4196352 | tf_op jit(solution)/shard_map/pallas_call | solution.py:33
  17.2 10.5 %all-to-all-done = bf16[32,16,512]{2,1,0:T(8,128)(2,1)S(1)} async-done(((bf16[32,16,512]{2,1,0:T(8,128)(2,1)}), bf16[32,16,512]{2,1,0:T(8,128)(2,1)S(1)}, u32[]{:S(2)}, u32[]{:S(2)}) %all-to-all-start) | async-done | bytes 524320 | tf_op jit(solution)/shard_map/all_to_all | solution.py:404
  28.3 1.9 %collective-permute-start = (bf16[512,512]{1,0:T(8,128)(2,1)S(1)}, bf16[512,512]{1,0:T(8,128)(2,1)S(1)}, u32[]{:S(2)}, u32[]{:S(2)}) collective-permute-start(bf16[512,512]{1,0:T(8,128)(2,1)S(1)} %get-tuple-element.45.refs_0_.refs_1_), channel_id=1, source_target_pairs={{0,1},{1,2},{2,3},{3,4},{4,5},{5,6},{6,7},{8,9},{9,10},{10,11},{11... | collective-permute-start | bytes 1572872 | tf_op jit(solution)/shard_map/ppermute | solution.py:346
  31.0 1.0 %copy-done.4 = bf16[512,512]{1,0:T(8,128)(2,1)S(1)} copy-done((bf16[512,512]{1,0:T(8,128)(2,1)S(1)}, bf16[512,512]{1,0:T(8,128)(2,1)}, u32[]{:S(2)}) %copy-start.4) | copy-done | bytes 524312
  33.1 1.0 %copy-done.8 = bf16[512,512]{1,0:T(8,128)(2,1)S(1)} copy-done((bf16[512,512]{1,0:T(8,128)(2,1)S(1)}, bf16[512,512]{1,0:T(8,128)(2,1)}, u32[]{:S(2)}) %copy-start.8) | copy-done | bytes 524312
  34.1 1.7 %shard_map.115 = (bf16[512,512]{1,0:T(8,128)(2,1)S(1)}, bf16[512,512]{1,0:T(8,128)(2,1)S(1)}, bf16[512,512]{1,0:T(8,128)(2,1)S(1)}, bf16[512,512]{1,0:T(8,128)(2...) custom-call(bf16[512,512]{1,0:T(8,128)(2,1)S(1)} %get-tuple-element., ...), custom_call_target="tpu_custom_call" | custom-call | flops 805306368 | bytes 6291456 | tf_op jit(solution)/shard_map/pallas_call | solution.py:33
  35.9 1.3 %copy-done.17 = bf16[512,512]{1,0:T(8,128)(2,1)S(1)} copy-done((bf16[512,512]{1,0:T(8,128)(2,1)S(1)}, bf16[512,512]{1,0:T(8,128)(2,1)}, u32[]{:S(2)}) %copy-start.17) | copy-done | bytes 524312
  37.2 12.5 %shard_map.116 = (bf16[16,768,256]{2,1,0:T(8,128)(2,1)S(1)}, bf16[16,768,256]{2,1,0:T(8,128)(2,1)S(1)}, bf16[512,512]{1,0:T(8,128)(2,1)S(1)}, bf16[512,512]{1,0:...) custom-call(s32[3]{0:T(128)S(1)} %pad_add_fusion.refs_0_, ...), custom_call_target="tpu_custom_call" | custom-call | flops 3221225472 | bytes 19922956 | tf_op jit(solution)/shard_map/pallas_call | solution.py:33
  49.7 1.3 %collective-permute-start.1 = (bf16[512,512]{1,0:T(8,128)(2,1)S(1)}, bf16[512,512]{1,0:T(8,128)(2,1)S(1)}, u32[]{:S(2)}, u32[]{:S(2)}) collective-permute-start(bf16[512,512]{1,0:T(8,128)(2,1)S(1)} %get-tuple-element.67), channel_id=1, source_target_pairs={{1,0},{2,1},{3,2},{4,3},{5,4},{6,5},{7,6},{9,8},{10,9},{11,10},{12... | collective-permute-start | bytes 1572872 | tf_op jit(solution)/shard_map/ppermute | solution.py:346
  52.1 9.4 %shard_map.117 = (bf16[256,2048]{1,0:T(8,128)(2,1)S(1)}, bf16[256,2048]{1,0:T(8,128)(2,1)}, bf16[512,512]{1,0:T(8,128)(2,1)}, f32[512,512]{1,0:T(8,128)S(1)}) custom-call(s32[3]{0:T(128)S(1)} %pad_add_fusion.refs_0_, bf16[512,512]{1,0:T(8,128)(2,1)S(1)} %get-tuple-element.45.refs_0_.refs_1_, bf16[512,512]{1,0:T(8,128)(2,1)S(1)} %copy-done.13, ...), custom_call_target="tpu_custom_call" | custom-call | flops 4831838208 | bytes 24641548 | tf_op jit(solution)/shard_map/pallas_call | solution.py:33
  61.5 1.3 %collective-permute-start.2 = (bf16[256,2048]{1,0:T(8,128)(2,1)}, bf16[256,2048]{1,0:T(8,128)(2,1)S(1)}, u32[]{:S(2)}, u32[]{:S(2)}) collective-permute-start(bf16[256,2048]{1,0:T(8,128)(2,1)} %get-tuple-element.71), channel_id=1, source_target_pairs={{0,1},{1,0},{2,3},{3,2},{4,5},{5,4},{6,7},{7,6},{8,9},{9,8},{10,11... | collective-permute-start | bytes 3145736 | tf_op jit(solution)/shard_map/ppermute | solution.py:468
  62.9 1.6 %shard_map.118 = bf16[512,512]{1,0:T(8,128)(2,1)} custom-call(bf16[512,512]{1,0:T(8,128)(2,1)S(1)} %get-tuple-element.46.refs_3_.frames_ref, f32[512,512]{1,0:T(8,128)S(1)} %get-tuple-element.65.slope_ref, bf16[512,512]{1,0:T(8,128)(2,1)S(1)} %collective-permute-done.1.extra_ref, bf16[512,512]{1,0:T(8,128)(2,1)S(1)} %bitcast.20, bf16[512,512]{1,0:T(8,128)(2,1)S(1)} %copy-done.11), custom_call_target="tpu_custom_call" | custom-call | flops 268435456 | bytes 3670016 | tf_op jit(solution)/shard_map/pallas_call | solution.py:33
  64.5 4.9 %all-to-all-start.1 = ((bf16[32,16,512]{2,1,0:T(8,128)(2,1)}), bf16[32,16,512]{2,1,0:T(8,128)(2,1)S(1)}, u32[]{:S(2)}, u32[]{:S(2)}) async-start(bf16[32,16,512]{2,1,0:T(8,128)(2,1)} %bitcast.8), calls=%async_computation.1 | async-start | bytes 1048576 | tf_op jit(solution)/shard_map/all_to_all | solution.py:404
  70.5 1.8 %collective-permute-start.3 = (bf16[64,2048]{1,0:T(8,128)(2,1)}, bf16[64,2048]{1,0:T(8,128)(2,1)S(1)}, u32[]{:S(2)}, u32[]{:S(2)}) collective-permute-start(bf16[64,2048]{1,0:T(8,128)(2,1)} %get-tuple-element.74), channel_id=1, source_target_pairs={{0,8},{8,0},{16,24},{24,16},{1,9},{9,1},{17,25},{25,17},{2,10},{10... | collective-permute-start | bytes 786440 | tf_op jit(solution)/shard_map/ppermute | solution.py:369
  72.3 1.5 %collective-permute-start.4 = (bf16[64,2048]{1,0:T(8,128)(2,1)}, bf16[64,2048]{1,0:T(8,128)(2,1)S(1)}, u32[]{:S(2)}, u32[]{:S(2)}) collective-permute-start(bf16[64,2048]{1,0:T(8,128)(2,1)} %get-tuple-element.75), channel_id=1, source_target_pairs={{0,16},{8,24},{16,0},{24,8},{1,17},{9,25},{17,1},{25,9},{2,18},{10... | collective-permute-start | bytes 786440 | tf_op jit(solution)/shard_map/ppermute | solution.py:369
  74.0 9.2 %collective-permute-done.3 = bf16[64,2048]{1,0:T(8,128)(2,1)S(1)} collective-permute-done((bf16[64,2048]{1,0:T(8,128)(2,1)}, bf16[64,2048]{1,0:T(8,128)(2,1)S(1)}, u32[]{:S(2)}, u32[]{:S(2)}) %collective-permute-start.3) | collective-permute-done | bytes 262176 | tf_op jit(solution)/shard_map/ppermute | solution.py:369
  83.4 6.7 %collective-permute-done.5 = bf16[64,2048]{1,0:T(8,128)(2,1)S(1)} collective-permute-done((bf16[64,2048]{1,0:T(8,128)(2,1)}, bf16[64,2048]{1,0:T(8,128)(2,1)S(1)}, u32[]{:S(2)}, u32[]{:S(2)}) %collective-permute-start.5) | collective-permute-done | bytes 262176 | tf_op jit(solution)/shard_map/ppermute | solution.py:369
  90.3 1.5 %collective-permute-start.6 = (bf16[16,2048]{1,0:T(8,128)(2,1)S(1)}, bf16[16,2048]{1,0:T(8,128)(2,1)S(1)}, u32[]{:S(2)}, u32[]{:S(2)}) collective-permute-start(bf16[16,2048]{1,0:T(8,128)(2,1)S(1)} %get-tuple-element.78), channel_id=1, source_target_pairs={{0,2},{1,3},{2,0},{3,1},{4,6},{5,7},{6,4},{7,5},{8,10},{9,11},{10,... | collective-permute-start | bytes 196616 | tf_op jit(solution)/shard_map/ppermute | solution.py:369
  91.8 2.4 %collective-permute-start.7 = (bf16[16,2048]{1,0:T(8,128)(2,1)S(1)}, bf16[16,2048]{1,0:T(8,128)(2,1)S(1)}, u32[]{:S(2)}, u32[]{:S(2)}) collective-permute-start(bf16[16,2048]{1,0:T(8,128)(2,1)S(1)} %get-tuple-element.79), channel_id=1, source_target_pairs={{0,4},{1,5},{2,6},{3,7},{4,0},{5,1},{6,2},{7,3},{8,12},{9,13},{10,... | collective-permute-start | bytes 196616 | tf_op jit(solution)/shard_map/ppermute | solution.py:369
  94.7 1.2 %shard_map.119 = bf16[512,512]{1,0:T(8,128)(2,1)} custom-call(bf16[512,512]{1,0:T(8,128)(2,1)S(1)} %get-tuple-element.64.placing_t_ref, bf16[512,512]{1,0:T(8,128)(2,1)S(1)} %bitcast.21), custom_call_target="tpu_custom_call" | custom-call | flops 268435456 | bytes 1572864 | tf_op jit(solution)/shard_map/pallas_call | solution.py:33
  95.9 3.1 %collective-permute-done.7 = bf16[16,2048]{1,0:T(8,128)(2,1)S(1)} collective-permute-done((bf16[16,2048]{1,0:T(8,128)(2,1)S(1)}, bf16[16,2048]{1,0:T(8,128)(2,1)S(1)}, u32[]{:S(2)}, u32[]{:S(2)}) %collective-permute-start.7) | collective-permute-done | bytes 65568 | tf_op jit(solution)/shard_map/ppermute | solution.py:369
  99.1 1.2 %collective-permute-done.8 = bf16[16,2048]{1,0:T(8,128)(2,1)S(1)} collective-permute-done((bf16[16,2048]{1,0:T(8,128)(2,1)S(1)}, bf16[16,2048]{1,0:T(8,128)(2,1)S(1)}, u32[]{:S(2)}, u32[]{:S(2)}) %collective-permute-start.8) | collective-permute-done | bytes 65568 | tf_op jit(solution)/shard_map/ppermute | solution.py:369
  (47 shorter events, 12.0 us)
Async XLA Ops:
  0.6 1.0 %copy-start.14 = (bf16[512,512]{1,0:T(8,128)(2,1)S(1)}, bf16[512,512]{1,0:T(8,128)(2,1)}, u32[]{:S(2)}) copy-start(bf16[512,512]{1,0:T(8,128)(2,1)} %refs_1_.2) | copy-start | bytes 1572868
  4.0 23.7 %all-to-all-start = ((bf16[32,16,512]{2,1,0:T(8,128)(2,1)}), bf16[32,16,512]{2,1,0:T(8,128)(2,1)S(1)}, u32[]{:S(2)}, u32[]{:S(2)}) async-start(bf16[32,16,512]{2,1,0:T(8,128)(2,1)} %bitcast.5), calls=%async_computation | async-start | bytes 1048576 | tf_op jit(solution)/shard_map/all_to_all | solution.py:404
  12.1 1.0 %copy-start = (bf16[1,512,512]{2,1,0:T(8,128)(2,1)S(1)}, bf16[1,512,512]{2,1,0:T(8,128)(2,1)}, u32[]{:S(2)}) copy-start(bf16[1,512,512]{2,1,0:T(8,128)(2,1)} %param.17) | copy-start | bytes 1572868
  13.2 1.0 %copy-start.2 = (bf16[512,512]{1,0:T(8,128)(2,1)S(1)}, bf16[512,512]{1,0:T(8,128)(2,1)}, u32[]{:S(2)}) copy-start(bf16[512,512]{1,0:T(8,128)(2,1)} %refs_8_.1) | copy-start | bytes 1572868
  28.3 7.6 %collective-permute-start = (bf16[512,512]{1,0:T(8,128)(2,1)S(1)}, bf16[512,512]{1,0:T(8,128)(2,1)S(1)}, u32[]{:S(2)}, u32[]{:S(2)}) collective-permute-start(bf16[512,512]{1,0:T(8,128)(2,1)S(1)} %get-tuple-element.45.refs_0_.refs_1_), channel_id=1, source_target_pairs={{0,1},{1,2},{2,3},{3,4},{4,5},{5,6},{6,7},{8,9},{9,10},{10,11},{11... | collective-permute-start | bytes 1572872 | tf_op jit(solution)/shard_map/ppermute | solution.py:346
  31.0 1.0 %copy-start.4 = (bf16[512,512]{1,0:T(8,128)(2,1)S(1)}, bf16[512,512]{1,0:T(8,128)(2,1)}, u32[]{:S(2)}) copy-start(bf16[512,512]{1,0:T(8,128)(2,1)} %refs_5_.1) | copy-start | bytes 1572868
  35.8 15.2 %copy-start.1 = (bf16[1,512,512]{2,1,0:T(8,128)(2,1)S(1)}, bf16[1,512,512]{2,1,0:T(8,128)(2,1)}, u32[]{:S(2)}) copy-start(bf16[1,512,512]{2,1,0:T(8,128)(2,1)} %param.17) | copy-start | bytes 1572868
  35.8 15.2 %copy-start.3 = (bf16[512,512]{1,0:T(8,128)(2,1)S(1)}, bf16[512,512]{1,0:T(8,128)(2,1)}, u32[]{:S(2)}) copy-start(bf16[512,512]{1,0:T(8,128)(2,1)} %refs_8_.1) | copy-start | bytes 1572868
  35.9 15.2 %copy-start.5 = (bf16[512,512]{1,0:T(8,128)(2,1)S(1)}, bf16[512,512]{1,0:T(8,128)(2,1)}, u32[]{:S(2)}) copy-start(bf16[512,512]{1,0:T(8,128)(2,1)} %refs_5_.1) | copy-start | bytes 1572868
  35.9 15.2 %copy-start.7 = (bf16[512,512]{1,0:T(8,128)(2,1)S(1)}, bf16[512,512]{1,0:T(8,128)(2,1)}, u32[]{:S(2)}) copy-start(bf16[512,512]{1,0:T(8,128)(2,1)} %refs_6_.1) | copy-start | bytes 1572868
  35.9 15.2 %copy-start.9 = (bf16[512,512]{1,0:T(8,128)(2,1)S(1)}, bf16[512,512]{1,0:T(8,128)(2,1)}, u32[]{:S(2)}) copy-start(bf16[512,512]{1,0:T(8,128)(2,1)} %refs_7_.1) | copy-start | bytes 1572868
  35.9 15.1 %copy-start.12 = (bf16[512,512]{1,0:T(8,128)(2,1)}, bf16[512,512]{1,0:T(8,128)(2,1)S(1)}, u32[]{:S(2)}) copy-start(bf16[512,512]{1,0:T(8,128)(2,1)S(1)} %collective-permute-done.refs_1_.refs_2_) | copy-start | bytes 1572868
  35.9 1.3 %copy-start.17 = (bf16[512,512]{1,0:T(8,128)(2,1)S(1)}, bf16[512,512]{1,0:T(8,128)(2,1)}, u32[]{:S(2)}) copy-start(bf16[512,512]{1,0:T(8,128)(2,1)} %copy-done.16) | copy-start | bytes 1572868
  49.7 11.9 %collective-permute-start.1 = (bf16[512,512]{1,0:T(8,128)(2,1)S(1)}, bf16[512,512]{1,0:T(8,128)(2,1)S(1)}, u32[]{:S(2)}, u32[]{:S(2)}) collective-permute-start(bf16[512,512]{1,0:T(8,128)(2,1)S(1)} %get-tuple-element.67), channel_id=1, source_target_pairs={{1,0},{2,1},{3,2},{4,3},{5,4},{6,5},{7,6},{9,8},{10,9},{11,10},{12... | collective-permute-start | bytes 1572872 | tf_op jit(solution)/shard_map/ppermute | solution.py:346
  51.0 1.0 %copy-start.13 = (bf16[512,512]{1,0:T(8,128)(2,1)S(1)}, bf16[512,512]{1,0:T(8,128)(2,1)}, u32[]{:S(2)}) copy-start(bf16[512,512]{1,0:T(8,128)(2,1)} %copy-done.12) | copy-start | bytes 1572868
  52.1 10.8 %copy-start.11 = (bf16[512,512]{1,0:T(8,128)(2,1)S(1)}, bf16[512,512]{1,0:T(8,128)(2,1)}, u32[]{:S(2)}) copy-start(bf16[512,512]{1,0:T(8,128)(2,1)} %copy-done.10) | copy-start | bytes 1572868
  61.5 7.9 %collective-permute-start.2 = (bf16[256,2048]{1,0:T(8,128)(2,1)}, bf16[256,2048]{1,0:T(8,128)(2,1)S(1)}, u32[]{:S(2)}, u32[]{:S(2)}) collective-permute-start(bf16[256,2048]{1,0:T(8,128)(2,1)} %get-tuple-element.71), channel_id=1, source_target_pairs={{0,1},{1,0},{2,3},{3,2},{4,5},{5,4},{6,7},{7,6},{8,9},{9,8},{10,11... | collective-permute-start | bytes 3145736 | tf_op jit(solution)/shard_map/ppermute | solution.py:468
  64.5 30.2 %all-to-all-start.1 = ((bf16[32,16,512]{2,1,0:T(8,128)(2,1)}), bf16[32,16,512]{2,1,0:T(8,128)(2,1)S(1)}, u32[]{:S(2)}, u32[]{:S(2)}) async-start(bf16[32,16,512]{2,1,0:T(8,128)(2,1)} %bitcast.8), calls=%async_computation.1 | async-start | bytes 1048576 | tf_op jit(solution)/shard_map/all_to_all | solution.py:404
  70.5 12.6 %collective-permute-start.3 = (bf16[64,2048]{1,0:T(8,128)(2,1)}, bf16[64,2048]{1,0:T(8,128)(2,1)S(1)}, u32[]{:S(2)}, u32[]{:S(2)}) collective-permute-start(bf16[64,2048]{1,0:T(8,128)(2,1)} %get-tuple-element.74), channel_id=1, source_target_pairs={{0,8},{8,0},{16,24},{24,16},{1,9},{9,1},{17,25},{25,17},{2,10},{10... | collective-permute-start | bytes 786440 | tf_op jit(solution)/shard_map/ppermute | solution.py:369
  72.3 11.2 %collective-permute-start.4 = (bf16[64,2048]{1,0:T(8,128)(2,1)}, bf16[64,2048]{1,0:T(8,128)(2,1)S(1)}, u32[]{:S(2)}, u32[]{:S(2)}) collective-permute-start(bf16[64,2048]{1,0:T(8,128)(2,1)} %get-tuple-element.75), channel_id=1, source_target_pairs={{0,16},{8,24},{16,0},{24,8},{1,17},{9,25},{17,1},{25,9},{2,18},{10... | collective-permute-start | bytes 786440 | tf_op jit(solution)/shard_map/ppermute | solution.py:369
  73.7 16.4 %collective-permute-start.5 = (bf16[64,2048]{1,0:T(8,128)(2,1)}, bf16[64,2048]{1,0:T(8,128)(2,1)S(1)}, u32[]{:S(2)}, u32[]{:S(2)}) collective-permute-start(bf16[64,2048]{1,0:T(8,128)(2,1)} %get-tuple-element.76), channel_id=1, source_target_pairs={{0,24},{8,16},{16,8},{24,0},{1,25},{9,17},{17,9},{25,1},{2,26},{10... | collective-permute-start | bytes 786440 | tf_op jit(solution)/shard_map/ppermute | solution.py:369
  90.3 5.7 %collective-permute-start.6 = (bf16[16,2048]{1,0:T(8,128)(2,1)S(1)}, bf16[16,2048]{1,0:T(8,128)(2,1)S(1)}, u32[]{:S(2)}, u32[]{:S(2)}) collective-permute-start(bf16[16,2048]{1,0:T(8,128)(2,1)S(1)} %get-tuple-element.78), channel_id=1, source_target_pairs={{0,2},{1,3},{2,0},{3,1},{4,6},{5,7},{6,4},{7,5},{8,10},{9,11},{10,... | collective-permute-start | bytes 196616 | tf_op jit(solution)/shard_map/ppermute | solution.py:369
  91.8 7.3 %collective-permute-start.7 = (bf16[16,2048]{1,0:T(8,128)(2,1)S(1)}, bf16[16,2048]{1,0:T(8,128)(2,1)S(1)}, u32[]{:S(2)}, u32[]{:S(2)}) collective-permute-start(bf16[16,2048]{1,0:T(8,128)(2,1)S(1)} %get-tuple-element.79), channel_id=1, source_target_pairs={{0,4},{1,5},{2,6},{3,7},{4,0},{5,1},{6,2},{7,3},{8,12},{9,13},{10,... | collective-permute-start | bytes 196616 | tf_op jit(solution)/shard_map/ppermute | solution.py:369
  94.1 6.2 %collective-permute-start.8 = (bf16[16,2048]{1,0:T(8,128)(2,1)S(1)}, bf16[16,2048]{1,0:T(8,128)(2,1)S(1)}, u32[]{:S(2)}, u32[]{:S(2)}) collective-permute-start(bf16[16,2048]{1,0:T(8,128)(2,1)S(1)} %get-tuple-element.80), channel_id=1, source_target_pairs={{0,6},{1,7},{2,4},{3,5},{4,2},{5,3},{6,0},{7,1},{8,14},{9,15},{10,... | collective-permute-start | bytes 196616 | tf_op jit(solution)/shard_map/ppermute | solution.py:369
  (5 other events, 4.4 us)

commit v3 on v2

--- a/solution.py
+++ b/solution.py
@@ -125,28 +125,27 @@
     vt_ref[...] = v.T
 
 
-BLOCK = 256
 TILE = 128
+REACH = WIN + TILE
 
 
 def softmax_parts(scores, slopes, first, begin, length):
     row = iota2((TILE, TILE), 0)
     col = iota2((TILE, TILE), 1)
     halo_bias = jnp.where(begin == 0, NEG, 0.0)
-    zero_tile = jnp.zeros((TILE, TILE), BF)
-    count = WIN // TILE + 1
+    count = REACH // TILE
+    time = begin + first + iota2((1, TILE), 1)
     prob_cols, grad_cols = [], []
-    for a in range(BLOCK // TILE):
-        at = slice(a * TILE, (a + 1) * TILE)
+    for h in range(2):
+        at = slice(h * TILE, (h + 1) * TILE)
         parts = []
         for n in range(count):
-            low = (a + n) * TILE
-            part = scores[low : low + TILE, at]
+            part = scores[n * TILE : (n + 1) * TILE, at]
             if n == 0:
                 part = jnp.where(row > col, part, NEG)
             if n == count - 1:
                 part = jnp.where(row <= col, part, NEG)
-            elif first + low < WIN:
+            elif first + n * TILE < WIN:
                 part = part + halo_bias
             parts.append(part)
         peak = parts[0]
@@ -158,26 +157,24 @@
         for part in parts[1:]:
             denom = denom + part
         denom = jnp.sum(denom, axis=0, keepdims=True)
-        time = begin + first + a * TILE + iota2((1, TILE), 1)
         scale = jnp.where(time < length, 1.0 / denom, 0.0)
         parts = [part * scale for part in parts]
-        moved = [part * slopes[(a + n) * TILE : (a + n + 1) * TILE, at] for n, part in enumerate(parts)]
+        moved = [part * slopes[n * TILE : (n + 1) * TILE, at] for n, part in enumerate(parts)]
         centre = moved[0]
         for part in moved[1:]:
             centre = centre + part
         centre = jnp.sum(centre, axis=0, keepdims=True)
         grads = [(move - part * centre).astype(BF) for part, move in zip(parts, moved)]
-        before = [zero_tile] * a
-        after = [zero_tile] * (BLOCK // TILE - 1 - a)
-        prob_cols.append(jnp.concatenate(before + [part.astype(BF) for part in parts] + after, axis=0))
-        grad_cols.append(jnp.concatenate(before + grads + after, axis=0))
+        prob_cols.append(jnp.concatenate([part.astype(BF) for part in parts], axis=0))
+        grad_cols.append(jnp.concatenate(grads, axis=0))
     return jnp.concatenate(prob_cols, axis=1), jnp.concatenate(grad_cols, axis=1)
 
 
-def one_head(value, h, head_size):
-    lane = iota2(value.shape, 1)
-    mine = (lane >= h * head_size) & (lane < (h + 1) * head_size)
-    return jnp.where(mine, value, jnp.zeros((), value.dtype))
+def both_heads(value, axis, along):
+    place = iota2(value.shape, axis)
+    half = value.shape[axis] // 2
+    zero = jnp.zeros((), value.dtype)
+    return jnp.concatenate([jnp.where(place < half, value, zero), jnp.where(place < half, zero, value)], axis=along)
 
 
 def scores_body(
@@ -198,53 +195,39 @@
     vx[WIN:] = v_ref[...]
 
     pair = 2 * head_size
-    reach = WIN + BLOCK
-    blocks = span // BLOCK
-    zeros_half = jnp.zeros((head_size, BLOCK), BF)
-    units = [(b, h) for b in range(blocks) for h in range(2)]
+    tiles = span // TILE
 
     def one_pair(p, carry):
         cols = pl.ds(pl.multiple_of(p * pair, pair), pair)
 
-        def multiply(b, h):
-            first = b * BLOCK
-            feats = pl.ds(pl.multiple_of(p * pair + h * head_size, head_size), head_size)
-            halves = [zeros_half, zeros_half]
-            halves[h] = qt_ref[feats, first : first + BLOCK]
-            scores = mm(kx[first : first + reach, cols], jnp.concatenate(halves, axis=0))
-            halves[h] = dot_ref[feats, first : first + BLOCK]
-            slopes = mm(vx[first : first + reach, cols], jnp.concatenate(halves, axis=0))
+        def multiply(a):
+            here = slice(a * TILE, (a + 1) * TILE)
+            keys = slice(a * TILE, a * TILE + REACH)
+            scores = mm(kx[keys, cols], both_heads(qt_ref[cols, here], 0, 1))
+            slopes = mm(vx[keys, cols], both_heads(dot_ref[cols, here], 0, 1))
             return scores, slopes
 
-        totals = {}
-
-        def finish(b, h, probs, grads):
-            first = b * BLOCK
-            at = (p * 2 + h) * blocks + b
-            probs_ref[at] = probs
-            grads_ref[at] = grads
-            far = WIN - first
-            queries = one_head(q_ref[first : first + BLOCK, cols], h, head_size)
-            slopes = one_head(do_ref[first : first + BLOCK, cols], h, head_size)
-            for name, part in (("k", mm(grads[:far], queries)), ("v", mm(probs[:far], slopes))):
-                totals[name, b] = totals[name, b] + part if (name, b) in totals else part
-
-        products = {0: multiply(*units[0])}
-        for n, (b, h) in enumerate(units):
-            if n + 1 < len(units):
-                products[n + 1] = multiply(*units[n + 1])
-            probs, grads = softmax_parts(*products.pop(n), b * BLOCK, begin, length)
-            finish(b, h, probs, grads)
-
-        for name, scale, out in (("k", math.log(2.0), dkh_ref), ("v", 1.0, dvh_ref)):
-            for low in range(0, WIN, BLOCK):
+        halo_grads = []
+        products = {0: multiply(0)}
+        for a in range(tiles):
+            if a + 1 < tiles:
+                products[a + 1] = multiply(a + 1)
+            probs, grads = softmax_parts(*products.pop(a), a * TILE, begin, length)
+            probs_ref[p * tiles + a] = probs
+            grads_ref[p * tiles + a] = grads
+            here = slice(a * TILE, (a + 1) * TILE)
+            far = WIN - a * TILE
+            halo_grads.append((
+                mm(grads[:far], both_heads(q_ref[here, cols], 1, 0)),
+                mm(probs[:far], both_heads(do_ref[here, cols], 1, 0)),
+            ))
+        for which, scale, out in ((0, math.log(2.0), dkh_ref), (1, 1.0, dvh_ref)):
+            for j in range(WIN // TILE):
                 total = None
-                for b in range(blocks):
-                    at = low - b * BLOCK
-                    if 0 <= at:
-                        piece = totals[name, b][at : at + BLOCK]
-                        total = piece if total is None else total + piece
-                out[low : low + BLOCK, cols] = (total * scale).astype(BF)
+                for a in range(min(j + 1, tiles)):
+                    piece = halo_grads[a][which][(j - a) * TILE : (j - a + 1) * TILE]
+                    total = piece if total is None else total + piece
+                out[j * TILE : (j + 1) * TILE, cols] = (total * scale).astype(BF)
         return carry
 
     lax.fori_loop(0, width // pair, one_pair, 0)
@@ -265,39 +248,32 @@
     vtx[:, :WIN] = vhalo_t_ref[...]
     vtx[:, WIN:] = vt_ref[...]
     pair = 2 * head_size
-    reach = WIN + BLOCK
-    blocks = span // BLOCK
+    tiles = span // TILE
+    upper = iota2((pair, TILE), 0) < head_size
 
     def one_pair(p, carry):
         cols = pl.ds(pl.multiple_of(p * pair, pair), pair)
-        totals = {}
-        for b in range(blocks):
-            first = b * BLOCK
-            span_keys = slice(first, first + reach)
-            for h in range(2):
-                feats = pl.ds(pl.multiple_of(p * pair + h * head_size, head_size), head_size)
-                at = (p * 2 + h) * blocks + b
-                ot[feats, first : first + BLOCK] = mm(vtx[feats, span_keys], probs_ref[at]).astype(BF)
-                dqt[feats, first : first + BLOCK] = (
-                    mm(ktx[feats, span_keys], grads_ref[at]) * head_size ** (-0.5)
-                ).astype(BF)
-                queries = one_head(q_ref[first : first + BLOCK, cols], h, head_size)
-                slopes = one_head(do_ref[first : first + BLOCK, cols], h, head_size)
-                near = slice(WIN - first, reach)
-                for name, part in (
-                    ("k", mm(grads_ref[at, near], queries)),
-                    ("v", mm(probs_ref[at, near], slopes)),
-                ):
-                    totals[name, b] = totals[name, b] + part if (name, b) in totals else part
-        for name, factor, out in (("k", math.log(2.0), dk), ("v", 1.0, dv)):
-            for low in range(0, span, BLOCK):
+        own_grads = []
+        for a in range(tiles):
+            here = slice(a * TILE, (a + 1) * TILE)
+            keys = slice(a * TILE, a * TILE + REACH)
+            at = p * tiles + a
+            mixed = mm(vtx[cols, keys], probs_ref[at])
+            ot[cols, here] = jnp.where(upper, mixed[:, :TILE], mixed[:, TILE:]).astype(BF)
+            moved = mm(ktx[cols, keys], grads_ref[at]) * head_size ** (-0.5)
+            dqt[cols, here] = jnp.where(upper, moved[:, :TILE], moved[:, TILE:]).astype(BF)
+            near = slice(WIN - a * TILE, REACH)
+            own_grads.append((
+                mm(grads_ref[at, near], both_heads(q_ref[here, cols], 1, 0)),
+                mm(probs_ref[at, near], both_heads(do_ref[here, cols], 1, 0)),
+            ))
+        for which, factor, out in ((0, math.log(2.0), dk), (1, 1.0, dv)):
+            for j in range(tiles):
                 total = None
-                for b in range(blocks):
-                    piece = totals[name, b]
-                    if low + BLOCK <= piece.shape[0]:
-                        piece = piece[low : low + BLOCK]
-                        total = piece if total is None else total + piece
-                out[low : low + BLOCK, cols] = (total * factor).astype(BF)
+                for a in range(j, tiles):
+                    piece = own_grads[a][which][j * TILE : (j + 1) * TILE]
+                    total = piece if total is None else total + piece
+                out[j * TILE : (j + 1) * TILE, cols] = (total * factor).astype(BF)
         return carry
 
     lax.fori_loop(0, width // pair, one_pair, 0)
@@ -357,28 +333,19 @@
         out[...] = total.astype(BF)
 
 
-def scattered(inputs, place, axis, parts, step):
+def spread(inputs, place, parts):
     columns = inputs[0].shape[-1]
     inputs = [shard.reshape(parts, -1, columns) for shard in inputs]
     piece = sds(inputs[0].shape[1:])
-    pieces = vmem_call(
-        spread_body, [piece] * parts, [place.reshape(1)] + inputs, smem=(0,)
-    )
+    return vmem_call(spread_body, [piece] * parts, [place.reshape(1)] + inputs, smem=(0,))
+
+
+def swapped(pieces, axis, step):
     count = lax.axis_size(axis)
     return [pieces[0]] + [
-        lax.ppermute(pieces[k], axis, [(i, i ^ (k * step)) for i in range(count)])
-        for k in range(1, parts)
+        lax.ppermute(piece, axis, [(i, i ^ (k * step)) for i in range(count)])
+        for k, piece in enumerate(pieces[1:], 1)
     ]
-
-
-def scatter_sums(keep, got):
-    seqs, streams = lax.axis_size("seq"), lax.axis_size("stream")
-    pieces = scattered([keep, got], lax.axis_index("stream"), "stream", streams, 1)
-    pieces = scattered(pieces, lax.axis_index("seq") >> 1, "seq", seqs // 2, 2)
-    total = pieces[0].astype(F32)
-    for piece in pieces[1:]:
-        total = total + piece.astype(F32)
-    return total
 
 
 def shards(
@@ -413,6 +380,7 @@
         hbm=(1,),
         scratch=[pltpu.VMEM((row_count, width), BF), pltpu.SemaphoreType.DMA((1,))],
         flops=cube,
+        limit=60,
     )
     incoming = exchanged(outgoing)
     pick, pick_t, placing_t, do, dot = vmem_call(
@@ -432,7 +400,7 @@
         scratch=[pltpu.VMEM((width, width), BF), pltpu.SemaphoreType.DMA((3,))],
         flops=3 * cube,
     )
-    saved = sds((H * (span // BLOCK), WIN + BLOCK, BLOCK))
+    saved = sds((H // 2 * (span // TILE), REACH, 2 * TILE))
     probs, grads, dkh, dvh, khalo_t, vhalo_t, back = vmem_call(
         lambda *refs: scores_body(head_size, *refs),
         [saved, saved] + [square] * 5,
@@ -469,10 +437,16 @@
     returning, = vmem_call(
         returning_body, [square], [frames, slope, extra, cot, pick_t], flops=cube
     )
-    got, _ = lax.optimization_barrier((got, returning))
+    got, returning = lax.optimization_barrier((got, returning))
+    pieces = spread([keep, got], lax.axis_index("stream"), lax.axis_size("stream"))
+    *pieces, returning = lax.optimization_barrier((*pieces, returning))
+    pieces = swapped(pieces, "stream", 1)
     arrived = exchanged(returning)
     frame_grads, = vmem_call(arrived_body, [square], [placing_t, arrived], flops=cube)
-    weight_grads = scatter_sums(keep, got)
+    pieces = swapped(spread(pieces, lax.axis_index("seq") >> 1, seqs // 2), "seq", 2)
+    weight_grads = pieces[0].astype(F32)
+    for piece in pieces[1:]:
+        weight_grads = weight_grads + piece.astype(F32)
     return (out_frames[None], frame_grads, weight_grads)
 
 

time: 102 us -> 112 us (1.098)
  local copies, waits for them, and re-layouts: 11.7 us -> 16 us
  Pallas kernels: 31.2 us -> 34.4 us
  starting transfers between devices: 24.8 us -> 27.2 us
    unnamed x36 -> x52, local copies, waits for them, and re-layouts: 10.9 us -> 15.2 us
    pallas_call x10, Pallas kernels: 31.2 us -> 34.4 us  [vmem_call(): pl.pallas_call(body, out_shape=tuple(outs), in_specs=[pl.BlockSpec(memory...]
    all_to_all x2, waiting for transfers between devices: 10.5 us -> 7.86 us  [exchanged(): lax.all_to_all(shard.reshape(devices, slots, width), AXES, split_axis=0,...]
    ppermute x6, waiting for transfers between devices: 20.5 us -> 22.7 us  [swapped(): lax.ppermute(piece, axis, [(i, i ^ k * step) for i in range(count)])]
    ppermute x1, starting transfers between devices: 1.34 us -> 3.52 us  [shards(): got = lax.ppermute(send, 'seq', [(i, i ^ 1) for i in range(seqs)])]
  transfers between devices with their start and end apart: 11 -> 11, of which waited for: 6 -> 5; matrix products, arithmetic and copies ran while one was open for 1% -> 1% of each run, Pallas kernels for 16% -> 14%
where the time goes in v3:
time: 112 us; the launch traced here: 111 us
  Pallas kernels  34.4 us (31%)
  waiting for transfers between devices  30.5 us (27%)
  starting transfers between devices  27.2 us (24%)
  local copies, waits for them, and re-layouts  16 us (14%)
  between operations  1.55 us (1%)
    pallas_call x10, Pallas kernels, vmem_call(): pl.pallas_call(body, out_shape=tuple(outs), in_specs=[pl.BlockSpec(memory...  34.4 us
    ppermute x6, waiting for transfers between devices, swapped(): lax.ppermute(piece, axis, [(i, i ^ k * step) for i in range(count)])  22.7 us
    unnamed x52, local copies, waits for them, and re-layouts  15.2 us
    all_to_all x2, starting transfers between devices, exchanged(): lax.all_to_all(shard.reshape(devices, slots, width), AXES, split_axis=0,...  12.4 us
    ppermute x6, starting transfers between devices, swapped(): lax.ppermute(piece, axis, [(i, i ^ k * step) for i in range(count)])  8.01 us
    all_to_all x2, waiting for transfers between devices, exchanged(): lax.all_to_all(shard.reshape(devices, slots, width), AXES, split_axis=0,...  7.86 us
    ppermute x1, starting transfers between devices, shards(): got = lax.ppermute(send, 'seq', [(i, i ^ 1) for i in range(seqs)])  3.52 us
    ppermute x2, starting transfers between devices, passed_along(): return lax.ppermute(shard, 'seq', pairs)  3.23 us
  transfers between devices with their start and end apart: 11, of which 5 were waited for; matrix products, arithmetic and copies ran while one was open for 1% of the time, Pallas kernels for 14%

profile of v3, /device:TPU:0, one launch (start us, length us, event | category | flops | bytes accessed | tf_op | source)
XLA Modules:
  0.0 110.5 jit_solution(3689389172170608837)
XLA Ops:
  0.7 3.1 %shard_map.112 = (bf16[512,512]{1,0:T(8,128)(2,1)}, bf16[512,512]{1,0:T(8,128)(2,1)}) custom-call(s32[1,512]{1,0:T(1,128)} %bitcast.31, bf16[512,512]{1,0:T(8,128)(2,1)} %refs_1_.2), custom_call_target="tpu_custom_call" | custom-call | flops 268435456 | bytes 1574912 | tf_op jit(solution)/shard_map/pallas_call | solution.py:33
  3.8 7.3 %all-to-all-start = ((bf16[32,16,512]{2,1,0:T(8,128)(2,1)}), bf16[32,16,512]{2,1,0:T(8,128)(2,1)S(1)}, u32[]{:S(2)}, u32[]{:S(2)}) async-start(bf16[32,16,512]{2,1,0:T(8,128)(2,1)} %bitcast.28), calls=%async_computation | async-start | bytes 1048576 | tf_op jit(solution)/shard_map/all_to_all | solution.py:371
  15.0 1.3 %shard_map.113 = (bf16[512,512]{1,0:T(8,128)(2,1)S(1)}, bf16[512,512]{1,0:T(8,128)(2,1)S(1)}, bf16[512,512]{1,0:T(8,128)(2,1)S(1)}, bf16[512,512]{1,0:T(8,128)(2,1)S(1)}, bf16[512,512]{1,0:T(8,128)(2,1)S(1)}) custom-call(s32[512,1]{1,0:T(8,128)S(1)} %copy.12.refs_0_, bf16[512,512]{1,0:T(8,128)(2,1)S(1)} %copy-done.25, bf16[512,512]{1,0:T(8,128)(2,1)S(1)} %bitcast.18, ...), custom_call_target="tpu_custom_call" | custom-call | flops 536870912 | bytes 4196352 | tf_op jit(solution)/shard_map/pallas_call | solution.py:33
  19.6 7.9 %all-to-all-done = bf16[32,16,512]{2,1,0:T(8,128)(2,1)S(1)} async-done(((bf16[32,16,512]{2,1,0:T(8,128)(2,1)}), bf16[32,16,512]{2,1,0:T(8,128)(2,1)S(1)}, u32[]{:S(2)}, u32[]{:S(2)}) %all-to-all-start) | async-done | bytes 524320 | tf_op jit(solution)/shard_map/all_to_all | solution.py:371
  28.5 1.4 %shard_map.114 = (bf16[512,512]{1,0:T(8,128)(2,1)S(1)}, bf16[512,512]{1,0:T(8,128)(2,1)}) custom-call(bf16[512,512]{1,0:T(8,128)(2,1)S(1)} %copy-done.22, bf16[512,512]{1,0:T(8,128)(2,1)S(1)} %bitcast.22), custom_call_target="tpu_custom_call" | custom-call | flops 268435456 | bytes 2097152 | tf_op jit(solution)/shard_map/pallas_call | solution.py:33
  29.9 1.9 %collective-permute-start = (bf16[512,512]{1,0:T(8,128)(2,1)}, bf16[512,512]{1,0:T(8,128)(2,1)S(1)}, u32[]{:S(2)}, u32[]{:S(2)}) collective-permute-start(bf16[512,512]{1,0:T(8,128)(2,1)} %get-tuple-element.51.refs_0_.refs_1_), channel_id=1, source_target_pairs={{0,1},{1,2},{2,3},{3,4},{4,5},{5,6},{6,7},{8,9},{9,10},{10,11},{11... | collective-permute-start | bytes 1572872 | tf_op jit(solution)/shard_map/ppermute | solution.py:322
  32.6 2.7 %shard_map.115 = (bf16[512,512]{1,0:T(8,128)(2,1)S(1)}, bf16[512,512]{1,0:T(8,128)(2,1)S(1)}, bf16[512,512]{1,0:T(8,128)(2,1)S(1)}, bf16[512,512]{1,0:T(8,128)(2...) custom-call(bf16[512,512]{1,0:T(8,128)(2,1)} %get-tuple-element.51.r, ...), custom_call_target="tpu_custom_call" | custom-call | flops 805306368 | bytes 6291456 | tf_op jit(solution)/shard_map/pallas_call | solution.py:33
  38.2 12.3 %shard_map.116 = (bf16[16,640,256]{2,1,0:T(8,128)(2,1)S(1)}, bf16[16,640,256]{2,1,0:T(8,128)(2,1)S(1)}, bf16[512,512]{1,0:T(8,128)(2,1)S(1)}, bf16[512,512]{1,0:...) custom-call(s32[3]{0:T(128)S(1)} %pad_add_fusion.refs_0_, ...), custom_call_target="tpu_custom_call" | custom-call | flops 3221225472 | bytes 17825804 | tf_op jit(solution)/shard_map/pallas_call | solution.py:33
  50.5 1.3 %collective-permute-start.1 = (bf16[512,512]{1,0:T(8,128)(2,1)S(1)}, bf16[512,512]{1,0:T(8,128)(2,1)S(1)}, u32[]{:S(2)}, u32[]{:S(2)}) collective-permute-start(bf16[512,512]{1,0:T(8,128)(2,1)S(1)} %get-tuple-element.73), channel_id=1, source_target_pairs={{1,0},{2,1},{3,2},{4,3},{5,4},{6,5},{7,6},{9,8},{10,9},{11,10},{12... | collective-permute-start | bytes 1572872 | tf_op jit(solution)/shard_map/ppermute | solution.py:322
  52.9 9.2 %shard_map.117 = (bf16[256,2048]{1,0:T(8,128)(2,1)S(1)}, bf16[256,2048]{1,0:T(8,128)(2,1)}, bf16[512,512]{1,0:T(8,128)(2,1)}, f32[512,512]{1,0:T(8,128)S(1)}) custom-call(s32[3]{0:T(128)S(1)} %pad_add_fusion.refs_0_, bf16[512,512]{1,0:T(8,128)(2,1)} %get-tuple-element.51.refs_0_.refs_1_, bf16[512,512]{1,0:T(8,128)(2,1)S(1)} %copy-done.18, ...), custom_call_target="tpu_custom_call" | custom-call | flops 4831838208 | bytes 22544396 | tf_op jit(solution)/shard_map/pallas_call | solution.py:33
  63.0 3.5 %collective-permute-start.2 = (bf16[256,2048]{1,0:T(8,128)(2,1)}, bf16[256,2048]{1,0:T(8,128)(2,1)}, u32[]{:S(2)}, u32[]{:S(2)}) collective-permute-start(bf16[256,2048]{1,0:T(8,128)(2,1)} %get-tuple-element.74), channel_id=1, source_target_pairs={{0,1},{1,0},{2,3},{3,2},{4,5},{5,4},{6,7},{7,6},{8,9},{9,8},{10,11... | collective-permute-start | bytes 3145736 | tf_op jit(solution)/shard_map/ppermute | solution.py:436
  68.6 1.6 %shard_map.118 = bf16[512,512]{1,0:T(8,128)(2,1)} custom-call(bf16[512,512]{1,0:T(8,128)(2,1)S(1)} %get-tuple-element.52.refs_3_.frames_ref, f32[512,512]{1,0:T(8,128)S(1)} %get-tuple-element.75.slope_ref, bf16[512,512]{1,0:T(8,128)(2,1)S(1)} %copy-done.20, bf16[512,512]{1,0:T(8,128)(2,1)S(1)} %bitcast.20, bf16[512,512]{1,0:T(8,128)(2,1)S(1)} %copy-done.13), custom_call_target="tpu_custom_call" | custom-call | flops 268435456 | bytes 3670016 | tf_op jit(solution)/shard_map/pallas_call | solution.py:33
  70.2 1.5 %shard_map.119 = (bf16[64,2048]{1,0:T(8,128)(2,1)S(1)}, bf16[64,2048]{1,0:T(8,128)(2,1)S(1)}, bf16[64,2048]{1,0:T(8,128)(2,1)S(1)}, bf16[64,2048]{1,0:T(8,128)(2,1)S(1)}) custom-call(s32[1]{0:T(128)} %bitcast.8.place_ref, bf16[4,64,2048]{2,1,0:T(8,128)(2,1)S(1)} %bitcast.23, bf16[4,64,2048]{2,1,0:T(8,128)(2,1)} %bitcast.10.refs_1_), custom_call_target="tpu_custom_call" | custom-call | bytes 3145732 | tf_op jit(solution)/shard_map/pallas_call | solution.py:33
  71.6 5.1 %all-to-all-start.1 = ((bf16[32,16,512]{2,1,0:T(8,128)(2,1)}), bf16[32,16,512]{2,1,0:T(8,128)(2,1)S(1)}, u32[]{:S(2)}, u32[]{:S(2)}) async-start(bf16[32,16,512]{2,1,0:T(8,128)(2,1)} %bitcast.11), calls=%async_computation.1 | async-start | bytes 1048576 | tf_op jit(solution)/shard_map/all_to_all | solution.py:371
  76.7 1.8 %collective-permute-start.3 = (bf16[64,2048]{1,0:T(8,128)(2,1)S(1)}, bf16[64,2048]{1,0:T(8,128)(2,1)S(1)}, u32[]{:S(2)}, u32[]{:S(2)}) collective-permute-start(bf16[64,2048]{1,0:T(8,128)(2,1)S(1)} %get-tuple-element.86), channel_id=1, source_target_pairs={{0,8},{8,0},{16,24},{24,16},{1,9},{9,1},{17,25},{25,17},{2,10},{10... | collective-permute-start | bytes 786440 | tf_op jit(solution)/shard_map/ppermute | solution.py:346
  78.6 1.5 %collective-permute-start.4 = (bf16[64,2048]{1,0:T(8,128)(2,1)S(1)}, bf16[64,2048]{1,0:T(8,128)(2,1)S(1)}, u32[]{:S(2)}, u32[]{:S(2)}) collective-permute-start(bf16[64,2048]{1,0:T(8,128)(2,1)S(1)} %get-tuple-element.87), channel_id=1, source_target_pairs={{0,16},{8,24},{16,0},{24,8},{1,17},{9,25},{17,1},{25,9},{2,18},{10... | collective-permute-start | bytes 786440 | tf_op jit(solution)/shard_map/ppermute | solution.py:346
  80.3 10.3 %collective-permute-done.3 = bf16[64,2048]{1,0:T(8,128)(2,1)S(1)} collective-permute-done((bf16[64,2048]{1,0:T(8,128)(2,1)S(1)}, bf16[64,2048]{1,0:T(8,128)(2,1)S(1)}, u32[]{:S(2)}, u32[]{:S(2)}) %collective-permute-start.3) | collective-permute-done | bytes 262176 | tf_op jit(solution)/shard_map/ppermute | solution.py:346
  90.6 6.8 %collective-permute-done.5 = bf16[64,2048]{1,0:T(8,128)(2,1)S(1)} collective-permute-done((bf16[64,2048]{1,0:T(8,128)(2,1)S(1)}, bf16[64,2048]{1,0:T(8,128)(2,1)S(1)}, u32[]{:S(2)}, u32[]{:S(2)}) %collective-permute-start.5) | collective-permute-done | bytes 262176 | tf_op jit(solution)/shard_map/ppermute | solution.py:346
  97.5 1.5 %collective-permute-start.6 = (bf16[16,2048]{1,0:T(8,128)(2,1)S(1)}, bf16[16,2048]{1,0:T(8,128)(2,1)S(1)}, u32[]{:S(2)}, u32[]{:S(2)}) collective-permute-start(bf16[16,2048]{1,0:T(8,128)(2,1)S(1)} %get-tuple-element.90), channel_id=1, source_target_pairs={{0,2},{1,3},{2,0},{3,1},{4,6},{5,7},{6,4},{7,5},{8,10},{9,11},{10,... | collective-permute-start | bytes 196616 | tf_op jit(solution)/shard_map/ppermute | solution.py:346
  99.0 2.4 %collective-permute-start.7 = (bf16[16,2048]{1,0:T(8,128)(2,1)S(1)}, bf16[16,2048]{1,0:T(8,128)(2,1)S(1)}, u32[]{:S(2)}, u32[]{:S(2)}) collective-permute-start(bf16[16,2048]{1,0:T(8,128)(2,1)S(1)} %get-tuple-element.91), channel_id=1, source_target_pairs={{0,4},{1,5},{2,6},{3,7},{4,0},{5,1},{6,2},{7,3},{8,12},{9,13},{10,... | collective-permute-start | bytes 196616 | tf_op jit(solution)/shard_map/ppermute | solution.py:346
  102.0 4.2 %collective-permute-done.7 = bf16[16,2048]{1,0:T(8,128)(2,1)S(1)} collective-permute-done((bf16[16,2048]{1,0:T(8,128)(2,1)S(1)}, bf16[16,2048]{1,0:T(8,128)(2,1)S(1)}, u32[]{:S(2)}, u32[]{:S(2)}) %collective-permute-start.7) | collective-permute-done | bytes 65568 | tf_op jit(solution)/shard_map/ppermute | solution.py:346
  106.2 1.4 %collective-permute-done.8 = bf16[16,2048]{1,0:T(8,128)(2,1)S(1)} collective-permute-done((bf16[16,2048]{1,0:T(8,128)(2,1)S(1)}, bf16[16,2048]{1,0:T(8,128)(2,1)S(1)}, u32[]{:S(2)}, u32[]{:S(2)}) %collective-permute-start.8) | collective-permute-done | bytes 65568 | tf_op jit(solution)/shard_map/ppermute | solution.py:346
  108.3 1.0 copy-done.11
  109.3 1.2 %shard_map.120 = bf16[512,512]{1,0:T(8,128)(2,1)} custom-call(bf16[512,512]{1,0:T(8,128)(2,1)S(1)} %copy-done.11, bf16[512,512]{1,0:T(8,128)(2,1)S(1)} %bitcast.21), custom_call_target="tpu_custom_call" | custom-call | flops 268435456 | bytes 1572864 | tf_op jit(solution)/shard_map/pallas_call | solution.py:33
  (63 shorter events, 16.8 us)
Async XLA Ops:
  0.6 31.9 %copy-start.8 = (bf16[512,512]{1,0:T(8,128)(2,1)S(1)}, bf16[512,512]{1,0:T(8,128)(2,1)}, u32[]{:S(2)}) copy-start(bf16[512,512]{1,0:T(8,128)(2,1)} %refs_7_.1) | copy-start | bytes 1572868
  0.6 31.9 %copy-start.6 = (bf16[512,512]{1,0:T(8,128)(2,1)S(1)}, bf16[512,512]{1,0:T(8,128)(2,1)}, u32[]{:S(2)}) copy-start(bf16[512,512]{1,0:T(8,128)(2,1)} %refs_6_.1) | copy-start | bytes 1572868
  0.7 31.9 %copy-start.4 = (bf16[512,512]{1,0:T(8,128)(2,1)S(1)}, bf16[512,512]{1,0:T(8,128)(2,1)}, u32[]{:S(2)}) copy-start(bf16[512,512]{1,0:T(8,128)(2,1)} %refs_5_.1) | copy-start | bytes 1572868
  3.8 23.7 %all-to-all-start = ((bf16[32,16,512]{2,1,0:T(8,128)(2,1)}), bf16[32,16,512]{2,1,0:T(8,128)(2,1)S(1)}, u32[]{:S(2)}, u32[]{:S(2)}) async-start(bf16[32,16,512]{2,1,0:T(8,128)(2,1)} %bitcast.28), calls=%async_computation | async-start | bytes 1048576 | tf_op jit(solution)/shard_map/all_to_all | solution.py:371
  11.9 1.0 copy-start
  19.6 31.0 %copy-start.14 = (bf16[512,512]{1,0:T(8,128)(2,1)}, bf16[512,512]{1,0:T(8,128)(2,1)S(1)}, u32[]{:S(2)}) copy-start(bf16[512,512]{1,0:T(8,128)(2,1)S(1)} %get-tuple-element.61.refs_8_.refs_14_) | copy-start | bytes 1572868
  29.9 5.4 %collective-permute-start = (bf16[512,512]{1,0:T(8,128)(2,1)}, bf16[512,512]{1,0:T(8,128)(2,1)S(1)}, u32[]{:S(2)}, u32[]{:S(2)}) collective-permute-start(bf16[512,512]{1,0:T(8,128)(2,1)} %get-tuple-element.51.refs_0_.refs_1_), channel_id=1, source_target_pairs={{0,1},{1,2},{2,3},{3,4},{4,5},{5,6},{6,7},{8,9},{9,10},{10,11},{11... | collective-permute-start | bytes 1572872 | tf_op jit(solution)/shard_map/ppermute | solution.py:322
  38.2 13.6 %copy-start.1 = (bf16[1,512,512]{2,1,0:T(8,128)(2,1)S(1)}, bf16[1,512,512]{2,1,0:T(8,128)(2,1)}, u32[]{:S(2)}) copy-start(bf16[1,512,512]{2,1,0:T(8,128)(2,1)} %param.17) | copy-start | bytes 1572868
  38.2 13.6 %copy-start.3 = (bf16[512,512]{1,0:T(8,128)(2,1)S(1)}, bf16[512,512]{1,0:T(8,128)(2,1)}, u32[]{:S(2)}) copy-start(bf16[512,512]{1,0:T(8,128)(2,1)} %refs_8_.1) | copy-start | bytes 1572868
  38.2 13.6 %copy-start.5 = (bf16[512,512]{1,0:T(8,128)(2,1)S(1)}, bf16[512,512]{1,0:T(8,128)(2,1)}, u32[]{:S(2)}) copy-start(bf16[512,512]{1,0:T(8,128)(2,1)} %refs_5_.1) | copy-start | bytes 1572868
  38.2 13.6 %copy-start.7 = (bf16[512,512]{1,0:T(8,128)(2,1)S(1)}, bf16[512,512]{1,0:T(8,128)(2,1)}, u32[]{:S(2)}) copy-start(bf16[512,512]{1,0:T(8,128)(2,1)} %refs_6_.1) | copy-start | bytes 1572868
  38.2 13.6 %copy-start.9 = (bf16[512,512]{1,0:T(8,128)(2,1)S(1)}, bf16[512,512]{1,0:T(8,128)(2,1)}, u32[]{:S(2)}) copy-start(bf16[512,512]{1,0:T(8,128)(2,1)} %refs_7_.1) | copy-start | bytes 1572868
  38.2 13.6 %copy-start.18 = (bf16[512,512]{1,0:T(8,128)(2,1)S(1)}, bf16[512,512]{1,0:T(8,128)(2,1)}, u32[]{:S(2)}) copy-start(bf16[512,512]{1,0:T(8,128)(2,1)} %copy-done.16) | copy-start | bytes 1572868
  50.5 11.7 %collective-permute-start.1 = (bf16[512,512]{1,0:T(8,128)(2,1)S(1)}, bf16[512,512]{1,0:T(8,128)(2,1)S(1)}, u32[]{:S(2)}, u32[]{:S(2)}) collective-permute-start(bf16[512,512]{1,0:T(8,128)(2,1)S(1)} %get-tuple-element.73), channel_id=1, source_target_pairs={{1,0},{2,1},{3,2},{4,3},{5,4},{6,5},{7,6},{9,8},{10,9},{11,10},{12... | collective-permute-start | bytes 1572872 | tf_op jit(solution)/shard_map/ppermute | solution.py:322
  51.9 1.0 copy-start.15
  63.0 7.2 %collective-permute-start.2 = (bf16[256,2048]{1,0:T(8,128)(2,1)}, bf16[256,2048]{1,0:T(8,128)(2,1)}, u32[]{:S(2)}, u32[]{:S(2)}) collective-permute-start(bf16[256,2048]{1,0:T(8,128)(2,1)} %get-tuple-element.74), channel_id=1, source_target_pairs={{0,1},{1,0},{2,3},{3,2},{4,5},{5,4},{6,7},{7,6},{8,9},{9,8},{10,11... | collective-permute-start | bytes 3145736 | tf_op jit(solution)/shard_map/ppermute | solution.py:436
  71.6 36.6 %all-to-all-start.1 = ((bf16[32,16,512]{2,1,0:T(8,128)(2,1)}), bf16[32,16,512]{2,1,0:T(8,128)(2,1)S(1)}, u32[]{:S(2)}, u32[]{:S(2)}) async-start(bf16[32,16,512]{2,1,0:T(8,128)(2,1)} %bitcast.11), calls=%async_computation.1 | async-start | bytes 1048576 | tf_op jit(solution)/shard_map/all_to_all | solution.py:371
  76.7 13.9 %collective-permute-start.3 = (bf16[64,2048]{1,0:T(8,128)(2,1)S(1)}, bf16[64,2048]{1,0:T(8,128)(2,1)S(1)}, u32[]{:S(2)}, u32[]{:S(2)}) collective-permute-start(bf16[64,2048]{1,0:T(8,128)(2,1)S(1)} %get-tuple-element.86), channel_id=1, source_target_pairs={{0,8},{8,0},{16,24},{24,16},{1,9},{9,1},{17,25},{25,17},{2,10},{10... | collective-permute-start | bytes 786440 | tf_op jit(solution)/shard_map/ppermute | solution.py:346
  78.6 12.0 %collective-permute-start.4 = (bf16[64,2048]{1,0:T(8,128)(2,1)S(1)}, bf16[64,2048]{1,0:T(8,128)(2,1)S(1)}, u32[]{:S(2)}, u32[]{:S(2)}) collective-permute-start(bf16[64,2048]{1,0:T(8,128)(2,1)S(1)} %get-tuple-element.87), channel_id=1, source_target_pairs={{0,16},{8,24},{16,0},{24,8},{1,17},{9,25},{17,1},{25,9},{2,18},{10... | collective-permute-start | bytes 786440 | tf_op jit(solution)/shard_map/ppermute | solution.py:346
  80.0 17.4 %collective-permute-start.5 = (bf16[64,2048]{1,0:T(8,128)(2,1)S(1)}, bf16[64,2048]{1,0:T(8,128)(2,1)S(1)}, u32[]{:S(2)}, u32[]{:S(2)}) collective-permute-start(bf16[64,2048]{1,0:T(8,128)(2,1)S(1)} %get-tuple-element.88), channel_id=1, source_target_pairs={{0,24},{8,16},{16,8},{24,0},{1,25},{9,17},{17,9},{25,1},{2,26},{10... | collective-permute-start | bytes 786440 | tf_op jit(solution)/shard_map/ppermute | solution.py:346
  97.5 4.5 %collective-permute-start.6 = (bf16[16,2048]{1,0:T(8,128)(2,1)S(1)}, bf16[16,2048]{1,0:T(8,128)(2,1)S(1)}, u32[]{:S(2)}, u32[]{:S(2)}) collective-permute-start(bf16[16,2048]{1,0:T(8,128)(2,1)S(1)} %get-tuple-element.90), channel_id=1, source_target_pairs={{0,2},{1,3},{2,0},{3,1},{4,6},{5,7},{6,4},{7,5},{8,10},{9,11},{10,... | collective-permute-start | bytes 196616 | tf_op jit(solution)/shard_map/ppermute | solution.py:346
  99.0 7.1 %collective-permute-start.7 = (bf16[16,2048]{1,0:T(8,128)(2,1)S(1)}, bf16[16,2048]{1,0:T(8,128)(2,1)S(1)}, u32[]{:S(2)}, u32[]{:S(2)}) collective-permute-start(bf16[16,2048]{1,0:T(8,128)(2,1)S(1)} %get-tuple-element.91), channel_id=1, source_target_pairs={{0,4},{1,5},{2,6},{3,7},{4,0},{5,1},{6,2},{7,3},{8,12},{9,13},{10,... | collective-permute-start | bytes 196616 | tf_op jit(solution)/shard_map/ppermute | solution.py:346
  101.4 6.2 %collective-permute-start.8 = (bf16[16,2048]{1,0:T(8,128)(2,1)S(1)}, bf16[16,2048]{1,0:T(8,128)(2,1)S(1)}, u32[]{:S(2)}, u32[]{:S(2)}) collective-permute-start(bf16[16,2048]{1,0:T(8,128)(2,1)S(1)} %get-tuple-element.92), channel_id=1, source_target_pairs={{0,6},{1,7},{2,4},{3,5},{4,2},{5,3},{6,0},{7,1},{8,14},{9,15},{10,... | collective-permute-start | bytes 196616 | tf_op jit(solution)/shard_map/ppermute | solution.py:346
  108.3 1.0 copy-start.11
  (13 other events, 12.1 us)

commit v4 on v3

--- a/solution.py
+++ b/solution.py
@@ -73,7 +73,7 @@
 
 
 def early_body(
-    slots, owner_ref, placing_ref, cot_ref, wo_ref, pick_ref, pick_t_ref, placing_t_ref, do_ref, dot_ref
+    slots, owner_ref, placing_ref, cot_ref, wo_ref, pick_ref, pick_t_ref, placing_t_ref, dot_ref
 ):
     span, lanes = owner_ref.shape[0], 128
     total = pick_ref.shape[1]
@@ -88,9 +88,7 @@
     pick_ref[...] = pick.astype(BF)
     pick_t_ref[...] = pick.T.astype(BF)
     placing_t_ref[...] = placing_ref[...].T
-    grad = mm(cot_ref[...], wo_ref[...], NT).astype(BF)
-    do_ref[...] = grad
-    dot_ref[...] = grad.T
+    dot_ref[...] = mm(cot_ref[...], wo_ref[...], NT).astype(BF).T
 
 
 def unit_frames(frames):
@@ -107,14 +105,12 @@
 
 def project_body(
     query_scale, normed_ref, wq_hbm, wk_hbm, wv_hbm,
-    q_ref, qt_ref, k_ref, kt_ref, v_ref, vt_ref, wk_ref, wv_ref, wq_ref, sems,
+    qt_ref, k_ref, kt_ref, v_ref, vt_ref, wk_ref, wv_ref, wq_ref, sems,
 ):
     copies = fetch([wq_hbm, wk_hbm, wv_hbm], [wq_ref, wk_ref, wv_ref], sems)
     normed = normed_ref[...]
     copies[0].wait()
-    q = (mm(normed, wq_ref[...]) * query_scale).astype(BF)
-    q_ref[...] = q
-    qt_ref[...] = q.T
+    qt_ref[...] = (mm(normed, wq_ref[...]) * query_scale).astype(BF).T
     copies[1].wait()
     k = mm(normed, wk_ref[...]).astype(BF)
     k_ref[...] = k
@@ -135,7 +131,7 @@
     halo_bias = jnp.where(begin == 0, NEG, 0.0)
     count = REACH // TILE
     time = begin + first + iota2((1, TILE), 1)
-    prob_cols, grad_cols = [], []
+    raised_cols, grad_cols, scales = [], [], []
     for h in range(2):
         at = slice(h * TILE, (h + 1) * TILE)
         parts = []
@@ -152,22 +148,25 @@
         for part in parts[1:]:
             peak = jnp.maximum(peak, part)
         peak = jnp.max(peak, axis=0, keepdims=True)
-        parts = [jnp.exp2(part - peak) for part in parts]
-        denom = parts[0]
-        for part in parts[1:]:
-            denom = denom + part
+        moves = [slopes[n * TILE : (n + 1) * TILE, at] for n in range(count)]
+        denom = centre = None
+        low_parts = []
+        for part, move in zip(parts, moves):
+            part = jnp.exp2(part - peak)
+            low_parts.append(part.astype(BF))
+            moved = part * move
+            denom = part if denom is None else denom + part
+            centre = moved if centre is None else centre + moved
         denom = jnp.sum(denom, axis=0, keepdims=True)
-        scale = jnp.where(time < length, 1.0 / denom, 0.0)
-        parts = [part * scale for part in parts]
-        moved = [part * slopes[n * TILE : (n + 1) * TILE, at] for n, part in enumerate(parts)]
-        centre = moved[0]
-        for part in moved[1:]:
-            centre = centre + part
-        centre = jnp.sum(centre, axis=0, keepdims=True)
-        grads = [(move - part * centre).astype(BF) for part, move in zip(parts, moved)]
-        prob_cols.append(jnp.concatenate([part.astype(BF) for part in parts], axis=0))
-        grad_cols.append(jnp.concatenate(grads, axis=0))
-    return jnp.concatenate(prob_cols, axis=1), jnp.concatenate(grad_cols, axis=1)
+        centre = jnp.sum(centre, axis=0, keepdims=True) / denom
+        scales.append(jnp.where(time < length, 1.0 / denom, 0.0))
+        raised_cols.append(jnp.concatenate(low_parts, axis=0))
+        grad_cols.append(jnp.concatenate(
+            [(part.astype(F32) * (move - centre)).astype(BF) for part, move in zip(low_parts, moves)], axis=0
+        ))
+    return (
+        jnp.concatenate(raised_cols, axis=1), jnp.concatenate(grad_cols, axis=1), jnp.concatenate(scales, axis=1)
+    )
 
 
 def both_heads(value, axis, along):
@@ -178,11 +177,11 @@
 
 
 def scores_body(
-    head_size, meta_ref, halo_ref, wk_ref, wv_ref, q_ref, qt_ref, k_ref, v_ref, do_ref, dot_ref,
-    probs_ref, grads_ref, dkh_ref, dvh_ref, khalo_t_ref, vhalo_t_ref, back_ref,
+    head_size, meta_ref, halo_ref, wk_ref, wv_ref, qt_ref, k_ref, v_ref, dot_ref,
+    raised_ref, grads_ref, scale_ref, q_ref, do_ref, dkh_ref, dvh_ref, khalo_t_ref, vhalo_t_ref, back_ref,
     kx, vx,
 ):
-    span, width = q_ref.shape
+    span, width = k_ref.shape
     begin, length = meta_ref[0], meta_ref[1]
     halo = halo_ref[...]
     kh = mm(halo, wk_ref[...]).astype(BF)
@@ -196,6 +195,7 @@
 
     pair = 2 * head_size
     tiles = span // TILE
+    upper = iota2((pair, TILE), 0) < head_size
 
     def one_pair(p, carry):
         cols = pl.ds(pl.multiple_of(p * pair, pair), pair)
@@ -212,14 +212,20 @@
         for a in range(tiles):
             if a + 1 < tiles:
                 products[a + 1] = multiply(a + 1)
-            probs, grads = softmax_parts(*products.pop(a), a * TILE, begin, length)
-            probs_ref[p * tiles + a] = probs
+            raised, grads, scale = softmax_parts(*products.pop(a), a * TILE, begin, length)
+            raised_ref[p * tiles + a] = raised
             grads_ref[p * tiles + a] = grads
+            scale_ref[p * tiles + a] = scale
             here = slice(a * TILE, (a + 1) * TILE)
             far = WIN - a * TILE
+            spread_scale = jnp.where(upper, scale[:, :TILE], scale[:, TILE:])
+            queries = (qt_ref[cols, here].astype(F32) * spread_scale).T.astype(BF)
+            slopes = (dot_ref[cols, here].astype(F32) * spread_scale).T.astype(BF)
+            q_ref[here, cols] = queries
+            do_ref[here, cols] = slopes
             halo_grads.append((
-                mm(grads[:far], both_heads(q_ref[here, cols], 1, 0)),
-                mm(probs[:far], both_heads(do_ref[here, cols], 1, 0)),
+                mm(grads[:far], both_heads(queries, 1, 0)),
+                mm(raised[:far], both_heads(slopes, 1, 0)),
             ))
         for which, scale, out in ((0, math.log(2.0), dkh_ref), (1, 1.0, dvh_ref)):
             for j in range(WIN // TILE):
@@ -235,14 +241,12 @@
 
 
 def weights_body(
-    scale, rows, head_size, meta_ref, normed_ref, halo_ref, frames_ref, cot_ref,
-    wq_hbm, wk_hbm, wv_hbm, wo_hbm,
-    q_ref, kt_ref, vt_ref, khalo_t_ref, vhalo_t_ref, do_ref, probs_ref, grads_ref, dkh_ref, dvh_ref,
-    keep_ref, send_ref, out_ref, slope_ref,
-    normed_t, halo_t, mixed_t, ktx, vtx, ot, dqt, dk, dv, wq, wk, wv, wo, sems,
+    scale, rows, head_size, meta_ref, normed_ref, halo_ref, cot_ref,
+    q_ref, kt_ref, vt_ref, khalo_t_ref, vhalo_t_ref, do_ref, raised_ref, grads_ref, scale_ref, dkh_ref, dvh_ref,
+    keep_ref, send_ref, ot, dqt, dk, dv,
+    normed_t, halo_t, mixed_t, ktx, vtx,
 ):
     span, width = q_ref.shape
-    copies = fetch([wq_hbm, wk_hbm, wv_hbm, wo_hbm], [wq, wk, wv, wo], sems)
     ktx[:, :WIN] = khalo_t_ref[...]
     ktx[:, WIN:] = kt_ref[...]
     vtx[:, :WIN] = vhalo_t_ref[...]
@@ -258,14 +262,15 @@
             here = slice(a * TILE, (a + 1) * TILE)
             keys = slice(a * TILE, a * TILE + REACH)
             at = p * tiles + a
-            mixed = mm(vtx[cols, keys], probs_ref[at])
+            shrink = scale_ref[at]
+            mixed = mm(vtx[cols, keys], raised_ref[at]) * shrink
             ot[cols, here] = jnp.where(upper, mixed[:, :TILE], mixed[:, TILE:]).astype(BF)
-            moved = mm(ktx[cols, keys], grads_ref[at]) * head_size ** (-0.5)
+            moved = mm(ktx[cols, keys], grads_ref[at]) * (shrink * head_size ** (-0.5))
             dqt[cols, here] = jnp.where(upper, moved[:, :TILE], moved[:, TILE:]).astype(BF)
             near = slice(WIN - a * TILE, REACH)
             own_grads.append((
                 mm(grads_ref[at, near], both_heads(q_ref[here, cols], 1, 0)),
-                mm(probs_ref[at, near], both_heads(do_ref[here, cols], 1, 0)),
+                mm(raised_ref[at, near], both_heads(do_ref[here, cols], 1, 0)),
             ))
         for which, factor, out in ((0, math.log(2.0), dk), (1, 1.0, dv)):
             for j in range(tiles):
@@ -295,21 +300,23 @@
             mm(mixed, cot_ref[...]),
         )):
             out[:, n * width : (n + 1) * width] = (total * scale).astype(BF)
-    for copy in copies:
-        copy.wait()
-    slope = mm(dqt[...].T, wq[...], NT)
-    slope = slope + mm(dk[...], wk[...], NT)
-    slope_ref[...] = slope + mm(dv[...], wv[...], NT)
-    out = mm(ot[...].T, wo[...]) + frames_ref[...].astype(F32)
-    out_ref[...] = out.astype(BF)
-
-
-def returning_body(frames_ref, slope_ref, extra_ref, cot_ref, pick_t_ref, out_ref):
+
+
+def returning_body(
+    frames_ref, dqt_ref, dk_ref, dv_ref, wq_ref, wk_ref, wv_ref, extra_ref, cot_ref, pick_t_ref, out_ref
+):
     _, inverse, normed32 = unit_frames(frames_ref[...])
-    slope = slope_ref[...] + extra_ref[...].astype(F32)
+    slope = mm(dqt_ref[...].T, wq_ref[...], NT)
+    slope = slope + mm(dk_ref[...], wk_ref[...], NT)
+    slope = slope + mm(dv_ref[...], wv_ref[...], NT)
+    slope = slope + extra_ref[...].astype(F32)
     centre = jnp.mean(slope * normed32, axis=1, keepdims=True)
     grad = inverse * (slope - normed32 * centre) + cot_ref[...].astype(F32)
     out_ref[...] = mm(pick_t_ref[...], grad.astype(BF)).astype(BF)
+
+
+def out_body(frames_ref, ot_ref, wo_ref, out_ref):
+    out_ref[...] = (mm(ot_ref[...].T, wo_ref[...]) + frames_ref[...].astype(F32)).astype(BF)
 
 
 def arrived_body(placing_t_ref, in_ref, out_ref):
@@ -380,52 +387,48 @@
         hbm=(1,),
         scratch=[pltpu.VMEM((row_count, width), BF), pltpu.SemaphoreType.DMA((1,))],
         flops=cube,
-        limit=60,
     )
     incoming = exchanged(outgoing)
-    pick, pick_t, placing_t, do, dot = vmem_call(
+    pick, pick_t, placing_t, dot = vmem_call(
         lambda *refs: early_body(slots, *refs),
-        [square, square, square, square, sds((width, span))],
+        [square, square, square, sds((width, span))],
         [frame_owner.reshape(span, 1), placing, cot, out_weight],
         flops=2 * cube,
     )
     frames, normed = vmem_call(frames_body, [square, square], [pick, incoming], flops=cube)
     halo = passed_along(normed, 1)
     query_scale = head_size ** (-0.5) * math.log2(math.e)
-    q, qt, k, kt, v, vt, wk, wv = vmem_call(
+    qt, k, kt, v, vt, wk, wv = vmem_call(
         lambda *refs: project_body(query_scale, *refs),
-        [square] * 8,
+        [square] * 7,
         [normed, query_weight, key_weight, value_weight],
         hbm=(1, 2, 3),
         scratch=[pltpu.VMEM((width, width), BF), pltpu.SemaphoreType.DMA((3,))],
         flops=3 * cube,
     )
-    saved = sds((H // 2 * (span // TILE), REACH, 2 * TILE))
-    probs, grads, dkh, dvh, khalo_t, vhalo_t, back = vmem_call(
+    units = H // 2 * (span // TILE)
+    saved = sds((units, REACH, 2 * TILE))
+    raised, grads, scales, q, do, dkh, dvh, khalo_t, vhalo_t, back = vmem_call(
         lambda *refs: scores_body(head_size, *refs),
-        [saved, saved] + [square] * 5,
-        [meta, halo, wk, wv, q, qt, k, v, do, dot],
+        [saved, saved, sds((units, 1, 2 * TILE), F32)] + [square] * 7,
+        [meta, halo, wk, wv, qt, k, v, dot],
         smem=(0,),
         scratch=[pltpu.VMEM((WIN + span, width), BF)] * 2,
         flops=12 * cube,
-        limit=24,
+        limit=14,
     )
     extra = passed_along(back, -1)
     chunk = rows if in_kernel else width // 2
     split = pltpu.VMEM((width // (2 * chunk), 2, chunk, span), BF)
-    whole = pltpu.VMEM((width, width), BF)
     half = sds((width // 2, 4 * width))
-    keep, send, out_frames, slope = vmem_call(
+    keep, send, ot, dqt, dk, dv = vmem_call(
         lambda *refs: weights_body(slab ** (-0.5), chunk, head_size, *refs),
-        [half, half, square, sds((span, width), F32)],
-        [meta, normed, halo, frames, cot, query_weight, key_weight, value_weight, out_weight,
-         q, kt, vt, khalo_t, vhalo_t, do, probs, grads, dkh, dvh],
+        [half, half] + [square] * 4,
+        [meta, normed, halo, cot, q, kt, vt, khalo_t, vhalo_t, do, raised, grads, scales, dkh, dvh],
         smem=(0,),
-        hbm=(5, 6, 7, 8),
-        scratch=[split] * 3 + [pltpu.VMEM((width, WIN + span), BF)] * 2 + [whole] * 8
-        + [pltpu.SemaphoreType.DMA((4,))],
-        flops=18 * cube,
-        limit=26,
+        scratch=[split] * 3 + [pltpu.VMEM((width, WIN + span), BF)] * 2,
+        flops=14 * cube,
+        limit=14,
     )
     send, extra = lax.optimization_barrier((send, extra))
     if not in_kernel:
@@ -435,13 +438,17 @@
     seqs = lax.axis_size("seq")
     got = lax.ppermute(send, "seq", [(i, i ^ 1) for i in range(seqs)])
     returning, = vmem_call(
-        returning_body, [square], [frames, slope, extra, cot, pick_t], flops=cube
+        returning_body,
+        [square],
+        [frames, dqt, dk, dv, query_weight, key_weight, value_weight, extra, cot, pick_t],
+        flops=4 * cube,
     )
     got, returning = lax.optimization_barrier((got, returning))
     pieces = spread([keep, got], lax.axis_index("stream"), lax.axis_size("stream"))
+    pieces = swapped(pieces, "stream", 1)
     *pieces, returning = lax.optimization_barrier((*pieces, returning))
-    pieces = swapped(pieces, "stream", 1)
     arrived = exchanged(returning)
+    out_frames, = vmem_call(out_body, [square], [frames, ot, out_weight], flops=cube)
     frame_grads, = vmem_call(arrived_body, [square], [placing_t, arrived], flops=cube)
     pieces = swapped(spread(pieces, lax.axis_index("seq") >> 1, seqs // 2), "seq", 2)
     weight_grads = pieces[0].astype(F32)

time: 112 us -> 117 us (1.045)
  local copies, waits for them, and re-layouts: 16 us -> 25.7 us
  Pallas kernels: 34.4 us -> 29.8 us
  waiting for transfers between devices: 30.5 us -> 32.4 us
  starting transfers between devices: 27.2 us -> 25.6 us
    unnamed x52 -> x56, local copies, waits for them, and re-layouts: 15.2 us -> 24.9 us
    pallas_call x10 -> x11, Pallas kernels: 34.4 us -> 29.8 us  [vmem_call(): pl.pallas_call(body, out_shape=tuple(outs), in_specs=[pl.BlockSpec(memory...]
    all_to_all x2, waiting for transfers between devices: 7.86 us -> 9.71 us  [exchanged(): lax.all_to_all(shard.reshape(devices, slots, width), AXES, split_axis=0,...]
    ppermute x1, starting transfers between devices: 3.52 us -> 2.17 us  [shards(): got = lax.ppermute(send, 'seq', [(i, i ^ 1) for i in range(seqs)])]
  transfers between devices with their start and end apart: 11 -> 11, of which waited for: 5 -> 5; matrix products, arithmetic and copies ran while one was open for 1% -> 1% of each run, Pallas kernels for 14% -> 12%
where the time goes in v4:
time: 117 us; the launch traced here: 116 us
  waiting for transfers between devices  32.4 us (28%)
  Pallas kernels  29.8 us (25%)
  local copies, waits for them, and re-layouts  25.7 us (22%)
  starting transfers between devices  25.6 us (22%)
  between operations  1.47 us (1%)
    pallas_call x11, Pallas kernels, vmem_call(): pl.pallas_call(body, out_shape=tuple(outs), in_specs=[pl.BlockSpec(memory...  29.8 us
    unnamed x56, local copies, waits for them, and re-layouts  24.9 us
    ppermute x6, waiting for transfers between devices, swapped(): lax.ppermute(piece, axis, [(i, i ^ k * step) for i in range(count)])  22.7 us
    all_to_all x2, starting transfers between devices, exchanged(): lax.all_to_all(shard.reshape(devices, slots, width), AXES, split_axis=0,...  12.2 us
    all_to_all x2, waiting for transfers between devices, exchanged(): lax.all_to_all(shard.reshape(devices, slots, width), AXES, split_axis=0,...  9.71 us
    ppermute x6, starting transfers between devices, swapped(): lax.ppermute(piece, axis, [(i, i ^ k * step) for i in range(count)])  8.01 us
    ppermute x2, starting transfers between devices, passed_along(): return lax.ppermute(shard, 'seq', pairs)  3.24 us
  transfers between devices with their start and end apart: 11, of which 5 were waited for; matrix products, arithmetic and copies ran while one was open for 1% of the time, Pallas kernels for 12%

profile of v4, /device:TPU:0, one launch (start us, length us, event | category | flops | bytes accessed | tf_op | source)
XLA Modules:
  0.0 115.7 jit_solution(1084375363180661911)
XLA Ops:
  0.7 1.1 copy-done.24
  2.4 1.6 %shard_map.112 = (bf16[512,512]{1,0:T(8,128)(2,1)}, bf16[512,512]{1,0:T(8,128)(2,1)S(1)}) custom-call(s32[1,512]{1,0:T(1,128)S(1)} %bitcast.29, bf16[512,512]{1,0:T(8,128)(2,1)S(1)} %copy-done.24), custom_call_target="tpu_custom_call" | custom-call | flops 268435456 | bytes 1574912 | tf_op jit(solution)/shard_map/pallas_call | solution.py:33
  4.1 7.3 %all-to-all-start = ((bf16[32,16,512]{2,1,0:T(8,128)(2,1)}), bf16[32,16,512]{2,1,0:T(8,128)(2,1)S(1)}, u32[]{:S(2)}, u32[]{:S(2)}) async-start(bf16[32,16,512]{2,1,0:T(8,128)(2,1)} %bitcast.3), calls=%async_computation | async-start | bytes 1048576 | tf_op jit(solution)/shard_map/all_to_all | solution.py:378
  14.3 1.3 %shard_map.113 = (bf16[512,512]{1,0:T(8,128)(2,1)S(1)}, bf16[512,512]{1,0:T(8,128)(2,1)S(1)}, bf16[512,512]{1,0:T(8,128)(2,1)S(1)}, bf16[512,512]{1,0:T(8,128)(2,1)S(1)}) custom-call(s32[512,1]{1,0:T(8,128)S(1)} %copy.12.refs_0_, bf16[512,512]{1,0:T(8,128)(2,1)S(1)} %get-tuple-element.51.refs_1_, bf16[512,512]{1,0:T(8,128)(2,1)S(1)} %bitcast.20, ...), custom_call_target="tpu_custom_call" | custom-call | flops 536870912 | bytes 3672064 | tf_op jit(solution)/shard_map/pallas_call | solution.py:33
  18.0 9.7 %all-to-all-done = bf16[32,16,512]{2,1,0:T(8,128)(2,1)S(1)} async-done(((bf16[32,16,512]{2,1,0:T(8,128)(2,1)}), bf16[32,16,512]{2,1,0:T(8,128)(2,1)S(1)}, u32[]{:S(2)}, u32[]{:S(2)}) %all-to-all-start) | async-done | bytes 524320 | tf_op jit(solution)/shard_map/all_to_all | solution.py:378
  28.4 1.9 %collective-permute-start = (bf16[512,512]{1,0:T(8,128)(2,1)S(1)}, bf16[512,512]{1,0:T(8,128)(2,1)S(1)}, u32[]{:S(2)}, u32[]{:S(2)}) collective-permute-start(bf16[512,512]{1,0:T(8,128)(2,1)S(1)} %get-tuple-element.55.refs_0_.refs_1_), channel_id=1, source_target_pairs={{0,1},{1,2},{2,3},{3,4},{4,5},{5,6},{6,7},{8,9},{9,10},{10,11},{11... | collective-permute-start | bytes 1572872 | tf_op jit(solution)/shard_map/ppermute | solution.py:329
  31.1 1.0 copy-done.10
  33.1 1.7 %shard_map.115 = (bf16[512,512]{1,0:T(8,128)(2,1)S(1)}, bf16[512,512]{1,0:T(8,128)(2,1)S(1)}, bf16[512,512]{1,0:T(8,128)(2,1)S(1)}, bf16[512,512]{1,0:T(8,128)(2...) custom-call(bf16[512,512]{1,0:T(8,128)(2,1)S(1)} %get-tuple-element.55.refs_0_.ref, ...), custom_call_target="tpu_custom_call" | custom-call | flops 805306368 | bytes 5767168 | tf_op jit(solution)/shard_map/pallas_call | solution.py:33
  35.9 11.8 %shard_map.116 = (bf16[16,640,256]{2,1,0:T(8,128)(2,1)S(1)}, bf16[16,640,256]{2,1,0:T(8,128)(2,1)S(1)}, f32[16,1,256]{2,1,0:T(1,128)S(1)}, bf16[512,512]{1,0:T(8...) custom-call(s32[3]{0:T(128)S(1)} %pad_add_fusion.refs_0_, ...), custom_call_target="tpu_custom_call" | custom-call | flops 3221225472 | bytes 17842188 | tf_op jit(solution)/shard_map/pallas_call | solution.py:33
  47.7 1.3 %collective-permute-start.1 = (bf16[512,512]{1,0:T(8,128)(2,1)S(1)}, bf16[512,512]{1,0:T(8,128)(2,1)S(1)}, u32[]{:S(2)}, u32[]{:S(2)}) collective-permute-start(bf16[512,512]{1,0:T(8,128)(2,1)S(1)} %get-tuple-element.77), channel_id=1, source_target_pairs={{1,0},{2,1},{3,2},{4,3},{5,4},{6,5},{7,6},{9,8},{10,9},{11,10},{12... | collective-permute-start | bytes 1572872 | tf_op jit(solution)/shard_map/ppermute | solution.py:329
  49.0 7.4 %shard_map.117 = (bf16[256,2048]{1,0:T(8,128)(2,1)S(1)}, bf16[256,2048]{1,0:T(8,128)(2,1)}, bf16[512,512]{1,0:T(8,128)(2,1)S(1)}, bf16[512,512]{1,0:T(8,128)(2,1...) custom-call(s32[3]{0:T(128)S(1)} %pad_add_fusion.refs_0_, ...), custom_call_target="tpu_custom_call" | custom-call | flops 3758096384 | bytes 20463628 | tf_op jit(solution)/shard_map/pallas_call | solution.py:33
  60.5 2.2 %collective-permute-start.2 = (bf16[256,2048]{1,0:T(8,128)(2,1)}, bf16[256,2048]{1,0:T(8,128)(2,1)S(1)}, u32[]{:S(2)}, u32[]{:S(2)}) collective-permute-start(bf16[256,2048]{1,0:T(8,128)(2,1)} %get-tuple-element.78), channel_id=1, source_target_pairs={{0,1},{1,0},{2,3},{3,2},{4,5},{5,4},{6,7},{7,6},{8,9},{9,8},{10,11... | collective-permute-start | bytes 3145736 | tf_op jit(solution)/shard_map/ppermute | solution.py:439
  71.0 2.4 %shard_map.119 = bf16[512,512]{1,0:T(8,128)(2,1)} custom-call(bf16[512,512]{1,0:T(8,128)(2,1)S(1)} %get-tuple-element.54.frames_ref, bf16[512,512]{1,0:T(8,128)(2,1)S(1)} %copy-done.19, bf16[512,512]{1,0:T(8,128)(2,1)S(1)} %copy-done.21, bf16[512,512]{1,0:T(8,128)(2,1)S(1)} %copy-done.23, bf16[512,512]{1,0:T(8,128)(2,1)S(1)} %copy-done.9, ...), custom_call_target="tpu_custom_call" | custom-call | flops 1073741824 | bytes 5767168 | tf_op jit(solution)/shard_map/pallas_call | solution.py:33
  75.1 2.1 %collective-permute-start.5 = (bf16[64,2048]{1,0:T(8,128)(2,1)S(1)}, bf16[64,2048]{1,0:T(8,128)(2,1)S(1)}, u32[]{:S(2)}, u32[]{:S(2)}) collective-permute-start(bf16[64,2048]{1,0:T(8,128)(2,1)S(1)} %get-tuple-element.88), channel_id=1, source_target_pairs={{0,24},{8,16},{16,8},{24,0},{1,25},{9,17},{17,9},{25,1},{2,26},{10... | collective-permute-start | bytes 786440 | tf_op jit(solution)/shard_map/ppermute | solution.py:353
  77.2 5.7 %collective-permute-done.3 = bf16[64,2048]{1,0:T(8,128)(2,1)S(1)} collective-permute-done((bf16[64,2048]{1,0:T(8,128)(2,1)S(1)}, bf16[64,2048]{1,0:T(8,128)(2,1)S(1)}, u32[]{:S(2)}, u32[]{:S(2)}) %collective-permute-start.3) | collective-permute-done | bytes 262176 | tf_op jit(solution)/shard_map/ppermute | solution.py:353
  82.9 5.2 %collective-permute-done.4 = bf16[64,2048]{1,0:T(8,128)(2,1)S(1)} collective-permute-done((bf16[64,2048]{1,0:T(8,128)(2,1)S(1)}, bf16[64,2048]{1,0:T(8,128)(2,1)S(1)}, u32[]{:S(2)}, u32[]{:S(2)}) %collective-permute-start.4) | collective-permute-done | bytes 262176 | tf_op jit(solution)/shard_map/ppermute | solution.py:353
  88.1 4.9 %all-to-all-start.1 = ((bf16[32,16,512]{2,1,0:T(8,128)(2,1)}), bf16[32,16,512]{2,1,0:T(8,128)(2,1)S(1)}, u32[]{:S(2)}, u32[]{:S(2)}) async-start(bf16[32,16,512]{2,1,0:T(8,128)(2,1)} %bitcast.11), calls=%async_computation.1 | async-start | bytes 1048576 | tf_op jit(solution)/shard_map/all_to_all | solution.py:378
  93.2 1.8 %collective-permute-start.6 = (bf16[16,2048]{1,0:T(8,128)(2,1)S(1)}, bf16[16,2048]{1,0:T(8,128)(2,1)S(1)}, u32[]{:S(2)}, u32[]{:S(2)}) collective-permute-start(bf16[16,2048]{1,0:T(8,128)(2,1)S(1)} %get-tuple-element.96), channel_id=1, source_target_pairs={{0,2},{1,3},{2,0},{3,1},{4,6},{5,7},{6,4},{7,5},{8,10},{9,11},{10,... | collective-permute-start | bytes 196616 | tf_op jit(solution)/shard_map/ppermute | solution.py:353
  95.0 2.4 %collective-permute-start.7 = (bf16[16,2048]{1,0:T(8,128)(2,1)S(1)}, bf16[16,2048]{1,0:T(8,128)(2,1)S(1)}, u32[]{:S(2)}, u32[]{:S(2)}) collective-permute-start(bf16[16,2048]{1,0:T(8,128)(2,1)S(1)} %get-tuple-element.97), channel_id=1, source_target_pairs={{0,4},{1,5},{2,6},{3,7},{4,0},{5,1},{6,2},{7,3},{8,12},{9,13},{10,... | collective-permute-start | bytes 196616 | tf_op jit(solution)/shard_map/ppermute | solution.py:353
  99.7 1.3 %shard_map.118 = bf16[512,512]{1,0:T(8,128)(2,1)} custom-call(bf16[512,512]{1,0:T(8,128)(2,1)S(1)} %get-tuple-element.54.frames_ref, bf16[512,512]{1,0:T(8,128)(2,1)S(1)} %copy-done.7, bf16[512,512]{1,0:T(8,128)(2,1)S(1)} %copy-done.5), custom_call_target="tpu_custom_call" | custom-call | flops 268435456 | bytes 2097152 | tf_op jit(solution)/shard_map/pallas_call | solution.py:33
  101.0 2.9 %collective-permute-done.6 = bf16[16,2048]{1,0:T(8,128)(2,1)S(1)} collective-permute-done((bf16[16,2048]{1,0:T(8,128)(2,1)S(1)}, bf16[16,2048]{1,0:T(8,128)(2,1)S(1)}, u32[]{:S(2)}, u32[]{:S(2)}) %collective-permute-start.6) | collective-permute-done | bytes 65568 | tf_op jit(solution)/shard_map/ppermute | solution.py:353
  103.9 8.8 %collective-permute-done.7 = bf16[16,2048]{1,0:T(8,128)(2,1)S(1)} collective-permute-done((bf16[16,2048]{1,0:T(8,128)(2,1)S(1)}, bf16[16,2048]{1,0:T(8,128)(2,1)S(1)}, u32[]{:S(2)}, u32[]{:S(2)}) %collective-permute-start.7) | collective-permute-done | bytes 65568 | tf_op jit(solution)/shard_map/ppermute | solution.py:353
  113.4 1.0 copy-done.3
  114.5 1.2 %shard_map.121 = bf16[512,512]{1,0:T(8,128)(2,1)} custom-call(bf16[512,512]{1,0:T(8,128)(2,1)S(1)} %copy-done.3, bf16[512,512]{1,0:T(8,128)(2,1)S(1)} %bitcast.18), custom_call_target="tpu_custom_call" | custom-call | flops 268435456 | bytes 1572864 | tf_op jit(solution)/shard_map/pallas_call | solution.py:33
  (68 shorter events, 26.0 us)
Async XLA Ops:
  0.6 30.4 %copy-start.8 = (bf16[512,512]{1,0:T(8,128)(2,1)S(1)}, bf16[512,512]{1,0:T(8,128)(2,1)}, u32[]{:S(2)}) copy-start(bf16[512,512]{1,0:T(8,128)(2,1)} %wq_ref.1) | copy-start | bytes 1572868
  0.6 1.1 copy-start.24
  4.1 23.7 %all-to-all-start = ((bf16[32,16,512]{2,1,0:T(8,128)(2,1)}), bf16[32,16,512]{2,1,0:T(8,128)(2,1)S(1)}, u32[]{:S(2)}, u32[]{:S(2)}) async-start(bf16[32,16,512]{2,1,0:T(8,128)(2,1)} %bitcast.3), calls=%async_computation | async-start | bytes 1048576 | tf_op jit(solution)/shard_map/all_to_all | solution.py:378
  12.2 1.0 copy-start
  13.3 1.0 copy-start.4
  28.4 6.5 %collective-permute-start = (bf16[512,512]{1,0:T(8,128)(2,1)S(1)}, bf16[512,512]{1,0:T(8,128)(2,1)S(1)}, u32[]{:S(2)}, u32[]{:S(2)}) collective-permute-start(bf16[512,512]{1,0:T(8,128)(2,1)S(1)} %get-tuple-element.55.refs_0_.refs_1_), channel_id=1, source_target_pairs={{0,1},{1,2},{2,3},{3,4},{4,5},{5,6},{6,7},{8,9},{9,10},{10,11},{11... | collective-permute-start | bytes 1572872 | tf_op jit(solution)/shard_map/ppermute | solution.py:329
  31.1 1.0 copy-start.10
  32.1 1.0 copy-start.12
  34.9 1.0 copy-start.27
  35.9 13.1 %copy-start.1 = (bf16[1,512,512]{2,1,0:T(8,128)(2,1)S(1)}, bf16[1,512,512]{2,1,0:T(8,128)(2,1)}, u32[]{:S(2)}) copy-start(bf16[1,512,512]{2,1,0:T(8,128)(2,1)} %param.17) | copy-start | bytes 1572868
  47.7 11.9 %collective-permute-start.1 = (bf16[512,512]{1,0:T(8,128)(2,1)S(1)}, bf16[512,512]{1,0:T(8,128)(2,1)S(1)}, u32[]{:S(2)}, u32[]{:S(2)}) collective-permute-start(bf16[512,512]{1,0:T(8,128)(2,1)S(1)} %get-tuple-element.77), channel_id=1, source_target_pairs={{1,0},{2,1},{3,2},{4,3},{5,4},{6,5},{7,6},{9,8},{10,9},{11,10},{12... | collective-permute-start | bytes 1572872 | tf_op jit(solution)/shard_map/ppermute | solution.py:329
  60.5 12.9 %collective-permute-start.2 = (bf16[256,2048]{1,0:T(8,128)(2,1)}, bf16[256,2048]{1,0:T(8,128)(2,1)S(1)}, u32[]{:S(2)}, u32[]{:S(2)}) collective-permute-start(bf16[256,2048]{1,0:T(8,128)(2,1)} %get-tuple-element.78), channel_id=1, source_target_pairs={{0,1},{1,0},{2,3},{3,2},{4,5},{5,4},{6,7},{7,6},{8,9},{9,8},{10,11... | collective-permute-start | bytes 3145736 | tf_op jit(solution)/shard_map/ppermute | solution.py:439
  62.6 1.0 copy-start.9
  63.7 1.0 copy-start.11
  64.7 1.0 copy-start.13
  65.8 1.0 copy-start.15
  73.6 9.2 %collective-permute-start.3 = (bf16[64,2048]{1,0:T(8,128)(2,1)S(1)}, bf16[64,2048]{1,0:T(8,128)(2,1)S(1)}, u32[]{:S(2)}, u32[]{:S(2)}) collective-permute-start(bf16[64,2048]{1,0:T(8,128)(2,1)S(1)} %get-tuple-element.86), channel_id=1, source_target_pairs={{0,8},{8,0},{16,24},{24,16},{1,9},{9,1},{17,25},{25,17},{2,10},{10... | collective-permute-start | bytes 786440 | tf_op jit(solution)/shard_map/ppermute | solution.py:353
  74.5 13.6 %collective-permute-start.4 = (bf16[64,2048]{1,0:T(8,128)(2,1)S(1)}, bf16[64,2048]{1,0:T(8,128)(2,1)S(1)}, u32[]{:S(2)}, u32[]{:S(2)}) collective-permute-start(bf16[64,2048]{1,0:T(8,128)(2,1)S(1)} %get-tuple-element.87), channel_id=1, source_target_pairs={{0,16},{8,24},{16,0},{24,8},{1,17},{9,25},{17,1},{25,9},{2,18},{10... | collective-permute-start | bytes 786440 | tf_op jit(solution)/shard_map/ppermute | solution.py:353
  75.1 13.0 %collective-permute-start.5 = (bf16[64,2048]{1,0:T(8,128)(2,1)S(1)}, bf16[64,2048]{1,0:T(8,128)(2,1)S(1)}, u32[]{:S(2)}, u32[]{:S(2)}) collective-permute-start(bf16[64,2048]{1,0:T(8,128)(2,1)S(1)} %get-tuple-element.88), channel_id=1, source_target_pairs={{0,24},{8,16},{16,8},{24,0},{1,25},{9,17},{17,9},{25,1},{2,26},{10... | collective-permute-start | bytes 786440 | tf_op jit(solution)/shard_map/ppermute | solution.py:353
  88.1 25.3 %all-to-all-start.1 = ((bf16[32,16,512]{2,1,0:T(8,128)(2,1)}), bf16[32,16,512]{2,1,0:T(8,128)(2,1)S(1)}, u32[]{:S(2)}, u32[]{:S(2)}) async-start(bf16[32,16,512]{2,1,0:T(8,128)(2,1)} %bitcast.11), calls=%async_computation.1 | async-start | bytes 1048576 | tf_op jit(solution)/shard_map/all_to_all | solution.py:378
  93.2 10.7 %collective-permute-start.6 = (bf16[16,2048]{1,0:T(8,128)(2,1)S(1)}, bf16[16,2048]{1,0:T(8,128)(2,1)S(1)}, u32[]{:S(2)}, u32[]{:S(2)}) collective-permute-start(bf16[16,2048]{1,0:T(8,128)(2,1)S(1)} %get-tuple-element.96), channel_id=1, source_target_pairs={{0,2},{1,3},{2,0},{3,1},{4,6},{5,7},{6,4},{7,5},{8,10},{9,11},{10,... | collective-permute-start | bytes 196616 | tf_op jit(solution)/shard_map/ppermute | solution.py:353
  95.0 17.7 %collective-permute-start.7 = (bf16[16,2048]{1,0:T(8,128)(2,1)S(1)}, bf16[16,2048]{1,0:T(8,128)(2,1)S(1)}, u32[]{:S(2)}, u32[]{:S(2)}) collective-permute-start(bf16[16,2048]{1,0:T(8,128)(2,1)S(1)} %get-tuple-element.97), channel_id=1, source_target_pairs={{0,4},{1,5},{2,6},{3,7},{4,0},{5,1},{6,2},{7,3},{8,12},{9,13},{10,... | collective-permute-start | bytes 196616 | tf_op jit(solution)/shard_map/ppermute | solution.py:353
  97.4 15.3 %collective-permute-start.8 = (bf16[16,2048]{1,0:T(8,128)(2,1)S(1)}, bf16[16,2048]{1,0:T(8,128)(2,1)S(1)}, u32[]{:S(2)}, u32[]{:S(2)}) collective-permute-start(bf16[16,2048]{1,0:T(8,128)(2,1)S(1)} %get-tuple-element.98), channel_id=1, source_target_pairs={{0,6},{1,7},{2,4},{3,5},{4,2},{5,3},{6,0},{7,1},{8,14},{9,15},{10,... | collective-permute-start | bytes 196616 | tf_op jit(solution)/shard_map/ppermute | solution.py:353
  113.4 1.0 copy-start.3
  (15 other events, 13.4 us)

commit v5 on v4

--- a/solution.py
+++ b/solution.py
@@ -241,12 +241,14 @@
 
 
 def weights_body(
-    scale, rows, head_size, meta_ref, normed_ref, halo_ref, cot_ref,
+    scale, rows, head_size, meta_ref, normed_ref, halo_ref, frames_ref, cot_ref,
+    wq_hbm, wk_hbm, wv_hbm, wo_hbm,
     q_ref, kt_ref, vt_ref, khalo_t_ref, vhalo_t_ref, do_ref, raised_ref, grads_ref, scale_ref, dkh_ref, dvh_ref,
-    keep_ref, send_ref, ot, dqt, dk, dv,
-    normed_t, halo_t, mixed_t, ktx, vtx,
+    keep_ref, send_ref, out_ref, slope_ref,
+    normed_t, halo_t, mixed_t, ktx, vtx, ot, dqt, dk, dv, wq, wk, wv, wo, sems,
 ):
     span, width = q_ref.shape
+    copies = fetch([wq_hbm, wk_hbm, wv_hbm, wo_hbm], [wq, wk, wv, wo], sems)
     ktx[:, :WIN] = khalo_t_ref[...]
     ktx[:, WIN:] = kt_ref[...]
     vtx[:, :WIN] = vhalo_t_ref[...]
@@ -300,23 +302,21 @@
             mm(mixed, cot_ref[...]),
         )):
             out[:, n * width : (n + 1) * width] = (total * scale).astype(BF)
-
-
-def returning_body(
-    frames_ref, dqt_ref, dk_ref, dv_ref, wq_ref, wk_ref, wv_ref, extra_ref, cot_ref, pick_t_ref, out_ref
-):
+    for copy in copies:
+        copy.wait()
+    slope = mm(dqt[...].T, wq[...], NT)
+    slope = slope + mm(dk[...], wk[...], NT)
+    slope_ref[...] = slope + mm(dv[...], wv[...], NT)
+    out = mm(ot[...].T, wo[...]) + frames_ref[...].astype(F32)
+    out_ref[...] = out.astype(BF)
+
+
+def returning_body(frames_ref, slope_ref, extra_ref, cot_ref, pick_t_ref, out_ref):
     _, inverse, normed32 = unit_frames(frames_ref[...])
-    slope = mm(dqt_ref[...].T, wq_ref[...], NT)
-    slope = slope + mm(dk_ref[...], wk_ref[...], NT)
-    slope = slope + mm(dv_ref[...], wv_ref[...], NT)
-    slope = slope + extra_ref[...].astype(F32)
+    slope = slope_ref[...] + extra_ref[...].astype(F32)
     centre = jnp.mean(slope * normed32, axis=1, keepdims=True)
     grad = inverse * (slope - normed32 * centre) + cot_ref[...].astype(F32)
     out_ref[...] = mm(pick_t_ref[...], grad.astype(BF)).astype(BF)
-
-
-def out_body(frames_ref, ot_ref, wo_ref, out_ref):
-    out_ref[...] = (mm(ot_ref[...].T, wo_ref[...]) + frames_ref[...].astype(F32)).astype(BF)
 
 
 def arrived_body(placing_t_ref, in_ref, out_ref):
@@ -415,20 +415,24 @@
         smem=(0,),
         scratch=[pltpu.VMEM((WIN + span, width), BF)] * 2,
         flops=12 * cube,
-        limit=14,
+        limit=24,
     )
     extra = passed_along(back, -1)
     chunk = rows if in_kernel else width // 2
     split = pltpu.VMEM((width // (2 * chunk), 2, chunk, span), BF)
     half = sds((width // 2, 4 * width))
-    keep, send, ot, dqt, dk, dv = vmem_call(
+    whole = pltpu.VMEM((width, width), BF)
+    keep, send, out_frames, slope = vmem_call(
         lambda *refs: weights_body(slab ** (-0.5), chunk, head_size, *refs),
-        [half, half] + [square] * 4,
-        [meta, normed, halo, cot, q, kt, vt, khalo_t, vhalo_t, do, raised, grads, scales, dkh, dvh],
+        [half, half, square, sds((span, width), F32)],
+        [meta, normed, halo, frames, cot, query_weight, key_weight, value_weight, out_weight,
+         q, kt, vt, khalo_t, vhalo_t, do, raised, grads, scales, dkh, dvh],
         smem=(0,),
-        scratch=[split] * 3 + [pltpu.VMEM((width, WIN + span), BF)] * 2,
-        flops=14 * cube,
-        limit=14,
+        hbm=(5, 6, 7, 8),
+        scratch=[split] * 3 + [pltpu.VMEM((width, WIN + span), BF)] * 2 + [whole] * 8
+        + [pltpu.SemaphoreType.DMA((4,))],
+        flops=18 * cube,
+        limit=26,
     )
     send, extra = lax.optimization_barrier((send, extra))
     if not in_kernel:
@@ -437,18 +441,15 @@
         send = lax.dynamic_index_in_dim(sums, 1 - core, 1, keepdims=False).reshape(half.shape)
     seqs = lax.axis_size("seq")
     got = lax.ppermute(send, "seq", [(i, i ^ 1) for i in range(seqs)])
+    seqs = lax.axis_size("seq")
+    got = lax.ppermute(send, "seq", [(i, i ^ 1) for i in range(seqs)])
+    pieces = spread([keep, got], lax.axis_index("stream"), lax.axis_size("stream"))
+    *pieces, extra = lax.optimization_barrier((*pieces, extra))
+    pieces = swapped(pieces, "stream", 1)
     returning, = vmem_call(
-        returning_body,
-        [square],
-        [frames, dqt, dk, dv, query_weight, key_weight, value_weight, extra, cot, pick_t],
-        flops=4 * cube,
-    )
-    got, returning = lax.optimization_barrier((got, returning))
-    pieces = spread([keep, got], lax.axis_index("stream"), lax.axis_size("stream"))
-    pieces = swapped(pieces, "stream", 1)
-    *pieces, returning = lax.optimization_barrier((*pieces, returning))
+        returning_body, [square], [frames, slope, extra, cot, pick_t], flops=cube
+    )
     arrived = exchanged(returning)
-    out_frames, = vmem_call(out_body, [square], [frames, ot, out_weight], flops=cube)
     frame_grads, = vmem_call(arrived_body, [square], [placing_t, arrived], flops=cube)
     pieces = swapped(spread(pieces, lax.axis_index("seq") >> 1, seqs // 2), "seq", 2)
     weight_grads = pieces[0].astype(F32)

time: 117 us -> 113 us (0.966)
  local copies, waits for them, and re-layouts: 25.7 us -> 17.2 us
  starting transfers between devices: 25.6 us -> 28 us
  waiting for transfers between devices: 32.4 us -> 34.2 us
    unnamed x56 -> x58, local copies, waits for them, and re-layouts: 24.9 us -> 16.4 us
    ppermute x1, waiting for transfers between devices: 0.01 us -> 2.63 us  [shards(): got = lax.ppermute(send, 'seq', [(i, i ^ 1) for i in range(seqs)])]
    ppermute x1, starting transfers between devices: 2.17 us -> 4.26 us  [shards(): got = lax.ppermute(send, 'seq', [(i, i ^ 1) for i in range(seqs)])]
    pallas_call x11 -> x10, Pallas kernels: 29.8 us -> 30.2 us  [vmem_call(): pl.pallas_call(body, out_shape=tuple(outs), in_specs=[pl.BlockSpec(memory...]
  transfers between devices with their start and end apart: 11 -> 11, of which waited for: 5 -> 7; matrix products, arithmetic and copies ran while one was open for 1% -> 1% of each run, Pallas kernels for 12% -> 11%
where the time goes in v5:
time: 113 us; the launch traced here: 112 us
  waiting for transfers between devices  34.2 us (30%)
  Pallas kernels  30.2 us (27%)
  starting transfers between devices  28 us (25%)
  local copies, waits for them, and re-layouts  17.2 us (15%)
  between operations  1.57 us (1%)
    pallas_call x10, Pallas kernels, vmem_call(): pl.pallas_call(body, out_shape=tuple(outs), in_specs=[pl.BlockSpec(memory...  30.2 us
    ppermute x6, waiting for transfers between devices, swapped(): lax.ppermute(piece, axis, [(i, i ^ k * step) for i in range(count)])  22.7 us
    unnamed x58, local copies, waits for them, and re-layouts  16.4 us
    all_to_all x2, starting transfers between devices, exchanged(): lax.all_to_all(shard.reshape(devices, slots, width), AXES, split_axis=0,...  12.5 us
    all_to_all x2, waiting for transfers between devices, exchanged(): lax.all_to_all(shard.reshape(devices, slots, width), AXES, split_axis=0,...  8.93 us
    ppermute x6, starting transfers between devices, swapped(): lax.ppermute(piece, axis, [(i, i ^ k * step) for i in range(count)])  8.01 us
    ppermute x1, starting transfers between devices, shards(): got = lax.ppermute(send, 'seq', [(i, i ^ 1) for i in range(seqs)])  4.26 us
    ppermute x2, starting transfers between devices, passed_along(): return lax.ppermute(shard, 'seq', pairs)  3.24 us
  transfers between devices with their start and end apart: 11, of which 7 were waited for; matrix products, arithmetic and copies ran while one was open for 1% of the time, Pallas kernels for 11%

profile of v5, /device:TPU:0, one launch (start us, length us, event | category | flops | bytes accessed | tf_op | source)
XLA Modules:
  0.0 112.0 jit_solution(15918709320586072774)
XLA Ops:
  0.7 1.1 %copy-done.22 = bf16[512,512]{1,0:T(8,128)(2,1)S(1)} copy-done((bf16[512,512]{1,0:T(8,128)(2,1)S(1)}, bf16[512,512]{1,0:T(8,128)(2,1)}, u32[]{:S(2)}) %copy-start.22) | copy-done | bytes 524312
  2.5 1.6 %shard_map.112 = (bf16[512,512]{1,0:T(8,128)(2,1)}, bf16[512,512]{1,0:T(8,128)(2,1)S(1)}) custom-call(s32[1,512]{1,0:T(1,128)S(1)} %bitcast.28, bf16[512,512]{1,0:T(8,128)(2,1)S(1)} %copy-done.22), custom_call_target="tpu_custom_call" | custom-call | flops 268435456 | bytes 1574912 | tf_op jit(solution)/shard_map/pallas_call | solution.py:33
  4.2 7.3 %all-to-all-start = ((bf16[32,16,512]{2,1,0:T(8,128)(2,1)}), bf16[32,16,512]{2,1,0:T(8,128)(2,1)S(1)}, u32[]{:S(2)}, u32[]{:S(2)}) async-start(bf16[32,16,512]{2,1,0:T(8,128)(2,1)} %bitcast.5), calls=%async_computation | async-start | bytes 1048576 | tf_op jit(solution)/shard_map/all_to_all | solution.py:378
  14.4 1.3 %shard_map.113 = (bf16[512,512]{1,0:T(8,128)(2,1)S(1)}, bf16[512,512]{1,0:T(8,128)(2,1)S(1)}, bf16[512,512]{1,0:T(8,128)(2,1)S(1)}, bf16[512,512]{1,0:T(8,128)(2,1)S(1)}) custom-call(s32[512,1]{1,0:T(8,128)S(1)} %copy.12.refs_0_, bf16[512,512]{1,0:T(8,128)(2,1)S(1)} %get-tuple-element.47.refs_1_, bf16[512,512]{1,0:T(8,128)(2,1)S(1)} %bitcast.18, ...), custom_call_target="tpu_custom_call" | custom-call | flops 536870912 | bytes 3672064 | tf_op jit(solution)/shard_map/pallas_call | solution.py:33
  18.9 8.9 %all-to-all-done = bf16[32,16,512]{2,1,0:T(8,128)(2,1)S(1)} async-done(((bf16[32,16,512]{2,1,0:T(8,128)(2,1)}), bf16[32,16,512]{2,1,0:T(8,128)(2,1)S(1)}, u32[]{:S(2)}, u32[]{:S(2)}) %all-to-all-start) | async-done | bytes 524320 | tf_op jit(solution)/shard_map/all_to_all | solution.py:378
  29.5 1.9 %collective-permute-start = (bf16[512,512]{1,0:T(8,128)(2,1)S(1)}, bf16[512,512]{1,0:T(8,128)(2,1)S(1)}, u32[]{:S(2)}, u32[]{:S(2)}) collective-permute-start(bf16[512,512]{1,0:T(8,128)(2,1)S(1)} %get-tuple-element.50.refs_0_.refs_1_), channel_id=1, source_target_pairs={{0,1},{1,2},{2,3},{3,4},{4,5},{5,6},{6,7},{8,9},{9,10},{10,11},{11... | collective-permute-start | bytes 1572872 | tf_op jit(solution)/shard_map/ppermute | solution.py:329
  32.2 1.7 %shard_map.115 = (bf16[512,512]{1,0:T(8,128)(2,1)S(1)}, bf16[512,512]{1,0:T(8,128)(2,1)S(1)}, bf16[512,512]{1,0:T(8,128)(2,1)S(1)}, bf16[512,512]{1,0:T(8,128)(2...) custom-call(bf16[512,512]{1,0:T(8,128)(2,1)S(1)} %get-tuple-element.50.refs_0_.ref, ...), custom_call_target="tpu_custom_call" | custom-call | flops 805306368 | bytes 5767168 | tf_op jit(solution)/shard_map/pallas_call | solution.py:33
  36.8 11.8 %shard_map.116 = (bf16[16,640,256]{2,1,0:T(8,128)(2,1)S(1)}, bf16[16,640,256]{2,1,0:T(8,128)(2,1)S(1)}, f32[16,1,256]{2,1,0:T(1,128)S(1)}, bf16[512,512]{1,0:T(8...) custom-call(s32[3]{0:T(128)S(1)} %pad_add_fusion.refs_0_, ...), custom_call_target="tpu_custom_call" | custom-call | flops 3221225472 | bytes 17842188 | tf_op jit(solution)/shard_map/pallas_call | solution.py:33
  48.6 1.3 %collective-permute-start.1 = (bf16[512,512]{1,0:T(8,128)(2,1)S(1)}, bf16[512,512]{1,0:T(8,128)(2,1)S(1)}, u32[]{:S(2)}, u32[]{:S(2)}) collective-permute-start(bf16[512,512]{1,0:T(8,128)(2,1)S(1)} %get-tuple-element.74), channel_id=1, source_target_pairs={{1,0},{2,1},{3,2},{4,3},{5,4},{6,5},{7,6},{9,8},{10,9},{11,10},{12... | collective-permute-start | bytes 1572872 | tf_op jit(solution)/shard_map/ppermute | solution.py:329
  51.0 8.7 %shard_map.117 = (bf16[256,2048]{1,0:T(8,128)(2,1)S(1)}, bf16[256,2048]{1,0:T(8,128)(2,1)}, bf16[512,512]{1,0:T(8,128)(2,1)}, f32[512,512]{1,0:T(8,128)S(1)}) custom-call(s32[3]{0:T(128)S(1)} %pad_add_fusion.refs_0_, bf16[512,512]{1,0:T(8,128)(2,1)S(1)} %copy-done.15, bf16[512,512]{1,0:T(8,128)(2,1)S(1)} %copy-done.17, ...), custom_call_target="tpu_custom_call" | custom-call | flops 4831838208 | bytes 22560780 | tf_op jit(solution)/shard_map/pallas_call | solution.py:33
  60.6 4.3 %collective-permute-start.2 = (bf16[256,2048]{1,0:T(8,128)(2,1)}, bf16[256,2048]{1,0:T(8,128)(2,1)}, u32[]{:S(2)}, u32[]{:S(2)}) collective-permute-start(bf16[256,2048]{1,0:T(8,128)(2,1)} %get-tuple-element.75), channel_id=1, source_target_pairs={{0,1},{1,0},{2,3},{3,2},{4,5},{5,4},{6,7},{7,6},{8,9},{9,8},{10,11... | collective-permute-start | bytes 3145736 | tf_op jit(solution)/shard_map/ppermute | solution.py:445
  64.8 2.6 %collective-permute-done.2 = bf16[256,2048]{1,0:T(8,128)(2,1)} collective-permute-done((bf16[256,2048]{1,0:T(8,128)(2,1)}, bf16[256,2048]{1,0:T(8,128)(2,1)}, u32[]{:S(2)}, u32[]{:S(2)}) %collective-permute-start.2) | collective-permute-done | bytes 1048608 | tf_op jit(solution)/shard_map/ppermute | solution.py:445
  67.5 1.5 %shard_map.118 = (bf16[64,2048]{1,0:T(8,128)(2,1)S(1)}, bf16[64,2048]{1,0:T(8,128)(2,1)S(1)}, bf16[64,2048]{1,0:T(8,128)(2,1)S(1)}, bf16[64,2048]{1,0:T(8,128)(2,1)S(1)}) custom-call(s32[1]{0:T(128)} %bitcast.8.place_ref, bf16[4,64,2048]{2,1,0:T(8,128)(2,1)S(1)} %bitcast.23, bf16[4,64,2048]{2,1,0:T(8,128)(2,1)} %bitcast.10.refs_1_), custom_call_target="tpu_custom_call" | custom-call | bytes 3145732 | tf_op jit(solution)/shard_map/pallas_call | solution.py:33
  72.4 1.6 %shard_map.119 = bf16[512,512]{1,0:T(8,128)(2,1)} custom-call(bf16[512,512]{1,0:T(8,128)(2,1)S(1)} %get-tuple-element.51.refs_3_.frames_ref, f32[512,512]{1,0:T(8,128)S(1)} %get-tuple-element.71.slope_ref, bf16[512,512]{1,0:T(8,128)(2,1)S(1)} %copy-done.19, bf16[512,512]{1,0:T(8,128)(2,1)S(1)} %bitcast.20, bf16[512,512]{1,0:T(8,128)(2,1)S(1)} %copy-done.13), custom_call_target="tpu_custom_call" | custom-call | flops 268435456 | bytes 3670016 | tf_op jit(solution)/shard_map/pallas_call | solution.py:33
  74.0 5.2 %all-to-all-start.1 = ((bf16[32,16,512]{2,1,0:T(8,128)(2,1)}), bf16[32,16,512]{2,1,0:T(8,128)(2,1)S(1)}, u32[]{:S(2)}, u32[]{:S(2)}) async-start(bf16[32,16,512]{2,1,0:T(8,128)(2,1)} %bitcast.11), calls=%async_computation.1 | async-start | bytes 1048576 | tf_op jit(solution)/shard_map/all_to_all | solution.py:378
  79.2 1.8 %collective-permute-start.3 = (bf16[64,2048]{1,0:T(8,128)(2,1)}, bf16[64,2048]{1,0:T(8,128)(2,1)S(1)}, u32[]{:S(2)}, u32[]{:S(2)}) collective-permute-start(bf16[64,2048]{1,0:T(8,128)(2,1)} %copy-done.25), channel_id=1, source_target_pairs={{0,8},{8,0},{16,24},{24,16},{1,9},{9,1},{17,25},{25,17},{2,10},{10... | collective-permute-start | bytes 786440 | tf_op jit(solution)/shard_map/ppermute | solution.py:353
  81.1 1.5 %collective-permute-start.4 = (bf16[64,2048]{1,0:T(8,128)(2,1)}, bf16[64,2048]{1,0:T(8,128)(2,1)S(1)}, u32[]{:S(2)}, u32[]{:S(2)}) collective-permute-start(bf16[64,2048]{1,0:T(8,128)(2,1)} %copy-done.24), channel_id=1, source_target_pairs={{0,16},{8,24},{16,0},{24,8},{1,17},{9,25},{17,1},{25,9},{2,18},{10... | collective-permute-start | bytes 786440 | tf_op jit(solution)/shard_map/ppermute | solution.py:353
  82.8 10.3 %collective-permute-done.3 = bf16[64,2048]{1,0:T(8,128)(2,1)S(1)} collective-permute-done((bf16[64,2048]{1,0:T(8,128)(2,1)}, bf16[64,2048]{1,0:T(8,128)(2,1)S(1)}, u32[]{:S(2)}, u32[]{:S(2)}) %collective-permute-start.3) | collective-permute-done | bytes 262176 | tf_op jit(solution)/shard_map/ppermute | solution.py:353
  93.2 6.7 %collective-permute-done.5 = bf16[64,2048]{1,0:T(8,128)(2,1)S(1)} collective-permute-done((bf16[64,2048]{1,0:T(8,128)(2,1)}, bf16[64,2048]{1,0:T(8,128)(2,1)S(1)}, u32[]{:S(2)}, u32[]{:S(2)}) %collective-permute-start.5) | collective-permute-done | bytes 262176 | tf_op jit(solution)/shard_map/ppermute | solution.py:353
  100.0 1.5 %collective-permute-start.6 = (bf16[16,2048]{1,0:T(8,128)(2,1)S(1)}, bf16[16,2048]{1,0:T(8,128)(2,1)S(1)}, u32[]{:S(2)}, u32[]{:S(2)}) collective-permute-start(bf16[16,2048]{1,0:T(8,128)(2,1)S(1)} %get-tuple-element.88), channel_id=1, source_target_pairs={{0,2},{1,3},{2,0},{3,1},{4,6},{5,7},{6,4},{7,5},{8,10},{9,11},{10,... | collective-permute-start | bytes 196616 | tf_op jit(solution)/shard_map/ppermute | solution.py:353
  101.5 2.4 %collective-permute-start.7 = (bf16[16,2048]{1,0:T(8,128)(2,1)S(1)}, bf16[16,2048]{1,0:T(8,128)(2,1)S(1)}, u32[]{:S(2)}, u32[]{:S(2)}) collective-permute-start(bf16[16,2048]{1,0:T(8,128)(2,1)S(1)} %get-tuple-element.89), channel_id=1, source_target_pairs={{0,4},{1,5},{2,6},{3,7},{4,0},{5,1},{6,2},{7,3},{8,12},{9,13},{10,... | collective-permute-start | bytes 196616 | tf_op jit(solution)/shard_map/ppermute | solution.py:353
  104.5 4.2 %collective-permute-done.7 = bf16[16,2048]{1,0:T(8,128)(2,1)S(1)} collective-permute-done((bf16[16,2048]{1,0:T(8,128)(2,1)S(1)}, bf16[16,2048]{1,0:T(8,128)(2,1)S(1)}, u32[]{:S(2)}, u32[]{:S(2)}) %collective-permute-start.7) | collective-permute-done | bytes 65568 | tf_op jit(solution)/shard_map/ppermute | solution.py:353
  108.6 1.4 %collective-permute-done.8 = bf16[16,2048]{1,0:T(8,128)(2,1)S(1)} collective-permute-done((bf16[16,2048]{1,0:T(8,128)(2,1)S(1)}, bf16[16,2048]{1,0:T(8,128)(2,1)S(1)}, u32[]{:S(2)}, u32[]{:S(2)}) %collective-permute-start.8) | collective-permute-done | bytes 65568 | tf_op jit(solution)/shard_map/ppermute | solution.py:353
  110.7 1.2 %shard_map.120 = bf16[512,512]{1,0:T(8,128)(2,1)} custom-call(bf16[512,512]{1,0:T(8,128)(2,1)S(1)} %copy-done.11, bf16[512,512]{1,0:T(8,128)(2,1)S(1)} %bitcast.21), custom_call_target="tpu_custom_call" | custom-call | flops 268435456 | bytes 1572864 | tf_op jit(solution)/shard_map/pallas_call | solution.py:33
  (69 shorter events, 18.5 us)
Async XLA Ops:
  0.6 31.6 %copy-start.8 = (bf16[512,512]{1,0:T(8,128)(2,1)S(1)}, bf16[512,512]{1,0:T(8,128)(2,1)}, u32[]{:S(2)}) copy-start(bf16[512,512]{1,0:T(8,128)(2,1)} %refs_7_.1) | copy-start | bytes 1572868
  0.6 31.6 %copy-start.6 = (bf16[512,512]{1,0:T(8,128)(2,1)S(1)}, bf16[512,512]{1,0:T(8,128)(2,1)}, u32[]{:S(2)}) copy-start(bf16[512,512]{1,0:T(8,128)(2,1)} %refs_6_.1) | copy-start | bytes 1572868
  0.7 31.5 %copy-start.4 = (bf16[512,512]{1,0:T(8,128)(2,1)S(1)}, bf16[512,512]{1,0:T(8,128)(2,1)}, u32[]{:S(2)}) copy-start(bf16[512,512]{1,0:T(8,128)(2,1)} %refs_5_.1) | copy-start | bytes 1572868
  0.7 1.2 %copy-start.22 = (bf16[512,512]{1,0:T(8,128)(2,1)S(1)}, bf16[512,512]{1,0:T(8,128)(2,1)}, u32[]{:S(2)}) copy-start(bf16[512,512]{1,0:T(8,128)(2,1)} %refs_1_.2) | copy-start | bytes 1572868
  4.2 23.7 %all-to-all-start = ((bf16[32,16,512]{2,1,0:T(8,128)(2,1)}), bf16[32,16,512]{2,1,0:T(8,128)(2,1)S(1)}, u32[]{:S(2)}, u32[]{:S(2)}) async-start(bf16[32,16,512]{2,1,0:T(8,128)(2,1)} %bitcast.5), calls=%async_computation | async-start | bytes 1048576 | tf_op jit(solution)/shard_map/all_to_all | solution.py:378
  12.3 1.0 copy-start
  29.5 19.1 %copy-start.14 = (bf16[512,512]{1,0:T(8,128)(2,1)}, bf16[512,512]{1,0:T(8,128)(2,1)S(1)}, u32[]{:S(2)}) copy-start(bf16[512,512]{1,0:T(8,128)(2,1)S(1)} %get-tuple-element.50.refs_0_.refs_1_) | copy-start | bytes 1572868
  29.5 4.4 %collective-permute-start = (bf16[512,512]{1,0:T(8,128)(2,1)S(1)}, bf16[512,512]{1,0:T(8,128)(2,1)S(1)}, u32[]{:S(2)}, u32[]{:S(2)}) collective-permute-start(bf16[512,512]{1,0:T(8,128)(2,1)S(1)} %get-tuple-element.50.refs_0_.refs_1_), channel_id=1, source_target_pairs={{0,1},{1,2},{2,3},{3,4},{4,5},{5,6},{6,7},{8,9},{9,10},{10,11},{11... | collective-permute-start | bytes 1572872 | tf_op jit(solution)/shard_map/ppermute | solution.py:329
  36.8 13.1 %copy-start.1 = (bf16[1,512,512]{2,1,0:T(8,128)(2,1)S(1)}, bf16[1,512,512]{2,1,0:T(8,128)(2,1)}, u32[]{:S(2)}) copy-start(bf16[1,512,512]{2,1,0:T(8,128)(2,1)} %param.17) | copy-start | bytes 1572868
  36.8 13.1 %copy-start.3 = (bf16[512,512]{1,0:T(8,128)(2,1)S(1)}, bf16[512,512]{1,0:T(8,128)(2,1)}, u32[]{:S(2)}) copy-start(bf16[512,512]{1,0:T(8,128)(2,1)} %refs_8_.1) | copy-start | bytes 1572868
  36.8 13.1 %copy-start.5 = (bf16[512,512]{1,0:T(8,128)(2,1)S(1)}, bf16[512,512]{1,0:T(8,128)(2,1)}, u32[]{:S(2)}) copy-start(bf16[512,512]{1,0:T(8,128)(2,1)} %refs_5_.1) | copy-start | bytes 1572868
  36.8 13.1 %copy-start.7 = (bf16[512,512]{1,0:T(8,128)(2,1)S(1)}, bf16[512,512]{1,0:T(8,128)(2,1)}, u32[]{:S(2)}) copy-start(bf16[512,512]{1,0:T(8,128)(2,1)} %refs_6_.1) | copy-start | bytes 1572868
  36.8 13.1 %copy-start.9 = (bf16[512,512]{1,0:T(8,128)(2,1)S(1)}, bf16[512,512]{1,0:T(8,128)(2,1)}, u32[]{:S(2)}) copy-start(bf16[512,512]{1,0:T(8,128)(2,1)} %refs_7_.1) | copy-start | bytes 1572868
  48.6 11.2 %collective-permute-start.1 = (bf16[512,512]{1,0:T(8,128)(2,1)S(1)}, bf16[512,512]{1,0:T(8,128)(2,1)S(1)}, u32[]{:S(2)}, u32[]{:S(2)}) collective-permute-start(bf16[512,512]{1,0:T(8,128)(2,1)S(1)} %get-tuple-element.74), channel_id=1, source_target_pairs={{1,0},{2,1},{3,2},{4,3},{5,4},{6,5},{7,6},{9,8},{10,9},{11,10},{12... | collective-permute-start | bytes 1572872 | tf_op jit(solution)/shard_map/ppermute | solution.py:329
  60.6 6.9 %collective-permute-start.2 = (bf16[256,2048]{1,0:T(8,128)(2,1)}, bf16[256,2048]{1,0:T(8,128)(2,1)}, u32[]{:S(2)}, u32[]{:S(2)}) collective-permute-start(bf16[256,2048]{1,0:T(8,128)(2,1)} %get-tuple-element.75), channel_id=1, source_target_pairs={{0,1},{1,0},{2,3},{3,2},{4,5},{5,4},{6,7},{7,6},{8,9},{9,8},{10,11... | collective-permute-start | bytes 3145736 | tf_op jit(solution)/shard_map/ppermute | solution.py:445
  69.6 4.4 %copy-start.23 = (bf16[64,2048]{1,0:T(8,128)(2,1)}, bf16[64,2048]{1,0:T(8,128)(2,1)S(1)}, u32[]{:S(2)}) copy-start(bf16[64,2048]{1,0:T(8,128)(2,1)S(1)} %get-tuple-element.86) | copy-start | bytes 786436
  69.6 41.1 %copy-start.11 = (bf16[512,512]{1,0:T(8,128)(2,1)S(1)}, bf16[512,512]{1,0:T(8,128)(2,1)}, u32[]{:S(2)}) copy-start(bf16[512,512]{1,0:T(8,128)(2,1)} %copy-done.10) | copy-start | bytes 1572868
  74.0 36.7 %all-to-all-start.1 = ((bf16[32,16,512]{2,1,0:T(8,128)(2,1)}), bf16[32,16,512]{2,1,0:T(8,128)(2,1)S(1)}, u32[]{:S(2)}, u32[]{:S(2)}) async-start(bf16[32,16,512]{2,1,0:T(8,128)(2,1)} %bitcast.11), calls=%async_computation.1 | async-start | bytes 1048576 | tf_op jit(solution)/shard_map/all_to_all | solution.py:378
  79.2 13.9 %collective-permute-start.3 = (bf16[64,2048]{1,0:T(8,128)(2,1)}, bf16[64,2048]{1,0:T(8,128)(2,1)S(1)}, u32[]{:S(2)}, u32[]{:S(2)}) collective-permute-start(bf16[64,2048]{1,0:T(8,128)(2,1)} %copy-done.25), channel_id=1, source_target_pairs={{0,8},{8,0},{16,24},{24,16},{1,9},{9,1},{17,25},{25,17},{2,10},{10... | collective-permute-start | bytes 786440 | tf_op jit(solution)/shard_map/ppermute | solution.py:353
  81.1 12.1 %collective-permute-start.4 = (bf16[64,2048]{1,0:T(8,128)(2,1)}, bf16[64,2048]{1,0:T(8,128)(2,1)S(1)}, u32[]{:S(2)}, u32[]{:S(2)}) collective-permute-start(bf16[64,2048]{1,0:T(8,128)(2,1)} %copy-done.24), channel_id=1, source_target_pairs={{0,16},{8,24},{16,0},{24,8},{1,17},{9,25},{17,1},{25,9},{2,18},{10... | collective-permute-start | bytes 786440 | tf_op jit(solution)/shard_map/ppermute | solution.py:353
  82.5 17.4 %collective-permute-start.5 = (bf16[64,2048]{1,0:T(8,128)(2,1)}, bf16[64,2048]{1,0:T(8,128)(2,1)S(1)}, u32[]{:S(2)}, u32[]{:S(2)}) collective-permute-start(bf16[64,2048]{1,0:T(8,128)(2,1)} %copy-done.23), channel_id=1, source_target_pairs={{0,24},{8,16},{16,8},{24,0},{1,25},{9,17},{17,9},{25,1},{2,26},{10... | collective-permute-start | bytes 786440 | tf_op jit(solution)/shard_map/ppermute | solution.py:353
  100.0 4.5 %collective-permute-start.6 = (bf16[16,2048]{1,0:T(8,128)(2,1)S(1)}, bf16[16,2048]{1,0:T(8,128)(2,1)S(1)}, u32[]{:S(2)}, u32[]{:S(2)}) collective-permute-start(bf16[16,2048]{1,0:T(8,128)(2,1)S(1)} %get-tuple-element.88), channel_id=1, source_target_pairs={{0,2},{1,3},{2,0},{3,1},{4,6},{5,7},{6,4},{7,5},{8,10},{9,11},{10,... | collective-permute-start | bytes 196616 | tf_op jit(solution)/shard_map/ppermute | solution.py:353
  101.5 7.1 %collective-permute-start.7 = (bf16[16,2048]{1,0:T(8,128)(2,1)S(1)}, bf16[16,2048]{1,0:T(8,128)(2,1)S(1)}, u32[]{:S(2)}, u32[]{:S(2)}) collective-permute-start(bf16[16,2048]{1,0:T(8,128)(2,1)S(1)} %get-tuple-element.89), channel_id=1, source_target_pairs={{0,4},{1,5},{2,6},{3,7},{4,0},{5,1},{6,2},{7,3},{8,12},{9,13},{10,... | collective-permute-start | bytes 196616 | tf_op jit(solution)/shard_map/ppermute | solution.py:353
  103.9 6.2 %collective-permute-start.8 = (bf16[16,2048]{1,0:T(8,128)(2,1)S(1)}, bf16[16,2048]{1,0:T(8,128)(2,1)S(1)}, u32[]{:S(2)}, u32[]{:S(2)}) collective-permute-start(bf16[16,2048]{1,0:T(8,128)(2,1)S(1)} %get-tuple-element.90), channel_id=1, source_target_pairs={{0,6},{1,7},{2,4},{3,5},{4,2},{5,3},{6,0},{7,1},{8,14},{9,15},{10,... | collective-permute-start | bytes 196616 | tf_op jit(solution)/shard_map/ppermute | solution.py:353
  (16 other events, 14.2 us)

commit v6 on v5

--- a/solution.py
+++ b/solution.py
@@ -27,7 +27,12 @@
     return lax.broadcasted_iota(jnp.int32, shape, dim)
 
 
-def vmem_call(body, outs, args, smem=(), hbm=(), scratch=(), flops=0, limit=12):
+def vmem_call(body, outs, args, smem=(), hbm=(), scratch=(), carry=(), flops=0, limit=12):
+    used, inner, args = len(args), body, list(args) + list(carry)
+
+    def body(*refs):
+        inner(*refs[:used], *refs[len(args) :])
+
     spaces = [pltpu.SMEM if i in smem else pltpu.HBM if i in hbm else pltpu.VMEM for i in range(len(args))]
     size = sum(math.prod(a.shape) * a.dtype.itemsize for a in list(args) + list(outs))
     return pl.pallas_call(
@@ -340,11 +345,11 @@
         out[...] = total.astype(BF)
 
 
-def spread(inputs, place, parts):
+def spread(inputs, place, parts, carry=()):
     columns = inputs[0].shape[-1]
     inputs = [shard.reshape(parts, -1, columns) for shard in inputs]
     piece = sds(inputs[0].shape[1:])
-    return vmem_call(spread_body, [piece] * parts, [place.reshape(1)] + inputs, smem=(0,))
+    return vmem_call(spread_body, [piece] * parts, [place.reshape(1)] + inputs, smem=(0,), carry=carry)
 
 
 def swapped(pieces, axis, step):
@@ -395,7 +400,9 @@
         [frame_owner.reshape(span, 1), placing, cot, out_weight],
         flops=2 * cube,
     )
-    frames, normed = vmem_call(frames_body, [square, square], [pick, incoming], flops=cube)
+    frames, normed = vmem_call(
+        frames_body, [square, square], [pick, incoming], carry=[pick_t, placing_t, dot], flops=cube
+    )
     halo = passed_along(normed, 1)
     query_scale = head_size ** (-0.5) * math.log2(math.e)
     qt, k, kt, v, vt, wk, wv = vmem_call(
@@ -404,6 +411,7 @@
         [normed, query_weight, key_weight, value_weight],
         hbm=(1, 2, 3),
         scratch=[pltpu.VMEM((width, width), BF), pltpu.SemaphoreType.DMA((3,))],
+        carry=[pick_t, placing_t, dot, frames],
         flops=3 * cube,
     )
     units = H // 2 * (span // TILE)
@@ -414,6 +422,7 @@
         [meta, halo, wk, wv, qt, k, v, dot],
         smem=(0,),
         scratch=[pltpu.VMEM((WIN + span, width), BF)] * 2,
+        carry=[normed, kt, vt, frames, pick_t, placing_t],
         flops=12 * cube,
         limit=24,
     )
@@ -431,6 +440,7 @@
         hbm=(5, 6, 7, 8),
         scratch=[split] * 3 + [pltpu.VMEM((width, WIN + span), BF)] * 2 + [whole] * 8
         + [pltpu.SemaphoreType.DMA((4,))],
+        carry=[pick_t, placing_t],
         flops=18 * cube,
         limit=26,
     )
@@ -443,12 +453,12 @@
     got = lax.ppermute(send, "seq", [(i, i ^ 1) for i in range(seqs)])
     seqs = lax.axis_size("seq")
     got = lax.ppermute(send, "seq", [(i, i ^ 1) for i in range(seqs)])
-    pieces = spread([keep, got], lax.axis_index("stream"), lax.axis_size("stream"))
-    *pieces, extra = lax.optimization_barrier((*pieces, extra))
+    returning, = vmem_call(
+        returning_body, [square], [frames, slope, extra, cot, pick_t], carry=[placing_t, keep], flops=cube
+    )
+    got, _ = lax.optimization_barrier((got, returning))
+    pieces = spread([keep, got], lax.axis_index("stream"), lax.axis_size("stream"), [placing_t])
     pieces = swapped(pieces, "stream", 1)
-    returning, = vmem_call(
-        returning_body, [square], [frames, slope, extra, cot, pick_t], flops=cube
-    )
     arrived = exchanged(returning)
     frame_grads, = vmem_call(arrived_body, [square], [placing_t, arrived], flops=cube)
     pieces = swapped(spread(pieces, lax.axis_index("seq") >> 1, seqs // 2), "seq", 2)

time: 113 us -> 104 us (0.920)
  local copies, waits for them, and re-layouts: 17.2 us -> 12.3 us
  waiting for transfers between devices: 34.2 us -> 29.5 us
  Pallas kernels: 30.2 us -> 33.6 us
  starting transfers between devices: 28 us -> 25.2 us
    unnamed x58 -> x36, local copies, waits for them, and re-layouts: 16.4 us -> 11.5 us
    pallas_call x10, Pallas kernels: 30.2 us -> 33.6 us  [vmem_call(): pl.pallas_call(body, out_shape=tuple(outs), in_specs=[pl.BlockSpec(memory...]
    ppermute x1, starting transfers between devices: 4.26 us -> 1.19 us  [shards(): got = lax.ppermute(send, 'seq', [(i, i ^ 1) for i in range(seqs)])]
    ppermute x6, waiting for transfers between devices: 22.7 us -> 20 us  [swapped(): lax.ppermute(piece, axis, [(i, i ^ k * step) for i in range(count)])]
    ppermute x1, waiting for transfers between devices: 2.63 us -> 0.01 us  [shards(): got = lax.ppermute(send, 'seq', [(i, i ^ 1) for i in range(seqs)])]
  transfers between devices with their start and end apart: 11 -> 11, of which waited for: 7 -> 6; matrix products, arithmetic and copies ran while one was open for 1% -> 1% of each run, Pallas kernels for 11% -> 17%
where the time goes in v6:
time: 104 us; the launch traced here: 103 us
  Pallas kernels  33.6 us (32%)
  waiting for transfers between devices  29.5 us (28%)
  starting transfers between devices  25.2 us (24%)
  local copies, waits for them, and re-layouts  12.3 us (12%)
  between operations  1.52 us (1%)
    pallas_call x10, Pallas kernels, vmem_call(): pl.pallas_call(body, out_shape=tuple(outs), in_specs=[pl.BlockSpec(memory...  33.6 us
    ppermute x6, waiting for transfers between devices, swapped(): lax.ppermute(piece, axis, [(i, i ^ k * step) for i in range(count)])  20 us
    all_to_all x2, starting transfers between devices, exchanged(): lax.all_to_all(shard.reshape(devices, slots, width), AXES, split_axis=0,...  12 us
    unnamed x36, local copies, waits for them, and re-layouts  11.5 us
    all_to_all x2, waiting for transfers between devices, exchanged(): lax.all_to_all(shard.reshape(devices, slots, width), AXES, split_axis=0,...  9.49 us
    ppermute x6, starting transfers between devices, swapped(): lax.ppermute(piece, axis, [(i, i ^ k * step) for i in range(count)])  8.01 us
    ppermute x2, starting transfers between devices, passed_along(): return lax.ppermute(shard, 'seq', pairs)  4.01 us
  transfers between devices with their start and end apart: 11, of which 6 were waited for; matrix products, arithmetic and copies ran while one was open for 1% of the time, Pallas kernels for 17%

profile of v6, /device:TPU:0, one launch (start us, length us, event | category | flops | bytes accessed | tf_op | source)
XLA Modules:
  0.0 102.9 jit_solution(16684957314582268752)
XLA Ops:
  0.7 1.1 %copy-done.14 = bf16[512,512]{1,0:T(8,128)(2,1)S(1)} copy-done((bf16[512,512]{1,0:T(8,128)(2,1)S(1)}, bf16[512,512]{1,0:T(8,128)(2,1)}, u32[]{:S(2)}) %copy-start.14) | copy-done | bytes 524312
  2.5 1.6 %shard_map.112 = (bf16[512,512]{1,0:T(8,128)(2,1)}, bf16[512,512]{1,0:T(8,128)(2,1)S(1)}) custom-call(s32[1,512]{1,0:T(1,128)S(1)} %bitcast.28, bf16[512,512]{1,0:T(8,128)(2,1)S(1)} %copy-done.14), custom_call_target="tpu_custom_call" | custom-call | flops 268435456 | bytes 1574912 | tf_op jit(solution)/shard_map/pallas_call | solution.py:38
  4.9 7.3 %all-to-all-start = ((bf16[32,16,512]{2,1,0:T(8,128)(2,1)}), bf16[32,16,512]{2,1,0:T(8,128)(2,1)S(1)}, u32[]{:S(2)}, u32[]{:S(2)}) async-start(bf16[32,16,512]{2,1,0:T(8,128)(2,1)} %bitcast.5), calls=%async_computation | async-start | bytes 1048576 | tf_op jit(solution)/shard_map/all_to_all | solution.py:383
  16.2 1.3 %shard_map.113 = (bf16[512,512]{1,0:T(8,128)(2,1)S(1)}, bf16[512,512]{1,0:T(8,128)(2,1)S(1)}, bf16[512,512]{1,0:T(8,128)(2,1)S(1)}, bf16[512,512]{1,0:T(8,128)(2,1)S(1)}) custom-call(s32[512,1]{1,0:T(8,128)S(1)} %copy.12.refs_0_, bf16[512,512]{1,0:T(8,128)(2,1)S(1)} %copy-done.17, bf16[512,512]{1,0:T(8,128)(2,1)S(1)} %bitcast.19, bf16[512,512]{1,0:T(8,128)(2,1)S(1)} %copy-done.10), custom_call_target="tpu_custom_call" | custom-call | flops 536870912 | bytes 3672064 | tf_op jit(solution)/shard_map/pallas_call | solution.py:38
  19.1 9.5 %all-to-all-done = bf16[32,16,512]{2,1,0:T(8,128)(2,1)S(1)} async-done(((bf16[32,16,512]{2,1,0:T(8,128)(2,1)}), bf16[32,16,512]{2,1,0:T(8,128)(2,1)S(1)}, u32[]{:S(2)}, u32[]{:S(2)}) %all-to-all-start) | async-done | bytes 524320 | tf_op jit(solution)/shard_map/all_to_all | solution.py:383
  30.7 1.4 %shard_map.114 = (bf16[512,512]{1,0:T(8,128)(2,1)S(1)}, bf16[512,512]{1,0:T(8,128)(2,1)}) custom-call(bf16[512,512]{1,0:T(8,128)(2,1)S(1)} %copy-done.13, bf16[512,512]{1,0:T(8,128)(2,1)S(1)} %bitcast.23, bf16[512,512]{1,0:T(8,128)(2,1)S(1)} %get-tuple-element.46.refs_2_.refs_4_.refs_12_.refs_20_, ...), custom_call_target="tpu_custom_call" | custom-call | flops 268435456 | bytes 3670016 | tf_op jit(solution)/shard_map/pallas_call | solution.py:38
  32.1 2.7 %collective-permute-start = (bf16[512,512]{1,0:T(8,128)(2,1)}, bf16[512,512]{1,0:T(8,128)(2,1)}, u32[]{:S(2)}, u32[]{:S(2)}) collective-permute-start(bf16[512,512]{1,0:T(8,128)(2,1)} %get-tuple-element.49.refs_0_.refs_8_.refs_1_), channel_id=1, source_target_pairs={{0,1},{1,2},{2,3},{3,4},{4,5},{5,6},{6,7},{8,9},{9,10},{10,11},{11... | collective-permute-start | bytes 1572872 | tf_op jit(solution)/shard_map/ppermute | solution.py:334
  37.6 2.7 %shard_map.115 = (bf16[512,512]{1,0:T(8,128)(2,1)S(1)}, bf16[512,512]{1,0:T(8,128)(2,1)S(1)}, bf16[512,512]{1,0:T(8,128)(2,1)S(1)}, bf16[512,512]{1,0:T(8,128)(2...) custom-call(bf16[512,512]{1,0:T(8,128)(2,1)} %get-tuple-element.49.refs_0_.refs_8_, ...), custom_call_target="tpu_custom_call" | custom-call | flops 805306368 | bytes 7864320 | tf_op jit(solution)/shard_map/pallas_call | solution.py:38
  40.4 12.6 %shard_map.116 = (bf16[16,640,256]{2,1,0:T(8,128)(2,1)S(1)}, bf16[16,640,256]{2,1,0:T(8,128)(2,1)S(1)}, f32[16,1,256]{2,1,0:T(1,128)S(1)}, bf16[512,512]{1,0:T(8...) custom-call(s32[3]{0:T(128)S(1)} %pad_add_fusion.refs_0_, ...), custom_call_target="tpu_custom_call" | custom-call | flops 3221225472 | bytes 20987916 | tf_op jit(solution)/shard_map/pallas_call | solution.py:38
  53.0 1.3 %collective-permute-start.1 = (bf16[512,512]{1,0:T(8,128)(2,1)S(1)}, bf16[512,512]{1,0:T(8,128)(2,1)S(1)}, u32[]{:S(2)}, u32[]{:S(2)}) collective-permute-start(bf16[512,512]{1,0:T(8,128)(2,1)S(1)} %get-tuple-element.70), channel_id=1, source_target_pairs={{1,0},{2,1},{3,2},{4,3},{5,4},{6,5},{7,6},{9,8},{10,9},{11,10},{12... | collective-permute-start | bytes 1572872 | tf_op jit(solution)/shard_map/ppermute | solution.py:334
  54.4 9.4 %shard_map.117 = (bf16[256,2048]{1,0:T(8,128)(2,1)S(1)}, bf16[256,2048]{1,0:T(8,128)(2,1)}, bf16[512,512]{1,0:T(8,128)(2,1)}, f32[512,512]{1,0:T(8,128)S(1)}) custom-call(s32[3]{0:T(128)S(1)} %pad_add_fusion.refs_0_, bf16[512,512]{1,0:T(8,128)(2,1)} %get-tuple-element.49.refs_0_.refs_8_.refs_1_, bf16[512,512]{1,0:T(8,128)(2,1)} %collective-permute-done.refs_1_.refs_2_, ...), custom_call_target="tpu_custom_call" | custom-call | flops 4831838208 | bytes 23609356 | tf_op jit(solution)/shard_map/pallas_call | solution.py:38
  63.8 1.2 %collective-permute-start.2 = (bf16[256,2048]{1,0:T(8,128)(2,1)}, bf16[256,2048]{1,0:T(8,128)(2,1)}, u32[]{:S(2)}, u32[]{:S(2)}) collective-permute-start(bf16[256,2048]{1,0:T(8,128)(2,1)} %get-tuple-element.73), channel_id=1, source_target_pairs={{0,1},{1,0},{2,3},{3,2},{4,5},{5,4},{6,7},{7,6},{8,9},{9,8},{10,11... | collective-permute-start | bytes 3145736 | tf_op jit(solution)/shard_map/ppermute | solution.py:455
  65.0 1.6 %shard_map.118 = bf16[512,512]{1,0:T(8,128)(2,1)} custom-call(bf16[512,512]{1,0:T(8,128)(2,1)S(1)} %get-tuple-element.50.refs_7_.refs_11_.refs_3_.refs_0_, f32[512,512]{1,0:T(8,128)S(1)} %get-tuple-element.68.refs_1_, bf16[512,512]{1,0:T(8,128)(2,1)S(1)} %collective-permute-done.1.refs_2_, bf16[512,512]{1,0:T(8,128)(2,1)S(1)} %bitcast.21, ...), custom_call_target="tpu_custom_call" | custom-call | flops 268435456 | bytes 5242880 | tf_op jit(solution)/shard_map/pallas_call | solution.py:38
  66.6 4.7 %all-to-all-start.1 = ((bf16[32,16,512]{2,1,0:T(8,128)(2,1)}), bf16[32,16,512]{2,1,0:T(8,128)(2,1)S(1)}, u32[]{:S(2)}, u32[]{:S(2)}) async-start(bf16[32,16,512]{2,1,0:T(8,128)(2,1)} %bitcast.8), calls=%async_computation.1 | async-start | bytes 1048576 | tf_op jit(solution)/shard_map/all_to_all | solution.py:383
  71.4 1.5 %shard_map.120 = (bf16[64,2048]{1,0:T(8,128)(2,1)S(1)}, bf16[64,2048]{1,0:T(8,128)(2,1)S(1)}, bf16[64,2048]{1,0:T(8,128)(2,1)S(1)}, bf16[64,2048]{1,0:T(8,128)(2,1)S(1)}) custom-call(s32[1]{0:T(128)} %bitcast.11.refs_0_, bf16[4,64,2048]{2,1,0:T(8,128)(2,1)S(1)} %bitcast.18, bf16[4,64,2048]{2,1,0:T(8,128)(2,1)} %bitcast.13.refs_2_, ...), custom_call_target="tpu_custom_call" | custom-call | bytes 3670020 | tf_op jit(solution)/shard_map/pallas_call | solution.py:38
  72.8 1.8 %collective-permute-start.3 = (bf16[64,2048]{1,0:T(8,128)(2,1)S(1)}, bf16[64,2048]{1,0:T(8,128)(2,1)S(1)}, u32[]{:S(2)}, u32[]{:S(2)}) collective-permute-start(bf16[64,2048]{1,0:T(8,128)(2,1)S(1)} %get-tuple-element.76), channel_id=1, source_target_pairs={{0,8},{8,0},{16,24},{24,16},{1,9},{9,1},{17,25},{25,17},{2,10},{10... | collective-permute-start | bytes 786440 | tf_op jit(solution)/shard_map/ppermute | solution.py:358
  74.7 1.5 %collective-permute-start.4 = (bf16[64,2048]{1,0:T(8,128)(2,1)S(1)}, bf16[64,2048]{1,0:T(8,128)(2,1)S(1)}, u32[]{:S(2)}, u32[]{:S(2)}) collective-permute-start(bf16[64,2048]{1,0:T(8,128)(2,1)S(1)} %get-tuple-element.77), channel_id=1, source_target_pairs={{0,16},{8,24},{16,0},{24,8},{1,17},{9,25},{17,1},{25,9},{2,18},{10... | collective-permute-start | bytes 786440 | tf_op jit(solution)/shard_map/ppermute | solution.py:358
  76.4 8.7 %collective-permute-done.3 = bf16[64,2048]{1,0:T(8,128)(2,1)S(1)} collective-permute-done((bf16[64,2048]{1,0:T(8,128)(2,1)S(1)}, bf16[64,2048]{1,0:T(8,128)(2,1)S(1)}, u32[]{:S(2)}, u32[]{:S(2)}) %collective-permute-start.3) | collective-permute-done | bytes 262176 | tf_op jit(solution)/shard_map/ppermute | solution.py:358
  85.6 6.4 %collective-permute-done.5 = bf16[64,2048]{1,0:T(8,128)(2,1)S(1)} collective-permute-done((bf16[64,2048]{1,0:T(8,128)(2,1)S(1)}, bf16[64,2048]{1,0:T(8,128)(2,1)S(1)}, u32[]{:S(2)}, u32[]{:S(2)}) %collective-permute-start.5) | collective-permute-done | bytes 262176 | tf_op jit(solution)/shard_map/ppermute | solution.py:358
  92.2 1.5 %collective-permute-start.6 = (bf16[16,2048]{1,0:T(8,128)(2,1)S(1)}, bf16[16,2048]{1,0:T(8,128)(2,1)S(1)}, u32[]{:S(2)}, u32[]{:S(2)}) collective-permute-start(bf16[16,2048]{1,0:T(8,128)(2,1)S(1)} %get-tuple-element.80), channel_id=1, source_target_pairs={{0,2},{1,3},{2,0},{3,1},{4,6},{5,7},{6,4},{7,5},{8,10},{9,11},{10,... | collective-permute-start | bytes 196616 | tf_op jit(solution)/shard_map/ppermute | solution.py:358
  93.6 2.4 %collective-permute-start.7 = (bf16[16,2048]{1,0:T(8,128)(2,1)S(1)}, bf16[16,2048]{1,0:T(8,128)(2,1)S(1)}, u32[]{:S(2)}, u32[]{:S(2)}) collective-permute-start(bf16[16,2048]{1,0:T(8,128)(2,1)S(1)} %get-tuple-element.81), channel_id=1, source_target_pairs={{0,4},{1,5},{2,6},{3,7},{4,0},{5,1},{6,2},{7,3},{8,12},{9,13},{10,... | collective-permute-start | bytes 196616 | tf_op jit(solution)/shard_map/ppermute | solution.py:358
  96.6 1.2 %shard_map.119 = bf16[512,512]{1,0:T(8,128)(2,1)} custom-call(bf16[512,512]{1,0:T(8,128)(2,1)S(1)} %get-tuple-element.47.refs_3_.refs_5_.refs_13_.refs_21_.refs_0_, bf16[512,512]{1,0:T(8,128)(2,1)S(1)} %bitcast.22), custom_call_target="tpu_custom_call" | custom-call | flops 268435456 | bytes 1572864 | tf_op jit(solution)/shard_map/pallas_call | solution.py:38
  97.8 3.1 %collective-permute-done.7 = bf16[16,2048]{1,0:T(8,128)(2,1)S(1)} collective-permute-done((bf16[16,2048]{1,0:T(8,128)(2,1)S(1)}, bf16[16,2048]{1,0:T(8,128)(2,1)S(1)}, u32[]{:S(2)}, u32[]{:S(2)}) %collective-permute-start.7) | collective-permute-done | bytes 65568 | tf_op jit(solution)/shard_map/ppermute | solution.py:358
  100.9 1.2 %collective-permute-done.8 = bf16[16,2048]{1,0:T(8,128)(2,1)S(1)} collective-permute-done((bf16[16,2048]{1,0:T(8,128)(2,1)S(1)}, bf16[16,2048]{1,0:T(8,128)(2,1)S(1)}, u32[]{:S(2)}, u32[]{:S(2)}) %collective-permute-start.8) | collective-permute-done | bytes 65568 | tf_op jit(solution)/shard_map/ppermute | solution.py:358
  (47 shorter events, 13.5 us)
Async XLA Ops:
  0.6 34.9 %copy-start.3 = (bf16[512,512]{1,0:T(8,128)(2,1)S(1)}, bf16[512,512]{1,0:T(8,128)(2,1)}, u32[]{:S(2)}) copy-start(bf16[512,512]{1,0:T(8,128)(2,1)} %refs_6_.1) | copy-start | bytes 1572868
  0.6 34.9 %copy-start.2 = (bf16[512,512]{1,0:T(8,128)(2,1)S(1)}, bf16[512,512]{1,0:T(8,128)(2,1)}, u32[]{:S(2)}) copy-start(bf16[512,512]{1,0:T(8,128)(2,1)} %refs_5_.1) | copy-start | bytes 1572868
  0.7 1.1 %copy-start.14 = (bf16[512,512]{1,0:T(8,128)(2,1)S(1)}, bf16[512,512]{1,0:T(8,128)(2,1)}, u32[]{:S(2)}) copy-start(bf16[512,512]{1,0:T(8,128)(2,1)} %refs_1_.2) | copy-start | bytes 1572868
  4.9 23.7 %all-to-all-start = ((bf16[32,16,512]{2,1,0:T(8,128)(2,1)}), bf16[32,16,512]{2,1,0:T(8,128)(2,1)S(1)}, u32[]{:S(2)}, u32[]{:S(2)}) async-start(bf16[32,16,512]{2,1,0:T(8,128)(2,1)} %bitcast.5), calls=%async_computation | async-start | bytes 1048576 | tf_op jit(solution)/shard_map/all_to_all | solution.py:383
  13.0 1.0 %copy-start = (bf16[1,512,512]{2,1,0:T(8,128)(2,1)S(1)}, bf16[1,512,512]{2,1,0:T(8,128)(2,1)}, u32[]{:S(2)}) copy-start(bf16[1,512,512]{2,1,0:T(8,128)(2,1)} %param.17) | copy-start | bytes 1572868
  14.1 1.0 %copy-start.10 = (bf16[512,512]{1,0:T(8,128)(2,1)S(1)}, bf16[512,512]{1,0:T(8,128)(2,1)}, u32[]{:S(2)}) copy-start(bf16[512,512]{1,0:T(8,128)(2,1)} %refs_8_.1) | copy-start | bytes 1572868
  15.1 1.0 %copy-start.17 = (bf16[512,512]{1,0:T(8,128)(2,1)S(1)}, bf16[512,512]{1,0:T(8,128)(2,1)}, u32[]{:S(2)}) copy-start(bf16[512,512]{1,0:T(8,128)(2,1)} %copy-done.16) | copy-start | bytes 1572868
  28.6 1.0 %copy-start.8 = (bf16[512,512]{1,0:T(8,128)(2,1)S(1)}, bf16[512,512]{1,0:T(8,128)(2,1)}, u32[]{:S(2)}) copy-start(bf16[512,512]{1,0:T(8,128)(2,1)} %copy-done.7) | copy-start | bytes 1572868
  29.6 1.0 %copy-start.13 = (bf16[512,512]{1,0:T(8,128)(2,1)S(1)}, bf16[512,512]{1,0:T(8,128)(2,1)}, u32[]{:S(2)}) copy-start(bf16[512,512]{1,0:T(8,128)(2,1)} %copy-done.12) | copy-start | bytes 1572868
  32.1 8.3 %collective-permute-start = (bf16[512,512]{1,0:T(8,128)(2,1)}, bf16[512,512]{1,0:T(8,128)(2,1)}, u32[]{:S(2)}, u32[]{:S(2)}) collective-permute-start(bf16[512,512]{1,0:T(8,128)(2,1)} %get-tuple-element.49.refs_0_.refs_8_.refs_1_), channel_id=1, source_target_pairs={{0,1},{1,2},{2,3},{3,4},{4,5},{5,6},{6,7},{8,9},{9,10},{10,11},{11... | collective-permute-start | bytes 1572872 | tf_op jit(solution)/shard_map/ppermute | solution.py:334
  35.5 1.0 %copy-start.5 = (bf16[512,512]{1,0:T(8,128)(2,1)S(1)}, bf16[512,512]{1,0:T(8,128)(2,1)}, u32[]{:S(2)}) copy-start(bf16[512,512]{1,0:T(8,128)(2,1)} %refs_7_.1) | copy-start | bytes 1572868
  40.4 14.0 %copy-start.1 = (bf16[1,512,512]{2,1,0:T(8,128)(2,1)S(1)}, bf16[1,512,512]{2,1,0:T(8,128)(2,1)}, u32[]{:S(2)}) copy-start(bf16[1,512,512]{2,1,0:T(8,128)(2,1)} %param.17) | copy-start | bytes 1572868
  40.4 14.0 %copy-start.4 = (bf16[512,512]{1,0:T(8,128)(2,1)S(1)}, bf16[512,512]{1,0:T(8,128)(2,1)}, u32[]{:S(2)}) copy-start(bf16[512,512]{1,0:T(8,128)(2,1)} %refs_6_.1) | copy-start | bytes 1572868
  40.4 14.0 %copy-start.6 = (bf16[512,512]{1,0:T(8,128)(2,1)S(1)}, bf16[512,512]{1,0:T(8,128)(2,1)}, u32[]{:S(2)}) copy-start(bf16[512,512]{1,0:T(8,128)(2,1)} %refs_7_.1) | copy-start | bytes 1572868
  40.4 14.0 %copy-start.11 = (bf16[512,512]{1,0:T(8,128)(2,1)S(1)}, bf16[512,512]{1,0:T(8,128)(2,1)}, u32[]{:S(2)}) copy-start(bf16[512,512]{1,0:T(8,128)(2,1)} %refs_8_.1) | copy-start | bytes 1572868
  53.0 10.8 %collective-permute-start.1 = (bf16[512,512]{1,0:T(8,128)(2,1)S(1)}, bf16[512,512]{1,0:T(8,128)(2,1)S(1)}, u32[]{:S(2)}, u32[]{:S(2)}) collective-permute-start(bf16[512,512]{1,0:T(8,128)(2,1)S(1)} %get-tuple-element.70), channel_id=1, source_target_pairs={{1,0},{2,1},{3,2},{4,3},{5,4},{6,5},{7,6},{9,8},{10,9},{11,10},{12... | collective-permute-start | bytes 1572872 | tf_op jit(solution)/shard_map/ppermute | solution.py:334
  63.8 7.5 %collective-permute-start.2 = (bf16[256,2048]{1,0:T(8,128)(2,1)}, bf16[256,2048]{1,0:T(8,128)(2,1)}, u32[]{:S(2)}, u32[]{:S(2)}) collective-permute-start(bf16[256,2048]{1,0:T(8,128)(2,1)} %get-tuple-element.73), channel_id=1, source_target_pairs={{0,1},{1,0},{2,3},{3,2},{4,5},{5,4},{6,7},{7,6},{8,9},{9,8},{10,11... | collective-permute-start | bytes 3145736 | tf_op jit(solution)/shard_map/ppermute | solution.py:455
  66.6 30.0 %all-to-all-start.1 = ((bf16[32,16,512]{2,1,0:T(8,128)(2,1)}), bf16[32,16,512]{2,1,0:T(8,128)(2,1)S(1)}, u32[]{:S(2)}, u32[]{:S(2)}) async-start(bf16[32,16,512]{2,1,0:T(8,128)(2,1)} %bitcast.8), calls=%async_computation.1 | async-start | bytes 1048576 | tf_op jit(solution)/shard_map/all_to_all | solution.py:383
  72.8 12.2 %collective-permute-start.3 = (bf16[64,2048]{1,0:T(8,128)(2,1)S(1)}, bf16[64,2048]{1,0:T(8,128)(2,1)S(1)}, u32[]{:S(2)}, u32[]{:S(2)}) collective-permute-start(bf16[64,2048]{1,0:T(8,128)(2,1)S(1)} %get-tuple-element.76), channel_id=1, source_target_pairs={{0,8},{8,0},{16,24},{24,16},{1,9},{9,1},{17,25},{25,17},{2,10},{10... | collective-permute-start | bytes 786440 | tf_op jit(solution)/shard_map/ppermute | solution.py:358
  74.7 10.9 %collective-permute-start.4 = (bf16[64,2048]{1,0:T(8,128)(2,1)S(1)}, bf16[64,2048]{1,0:T(8,128)(2,1)S(1)}, u32[]{:S(2)}, u32[]{:S(2)}) collective-permute-start(bf16[64,2048]{1,0:T(8,128)(2,1)S(1)} %get-tuple-element.77), channel_id=1, source_target_pairs={{0,16},{8,24},{16,0},{24,8},{1,17},{9,25},{17,1},{25,9},{2,18},{10... | collective-permute-start | bytes 786440 | tf_op jit(solution)/shard_map/ppermute | solution.py:358
  76.1 15.9 %collective-permute-start.5 = (bf16[64,2048]{1,0:T(8,128)(2,1)S(1)}, bf16[64,2048]{1,0:T(8,128)(2,1)S(1)}, u32[]{:S(2)}, u32[]{:S(2)}) collective-permute-start(bf16[64,2048]{1,0:T(8,128)(2,1)S(1)} %get-tuple-element.78), channel_id=1, source_target_pairs={{0,24},{8,16},{16,8},{24,0},{1,25},{9,17},{17,9},{25,1},{2,26},{10... | collective-permute-start | bytes 786440 | tf_op jit(solution)/shard_map/ppermute | solution.py:358
  92.2 5.7 %collective-permute-start.6 = (bf16[16,2048]{1,0:T(8,128)(2,1)S(1)}, bf16[16,2048]{1,0:T(8,128)(2,1)S(1)}, u32[]{:S(2)}, u32[]{:S(2)}) collective-permute-start(bf16[16,2048]{1,0:T(8,128)(2,1)S(1)} %get-tuple-element.80), channel_id=1, source_target_pairs={{0,2},{1,3},{2,0},{3,1},{4,6},{5,7},{6,4},{7,5},{8,10},{9,11},{10,... | collective-permute-start | bytes 196616 | tf_op jit(solution)/shard_map/ppermute | solution.py:358
  93.6 7.3 %collective-permute-start.7 = (bf16[16,2048]{1,0:T(8,128)(2,1)S(1)}, bf16[16,2048]{1,0:T(8,128)(2,1)S(1)}, u32[]{:S(2)}, u32[]{:S(2)}) collective-permute-start(bf16[16,2048]{1,0:T(8,128)(2,1)S(1)} %get-tuple-element.81), channel_id=1, source_target_pairs={{0,4},{1,5},{2,6},{3,7},{4,0},{5,1},{6,2},{7,3},{8,12},{9,13},{10,... | collective-permute-start | bytes 196616 | tf_op jit(solution)/shard_map/ppermute | solution.py:358
  96.0 6.2 %collective-permute-start.8 = (bf16[16,2048]{1,0:T(8,128)(2,1)S(1)}, bf16[16,2048]{1,0:T(8,128)(2,1)S(1)}, u32[]{:S(2)}, u32[]{:S(2)}) collective-permute-start(bf16[16,2048]{1,0:T(8,128)(2,1)S(1)} %get-tuple-element.82), channel_id=1, source_target_pairs={{0,6},{1,7},{2,4},{3,5},{4,2},{5,3},{6,0},{7,1},{8,14},{9,15},{10,... | collective-permute-start | bytes 196616 | tf_op jit(solution)/shard_map/ppermute | solution.py:358
  (5 other events, 4.1 us)

commit v7 on v5

--- a/solution.py
+++ b/solution.py
@@ -55,26 +55,29 @@
     return jax.ShapeDtypeStruct(shape, dtype)
 
 
-def outgoing_body(span, slots, rf_ref, rows_hbm, out_ref, placing_ref, rows_ref, sems):
-    (rows_copy,) = fetch([rows_hbm], [rows_ref], sems)
-    count = rf_ref.shape[1]
-    total = out_ref.shape[0]
-    rf = rf_ref[...]
+def placing_of(span, slots, rf, total):
+    count = rf.shape[1]
     target = jnp.where(rf >= 0, lax.div(rf, span), 1 << 20)
     slot = iota2((total, count), 0)
     owner = lax.div(slot, slots)
     rank = slot - owner * slots
     start = jnp.sum(jnp.where(target < owner, 1.0, 0.0), axis=1, keepdims=True)
     here = iota2((total, count), 1) - start.astype(jnp.int32)
-    placing = jnp.where((target == owner) & (here == rank), 1.0, 0.0).astype(BF)
-    placing_ref[...] = placing
+    return jnp.where((target == owner) & (here == rank), 1.0, 0.0)
+
+
+def outgoing_body(span, slots, rf_ref, rows_hbm, out_ref, rows_ref, sems):
+    (rows_copy,) = fetch([rows_hbm], [rows_ref], sems)
+    placing = placing_of(span, slots, rf_ref[...], out_ref.shape[0]).astype(BF)
     rows_copy.wait()
     out_ref[...] = mm(placing, rows_ref[...]).astype(BF)
 
 
-def early_body(
-    slots, owner_ref, placing_ref, cot_ref, wo_ref, pick_ref, pick_t_ref, placing_t_ref, dot_ref
-):
+def placing_t_body(span, slots, rf_ref, out_ref):
+    out_ref[...] = placing_of(span, slots, rf_ref[...], out_ref.shape[1]).T.astype(BF)
+
+
+def early_body(slots, owner_ref, pick_ref, pick_t_ref):
     span, lanes = owner_ref.shape[0], 128
     total = pick_ref.shape[1]
     owner = owner_ref[...]
@@ -87,8 +90,6 @@
     pick = jnp.where(iota2((span, total), 1) == slot, 1.0, 0.0)
     pick_ref[...] = pick.astype(BF)
     pick_t_ref[...] = pick.T.astype(BF)
-    placing_t_ref[...] = placing_ref[...].T
-    dot_ref[...] = mm(cot_ref[...], wo_ref[...], NT).astype(BF).T
 
 
 def unit_frames(frames):
@@ -177,10 +178,11 @@
 
 
 def scores_body(
-    head_size, meta_ref, halo_ref, wk_ref, wv_ref, qt_ref, k_ref, v_ref, dot_ref,
+    head_size, meta_ref, halo_ref, wk_ref, wv_ref, qt_ref, k_ref, v_ref, cot_hbm, wo_hbm,
     raised_ref, grads_ref, scale_ref, q_ref, do_ref, dkh_ref, dvh_ref, khalo_t_ref, vhalo_t_ref, back_ref,
-    kx, vx,
+    kx, vx, dot_ref, cot_ref, wo_ref, sems,
 ):
+    copies = fetch([cot_hbm, wo_hbm], [cot_ref, wo_ref], sems)
     span, width = k_ref.shape
     begin, length = meta_ref[0], meta_ref[1]
     halo = halo_ref[...]
@@ -236,19 +238,26 @@
                 out[j * TILE : (j + 1) * TILE, cols] = (total * scale).astype(BF)
         return carry
 
+    for copy in copies:
+        copy.wait()
+    dot_ref[...] = mm(cot_ref[...], wo_ref[...], NT).astype(BF).T
     lax.fori_loop(0, width // pair, one_pair, 0)
     back_ref[...] = (mm(dkh_ref[...], wk_ref[...], NT) + mm(dvh_ref[...], wv_ref[...], NT)).astype(BF)
 
 
 def weights_body(
-    scale, rows, head_size, meta_ref, normed_ref, halo_ref, frames_ref, cot_ref,
+    scale, rows, head_size, meta_ref, normed_hbm, halo_hbm, frames_ref, cot_hbm,
     wq_hbm, wk_hbm, wv_hbm, wo_hbm,
     q_ref, kt_ref, vt_ref, khalo_t_ref, vhalo_t_ref, do_ref, raised_ref, grads_ref, scale_ref, dkh_ref, dvh_ref,
     keep_ref, send_ref, out_ref, slope_ref,
-    normed_t, halo_t, mixed_t, ktx, vtx, ot, dqt, dk, dv, wq, wk, wv, wo, sems,
+    normed_t, halo_t, mixed_t, ktx, vtx, ot, dqt, dk, dv,
+    wq, wk, wv, wo, normed_ref, halo_ref, cot_ref, sems,
 ):
     span, width = q_ref.shape
-    copies = fetch([wq_hbm, wk_hbm, wv_hbm, wo_hbm], [wq, wk, wv, wo], sems)
+    copies = fetch(
+        [wq_hbm, wk_hbm, wv_hbm, wo_hbm, normed_hbm, halo_hbm, cot_hbm],
+        [wq, wk, wv, wo, normed_ref, halo_ref, cot_ref], sems,
+    )
     ktx[:, :WIN] = khalo_t_ref[...]
     ktx[:, WIN:] = kt_ref[...]
     vtx[:, :WIN] = vhalo_t_ref[...]
@@ -285,6 +294,8 @@
 
     lax.fori_loop(0, width // pair, one_pair, 0)
 
+    for copy in copies:
+        copy.wait()
     chunks = width // (2 * rows)
     split = (chunks, 2, rows, span)
     normed_t[...] = normed_ref[...].T.reshape(split)
@@ -302,8 +313,6 @@
             mm(mixed, cot_ref[...]),
         )):
             out[:, n * width : (n + 1) * width] = (total * scale).astype(BF)
-    for copy in copies:
-        copy.wait()
     slope = mm(dqt[...].T, wq[...], NT)
     slope = slope + mm(dk[...], wk[...], NT)
     slope_ref[...] = slope + mm(dv[...], wv[...], NT)
@@ -311,11 +320,16 @@
     out_ref[...] = out.astype(BF)
 
 
-def returning_body(frames_ref, slope_ref, extra_ref, cot_ref, pick_t_ref, out_ref):
+def returning_body(
+    frames_ref, slope_ref, extra_ref, cot_hbm, pick_t_hbm, out_ref, cot_ref, pick_t_ref, sems
+):
+    copies = fetch([cot_hbm, pick_t_hbm], [cot_ref, pick_t_ref], sems)
     _, inverse, normed32 = unit_frames(frames_ref[...])
     slope = slope_ref[...] + extra_ref[...].astype(F32)
     centre = jnp.mean(slope * normed32, axis=1, keepdims=True)
+    copies[0].wait()
     grad = inverse * (slope - normed32 * centre) + cot_ref[...].astype(F32)
+    copies[1].wait()
     out_ref[...] = mm(pick_t_ref[...], grad.astype(BF)).astype(BF)
 
 
@@ -380,20 +394,20 @@
         )
         return got.reshape(devices * slots, width)
 
-    outgoing, placing = vmem_call(
+    outgoing, = vmem_call(
         lambda *refs: outgoing_body(span, slots, *refs),
-        [square, sds((devices * slots, row_count))],
+        [square],
         [row_frame.reshape(1, row_count), frame_rows],
         hbm=(1,),
         scratch=[pltpu.VMEM((row_count, width), BF), pltpu.SemaphoreType.DMA((1,))],
         flops=cube,
     )
     incoming = exchanged(outgoing)
-    pick, pick_t, placing_t, dot = vmem_call(
+    pick, pick_t = vmem_call(
         lambda *refs: early_body(slots, *refs),
-        [square, square, square, sds((width, span))],
-        [frame_owner.reshape(span, 1), placing, cot, out_weight],
-        flops=2 * cube,
+        [square, square],
+        [frame_owner.reshape(span, 1)],
+        flops=cube,
     )
     frames, normed = vmem_call(frames_body, [square, square], [pick, incoming], flops=cube)
     halo = passed_along(normed, 1)
@@ -411,9 +425,11 @@
     raised, grads, scales, q, do, dkh, dvh, khalo_t, vhalo_t, back = vmem_call(
         lambda *refs: scores_body(head_size, *refs),
         [saved, saved, sds((units, 1, 2 * TILE), F32)] + [square] * 7,
-        [meta, halo, wk, wv, qt, k, v, dot],
+        [meta, halo, wk, wv, qt, k, v, cot, out_weight],
         smem=(0,),
-        scratch=[pltpu.VMEM((WIN + span, width), BF)] * 2,
+        hbm=(7, 8),
+        scratch=[pltpu.VMEM((WIN + span, width), BF)] * 2
+        + [pltpu.VMEM((width, span), BF)] * 3 + [pltpu.SemaphoreType.DMA((2,))],
         flops=12 * cube,
         limit=24,
     )
@@ -428,9 +444,9 @@
         [meta, normed, halo, frames, cot, query_weight, key_weight, value_weight, out_weight,
          q, kt, vt, khalo_t, vhalo_t, do, raised, grads, scales, dkh, dvh],
         smem=(0,),
-        hbm=(5, 6, 7, 8),
-        scratch=[split] * 3 + [pltpu.VMEM((width, WIN + span), BF)] * 2 + [whole] * 8
-        + [pltpu.SemaphoreType.DMA((4,))],
+        hbm=(1, 2, 4, 5, 6, 7, 8),
+        scratch=[split] * 3 + [pltpu.VMEM((width, WIN + span), BF)] * 2 + [whole] * 11
+        + [pltpu.SemaphoreType.DMA((7,))],
         flops=18 * cube,
         limit=26,
     )
@@ -443,13 +459,23 @@
     got = lax.ppermute(send, "seq", [(i, i ^ 1) for i in range(seqs)])
     seqs = lax.axis_size("seq")
     got = lax.ppermute(send, "seq", [(i, i ^ 1) for i in range(seqs)])
+    returning, = vmem_call(
+        returning_body,
+        [square],
+        [frames, slope, extra, cot, pick_t],
+        hbm=(3, 4),
+        scratch=[whole, whole, pltpu.SemaphoreType.DMA((2,))],
+        flops=cube,
+    )
     pieces = spread([keep, got], lax.axis_index("stream"), lax.axis_size("stream"))
-    *pieces, extra = lax.optimization_barrier((*pieces, extra))
     pieces = swapped(pieces, "stream", 1)
-    returning, = vmem_call(
-        returning_body, [square], [frames, slope, extra, cot, pick_t], flops=cube
-    )
+    late_rows, returning = lax.optimization_barrier((row_frame.reshape(1, row_count), returning))
     arrived = exchanged(returning)
+    placing_t, = vmem_call(
+        lambda *refs: placing_t_body(span, slots, *refs),
+        [sds((row_count, devices * slots))],
+        [late_rows],
+    )
     frame_grads, = vmem_call(arrived_body, [square], [placing_t, arrived], flops=cube)
     pieces = swapped(spread(pieces, lax.axis_index("seq") >> 1, seqs // 2), "seq", 2)
     weight_grads = pieces[0].astype(F32)

time: 113 us -> 100 us (0.88)
  local copies, waits for them, and re-layouts: 17.2 us -> 7.62 us
  starting transfers between devices: 28 us -> 24.9 us
    unnamed x58 -> x30, local copies, waits for them, and re-layouts: 16.4 us -> 6.8 us
    all_to_all x2, waiting for transfers between devices: 8.93 us -> 13.7 us  [exchanged(): lax.all_to_all(shard.reshape(devices, slots, width), AXES, split_axis=0,...]
    ppermute x1, starting transfers between devices: 4.26 us -> 1.19 us  [shards(): got = lax.ppermute(send, 'seq', [(i, i ^ 1) for i in range(seqs)])]
    ppermute x6, waiting for transfers between devices: 22.7 us -> 20 us  [swapped(): lax.ppermute(piece, axis, [(i, i ^ k * step) for i in range(count)])]
    ppermute x1, waiting for transfers between devices: 2.63 us -> 0.01 us  [shards(): got = lax.ppermute(send, 'seq', [(i, i ^ 1) for i in range(seqs)])]
    pallas_call x10 -> x11, Pallas kernels: 30.2 us -> 30.9 us  [vmem_call(): pl.pallas_call(body, out_shape=tuple(outs), in_specs=[pl.BlockSpec(memory...]
  transfers between devices with their start and end apart: 11 -> 11, of which waited for: 7 -> 6; matrix products, arithmetic and copies ran while one was open for 1% -> 1% of each run, Pallas kernels for 11% -> 16%
where the time goes in v7:
time: 100 us; the launch traced here: 99.5 us
  waiting for transfers between devices  33.8 us (34%)
  Pallas kernels  30.9 us (31%)
  starting transfers between devices  24.9 us (25%)
  local copies, waits for them, and re-layouts  7.62 us (8%)
  between operations  1.56 us (2%)
    pallas_call x11, Pallas kernels, vmem_call(): pl.pallas_call(body, out_shape=tuple(outs), in_specs=[pl.BlockSpec(memory...  30.9 us
    ppermute x6, waiting for transfers between devices, swapped(): lax.ppermute(piece, axis, [(i, i ^ k * step) for i in range(count)])  20 us
    all_to_all x2, waiting for transfers between devices, exchanged(): lax.all_to_all(shard.reshape(devices, slots, width), AXES, split_axis=0,...  13.7 us
    all_to_all x2, starting transfers between devices, exchanged(): lax.all_to_all(shard.reshape(devices, slots, width), AXES, split_axis=0,...  12.5 us
    ppermute x6, starting transfers between devices, swapped(): lax.ppermute(piece, axis, [(i, i ^ k * step) for i in range(count)])  7.94 us
    unnamed x30, local copies, waits for them, and re-layouts  6.8 us
    ppermute x2, starting transfers between devices, passed_along(): return lax.ppermute(shard, 'seq', pairs)  3.24 us
  transfers between devices with their start and end apart: 11, of which 6 were waited for; matrix products, arithmetic and copies ran while one was open for 1% of the time, Pallas kernels for 16%

profile of v7, /device:TPU:0, one launch (start us, length us, event | category | flops | bytes accessed | tf_op | source)
XLA Modules:
  0.0 99.5 jit_solution(9175269098210994603)
XLA Ops:
  0.7 1.1 %copy-done.12 = bf16[512,512]{1,0:T(8,128)(2,1)S(1)} copy-done((bf16[512,512]{1,0:T(8,128)(2,1)S(1)}, bf16[512,512]{1,0:T(8,128)(2,1)}, u32[]{:S(2)}) %copy-start.12) | copy-done | bytes 524312
  2.5 1.6 %shard_map.113 = bf16[512,512]{1,0:T(8,128)(2,1)} custom-call(s32[1,512]{1,0:T(1,128)S(1)} %bitcast.29, bf16[512,512]{1,0:T(8,128)(2,1)S(1)} %copy-done.12), custom_call_target="tpu_custom_call" | custom-call | flops 268435456 | bytes 1050624 | tf_op jit(solution)/shard_map/pallas_call | solution.py:33
  4.0 7.3 %all-to-all-start = ((bf16[32,16,512]{2,1,0:T(8,128)(2,1)}), bf16[32,16,512]{2,1,0:T(8,128)(2,1)S(1)}, u32[]{:S(2)}, u32[]{:S(2)}) async-start(bf16[32,16,512]{2,1,0:T(8,128)(2,1)} %bitcast.4), calls=%async_computation | async-start | bytes 1048576 | tf_op jit(solution)/shard_map/all_to_all | solution.py:392
  14.0 13.7 %all-to-all-done = bf16[32,16,512]{2,1,0:T(8,128)(2,1)S(1)} async-done(((bf16[32,16,512]{2,1,0:T(8,128)(2,1)}), bf16[32,16,512]{2,1,0:T(8,128)(2,1)S(1)}, u32[]{:S(2)}, u32[]{:S(2)}) %all-to-all-start) | async-done | bytes 524320 | tf_op jit(solution)/shard_map/all_to_all | solution.py:392
  28.3 1.9 %collective-permute-start = (bf16[512,512]{1,0:T(8,128)(2,1)S(1)}, bf16[512,512]{1,0:T(8,128)(2,1)S(1)}, u32[]{:S(2)}, u32[]{:S(2)}) collective-permute-start(bf16[512,512]{1,0:T(8,128)(2,1)S(1)} %get-tuple-element.41.refs_0_.refs_1_), channel_id=1, source_target_pairs={{0,1},{1,2},{2,3},{3,4},{4,5},{5,6},{6,7},{8,9},{9,10},{10,11},{11... | collective-permute-start | bytes 1572872 | tf_op jit(solution)/shard_map/ppermute | solution.py:343
  31.0 1.0 %copy-done.1 = bf16[512,512]{1,0:T(8,128)(2,1)S(1)} copy-done((bf16[512,512]{1,0:T(8,128)(2,1)S(1)}, bf16[512,512]{1,0:T(8,128)(2,1)}, u32[]{:S(2)}) %copy-start.1) | copy-done | bytes 524312
  32.1 1.0 %copy-done.3 = bf16[512,512]{1,0:T(8,128)(2,1)S(1)} copy-done((bf16[512,512]{1,0:T(8,128)(2,1)S(1)}, bf16[512,512]{1,0:T(8,128)(2,1)}, u32[]{:S(2)}) %copy-start.3) | copy-done | bytes 524312
  33.1 1.0 %copy-done.5 = bf16[512,512]{1,0:T(8,128)(2,1)S(1)} copy-done((bf16[512,512]{1,0:T(8,128)(2,1)S(1)}, bf16[512,512]{1,0:T(8,128)(2,1)}, u32[]{:S(2)}) %copy-start.5) | copy-done | bytes 524312
  34.1 1.7 %shard_map.115 = (bf16[512,512]{1,0:T(8,128)(2,1)S(1)}, bf16[512,512]{1,0:T(8,128)(2,1)S(1)}, bf16[512,512]{1,0:T(8,128)(2,1)S(1)}, bf16[512,512]{1,0:T(8,128)(2...) custom-call(bf16[512,512]{1,0:T(8,128)(2,1)S(1)} %get-tuple-element.41.refs_0_.ref, ...), custom_call_target="tpu_custom_call" | custom-call | flops 805306368 | bytes 5767168 | tf_op jit(solution)/shard_map/pallas_call | solution.py:33
  35.9 12.4 %shard_map.116 = (bf16[16,640,256]{2,1,0:T(8,128)(2,1)S(1)}, bf16[16,640,256]{2,1,0:T(8,128)(2,1)S(1)}, f32[16,1,256]{2,1,0:T(1,128)S(1)}, bf16[512,512]{1,0:T(8...) custom-call(s32[3]{0:T(128)S(1)} %pad_add_fusion.refs_0_, ...), custom_call_target="tpu_custom_call" | custom-call | flops 3221225472 | bytes 18366476 | tf_op jit(solution)/shard_map/pallas_call | solution.py:33
  48.4 1.3 %collective-permute-start.1 = (bf16[512,512]{1,0:T(8,128)(2,1)S(1)}, bf16[512,512]{1,0:T(8,128)(2,1)S(1)}, u32[]{:S(2)}, u32[]{:S(2)}) collective-permute-start(bf16[512,512]{1,0:T(8,128)(2,1)S(1)} %get-tuple-element.62), channel_id=1, source_target_pairs={{1,0},{2,1},{3,2},{4,3},{5,4},{6,5},{7,6},{9,8},{10,9},{11,10},{12... | collective-permute-start | bytes 1572872 | tf_op jit(solution)/shard_map/ppermute | solution.py:343
  50.8 8.7 %shard_map.117 = (bf16[256,2048]{1,0:T(8,128)(2,1)S(1)}, bf16[256,2048]{1,0:T(8,128)(2,1)}, bf16[512,512]{1,0:T(8,128)(2,1)}, f32[512,512]{1,0:T(8,128)S(1)}) custom-call(s32[3]{0:T(128)S(1)} %pad_add_fusion.refs_0_, bf16[512,512]{1,0:T(8,128)(2,1)S(1)} %get-tuple-element.41.refs_0_.refs_1_, bf16[512,512]{1,0:T(8,128)(2,1)S(1)} %copy-done.11, ...), custom_call_target="tpu_custom_call" | custom-call | flops 4831838208 | bytes 22560780 | tf_op jit(solution)/shard_map/pallas_call | solution.py:33
  59.5 1.2 %collective-permute-start.2 = (bf16[256,2048]{1,0:T(8,128)(2,1)}, bf16[256,2048]{1,0:T(8,128)(2,1)S(1)}, u32[]{:S(2)}, u32[]{:S(2)}) collective-permute-start(bf16[256,2048]{1,0:T(8,128)(2,1)} %get-tuple-element.68), channel_id=1, source_target_pairs={{0,1},{1,0},{2,3},{3,2},{4,5},{5,4},{6,7},{7,6},{8,9},{9,8},{10,11... | collective-permute-start | bytes 3145736 | tf_op jit(solution)/shard_map/ppermute | solution.py:461
  60.7 2.1 %shard_map.118 = bf16[512,512]{1,0:T(8,128)(2,1)} custom-call(bf16[512,512]{1,0:T(8,128)(2,1)S(1)} %get-tuple-element.42.refs_3_.frames_ref, f32[512,512]{1,0:T(8,128)S(1)} %get-tuple-element.60.slope_ref, bf16[512,512]{1,0:T(8,128)(2,1)S(1)} %collective-permute-done.1.extra_ref, bf16[512,512]{1,0:T(8,128)(2,1)S(1)} %bitcast.20, bf16[512,512]{1,0:T(8,128)(2,1)S(1)} %copy-done.9), custom_call_target="tpu_custom_call" | custom-call | flops 268435456 | bytes 3670016 | tf_op jit(solution)/shard_map/pallas_call | solution.py:33
  62.8 5.2 %all-to-all-start.1 = ((bf16[32,16,512]{2,1,0:T(8,128)(2,1)}), bf16[32,16,512]{2,1,0:T(8,128)(2,1)S(1)}, u32[]{:S(2)}, u32[]{:S(2)}) async-start(bf16[32,16,512]{2,1,0:T(8,128)(2,1)} %bitcast.8), calls=%async_computation.1 | async-start | bytes 1048576 | tf_op jit(solution)/shard_map/all_to_all | solution.py:392
  69.0 1.8 %collective-permute-start.3 = (bf16[64,2048]{1,0:T(8,128)(2,1)}, bf16[64,2048]{1,0:T(8,128)(2,1)S(1)}, u32[]{:S(2)}, u32[]{:S(2)}) collective-permute-start(bf16[64,2048]{1,0:T(8,128)(2,1)} %get-tuple-element.70), channel_id=1, source_target_pairs={{0,8},{8,0},{16,24},{24,16},{1,9},{9,1},{17,25},{25,17},{2,10},{10... | collective-permute-start | bytes 786440 | tf_op jit(solution)/shard_map/ppermute | solution.py:367
  70.7 1.5 %collective-permute-start.4 = (bf16[64,2048]{1,0:T(8,128)(2,1)}, bf16[64,2048]{1,0:T(8,128)(2,1)S(1)}, u32[]{:S(2)}, u32[]{:S(2)}) collective-permute-start(bf16[64,2048]{1,0:T(8,128)(2,1)} %get-tuple-element.71), channel_id=1, source_target_pairs={{0,16},{8,24},{16,0},{24,8},{1,17},{9,25},{17,1},{25,9},{2,18},{10... | collective-permute-start | bytes 786440 | tf_op jit(solution)/shard_map/ppermute | solution.py:367
  72.4 9.2 %collective-permute-done.3 = bf16[64,2048]{1,0:T(8,128)(2,1)S(1)} collective-permute-done((bf16[64,2048]{1,0:T(8,128)(2,1)}, bf16[64,2048]{1,0:T(8,128)(2,1)S(1)}, u32[]{:S(2)}, u32[]{:S(2)}) %collective-permute-start.3) | collective-permute-done | bytes 262176 | tf_op jit(solution)/shard_map/ppermute | solution.py:367
  81.9 6.7 %collective-permute-done.5 = bf16[64,2048]{1,0:T(8,128)(2,1)S(1)} collective-permute-done((bf16[64,2048]{1,0:T(8,128)(2,1)S(1)}, bf16[64,2048]{1,0:T(8,128)(2,1)S(1)}, u32[]{:S(2)}, u32[]{:S(2)}) %collective-permute-start.5) | collective-permute-done | bytes 262176 | tf_op jit(solution)/shard_map/ppermute | solution.py:367
  88.8 1.5 %collective-permute-start.6 = (bf16[16,2048]{1,0:T(8,128)(2,1)S(1)}, bf16[16,2048]{1,0:T(8,128)(2,1)S(1)}, u32[]{:S(2)}, u32[]{:S(2)}) collective-permute-start(bf16[16,2048]{1,0:T(8,128)(2,1)S(1)} %get-tuple-element.74), channel_id=1, source_target_pairs={{0,2},{1,3},{2,0},{3,1},{4,6},{5,7},{6,4},{7,5},{8,10},{9,11},{10,... | collective-permute-start | bytes 196616 | tf_op jit(solution)/shard_map/ppermute | solution.py:367
  90.3 2.4 %collective-permute-start.7 = (bf16[16,2048]{1,0:T(8,128)(2,1)S(1)}, bf16[16,2048]{1,0:T(8,128)(2,1)S(1)}, u32[]{:S(2)}, u32[]{:S(2)}) collective-permute-start(bf16[16,2048]{1,0:T(8,128)(2,1)S(1)} %get-tuple-element.75), channel_id=1, source_target_pairs={{0,4},{1,5},{2,6},{3,7},{4,0},{5,1},{6,2},{7,3},{8,12},{9,13},{10,... | collective-permute-start | bytes 196616 | tf_op jit(solution)/shard_map/ppermute | solution.py:367
  93.7 1.2 %shard_map.120 = bf16[512,512]{1,0:T(8,128)(2,1)} custom-call(bf16[512,512]{1,0:T(8,128)(2,1)S(1)} %shard_map.119.placing_t_ref, bf16[512,512]{1,0:T(8,128)(2,1)S(1)} %bitcast.21), custom_call_target="tpu_custom_call" | custom-call | flops 268435456 | bytes 1572864 | tf_op jit(solution)/shard_map/pallas_call | solution.py:33
  94.9 2.6 %collective-permute-done.7 = bf16[16,2048]{1,0:T(8,128)(2,1)S(1)} collective-permute-done((bf16[16,2048]{1,0:T(8,128)(2,1)S(1)}, bf16[16,2048]{1,0:T(8,128)(2,1)S(1)}, u32[]{:S(2)}, u32[]{:S(2)}) %collective-permute-start.7) | collective-permute-done | bytes 65568 | tf_op jit(solution)/shard_map/ppermute | solution.py:367
  97.6 1.2 %collective-permute-done.8 = bf16[16,2048]{1,0:T(8,128)(2,1)S(1)} collective-permute-done((bf16[16,2048]{1,0:T(8,128)(2,1)S(1)}, bf16[16,2048]{1,0:T(8,128)(2,1)S(1)}, u32[]{:S(2)}, u32[]{:S(2)}) %collective-permute-start.8) | collective-permute-done | bytes 65568 | tf_op jit(solution)/shard_map/ppermute | solution.py:367
  (42 shorter events, 8.5 us)
Async XLA Ops:
  0.6 35.2 %copy-start.7 = (bf16[512,512]{1,0:T(8,128)(2,1)S(1)}, bf16[512,512]{1,0:T(8,128)(2,1)}, u32[]{:S(2)}) copy-start(bf16[512,512]{1,0:T(8,128)(2,1)} %refs_8_.3) | copy-start | bytes 1572868
  0.6 35.2 %copy-start = (bf16[1,512,512]{2,1,0:T(8,128)(2,1)S(1)}, bf16[1,512,512]{2,1,0:T(8,128)(2,1)}, u32[]{:S(2)}) copy-start(bf16[1,512,512]{2,1,0:T(8,128)(2,1)} %param.17) | copy-start | bytes 1572868
  0.7 1.1 %copy-start.12 = (bf16[512,512]{1,0:T(8,128)(2,1)S(1)}, bf16[512,512]{1,0:T(8,128)(2,1)}, u32[]{:S(2)}) copy-start(bf16[512,512]{1,0:T(8,128)(2,1)} %refs_1_.2) | copy-start | bytes 1572868
  4.0 23.7 %all-to-all-start = ((bf16[32,16,512]{2,1,0:T(8,128)(2,1)}), bf16[32,16,512]{2,1,0:T(8,128)(2,1)S(1)}, u32[]{:S(2)}, u32[]{:S(2)}) async-start(bf16[32,16,512]{2,1,0:T(8,128)(2,1)} %bitcast.4), calls=%async_computation | async-start | bytes 1048576 | tf_op jit(solution)/shard_map/all_to_all | solution.py:392
  28.3 7.5 %collective-permute-start = (bf16[512,512]{1,0:T(8,128)(2,1)S(1)}, bf16[512,512]{1,0:T(8,128)(2,1)S(1)}, u32[]{:S(2)}, u32[]{:S(2)}) collective-permute-start(bf16[512,512]{1,0:T(8,128)(2,1)S(1)} %get-tuple-element.41.refs_0_.refs_1_), channel_id=1, source_target_pairs={{0,1},{1,2},{2,3},{3,4},{4,5},{5,6},{6,7},{8,9},{9,10},{10,11},{11... | collective-permute-start | bytes 1572872 | tf_op jit(solution)/shard_map/ppermute | solution.py:343
  31.0 1.0 %copy-start.1 = (bf16[512,512]{1,0:T(8,128)(2,1)S(1)}, bf16[512,512]{1,0:T(8,128)(2,1)}, u32[]{:S(2)}) copy-start(bf16[512,512]{1,0:T(8,128)(2,1)} %refs_5_.1) | copy-start | bytes 1572868
  32.1 1.0 %copy-start.3 = (bf16[512,512]{1,0:T(8,128)(2,1)S(1)}, bf16[512,512]{1,0:T(8,128)(2,1)}, u32[]{:S(2)}) copy-start(bf16[512,512]{1,0:T(8,128)(2,1)} %refs_6_.1) | copy-start | bytes 1572868
  33.1 1.0 %copy-start.5 = (bf16[512,512]{1,0:T(8,128)(2,1)S(1)}, bf16[512,512]{1,0:T(8,128)(2,1)}, u32[]{:S(2)}) copy-start(bf16[512,512]{1,0:T(8,128)(2,1)} %refs_7_.1) | copy-start | bytes 1572868
  35.9 12.5 %copy-start.10 = (bf16[512,512]{1,0:T(8,128)(2,1)}, bf16[512,512]{1,0:T(8,128)(2,1)S(1)}, u32[]{:S(2)}) copy-start(bf16[512,512]{1,0:T(8,128)(2,1)S(1)} %collective-permute-done.refs_1_.refs_2_) | copy-start | bytes 1572868
  35.9 13.8 %copy-start.2 = (bf16[512,512]{1,0:T(8,128)(2,1)S(1)}, bf16[512,512]{1,0:T(8,128)(2,1)}, u32[]{:S(2)}) copy-start(bf16[512,512]{1,0:T(8,128)(2,1)} %refs_5_.1) | copy-start | bytes 1572868
  35.9 13.8 %copy-start.4 = (bf16[512,512]{1,0:T(8,128)(2,1)S(1)}, bf16[512,512]{1,0:T(8,128)(2,1)}, u32[]{:S(2)}) copy-start(bf16[512,512]{1,0:T(8,128)(2,1)} %refs_6_.1) | copy-start | bytes 1572868
  35.9 13.8 %copy-start.6 = (bf16[512,512]{1,0:T(8,128)(2,1)S(1)}, bf16[512,512]{1,0:T(8,128)(2,1)}, u32[]{:S(2)}) copy-start(bf16[512,512]{1,0:T(8,128)(2,1)} %refs_7_.1) | copy-start | bytes 1572868
  48.4 11.1 %collective-permute-start.1 = (bf16[512,512]{1,0:T(8,128)(2,1)S(1)}, bf16[512,512]{1,0:T(8,128)(2,1)S(1)}, u32[]{:S(2)}, u32[]{:S(2)}) collective-permute-start(bf16[512,512]{1,0:T(8,128)(2,1)S(1)} %get-tuple-element.62), channel_id=1, source_target_pairs={{1,0},{2,1},{3,2},{4,3},{5,4},{6,5},{7,6},{9,8},{10,9},{11,10},{12... | collective-permute-start | bytes 1572872 | tf_op jit(solution)/shard_map/ppermute | solution.py:343
  49.7 1.0 %copy-start.11 = (bf16[512,512]{1,0:T(8,128)(2,1)S(1)}, bf16[512,512]{1,0:T(8,128)(2,1)}, u32[]{:S(2)}) copy-start(bf16[512,512]{1,0:T(8,128)(2,1)} %copy-done.10) | copy-start | bytes 1572868
  50.8 9.9 %copy-start.9 = (bf16[512,512]{1,0:T(8,128)(2,1)S(1)}, bf16[512,512]{1,0:T(8,128)(2,1)}, u32[]{:S(2)}) copy-start(bf16[512,512]{1,0:T(8,128)(2,1)} %copy-done.8) | copy-start | bytes 1572868
  59.5 33.8 %copy-start.14 = (s32[512]{0:T(512)S(1)}, s32[512]{0:T(512)}, u32[]{:S(2)}) copy-start(s32[512]{0:T(512)} %param.10) | copy-start | bytes 6148
  59.5 8.5 %collective-permute-start.2 = (bf16[256,2048]{1,0:T(8,128)(2,1)}, bf16[256,2048]{1,0:T(8,128)(2,1)S(1)}, u32[]{:S(2)}, u32[]{:S(2)}) collective-permute-start(bf16[256,2048]{1,0:T(8,128)(2,1)} %get-tuple-element.68), channel_id=1, source_target_pairs={{0,1},{1,0},{2,3},{3,2},{4,5},{5,4},{6,7},{7,6},{8,9},{9,8},{10,11... | collective-permute-start | bytes 3145736 | tf_op jit(solution)/shard_map/ppermute | solution.py:461
  62.8 30.9 %all-to-all-start.1 = ((bf16[32,16,512]{2,1,0:T(8,128)(2,1)}), bf16[32,16,512]{2,1,0:T(8,128)(2,1)S(1)}, u32[]{:S(2)}, u32[]{:S(2)}) async-start(bf16[32,16,512]{2,1,0:T(8,128)(2,1)} %bitcast.8), calls=%async_computation.1 | async-start | bytes 1048576 | tf_op jit(solution)/shard_map/all_to_all | solution.py:392
  69.0 12.7 %collective-permute-start.3 = (bf16[64,2048]{1,0:T(8,128)(2,1)}, bf16[64,2048]{1,0:T(8,128)(2,1)S(1)}, u32[]{:S(2)}, u32[]{:S(2)}) collective-permute-start(bf16[64,2048]{1,0:T(8,128)(2,1)} %get-tuple-element.70), channel_id=1, source_target_pairs={{0,8},{8,0},{16,24},{24,16},{1,9},{9,1},{17,25},{25,17},{2,10},{10... | collective-permute-start | bytes 786440 | tf_op jit(solution)/shard_map/ppermute | solution.py:367
  70.7 11.2 %collective-permute-start.4 = (bf16[64,2048]{1,0:T(8,128)(2,1)}, bf16[64,2048]{1,0:T(8,128)(2,1)S(1)}, u32[]{:S(2)}, u32[]{:S(2)}) collective-permute-start(bf16[64,2048]{1,0:T(8,128)(2,1)} %get-tuple-element.71), channel_id=1, source_target_pairs={{0,16},{8,24},{16,0},{24,8},{1,17},{9,25},{17,1},{25,9},{2,18},{10... | collective-permute-start | bytes 786440 | tf_op jit(solution)/shard_map/ppermute | solution.py:367
  72.2 16.4 %collective-permute-start.5 = (bf16[64,2048]{1,0:T(8,128)(2,1)S(1)}, bf16[64,2048]{1,0:T(8,128)(2,1)S(1)}, u32[]{:S(2)}, u32[]{:S(2)}) collective-permute-start(bf16[64,2048]{1,0:T(8,128)(2,1)S(1)} %get-tuple-element.72), channel_id=1, source_target_pairs={{0,24},{8,16},{16,8},{24,0},{1,25},{9,17},{17,9},{25,1},{2,26},{10... | collective-permute-start | bytes 786440 | tf_op jit(solution)/shard_map/ppermute | solution.py:367
  88.8 6.2 %collective-permute-start.6 = (bf16[16,2048]{1,0:T(8,128)(2,1)S(1)}, bf16[16,2048]{1,0:T(8,128)(2,1)S(1)}, u32[]{:S(2)}, u32[]{:S(2)}) collective-permute-start(bf16[16,2048]{1,0:T(8,128)(2,1)S(1)} %get-tuple-element.74), channel_id=1, source_target_pairs={{0,2},{1,3},{2,0},{3,1},{4,6},{5,7},{6,4},{7,5},{8,10},{9,11},{10,... | collective-permute-start | bytes 196616 | tf_op jit(solution)/shard_map/ppermute | solution.py:367
  90.3 7.3 %collective-permute-start.7 = (bf16[16,2048]{1,0:T(8,128)(2,1)S(1)}, bf16[16,2048]{1,0:T(8,128)(2,1)S(1)}, u32[]{:S(2)}, u32[]{:S(2)}) collective-permute-start(bf16[16,2048]{1,0:T(8,128)(2,1)S(1)} %get-tuple-element.75), channel_id=1, source_target_pairs={{0,4},{1,5},{2,6},{3,7},{4,0},{5,1},{6,2},{7,3},{8,12},{9,13},{10,... | collective-permute-start | bytes 196616 | tf_op jit(solution)/shard_map/ppermute | solution.py:367
  92.6 6.2 %collective-permute-start.8 = (bf16[16,2048]{1,0:T(8,128)(2,1)S(1)}, bf16[16,2048]{1,0:T(8,128)(2,1)S(1)}, u32[]{:S(2)}, u32[]{:S(2)}) collective-permute-start(bf16[16,2048]{1,0:T(8,128)(2,1)S(1)} %get-tuple-element.76), channel_id=1, source_target_pairs={{0,6},{1,7},{2,4},{3,5},{4,2},{5,3},{6,0},{7,1},{8,14},{9,15},{10,... | collective-permute-start | bytes 196616 | tf_op jit(solution)/shard_map/ppermute | solution.py:367
  (2 other events, 1.5 us)

commit v8 on v7

--- a/solution.py
+++ b/solution.py
@@ -126,13 +126,12 @@
 REACH = WIN + TILE
 
 
-def softmax_parts(scores, slopes, first, begin, length):
+def raised_scores(scores, first, begin):
     row = iota2((TILE, TILE), 0)
     col = iota2((TILE, TILE), 1)
     halo_bias = jnp.where(begin == 0, NEG, 0.0)
     count = REACH // TILE
-    time = begin + first + iota2((1, TILE), 1)
-    raised_cols, grad_cols, scales = [], [], []
+    raised_cols = []
     for h in range(2):
         at = slice(h * TILE, (h + 1) * TILE)
         parts = []
@@ -149,25 +148,8 @@
         for part in parts[1:]:
             peak = jnp.maximum(peak, part)
         peak = jnp.max(peak, axis=0, keepdims=True)
-        moves = [slopes[n * TILE : (n + 1) * TILE, at] for n in range(count)]
-        denom = centre = None
-        low_parts = []
-        for part, move in zip(parts, moves):
-            part = jnp.exp2(part - peak)
-            low_parts.append(part.astype(BF))
-            moved = part * move
-            denom = part if denom is None else denom + part
-            centre = moved if centre is None else centre + moved
-        denom = jnp.sum(denom, axis=0, keepdims=True)
-        centre = jnp.sum(centre, axis=0, keepdims=True) / denom
-        scales.append(jnp.where(time < length, 1.0 / denom, 0.0))
-        raised_cols.append(jnp.concatenate(low_parts, axis=0))
-        grad_cols.append(jnp.concatenate(
-            [(part.astype(F32) * (move - centre)).astype(BF) for part, move in zip(low_parts, moves)], axis=0
-        ))
-    return (
-        jnp.concatenate(raised_cols, axis=1), jnp.concatenate(grad_cols, axis=1), jnp.concatenate(scales, axis=1)
-    )
+        raised_cols.append(jnp.concatenate([jnp.exp2((part - peak).astype(BF)) for part in parts], axis=0))
+    return jnp.concatenate(raised_cols, axis=1)
 
 
 def both_heads(value, axis, along):
@@ -178,9 +160,9 @@
 
 
 def scores_body(
-    head_size, meta_ref, halo_ref, wk_ref, wv_ref, qt_ref, k_ref, v_ref, cot_hbm, wo_hbm,
-    raised_ref, grads_ref, scale_ref, q_ref, do_ref, dkh_ref, dvh_ref, khalo_t_ref, vhalo_t_ref, back_ref,
-    kx, vx, dot_ref, cot_ref, wo_ref, sems,
+    head_size, meta_ref, halo_ref, wk_ref, wv_ref, qt_ref, k_ref, v_ref, vt_ref, cot_hbm, wo_hbm,
+    raised_ref, grads_ref, scale_ref, q_ref, do_ref, dkh_ref, dvh_ref, khalo_t_ref, halo_t_ref, ot_ref, back_ref,
+    kx, vx, vtx, dot_ref, cot_ref, wo_ref, sems,
 ):
     copies = fetch([cot_hbm, wo_hbm], [cot_ref, wo_ref], sems)
     span, width = k_ref.shape
@@ -191,13 +173,16 @@
     khalo_t_ref[...] = kh.T
     vh = mm(halo, wv_ref[...]).astype(BF)
     vx[:WIN] = vh
-    vhalo_t_ref[...] = vh.T
+    vtx[:, :WIN] = vh.T
+    vtx[:, WIN:] = vt_ref[...]
+    halo_t_ref[...] = halo.T
     kx[WIN:] = k_ref[...]
     vx[WIN:] = v_ref[...]
 
     pair = 2 * head_size
     tiles = span // TILE
     upper = iota2((pair, TILE), 0) < head_size
+    ones = jnp.ones((16, REACH), BF)
 
     def one_pair(p, carry):
         cols = pl.ds(pl.multiple_of(p * pair, pair), pair)
@@ -210,25 +195,53 @@
             return scores, slopes
 
         halo_grads = []
-        products = {0: multiply(0)}
-        for a in range(tiles):
-            if a + 1 < tiles:
-                products[a + 1] = multiply(a + 1)
-            raised, grads, scale = softmax_parts(*products.pop(a), a * TILE, begin, length)
+
+        def raise_and_mix(a, scores):
+            here = slice(a * TILE, (a + 1) * TILE)
+            keys = slice(a * TILE, a * TILE + REACH)
+            raised = raised_scores(scores, a * TILE, begin)
             raised_ref[p * tiles + a] = raised
+            mixed = mm(jnp.concatenate([vtx[cols, keys], ones], axis=0), raised)
+            time = begin + a * TILE + iota2((1, 2 * TILE), 1) % TILE
+            scale = jnp.where(time < length, 1.0 / mixed[pair : pair + 1], 0.0)
+            scale_ref[p * tiles + a] = scale
+            spread_scale = jnp.where(upper, scale[:, :TILE], scale[:, TILE:])
+            mixed = jnp.where(upper, mixed[:pair, :TILE], mixed[:pair, TILE:]) * spread_scale
+            ot_ref[cols, here] = mixed.astype(BF)
+            return raised, mixed, spread_scale
+
+        def finish(a, slopes, raised, mixed, spread_scale):
+            here = slice(a * TILE, (a + 1) * TILE)
+            out_grad = dot_ref[cols, here].astype(F32)
+            product = mixed * out_grad
+            grad_cols = []
+            for h in range(2):
+                at = slice(h * TILE, (h + 1) * TILE)
+                centre = jnp.sum(product[h * head_size : (h + 1) * head_size], axis=0, keepdims=True)
+                grad_cols.append(raised[:, at] * (slopes[:, at] - centre).astype(BF))
+            grads = jnp.concatenate(grad_cols, axis=1)
             grads_ref[p * tiles + a] = grads
-            scale_ref[p * tiles + a] = scale
-            here = slice(a * TILE, (a + 1) * TILE)
             far = WIN - a * TILE
-            spread_scale = jnp.where(upper, scale[:, :TILE], scale[:, TILE:])
             queries = (qt_ref[cols, here].astype(F32) * spread_scale).T.astype(BF)
-            slopes = (dot_ref[cols, here].astype(F32) * spread_scale).T.astype(BF)
+            out_grad = (out_grad * spread_scale).T.astype(BF)
             q_ref[here, cols] = queries
-            do_ref[here, cols] = slopes
+            do_ref[here, cols] = out_grad
             halo_grads.append((
                 mm(grads[:far], both_heads(queries, 1, 0)),
-                mm(raised[:far], both_heads(slopes, 1, 0)),
+                mm(raised[:far], both_heads(out_grad, 1, 0)),
             ))
+
+        scores, slopes = multiply(0)
+        waiting = None
+        for a in range(tiles):
+            ahead = multiply(a + 1) if a + 1 < tiles else None
+            mixed = raise_and_mix(a, scores)
+            if waiting is not None:
+                finish(*waiting)
+            waiting = (a, slopes, *mixed)
+            if ahead is not None:
+                scores, slopes = ahead
+        finish(*waiting)
         for which, scale, out in ((0, math.log(2.0), dkh_ref), (1, 1.0, dvh_ref)):
             for j in range(WIN // TILE):
                 total = None
@@ -246,22 +259,20 @@
 
 
 def weights_body(
-    scale, rows, head_size, meta_ref, normed_hbm, halo_hbm, frames_ref, cot_hbm,
+    scale, rows, head_size, meta_ref, normed_hbm, halo_t_ref, frames_ref, cot_hbm,
     wq_hbm, wk_hbm, wv_hbm, wo_hbm,
-    q_ref, kt_ref, vt_ref, khalo_t_ref, vhalo_t_ref, do_ref, raised_ref, grads_ref, scale_ref, dkh_ref, dvh_ref,
+    q_ref, kt_ref, khalo_t_ref, ot, do_ref, raised_ref, grads_ref, scale_ref, dkh_ref, dvh_ref,
     keep_ref, send_ref, out_ref, slope_ref,
-    normed_t, halo_t, mixed_t, ktx, vtx, ot, dqt, dk, dv,
-    wq, wk, wv, wo, normed_ref, halo_ref, cot_ref, sems,
+    normed_t, halo_t, mixed_t, ktx, dqt, dk, dv,
+    wq, wk, wv, wo, normed_ref, cot_ref, sems,
 ):
     span, width = q_ref.shape
     copies = fetch(
-        [wq_hbm, wk_hbm, wv_hbm, wo_hbm, normed_hbm, halo_hbm, cot_hbm],
-        [wq, wk, wv, wo, normed_ref, halo_ref, cot_ref], sems,
+        [wq_hbm, wk_hbm, wv_hbm, wo_hbm, normed_hbm, cot_hbm],
+        [wq, wk, wv, wo, normed_ref, cot_ref], sems,
     )
     ktx[:, :WIN] = khalo_t_ref[...]
     ktx[:, WIN:] = kt_ref[...]
-    vtx[:, :WIN] = vhalo_t_ref[...]
-    vtx[:, WIN:] = vt_ref[...]
     pair = 2 * head_size
     tiles = span // TILE
     upper = iota2((pair, TILE), 0) < head_size
@@ -274,8 +285,6 @@
             keys = slice(a * TILE, a * TILE + REACH)
             at = p * tiles + a
             shrink = scale_ref[at]
-            mixed = mm(vtx[cols, keys], raised_ref[at]) * shrink
-            ot[cols, here] = jnp.where(upper, mixed[:, :TILE], mixed[:, TILE:]).astype(BF)
             moved = mm(ktx[cols, keys], grads_ref[at]) * (shrink * head_size ** (-0.5))
             dqt[cols, here] = jnp.where(upper, moved[:, :TILE], moved[:, TILE:]).astype(BF)
             near = slice(WIN - a * TILE, REACH)
@@ -299,7 +308,7 @@
     chunks = width // (2 * rows)
     split = (chunks, 2, rows, span)
     normed_t[...] = normed_ref[...].T.reshape(split)
-    halo_t[...] = halo_ref[...].T.reshape(split)
+    halo_t[...] = halo_t_ref[...].reshape(split)
     mixed_t[...] = ot[...].reshape(split)
     mine = meta_ref[2]
     for side, out in ((1 - mine, send_ref), (mine, keep_ref)):
@@ -422,13 +431,13 @@
     )
     units = H // 2 * (span // TILE)
     saved = sds((units, REACH, 2 * TILE))
-    raised, grads, scales, q, do, dkh, dvh, khalo_t, vhalo_t, back = vmem_call(
+    raised, grads, scales, q, do, dkh, dvh, khalo_t, halo_t, ot, back = vmem_call(
         lambda *refs: scores_body(head_size, *refs),
-        [saved, saved, sds((units, 1, 2 * TILE), F32)] + [square] * 7,
-        [meta, halo, wk, wv, qt, k, v, cot, out_weight],
+        [saved, saved, sds((units, 1, 2 * TILE), F32)] + [square] * 8,
+        [meta, halo, wk, wv, qt, k, v, vt, cot, out_weight],
         smem=(0,),
-        hbm=(7, 8),
-        scratch=[pltpu.VMEM((WIN + span, width), BF)] * 2
+        hbm=(8, 9),
+        scratch=[pltpu.VMEM((WIN + span, width), BF)] * 2 + [pltpu.VMEM((width, WIN + span), BF)]
         + [pltpu.VMEM((width, span), BF)] * 3 + [pltpu.SemaphoreType.DMA((2,))],
         flops=12 * cube,
         limit=24,
@@ -441,12 +450,12 @@
     keep, send, out_frames, slope = vmem_call(
         lambda *refs: weights_body(slab ** (-0.5), chunk, head_size, *refs),
         [half, half, square, sds((span, width), F32)],
-        [meta, normed, halo, frames, cot, query_weight, key_weight, value_weight, out_weight,
-         q, kt, vt, khalo_t, vhalo_t, do, raised, grads, scales, dkh, dvh],
+        [meta, normed, halo_t, frames, cot, query_weight, key_weight, value_weight, out_weight,
+         q, kt, khalo_t, ot, do, raised, grads, scales, dkh, dvh],
         smem=(0,),
-        hbm=(1, 2, 4, 5, 6, 7, 8),
-        scratch=[split] * 3 + [pltpu.VMEM((width, WIN + span), BF)] * 2 + [whole] * 11
-        + [pltpu.SemaphoreType.DMA((7,))],
+        hbm=(1, 4, 5, 6, 7, 8),
+        scratch=[split] * 3 + [pltpu.VMEM((width, WIN + span), BF)] + [whole] * 9
+        + [pltpu.SemaphoreType.DMA((6,))],
         flops=18 * cube,
         limit=26,
     )

time: 100 us -> 97.1 us (0.971)
  Pallas kernels: 30.9 us -> 29.1 us
  local copies, waits for them, and re-layouts: 7.62 us -> 6.59 us
    pallas_call x11, Pallas kernels: 30.9 us -> 29.1 us  [vmem_call(): pl.pallas_call(body, out_shape=tuple(outs), in_specs=[pl.BlockSpec(memory...]
    ppermute x1, starting transfers between devices: 1.19 us -> 2.59 us  [shards(): got = lax.ppermute(send, 'seq', [(i, i ^ 1) for i in range(seqs)])]
    all_to_all x2, starting transfers between devices: 12.5 us -> 11.1 us  [exchanged(): lax.all_to_all(shard.reshape(devices, slots, width), AXES, split_axis=0,...]
    unnamed x30 -> x26, local copies, waits for them, and re-layouts: 6.8 us -> 5.76 us
where the time goes in v8:
time: 97.1 us; the launch traced here: 96.6 us
  waiting for transfers between devices  33.7 us (35%)
  Pallas kernels  29.1 us (30%)
  starting transfers between devices  24.9 us (26%)
  local copies, waits for them, and re-layouts  6.59 us (7%)
  between operations  1.55 us (2%)
    pallas_call x11, Pallas kernels, vmem_call(): pl.pallas_call(body, out_shape=tuple(outs), in_specs=[pl.BlockSpec(memory...  29.1 us
    ppermute x6, waiting for transfers between devices, swapped(): lax.ppermute(piece, axis, [(i, i ^ k * step) for i in range(count)])  20 us
    all_to_all x2, waiting for transfers between devices, exchanged(): lax.all_to_all(shard.reshape(devices, slots, width), AXES, split_axis=0,...  13.7 us
    all_to_all x2, starting transfers between devices, exchanged(): lax.all_to_all(shard.reshape(devices, slots, width), AXES, split_axis=0,...  11.1 us
    ppermute x6, starting transfers between devices, swapped(): lax.ppermute(piece, axis, [(i, i ^ k * step) for i in range(count)])  7.94 us
    unnamed x26, local copies, waits for them, and re-layouts  5.76 us
    ppermute x2, starting transfers between devices, passed_along(): return lax.ppermute(shard, 'seq', pairs)  3.24 us
    ppermute x1, starting transfers between devices, shards(): got = lax.ppermute(send, 'seq', [(i, i ^ 1) for i in range(seqs)])  2.59 us
  transfers between devices with their start and end apart: 11, of which 6 were waited for; matrix products, arithmetic and copies ran while one was open for 1% of the time, Pallas kernels for 16%

profile of v8, /device:TPU:0, one launch (start us, length us, event | category | flops | bytes accessed | tf_op | source)
XLA Modules:
  0.0 96.6 jit_solution(14483461444102962176)
XLA Ops:
  0.7 1.1 %copy-done.10 = bf16[512,512]{1,0:T(8,128)(2,1)S(1)} copy-done((bf16[512,512]{1,0:T(8,128)(2,1)S(1)}, bf16[512,512]{1,0:T(8,128)(2,1)}, u32[]{:S(2)}) %copy-start.10) | copy-done | bytes 524312
  2.5 1.6 %shard_map.113 = bf16[512,512]{1,0:T(8,128)(2,1)} custom-call(s32[1,512]{1,0:T(1,128)S(1)} %bitcast.29, bf16[512,512]{1,0:T(8,128)(2,1)S(1)} %copy-done.10), custom_call_target="tpu_custom_call" | custom-call | flops 268435456 | bytes 1050624 | tf_op jit(solution)/shard_map/pallas_call | solution.py:33
  4.0 7.3 %all-to-all-start = ((bf16[32,16,512]{2,1,0:T(8,128)(2,1)}), bf16[32,16,512]{2,1,0:T(8,128)(2,1)S(1)}, u32[]{:S(2)}, u32[]{:S(2)}) async-start(bf16[32,16,512]{2,1,0:T(8,128)(2,1)} %bitcast.4), calls=%async_computation | async-start | bytes 1048576 | tf_op jit(solution)/shard_map/all_to_all | solution.py:401
  14.0 13.7 %all-to-all-done = bf16[32,16,512]{2,1,0:T(8,128)(2,1)S(1)} async-done(((bf16[32,16,512]{2,1,0:T(8,128)(2,1)}), bf16[32,16,512]{2,1,0:T(8,128)(2,1)S(1)}, u32[]{:S(2)}, u32[]{:S(2)}) %all-to-all-start) | async-done | bytes 524320 | tf_op jit(solution)/shard_map/all_to_all | solution.py:401
  28.3 1.9 %collective-permute-start = (bf16[512,512]{1,0:T(8,128)(2,1)S(1)}, bf16[512,512]{1,0:T(8,128)(2,1)S(1)}, u32[]{:S(2)}, u32[]{:S(2)}) collective-permute-start(bf16[512,512]{1,0:T(8,128)(2,1)S(1)} %get-tuple-element.42.refs_0_.refs_1_), channel_id=1, source_target_pairs={{0,1},{1,2},{2,3},{3,4},{4,5},{5,6},{6,7},{8,9},{9,10},{10,11},{11... | collective-permute-start | bytes 1572872 | tf_op jit(solution)/shard_map/ppermute | solution.py:352
  31.0 1.0 %copy-done.1 = bf16[512,512]{1,0:T(8,128)(2,1)S(1)} copy-done((bf16[512,512]{1,0:T(8,128)(2,1)S(1)}, bf16[512,512]{1,0:T(8,128)(2,1)}, u32[]{:S(2)}) %copy-start.1) | copy-done | bytes 524312
  32.1 1.0 %copy-done.3 = bf16[512,512]{1,0:T(8,128)(2,1)S(1)} copy-done((bf16[512,512]{1,0:T(8,128)(2,1)S(1)}, bf16[512,512]{1,0:T(8,128)(2,1)}, u32[]{:S(2)}) %copy-start.3) | copy-done | bytes 524312
  33.1 1.0 %copy-done.5 = bf16[512,512]{1,0:T(8,128)(2,1)S(1)} copy-done((bf16[512,512]{1,0:T(8,128)(2,1)S(1)}, bf16[512,512]{1,0:T(8,128)(2,1)}, u32[]{:S(2)}) %copy-start.5) | copy-done | bytes 524312
  34.1 1.7 %shard_map.115 = (bf16[512,512]{1,0:T(8,128)(2,1)S(1)}, bf16[512,512]{1,0:T(8,128)(2,1)S(1)}, bf16[512,512]{1,0:T(8,128)(2,1)S(1)}, bf16[512,512]{1,0:T(8,128)(2...) custom-call(bf16[512,512]{1,0:T(8,128)(2,1)S(1)} %get-tuple-element.42.refs_0_.ref, ...), custom_call_target="tpu_custom_call" | custom-call | flops 805306368 | bytes 5767168 | tf_op jit(solution)/shard_map/pallas_call | solution.py:33
  35.9 11.5 %shard_map.116 = (bf16[16,640,256]{2,1,0:T(8,128)(2,1)S(1)}, bf16[16,640,256]{2,1,0:T(8,128)(2,1)S(1)}, f32[16,1,256]{2,1,0:T(1,128)S(1)}, bf16[512,512]{1,0:T(8...) custom-call(s32[3]{0:T(128)S(1)} %pad_add_fusion.refs_0_, ...), custom_call_target="tpu_custom_call" | custom-call | flops 3221225472 | bytes 19415052 | tf_op jit(solution)/shard_map/pallas_call | solution.py:33
  47.5 1.3 %collective-permute-start.1 = (bf16[512,512]{1,0:T(8,128)(2,1)S(1)}, bf16[512,512]{1,0:T(8,128)(2,1)S(1)}, u32[]{:S(2)}, u32[]{:S(2)}) collective-permute-start(bf16[512,512]{1,0:T(8,128)(2,1)S(1)} %get-tuple-element.64), channel_id=1, source_target_pairs={{1,0},{2,1},{3,2},{4,3},{5,4},{6,5},{7,6},{9,8},{10,9},{11,10},{12... | collective-permute-start | bytes 1572872 | tf_op jit(solution)/shard_map/ppermute | solution.py:352
  48.8 7.8 %shard_map.117 = (bf16[256,2048]{1,0:T(8,128)(2,1)S(1)}, bf16[256,2048]{1,0:T(8,128)(2,1)}, bf16[512,512]{1,0:T(8,128)(2,1)}, f32[512,512]{1,0:T(8,128)S(1)}) custom-call(s32[3]{0:T(128)S(1)} %pad_add_fusion.refs_0_, bf16[512,512]{1,0:T(8,128)(2,1)S(1)} %get-tuple-element.42.refs_0_.refs_1_, bf16[512,512]{1,0:T(8,128)(2,1)S(1)} %get-tuple-element.49.refs_2_, ...), custom_call_target="tpu_custom_call" | custom-call | flops 4831838208 | bytes 22036492 | tf_op jit(solution)/shard_map/pallas_call | solution.py:33
  56.6 2.6 %collective-permute-start.2 = (bf16[256,2048]{1,0:T(8,128)(2,1)}, bf16[256,2048]{1,0:T(8,128)(2,1)S(1)}, u32[]{:S(2)}, u32[]{:S(2)}) collective-permute-start(bf16[256,2048]{1,0:T(8,128)(2,1)} %get-tuple-element.70), channel_id=1, source_target_pairs={{0,1},{1,0},{2,3},{3,2},{4,5},{5,4},{6,7},{7,6},{8,9},{9,8},{10,11... | collective-permute-start | bytes 3145736 | tf_op jit(solution)/shard_map/ppermute | solution.py:470
  59.2 2.1 %shard_map.118 = bf16[512,512]{1,0:T(8,128)(2,1)} custom-call(bf16[512,512]{1,0:T(8,128)(2,1)S(1)} %get-tuple-element.50.refs_3_.frames_ref, f32[512,512]{1,0:T(8,128)S(1)} %get-tuple-element.62.slope_ref, bf16[512,512]{1,0:T(8,128)(2,1)S(1)} %collective-permute-done.1.extra_ref, bf16[512,512]{1,0:T(8,128)(2,1)S(1)} %bitcast.20, bf16[512,512]{1,0:T(8,128)(2,1)S(1)} %copy-done.9), custom_call_target="tpu_custom_call" | custom-call | flops 268435456 | bytes 3670016 | tf_op jit(solution)/shard_map/pallas_call | solution.py:33
  61.3 3.8 %all-to-all-start.1 = ((bf16[32,16,512]{2,1,0:T(8,128)(2,1)}), bf16[32,16,512]{2,1,0:T(8,128)(2,1)S(1)}, u32[]{:S(2)}, u32[]{:S(2)}) async-start(bf16[32,16,512]{2,1,0:T(8,128)(2,1)} %bitcast.8), calls=%async_computation.1 | async-start | bytes 1048576 | tf_op jit(solution)/shard_map/all_to_all | solution.py:401
  66.1 1.8 %collective-permute-start.3 = (bf16[64,2048]{1,0:T(8,128)(2,1)}, bf16[64,2048]{1,0:T(8,128)(2,1)S(1)}, u32[]{:S(2)}, u32[]{:S(2)}) collective-permute-start(bf16[64,2048]{1,0:T(8,128)(2,1)} %get-tuple-element.72), channel_id=1, source_target_pairs={{0,8},{8,0},{16,24},{24,16},{1,9},{9,1},{17,25},{25,17},{2,10},{10... | collective-permute-start | bytes 786440 | tf_op jit(solution)/shard_map/ppermute | solution.py:376
  67.9 1.5 %collective-permute-start.4 = (bf16[64,2048]{1,0:T(8,128)(2,1)}, bf16[64,2048]{1,0:T(8,128)(2,1)S(1)}, u32[]{:S(2)}, u32[]{:S(2)}) collective-permute-start(bf16[64,2048]{1,0:T(8,128)(2,1)} %get-tuple-element.73), channel_id=1, source_target_pairs={{0,16},{8,24},{16,0},{24,8},{1,17},{9,25},{17,1},{25,9},{2,18},{10... | collective-permute-start | bytes 786440 | tf_op jit(solution)/shard_map/ppermute | solution.py:376
  69.6 9.2 %collective-permute-done.3 = bf16[64,2048]{1,0:T(8,128)(2,1)S(1)} collective-permute-done((bf16[64,2048]{1,0:T(8,128)(2,1)}, bf16[64,2048]{1,0:T(8,128)(2,1)S(1)}, u32[]{:S(2)}, u32[]{:S(2)}) %collective-permute-start.3) | collective-permute-done | bytes 262176 | tf_op jit(solution)/shard_map/ppermute | solution.py:376
  79.1 6.7 %collective-permute-done.5 = bf16[64,2048]{1,0:T(8,128)(2,1)S(1)} collective-permute-done((bf16[64,2048]{1,0:T(8,128)(2,1)S(1)}, bf16[64,2048]{1,0:T(8,128)(2,1)S(1)}, u32[]{:S(2)}, u32[]{:S(2)}) %collective-permute-start.5) | collective-permute-done | bytes 262176 | tf_op jit(solution)/shard_map/ppermute | solution.py:376
  85.9 1.5 %collective-permute-start.6 = (bf16[16,2048]{1,0:T(8,128)(2,1)S(1)}, bf16[16,2048]{1,0:T(8,128)(2,1)S(1)}, u32[]{:S(2)}, u32[]{:S(2)}) collective-permute-start(bf16[16,2048]{1,0:T(8,128)(2,1)S(1)} %get-tuple-element.76), channel_id=1, source_target_pairs={{0,2},{1,3},{2,0},{3,1},{4,6},{5,7},{6,4},{7,5},{8,10},{9,11},{10,... | collective-permute-start | bytes 196616 | tf_op jit(solution)/shard_map/ppermute | solution.py:376
  87.4 2.4 %collective-permute-start.7 = (bf16[16,2048]{1,0:T(8,128)(2,1)S(1)}, bf16[16,2048]{1,0:T(8,128)(2,1)S(1)}, u32[]{:S(2)}, u32[]{:S(2)}) collective-permute-start(bf16[16,2048]{1,0:T(8,128)(2,1)S(1)} %get-tuple-element.77), channel_id=1, source_target_pairs={{0,4},{1,5},{2,6},{3,7},{4,0},{5,1},{6,2},{7,3},{8,12},{9,13},{10,... | collective-permute-start | bytes 196616 | tf_op jit(solution)/shard_map/ppermute | solution.py:376
  90.8 1.2 %shard_map.120 = bf16[512,512]{1,0:T(8,128)(2,1)} custom-call(bf16[512,512]{1,0:T(8,128)(2,1)S(1)} %shard_map.119.placing_t_ref, bf16[512,512]{1,0:T(8,128)(2,1)S(1)} %bitcast.21), custom_call_target="tpu_custom_call" | custom-call | flops 268435456 | bytes 1572864 | tf_op jit(solution)/shard_map/pallas_call | solution.py:33
  92.1 2.6 %collective-permute-done.7 = bf16[16,2048]{1,0:T(8,128)(2,1)S(1)} collective-permute-done((bf16[16,2048]{1,0:T(8,128)(2,1)S(1)}, bf16[16,2048]{1,0:T(8,128)(2,1)S(1)}, u32[]{:S(2)}, u32[]{:S(2)}) %collective-permute-start.7) | collective-permute-done | bytes 65568 | tf_op jit(solution)/shard_map/ppermute | solution.py:376
  94.7 1.2 %collective-permute-done.8 = bf16[16,2048]{1,0:T(8,128)(2,1)S(1)} collective-permute-done((bf16[16,2048]{1,0:T(8,128)(2,1)S(1)}, bf16[16,2048]{1,0:T(8,128)(2,1)S(1)}, u32[]{:S(2)}, u32[]{:S(2)}) %collective-permute-start.8) | collective-permute-done | bytes 65568 | tf_op jit(solution)/shard_map/ppermute | solution.py:376
  (38 shorter events, 7.5 us)
Async XLA Ops:
  0.6 35.2 %copy-start.7 = (bf16[512,512]{1,0:T(8,128)(2,1)S(1)}, bf16[512,512]{1,0:T(8,128)(2,1)}, u32[]{:S(2)}) copy-start(bf16[512,512]{1,0:T(8,128)(2,1)} %refs_8_.1) | copy-start | bytes 1572868
  0.6 35.2 %copy-start = (bf16[1,512,512]{2,1,0:T(8,128)(2,1)S(1)}, bf16[1,512,512]{2,1,0:T(8,128)(2,1)}, u32[]{:S(2)}) copy-start(bf16[1,512,512]{2,1,0:T(8,128)(2,1)} %param.17) | copy-start | bytes 1572868
  0.7 1.1 %copy-start.10 = (bf16[512,512]{1,0:T(8,128)(2,1)S(1)}, bf16[512,512]{1,0:T(8,128)(2,1)}, u32[]{:S(2)}) copy-start(bf16[512,512]{1,0:T(8,128)(2,1)} %refs_1_.2) | copy-start | bytes 1572868
  1.8 0.7 copy-start.11
  4.0 23.7 %all-to-all-start = ((bf16[32,16,512]{2,1,0:T(8,128)(2,1)}), bf16[32,16,512]{2,1,0:T(8,128)(2,1)S(1)}, u32[]{:S(2)}, u32[]{:S(2)}) async-start(bf16[32,16,512]{2,1,0:T(8,128)(2,1)} %bitcast.4), calls=%async_computation | async-start | bytes 1048576 | tf_op jit(solution)/shard_map/all_to_all | solution.py:401
  13.2 0.8 copy-start.8
  28.3 7.5 %collective-permute-start = (bf16[512,512]{1,0:T(8,128)(2,1)S(1)}, bf16[512,512]{1,0:T(8,128)(2,1)S(1)}, u32[]{:S(2)}, u32[]{:S(2)}) collective-permute-start(bf16[512,512]{1,0:T(8,128)(2,1)S(1)} %get-tuple-element.42.refs_0_.refs_1_), channel_id=1, source_target_pairs={{0,1},{1,2},{2,3},{3,4},{4,5},{5,6},{6,7},{8,9},{9,10},{10,11},{11... | collective-permute-start | bytes 1572872 | tf_op jit(solution)/shard_map/ppermute | solution.py:352
  31.0 1.0 %copy-start.1 = (bf16[512,512]{1,0:T(8,128)(2,1)S(1)}, bf16[512,512]{1,0:T(8,128)(2,1)}, u32[]{:S(2)}) copy-start(bf16[512,512]{1,0:T(8,128)(2,1)} %refs_5_.1) | copy-start | bytes 1572868
  32.1 1.0 %copy-start.3 = (bf16[512,512]{1,0:T(8,128)(2,1)S(1)}, bf16[512,512]{1,0:T(8,128)(2,1)}, u32[]{:S(2)}) copy-start(bf16[512,512]{1,0:T(8,128)(2,1)} %refs_6_.1) | copy-start | bytes 1572868
  33.1 1.0 %copy-start.5 = (bf16[512,512]{1,0:T(8,128)(2,1)S(1)}, bf16[512,512]{1,0:T(8,128)(2,1)}, u32[]{:S(2)}) copy-start(bf16[512,512]{1,0:T(8,128)(2,1)} %refs_7_.1) | copy-start | bytes 1572868
  35.9 12.9 %copy-start.2 = (bf16[512,512]{1,0:T(8,128)(2,1)S(1)}, bf16[512,512]{1,0:T(8,128)(2,1)}, u32[]{:S(2)}) copy-start(bf16[512,512]{1,0:T(8,128)(2,1)} %refs_5_.1) | copy-start | bytes 1572868
  35.9 12.9 %copy-start.4 = (bf16[512,512]{1,0:T(8,128)(2,1)S(1)}, bf16[512,512]{1,0:T(8,128)(2,1)}, u32[]{:S(2)}) copy-start(bf16[512,512]{1,0:T(8,128)(2,1)} %refs_6_.1) | copy-start | bytes 1572868
  35.9 12.9 %copy-start.6 = (bf16[512,512]{1,0:T(8,128)(2,1)S(1)}, bf16[512,512]{1,0:T(8,128)(2,1)}, u32[]{:S(2)}) copy-start(bf16[512,512]{1,0:T(8,128)(2,1)} %refs_7_.1) | copy-start | bytes 1572868
  47.5 9.1 %collective-permute-start.1 = (bf16[512,512]{1,0:T(8,128)(2,1)S(1)}, bf16[512,512]{1,0:T(8,128)(2,1)S(1)}, u32[]{:S(2)}, u32[]{:S(2)}) collective-permute-start(bf16[512,512]{1,0:T(8,128)(2,1)S(1)} %get-tuple-element.64), channel_id=1, source_target_pairs={{1,0},{2,1},{3,2},{4,3},{5,4},{6,5},{7,6},{9,8},{10,9},{11,10},{12... | collective-permute-start | bytes 1572872 | tf_op jit(solution)/shard_map/ppermute | solution.py:352
  48.8 10.4 %copy-start.9 = (bf16[512,512]{1,0:T(8,128)(2,1)S(1)}, bf16[512,512]{1,0:T(8,128)(2,1)}, u32[]{:S(2)}) copy-start(bf16[512,512]{1,0:T(8,128)(2,1)} %copy-done.8) | copy-start | bytes 1572868
  56.6 33.8 %copy-start.12 = (s32[512]{0:T(512)S(1)}, s32[512]{0:T(512)}, u32[]{:S(2)}) copy-start(s32[512]{0:T(512)} %param.10) | copy-start | bytes 6148
  56.6 8.5 %collective-permute-start.2 = (bf16[256,2048]{1,0:T(8,128)(2,1)}, bf16[256,2048]{1,0:T(8,128)(2,1)S(1)}, u32[]{:S(2)}, u32[]{:S(2)}) collective-permute-start(bf16[256,2048]{1,0:T(8,128)(2,1)} %get-tuple-element.70), channel_id=1, source_target_pairs={{0,1},{1,0},{2,3},{3,2},{4,5},{5,4},{6,7},{7,6},{8,9},{9,8},{10,11... | collective-permute-start | bytes 3145736 | tf_op jit(solution)/shard_map/ppermute | solution.py:470
  61.3 29.5 %all-to-all-start.1 = ((bf16[32,16,512]{2,1,0:T(8,128)(2,1)}), bf16[32,16,512]{2,1,0:T(8,128)(2,1)S(1)}, u32[]{:S(2)}, u32[]{:S(2)}) async-start(bf16[32,16,512]{2,1,0:T(8,128)(2,1)} %bitcast.8), calls=%async_computation.1 | async-start | bytes 1048576 | tf_op jit(solution)/shard_map/all_to_all | solution.py:401
  66.1 12.7 %collective-permute-start.3 = (bf16[64,2048]{1,0:T(8,128)(2,1)}, bf16[64,2048]{1,0:T(8,128)(2,1)S(1)}, u32[]{:S(2)}, u32[]{:S(2)}) collective-permute-start(bf16[64,2048]{1,0:T(8,128)(2,1)} %get-tuple-element.72), channel_id=1, source_target_pairs={{0,8},{8,0},{16,24},{24,16},{1,9},{9,1},{17,25},{25,17},{2,10},{10... | collective-permute-start | bytes 786440 | tf_op jit(solution)/shard_map/ppermute | solution.py:376
  67.9 11.2 %collective-permute-start.4 = (bf16[64,2048]{1,0:T(8,128)(2,1)}, bf16[64,2048]{1,0:T(8,128)(2,1)S(1)}, u32[]{:S(2)}, u32[]{:S(2)}) collective-permute-start(bf16[64,2048]{1,0:T(8,128)(2,1)} %get-tuple-element.73), channel_id=1, source_target_pairs={{0,16},{8,24},{16,0},{24,8},{1,17},{9,25},{17,1},{25,9},{2,18},{10... | collective-permute-start | bytes 786440 | tf_op jit(solution)/shard_map/ppermute | solution.py:376
  69.3 16.4 %collective-permute-start.5 = (bf16[64,2048]{1,0:T(8,128)(2,1)S(1)}, bf16[64,2048]{1,0:T(8,128)(2,1)S(1)}, u32[]{:S(2)}, u32[]{:S(2)}) collective-permute-start(bf16[64,2048]{1,0:T(8,128)(2,1)S(1)} %get-tuple-element.74), channel_id=1, source_target_pairs={{0,24},{8,16},{16,8},{24,0},{1,25},{9,17},{17,9},{25,1},{2,26},{10... | collective-permute-start | bytes 786440 | tf_op jit(solution)/shard_map/ppermute | solution.py:376
  85.9 6.2 %collective-permute-start.6 = (bf16[16,2048]{1,0:T(8,128)(2,1)S(1)}, bf16[16,2048]{1,0:T(8,128)(2,1)S(1)}, u32[]{:S(2)}, u32[]{:S(2)}) collective-permute-start(bf16[16,2048]{1,0:T(8,128)(2,1)S(1)} %get-tuple-element.76), channel_id=1, source_target_pairs={{0,2},{1,3},{2,0},{3,1},{4,6},{5,7},{6,4},{7,5},{8,10},{9,11},{10,... | collective-permute-start | bytes 196616 | tf_op jit(solution)/shard_map/ppermute | solution.py:376
  87.4 7.3 %collective-permute-start.7 = (bf16[16,2048]{1,0:T(8,128)(2,1)S(1)}, bf16[16,2048]{1,0:T(8,128)(2,1)S(1)}, u32[]{:S(2)}, u32[]{:S(2)}) collective-permute-start(bf16[16,2048]{1,0:T(8,128)(2,1)S(1)} %get-tuple-element.77), channel_id=1, source_target_pairs={{0,4},{1,5},{2,6},{3,7},{4,0},{5,1},{6,2},{7,3},{8,12},{9,13},{10,... | collective-permute-start | bytes 196616 | tf_op jit(solution)/shard_map/ppermute | solution.py:376
  89.8 6.2 %collective-permute-start.8 = (bf16[16,2048]{1,0:T(8,128)(2,1)S(1)}, bf16[16,2048]{1,0:T(8,128)(2,1)S(1)}, u32[]{:S(2)}, u32[]{:S(2)}) collective-permute-start(bf16[16,2048]{1,0:T(8,128)(2,1)S(1)} %get-tuple-element.78), channel_id=1, source_target_pairs={{0,6},{1,7},{2,4},{3,5},{4,2},{5,3},{6,0},{7,1},{8,14},{9,15},{10,... | collective-permute-start | bytes 196616 | tf_op jit(solution)/shard_map/ppermute | solution.py:376

commit v9 on v8

--- a/solution.py
+++ b/solution.py
@@ -27,7 +27,12 @@
     return lax.broadcasted_iota(jnp.int32, shape, dim)
 
 
-def vmem_call(body, outs, args, smem=(), hbm=(), scratch=(), flops=0, limit=12):
+def vmem_call(body, outs, args, smem=(), hbm=(), scratch=(), carry=(), flops=0, limit=12):
+    used, inner, args = len(args), body, list(args) + list(carry)
+
+    def body(*refs):
+        inner(*refs[:used], *refs[len(args) :])
+
     spaces = [pltpu.SMEM if i in smem else pltpu.HBM if i in hbm else pltpu.VMEM for i in range(len(args))]
     size = sum(math.prod(a.shape) * a.dtype.itemsize for a in list(args) + list(outs))
     return pl.pallas_call(
@@ -106,10 +111,11 @@
 
 def project_body(
     query_scale, normed_ref, wq_hbm, wk_hbm, wv_hbm,
-    qt_ref, k_ref, kt_ref, v_ref, vt_ref, wk_ref, wv_ref, wq_ref, sems,
+    qt_ref, k_ref, kt_ref, v_ref, vt_ref, wk_ref, wv_ref, normed_t_ref, wq_ref, sems,
 ):
     copies = fetch([wq_hbm, wk_hbm, wv_hbm], [wq_ref, wk_ref, wv_ref], sems)
     normed = normed_ref[...]
+    normed_t_ref[...] = normed.T
     copies[0].wait()
     qt_ref[...] = (mm(normed, wq_ref[...]) * query_scale).astype(BF).T
     copies[1].wait()
@@ -259,17 +265,16 @@
 
 
 def weights_body(
-    scale, rows, head_size, meta_ref, normed_hbm, halo_t_ref, frames_ref, cot_hbm,
+    scale, rows, head_size, meta_ref, normed_turned_ref, halo_t_ref, frames_ref, cot_hbm,
     wq_hbm, wk_hbm, wv_hbm, wo_hbm,
     q_ref, kt_ref, khalo_t_ref, ot, do_ref, raised_ref, grads_ref, scale_ref, dkh_ref, dvh_ref,
     keep_ref, send_ref, out_ref, slope_ref,
     normed_t, halo_t, mixed_t, ktx, dqt, dk, dv,
-    wq, wk, wv, wo, normed_ref, cot_ref, sems,
+    wq, wk, wv, wo, cot_ref, sems,
 ):
     span, width = q_ref.shape
     copies = fetch(
-        [wq_hbm, wk_hbm, wv_hbm, wo_hbm, normed_hbm, cot_hbm],
-        [wq, wk, wv, wo, normed_ref, cot_ref], sems,
+        [wq_hbm, wk_hbm, wv_hbm, wo_hbm, cot_hbm], [wq, wk, wv, wo, cot_ref], sems
     )
     ktx[:, :WIN] = khalo_t_ref[...]
     ktx[:, WIN:] = kt_ref[...]
@@ -307,7 +312,7 @@
         copy.wait()
     chunks = width // (2 * rows)
     split = (chunks, 2, rows, span)
-    normed_t[...] = normed_ref[...].T.reshape(split)
+    normed_t[...] = normed_turned_ref[...].reshape(split)
     halo_t[...] = halo_t_ref[...].reshape(split)
     mixed_t[...] = ot[...].reshape(split)
     mine = meta_ref[2]
@@ -363,11 +368,11 @@
         out[...] = total.astype(BF)
 
 
-def spread(inputs, place, parts):
+def spread(inputs, place, parts, carry=()):
     columns = inputs[0].shape[-1]
     inputs = [shard.reshape(parts, -1, columns) for shard in inputs]
     piece = sds(inputs[0].shape[1:])
-    return vmem_call(spread_body, [piece] * parts, [place.reshape(1)] + inputs, smem=(0,))
+    return vmem_call(spread_body, [piece] * parts, [place.reshape(1)] + inputs, smem=(0,), carry=carry)
 
 
 def swapped(pieces, axis, step):
@@ -421,9 +426,9 @@
     frames, normed = vmem_call(frames_body, [square, square], [pick, incoming], flops=cube)
     halo = passed_along(normed, 1)
     query_scale = head_size ** (-0.5) * math.log2(math.e)
-    qt, k, kt, v, vt, wk, wv = vmem_call(
+    qt, k, kt, v, vt, wk, wv, normed_turned = vmem_call(
         lambda *refs: project_body(query_scale, *refs),
-        [square] * 7,
+        [square] * 8,
         [normed, query_weight, key_weight, value_weight],
         hbm=(1, 2, 3),
         scratch=[pltpu.VMEM((width, width), BF), pltpu.SemaphoreType.DMA((3,))],
@@ -450,12 +455,12 @@
     keep, send, out_frames, slope = vmem_call(
         lambda *refs: weights_body(slab ** (-0.5), chunk, head_size, *refs),
         [half, half, square, sds((span, width), F32)],
-        [meta, normed, halo_t, frames, cot, query_weight, key_weight, value_weight, out_weight,
+        [meta, normed_turned, halo_t, frames, cot, query_weight, key_weight, value_weight, out_weight,
          q, kt, khalo_t, ot, do, raised, grads, scales, dkh, dvh],
         smem=(0,),
-        hbm=(1, 4, 5, 6, 7, 8),
-        scratch=[split] * 3 + [pltpu.VMEM((width, WIN + span), BF)] + [whole] * 9
-        + [pltpu.SemaphoreType.DMA((6,))],
+        hbm=(4, 5, 6, 7, 8),
+        scratch=[split] * 3 + [pltpu.VMEM((width, WIN + span), BF)] + [whole] * 8
+        + [pltpu.SemaphoreType.DMA((5,))],
         flops=18 * cube,
         limit=26,
     )
@@ -476,7 +481,7 @@
         scratch=[whole, whole, pltpu.SemaphoreType.DMA((2,))],
         flops=cube,
     )
-    pieces = spread([keep, got], lax.axis_index("stream"), lax.axis_size("stream"))
+    pieces = spread([keep, got], lax.axis_index("stream"), lax.axis_size("stream"), [returning])
     pieces = swapped(pieces, "stream", 1)
     late_rows, returning = lax.optimization_barrier((row_frame.reshape(1, row_count), returning))
     arrived = exchanged(returning)
@@ -484,6 +489,7 @@
         lambda *refs: placing_t_body(span, slots, *refs),
         [sds((row_count, devices * slots))],
         [late_rows],
+        flops=40 * cube,
     )
     frame_grads, = vmem_call(arrived_body, [square], [placing_t, arrived], flops=cube)
     pieces = swapped(spread(pieces, lax.axis_index("seq") >> 1, seqs // 2), "seq", 2)

time: 97.1 us -> 94.3 us (0.971)
  waiting for transfers between devices: 33.7 us -> 27.5 us
  local copies, waits for them, and re-layouts: 6.59 us -> 9.46 us
    ppermute x6, waiting for transfers between devices: 20 us -> 12.2 us  [swapped(): lax.ppermute(piece, axis, [(i, i ^ k * step) for i in range(count)])]
    unnamed x26 -> x32, local copies, waits for them, and re-layouts: 5.76 us -> 8.64 us
    all_to_all x2, waiting for transfers between devices: 13.7 us -> 15.2 us  [exchanged(): lax.all_to_all(shard.reshape(devices, slots, width), AXES, split_axis=0,...]
  transfers between devices with their start and end apart: 11 -> 11, of which waited for: 6 -> 7; matrix products, arithmetic and copies ran while one was open for 1% -> 1% of each run, Pallas kernels for 16% -> 15%
where the time goes in v9:
time: 94.3 us; the launch traced here: 93.7 us
  Pallas kernels  29.7 us (31%)
  waiting for transfers between devices  27.5 us (29%)
  starting transfers between devices  24.7 us (26%)
  local copies, waits for them, and re-layouts  9.46 us (10%)
  between operations  1.56 us (2%)
    pallas_call x11, Pallas kernels, vmem_call(): pl.pallas_call(body, out_shape=tuple(outs), in_specs=[pl.BlockSpec(memory...  29.7 us
    all_to_all x2, waiting for transfers between devices, exchanged(): lax.all_to_all(shard.reshape(devices, slots, width), AXES, split_axis=0,...  15.2 us
    ppermute x6, waiting for transfers between devices, swapped(): lax.ppermute(piece, axis, [(i, i ^ k * step) for i in range(count)])  12.2 us
    all_to_all x2, starting transfers between devices, exchanged(): lax.all_to_all(shard.reshape(devices, slots, width), AXES, split_axis=0,...  10.9 us
    unnamed x32, local copies, waits for them, and re-layouts  8.64 us
    ppermute x6, starting transfers between devices, swapped(): lax.ppermute(piece, axis, [(i, i ^ k * step) for i in range(count)])  8.01 us
    ppermute x2, starting transfers between devices, passed_along(): return lax.ppermute(shard, 'seq', pairs)  3.24 us
    ppermute x1, starting transfers between devices, shards(): got = lax.ppermute(send, 'seq', [(i, i ^ 1) for i in range(seqs)])  2.58 us
  transfers between devices with their start and end apart: 11, of which 7 were waited for; matrix products, arithmetic and copies ran while one was open for 1% of the time, Pallas kernels for 15%

profile of v9, /device:TPU:0, one launch (start us, length us, event | category | flops | bytes accessed | tf_op | source)
XLA Modules:
  0.0 93.7 jit_solution(8641943900739512949)
XLA Ops:
  0.7 1.1 %copy-done.13 = bf16[512,512]{1,0:T(8,128)(2,1)S(1)} copy-done((bf16[512,512]{1,0:T(8,128)(2,1)S(1)}, bf16[512,512]{1,0:T(8,128)(2,1)}, u32[]{:S(2)}) %copy-start.13) | copy-done | bytes 524312
  2.5 1.6 %shard_map.113 = bf16[512,512]{1,0:T(8,128)(2,1)} custom-call(s32[1,512]{1,0:T(1,128)S(1)} %bitcast.28, bf16[512,512]{1,0:T(8,128)(2,1)S(1)} %copy-done.13), custom_call_target="tpu_custom_call" | custom-call | flops 268435456 | bytes 1050624 | tf_op jit(solution)/shard_map/pallas_call | solution.py:38
  4.0 7.3 %all-to-all-start = ((bf16[32,16,512]{2,1,0:T(8,128)(2,1)}), bf16[32,16,512]{2,1,0:T(8,128)(2,1)S(1)}, u32[]{:S(2)}, u32[]{:S(2)}) async-start(bf16[32,16,512]{2,1,0:T(8,128)(2,1)} %bitcast.4), calls=%async_computation | async-start | bytes 1048576 | tf_op jit(solution)/shard_map/all_to_all | solution.py:406
  14.0 13.7 %all-to-all-done = bf16[32,16,512]{2,1,0:T(8,128)(2,1)S(1)} async-done(((bf16[32,16,512]{2,1,0:T(8,128)(2,1)}), bf16[32,16,512]{2,1,0:T(8,128)(2,1)S(1)}, u32[]{:S(2)}, u32[]{:S(2)}) %all-to-all-start) | async-done | bytes 524320 | tf_op jit(solution)/shard_map/all_to_all | solution.py:406
  28.3 1.9 %collective-permute-start = (bf16[512,512]{1,0:T(8,128)(2,1)S(1)}, bf16[512,512]{1,0:T(8,128)(2,1)S(1)}, u32[]{:S(2)}, u32[]{:S(2)}) collective-permute-start(bf16[512,512]{1,0:T(8,128)(2,1)S(1)} %get-tuple-element.43.refs_0_), channel_id=1, source_target_pairs={{0,1},{1,2},{2,3},{3,4},{4,5},{5,6},{6,7},{8,9},{9,10},{10,11},{11... | collective-permute-start | bytes 1572872 | tf_op jit(solution)/shard_map/ppermute | solution.py:357
  31.0 1.0 %copy-done.1 = bf16[512,512]{1,0:T(8,128)(2,1)S(1)} copy-done((bf16[512,512]{1,0:T(8,128)(2,1)S(1)}, bf16[512,512]{1,0:T(8,128)(2,1)}, u32[]{:S(2)}) %copy-start.1) | copy-done | bytes 524312
  32.1 1.0 %copy-done.3 = bf16[512,512]{1,0:T(8,128)(2,1)S(1)} copy-done((bf16[512,512]{1,0:T(8,128)(2,1)S(1)}, bf16[512,512]{1,0:T(8,128)(2,1)}, u32[]{:S(2)}) %copy-start.3) | copy-done | bytes 524312
  34.1 1.9 %shard_map.115 = (bf16[512,512]{1,0:T(8,128)(2,1)S(1)}, bf16[512,512]{1,0:T(8,128)(2,1)S(1)}, bf16[512,512]{1,0:T(8,128)(2,1)S(1)}, bf16[512,512]{1,0:T(8,128)(2...) custom-call(bf16[512,512]{1,0:T(8,128)(2,1)S(1)} %get-tuple-element., ...), custom_call_target="tpu_custom_call" | custom-call | flops 805306368 | bytes 6291456 | tf_op jit(solution)/shard_map/pallas_call | solution.py:38
  36.1 11.5 %shard_map.116 = (bf16[16,640,256]{2,1,0:T(8,128)(2,1)S(1)}, bf16[16,640,256]{2,1,0:T(8,128)(2,1)S(1)}, f32[16,1,256]{2,1,0:T(1,128)S(1)}, bf16[512,512]{1,0:T(8...) custom-call(s32[3]{0:T(128)S(1)} %pad_add_fusion.refs_0_, ...), custom_call_target="tpu_custom_call" | custom-call | flops 3221225472 | bytes 19415052 | tf_op jit(solution)/shard_map/pallas_call | solution.py:38
  47.6 1.3 %collective-permute-start.1 = (bf16[512,512]{1,0:T(8,128)(2,1)S(1)}, bf16[512,512]{1,0:T(8,128)(2,1)S(1)}, u32[]{:S(2)}, u32[]{:S(2)}) collective-permute-start(bf16[512,512]{1,0:T(8,128)(2,1)S(1)} %get-tuple-element.66), channel_id=1, source_target_pairs={{1,0},{2,1},{3,2},{4,3},{5,4},{6,5},{7,6},{9,8},{10,9},{11,10},{12... | collective-permute-start | bytes 1572872 | tf_op jit(solution)/shard_map/ppermute | solution.py:357
  49.0 7.6 %shard_map.117 = (bf16[256,2048]{1,0:T(8,128)(2,1)S(1)}, bf16[256,2048]{1,0:T(8,128)(2,1)}, bf16[512,512]{1,0:T(8,128)(2,1)}, f32[512,512]{1,0:T(8,128)S(1)}) custom-call(s32[3]{0:T(128)S(1)} %pad_add_fusion.refs_0_, bf16[512,512]{1,0:T(8,128)(2,1)S(1)} %get-tuple-element.44.refs_1_, bf16[512,512]{1,0:T(8,128)(2,1)S(1)} %get-tuple-element.51.refs_2_, ...), custom_call_target="tpu_custom_call" | custom-call | flops 4831838208 | bytes 22036492 | tf_op jit(solution)/shard_map/pallas_call | solution.py:38
  57.4 2.6 %collective-permute-start.2 = (bf16[256,2048]{1,0:T(8,128)(2,1)}, bf16[256,2048]{1,0:T(8,128)(2,1)}, u32[]{:S(2)}, u32[]{:S(2)}) collective-permute-start(bf16[256,2048]{1,0:T(8,128)(2,1)} %get-tuple-element.72), channel_id=1, source_target_pairs={{0,1},{1,0},{2,3},{3,2},{4,5},{5,4},{6,7},{7,6},{8,9},{9,8},{10,11... | collective-permute-start | bytes 3145736 | tf_op jit(solution)/shard_map/ppermute | solution.py:475
  62.1 2.1 %shard_map.118.refs_3_ = bf16[512,512]{1,0:T(8,128)(2,1)} custom-call(bf16[512,512]{1,0:T(8,128)(2,1)S(1)} %get-tuple-element.52.refs_3_.refs_0_, f32[512,512]{1,0:T(8,128)S(1)} %get-tuple-element.64.refs_1_, bf16[512,512]{1,0:T(8,128)(2,1)S(1)} %copy-done.12, bf16[512,512]{1,0:T(8,128)(2,1)S(1)} %bitcast.20, bf16[512,512]{1,0:T(8,128)(2,1)S(1)} %copy-done.10), custom_call_target="tpu_custom_call" | custom-call | flops 268435456 | bytes 3670016 | tf_op jit(solution)/shard_map/pallas_call | solution.py:38
  64.2 1.6 %shard_map.121 = (bf16[64,2048]{1,0:T(8,128)(2,1)S(1)}, bf16[64,2048]{1,0:T(8,128)(2,1)S(1)}, bf16[64,2048]{1,0:T(8,128)(2,1)S(1)}, bf16[64,2048]{1,0:T(8,128)(2,1)S(1)}) custom-call(s32[1]{0:T(128)} %bitcast.11.refs_0_, bf16[4,64,2048]{2,1,0:T(8,128)(2,1)S(1)} %bitcast.23, bf16[4,64,2048]{2,1,0:T(8,128)(2,1)} %bitcast.13.refs_2_, ...), custom_call_target="tpu_custom_call" | custom-call | bytes 3670020 | tf_op jit(solution)/shard_map/pallas_call | solution.py:38
  67.2 2.1 %collective-permute-start.5 = (bf16[64,2048]{1,0:T(8,128)(2,1)S(1)}, bf16[64,2048]{1,0:T(8,128)(2,1)S(1)}, u32[]{:S(2)}, u32[]{:S(2)}) collective-permute-start(bf16[64,2048]{1,0:T(8,128)(2,1)S(1)} %get-tuple-element.76), channel_id=1, source_target_pairs={{0,24},{8,16},{16,8},{24,0},{1,25},{9,17},{17,9},{25,1},{2,26},{10... | collective-permute-start | bytes 786440 | tf_op jit(solution)/shard_map/ppermute | solution.py:381
  69.3 3.6 %all-to-all-start.1 = ((bf16[32,16,512]{2,1,0:T(8,128)(2,1)}), bf16[32,16,512]{2,1,0:T(8,128)(2,1)S(1)}, u32[]{:S(2)}, u32[]{:S(2)}) async-start(bf16[32,16,512]{2,1,0:T(8,128)(2,1)} %bitcast.8), calls=%async_computation.1 | async-start | bytes 1048576 | tf_op jit(solution)/shard_map/all_to_all | solution.py:406
  72.9 2.1 %collective-permute-done.3 = bf16[64,2048]{1,0:T(8,128)(2,1)S(1)} collective-permute-done((bf16[64,2048]{1,0:T(8,128)(2,1)S(1)}, bf16[64,2048]{1,0:T(8,128)(2,1)S(1)}, u32[]{:S(2)}, u32[]{:S(2)}) %collective-permute-start.3) | collective-permute-done | bytes 262176 | tf_op jit(solution)/shard_map/ppermute | solution.py:381
  75.0 7.5 %collective-permute-done.4 = bf16[64,2048]{1,0:T(8,128)(2,1)S(1)} collective-permute-done((bf16[64,2048]{1,0:T(8,128)(2,1)S(1)}, bf16[64,2048]{1,0:T(8,128)(2,1)S(1)}, u32[]{:S(2)}, u32[]{:S(2)}) %collective-permute-start.4) | collective-permute-done | bytes 262176 | tf_op jit(solution)/shard_map/ppermute | solution.py:381
  83.5 1.7 %collective-permute-start.6 = (bf16[16,2048]{1,0:T(8,128)(2,1)S(1)}, bf16[16,2048]{1,0:T(8,128)(2,1)S(1)}, u32[]{:S(2)}, u32[]{:S(2)}) collective-permute-start(bf16[16,2048]{1,0:T(8,128)(2,1)S(1)} %get-tuple-element.78), channel_id=1, source_target_pairs={{0,2},{1,3},{2,0},{3,1},{4,6},{5,7},{6,4},{7,5},{8,10},{9,11},{10,... | collective-permute-start | bytes 196616 | tf_op jit(solution)/shard_map/ppermute | solution.py:381
  85.2 1.6 %collective-permute-start.7 = (bf16[16,2048]{1,0:T(8,128)(2,1)S(1)}, bf16[16,2048]{1,0:T(8,128)(2,1)S(1)}, u32[]{:S(2)}, u32[]{:S(2)}) collective-permute-start(bf16[16,2048]{1,0:T(8,128)(2,1)S(1)} %get-tuple-element.79), channel_id=1, source_target_pairs={{0,4},{1,5},{2,6},{3,7},{4,0},{5,1},{6,2},{7,3},{8,12},{9,13},{10,... | collective-permute-start | bytes 196616 | tf_op jit(solution)/shard_map/ppermute | solution.py:381
  86.8 1.2 %collective-permute-start.8 = (bf16[16,2048]{1,0:T(8,128)(2,1)S(1)}, bf16[16,2048]{1,0:T(8,128)(2,1)S(1)}, u32[]{:S(2)}, u32[]{:S(2)}) collective-permute-start(bf16[16,2048]{1,0:T(8,128)(2,1)S(1)} %get-tuple-element.80), channel_id=1, source_target_pairs={{0,6},{1,7},{2,4},{3,5},{4,2},{5,3},{6,0},{7,1},{8,14},{9,15},{10,... | collective-permute-start | bytes 196616 | tf_op jit(solution)/shard_map/ppermute | solution.py:381
  88.4 1.5 %all-to-all-done.1 = bf16[32,16,512]{2,1,0:T(8,128)(2,1)S(1)} async-done(((bf16[32,16,512]{2,1,0:T(8,128)(2,1)}), bf16[32,16,512]{2,1,0:T(8,128)(2,1)S(1)}, u32[]{:S(2)}, u32[]{:S(2)}) %all-to-all-start.1) | async-done | bytes 524320 | tf_op jit(solution)/shard_map/all_to_all | solution.py:406
  90.0 1.2 %shard_map.120 = bf16[512,512]{1,0:T(8,128)(2,1)} custom-call(bf16[512,512]{1,0:T(8,128)(2,1)S(1)} %shard_map.119.refs_0_, bf16[512,512]{1,0:T(8,128)(2,1)S(1)} %bitcast.21), custom_call_target="tpu_custom_call" | custom-call | flops 268435456 | bytes 1572864 | tf_op jit(solution)/shard_map/pallas_call | solution.py:38
  91.9 1.1 %collective-permute-done.8 = bf16[16,2048]{1,0:T(8,128)(2,1)S(1)} collective-permute-done((bf16[16,2048]{1,0:T(8,128)(2,1)S(1)}, bf16[16,2048]{1,0:T(8,128)(2,1)S(1)}, u32[]{:S(2)}, u32[]{:S(2)}) %collective-permute-start.8) | collective-permute-done | bytes 65568 | tf_op jit(solution)/shard_map/ppermute | solution.py:381
  (44 shorter events, 12.2 us)
Async XLA Ops:
  0.6 35.4 %copy-start.7 = (bf16[512,512]{1,0:T(8,128)(2,1)S(1)}, bf16[512,512]{1,0:T(8,128)(2,1)}, u32[]{:S(2)}) copy-start(bf16[512,512]{1,0:T(8,128)(2,1)} %refs_8_.1) | copy-start | bytes 1572868
  0.6 35.4 %copy-start = (bf16[1,512,512]{2,1,0:T(8,128)(2,1)S(1)}, bf16[1,512,512]{2,1,0:T(8,128)(2,1)}, u32[]{:S(2)}) copy-start(bf16[1,512,512]{2,1,0:T(8,128)(2,1)} %param.17) | copy-start | bytes 1572868
  0.7 1.1 %copy-start.13 = (bf16[512,512]{1,0:T(8,128)(2,1)S(1)}, bf16[512,512]{1,0:T(8,128)(2,1)}, u32[]{:S(2)}) copy-start(bf16[512,512]{1,0:T(8,128)(2,1)} %refs_1_.2) | copy-start | bytes 1572868
  4.0 23.7 %all-to-all-start = ((bf16[32,16,512]{2,1,0:T(8,128)(2,1)}), bf16[32,16,512]{2,1,0:T(8,128)(2,1)S(1)}, u32[]{:S(2)}, u32[]{:S(2)}) async-start(bf16[32,16,512]{2,1,0:T(8,128)(2,1)} %bitcast.4), calls=%async_computation | async-start | bytes 1048576 | tf_op jit(solution)/shard_map/all_to_all | solution.py:406
  28.3 7.7 %collective-permute-start = (bf16[512,512]{1,0:T(8,128)(2,1)S(1)}, bf16[512,512]{1,0:T(8,128)(2,1)S(1)}, u32[]{:S(2)}, u32[]{:S(2)}) collective-permute-start(bf16[512,512]{1,0:T(8,128)(2,1)S(1)} %get-tuple-element.43.refs_0_), channel_id=1, source_target_pairs={{0,1},{1,2},{2,3},{3,4},{4,5},{5,6},{6,7},{8,9},{9,10},{10,11},{11... | collective-permute-start | bytes 1572872 | tf_op jit(solution)/shard_map/ppermute | solution.py:357
  31.0 1.0 %copy-start.1 = (bf16[512,512]{1,0:T(8,128)(2,1)S(1)}, bf16[512,512]{1,0:T(8,128)(2,1)}, u32[]{:S(2)}) copy-start(bf16[512,512]{1,0:T(8,128)(2,1)} %refs_5_.1) | copy-start | bytes 1572868
  32.1 1.0 %copy-start.3 = (bf16[512,512]{1,0:T(8,128)(2,1)S(1)}, bf16[512,512]{1,0:T(8,128)(2,1)}, u32[]{:S(2)}) copy-start(bf16[512,512]{1,0:T(8,128)(2,1)} %refs_6_.1) | copy-start | bytes 1572868
  33.1 1.0 %copy-start.5 = (bf16[512,512]{1,0:T(8,128)(2,1)S(1)}, bf16[512,512]{1,0:T(8,128)(2,1)}, u32[]{:S(2)}) copy-start(bf16[512,512]{1,0:T(8,128)(2,1)} %refs_7_.1) | copy-start | bytes 1572868
  36.0 12.9 %copy-start.2 = (bf16[512,512]{1,0:T(8,128)(2,1)S(1)}, bf16[512,512]{1,0:T(8,128)(2,1)}, u32[]{:S(2)}) copy-start(bf16[512,512]{1,0:T(8,128)(2,1)} %refs_5_.1) | copy-start | bytes 1572868
  36.1 12.9 %copy-start.4 = (bf16[512,512]{1,0:T(8,128)(2,1)S(1)}, bf16[512,512]{1,0:T(8,128)(2,1)}, u32[]{:S(2)}) copy-start(bf16[512,512]{1,0:T(8,128)(2,1)} %refs_6_.1) | copy-start | bytes 1572868
  36.1 12.9 %copy-start.6 = (bf16[512,512]{1,0:T(8,128)(2,1)S(1)}, bf16[512,512]{1,0:T(8,128)(2,1)}, u32[]{:S(2)}) copy-start(bf16[512,512]{1,0:T(8,128)(2,1)} %refs_7_.1) | copy-start | bytes 1572868
  36.1 12.9 %copy-start.8 = (bf16[512,512]{1,0:T(8,128)(2,1)S(1)}, bf16[512,512]{1,0:T(8,128)(2,1)}, u32[]{:S(2)}) copy-start(bf16[512,512]{1,0:T(8,128)(2,1)} %refs_8_.1) | copy-start | bytes 1572868
  47.6 9.0 %collective-permute-start.1 = (bf16[512,512]{1,0:T(8,128)(2,1)S(1)}, bf16[512,512]{1,0:T(8,128)(2,1)S(1)}, u32[]{:S(2)}, u32[]{:S(2)}) collective-permute-start(bf16[512,512]{1,0:T(8,128)(2,1)S(1)} %get-tuple-element.66), channel_id=1, source_target_pairs={{1,0},{2,1},{3,2},{4,3},{5,4},{6,5},{7,6},{9,8},{10,9},{11,10},{12... | collective-permute-start | bytes 1572872 | tf_op jit(solution)/shard_map/ppermute | solution.py:357
  56.6 31.4 %copy-start.15 = (s32[512]{0:T(512)S(1)}, s32[512]{0:T(512)}, u32[]{:S(2)}) copy-start(s32[512]{0:T(512)} %param.10) | copy-start | bytes 6148
  57.4 6.7 %collective-permute-start.2 = (bf16[256,2048]{1,0:T(8,128)(2,1)}, bf16[256,2048]{1,0:T(8,128)(2,1)}, u32[]{:S(2)}, u32[]{:S(2)}) collective-permute-start(bf16[256,2048]{1,0:T(8,128)(2,1)} %get-tuple-element.72), channel_id=1, source_target_pairs={{0,1},{1,0},{2,3},{3,2},{4,5},{5,4},{6,7},{7,6},{8,9},{9,8},{10,11... | collective-permute-start | bytes 3145736 | tf_op jit(solution)/shard_map/ppermute | solution.py:475
  60.0 1.0 %copy-start.10 = (bf16[512,512]{1,0:T(8,128)(2,1)S(1)}, bf16[512,512]{1,0:T(8,128)(2,1)}, u32[]{:S(2)}) copy-start(bf16[512,512]{1,0:T(8,128)(2,1)} %copy-done.9) | copy-start | bytes 1572868
  61.0 1.0 %copy-start.12 = (bf16[512,512]{1,0:T(8,128)(2,1)S(1)}, bf16[512,512]{1,0:T(8,128)(2,1)}, u32[]{:S(2)}) copy-start(bf16[512,512]{1,0:T(8,128)(2,1)} %copy-done.11) | copy-start | bytes 1572868
  65.8 9.2 %collective-permute-start.3 = (bf16[64,2048]{1,0:T(8,128)(2,1)S(1)}, bf16[64,2048]{1,0:T(8,128)(2,1)S(1)}, u32[]{:S(2)}, u32[]{:S(2)}) collective-permute-start(bf16[64,2048]{1,0:T(8,128)(2,1)S(1)} %get-tuple-element.74), channel_id=1, source_target_pairs={{0,8},{8,0},{16,24},{24,16},{1,9},{9,1},{17,25},{25,17},{2,10},{10... | collective-permute-start | bytes 786440 | tf_op jit(solution)/shard_map/ppermute | solution.py:381
  66.7 15.9 %collective-permute-start.4 = (bf16[64,2048]{1,0:T(8,128)(2,1)S(1)}, bf16[64,2048]{1,0:T(8,128)(2,1)S(1)}, u32[]{:S(2)}, u32[]{:S(2)}) collective-permute-start(bf16[64,2048]{1,0:T(8,128)(2,1)S(1)} %get-tuple-element.75), channel_id=1, source_target_pairs={{0,16},{8,24},{16,0},{24,8},{1,17},{9,25},{17,1},{25,9},{2,18},{10... | collective-permute-start | bytes 786440 | tf_op jit(solution)/shard_map/ppermute | solution.py:381
  67.2 16.1 %collective-permute-start.5 = (bf16[64,2048]{1,0:T(8,128)(2,1)S(1)}, bf16[64,2048]{1,0:T(8,128)(2,1)S(1)}, u32[]{:S(2)}, u32[]{:S(2)}) collective-permute-start(bf16[64,2048]{1,0:T(8,128)(2,1)S(1)} %get-tuple-element.76), channel_id=1, source_target_pairs={{0,24},{8,16},{16,8},{24,0},{1,25},{9,17},{17,9},{25,1},{2,26},{10... | collective-permute-start | bytes 786440 | tf_op jit(solution)/shard_map/ppermute | solution.py:381
  69.3 20.6 %all-to-all-start.1 = ((bf16[32,16,512]{2,1,0:T(8,128)(2,1)}), bf16[32,16,512]{2,1,0:T(8,128)(2,1)S(1)}, u32[]{:S(2)}, u32[]{:S(2)}) async-start(bf16[32,16,512]{2,1,0:T(8,128)(2,1)} %bitcast.8), calls=%async_computation.1 | async-start | bytes 1048576 | tf_op jit(solution)/shard_map/all_to_all | solution.py:406
  83.5 7.7 %collective-permute-start.6 = (bf16[16,2048]{1,0:T(8,128)(2,1)S(1)}, bf16[16,2048]{1,0:T(8,128)(2,1)S(1)}, u32[]{:S(2)}, u32[]{:S(2)}) collective-permute-start(bf16[16,2048]{1,0:T(8,128)(2,1)S(1)} %get-tuple-element.78), channel_id=1, source_target_pairs={{0,2},{1,3},{2,0},{3,1},{4,6},{5,7},{6,4},{7,5},{8,10},{9,11},{10,... | collective-permute-start | bytes 196616 | tf_op jit(solution)/shard_map/ppermute | solution.py:381
  85.2 6.6 %collective-permute-start.7 = (bf16[16,2048]{1,0:T(8,128)(2,1)S(1)}, bf16[16,2048]{1,0:T(8,128)(2,1)S(1)}, u32[]{:S(2)}, u32[]{:S(2)}) collective-permute-start(bf16[16,2048]{1,0:T(8,128)(2,1)S(1)} %get-tuple-element.79), channel_id=1, source_target_pairs={{0,4},{1,5},{2,6},{3,7},{4,0},{5,1},{6,2},{7,3},{8,12},{9,13},{10,... | collective-permute-start | bytes 196616 | tf_op jit(solution)/shard_map/ppermute | solution.py:381
  86.8 6.2 %collective-permute-start.8 = (bf16[16,2048]{1,0:T(8,128)(2,1)S(1)}, bf16[16,2048]{1,0:T(8,128)(2,1)S(1)}, u32[]{:S(2)}, u32[]{:S(2)}) collective-permute-start(bf16[16,2048]{1,0:T(8,128)(2,1)S(1)} %get-tuple-element.80), channel_id=1, source_target_pairs={{0,6},{1,7},{2,4},{3,5},{4,2},{5,3},{6,0},{7,1},{8,14},{9,15},{10,... | collective-permute-start | bytes 196616 | tf_op jit(solution)/shard_map/ppermute | solution.py:381
  (3 other events, 2.3 us)

commit v10 on v9

--- a/solution.py
+++ b/solution.py
@@ -481,7 +481,7 @@
         scratch=[whole, whole, pltpu.SemaphoreType.DMA((2,))],
         flops=cube,
     )
-    pieces = spread([keep, got], lax.axis_index("stream"), lax.axis_size("stream"), [returning])
+    pieces = spread([keep, got], lax.axis_index("stream"), lax.axis_size("stream"))
     pieces = swapped(pieces, "stream", 1)
     late_rows, returning = lax.optimization_barrier((row_frame.reshape(1, row_count), returning))
     arrived = exchanged(returning)

time: 94.3 us -> 97.3 us (1.032)
  waiting for transfers between devices: 27.5 us -> 29.7 us
    ppermute x6, waiting for transfers between devices: 12.2 us -> 5.52 us  [swapped(): lax.ppermute(piece, axis, [(i, i ^ k * step) for i in range(count)])]
    all_to_all x2, waiting for transfers between devices: 15.2 us -> 21.6 us  [exchanged(): lax.all_to_all(shard.reshape(devices, slots, width), AXES, split_axis=0,...]
    ppermute x1, waiting for transfers between devices: 0.01 us -> 2.63 us  [shards(): got = lax.ppermute(send, 'seq', [(i, i ^ 1) for i in range(seqs)])]
  transfers between devices with their start and end apart: 11 -> 11, of which waited for: 7 -> 5; matrix products, arithmetic and copies ran while one was open for 1% -> 1% of each run, Pallas kernels for 15% -> 15%
where the time goes in v10:
time: 97.3 us; the launch traced here: 96.5 us
  Pallas kernels  30.4 us (31%)
  waiting for transfers between devices  29.7 us (31%)
  starting transfers between devices  24.6 us (25%)
  local copies, waits for them, and re-layouts  9.46 us (10%)
  between operations  1.56 us (2%)
    pallas_call x11, Pallas kernels, vmem_call(): pl.pallas_call(body, out_shape=tuple(outs), in_specs=[pl.BlockSpec(memory...  30.4 us
    all_to_all x2, waiting for transfers between devices, exchanged(): lax.all_to_all(shard.reshape(devices, slots, width), AXES, split_axis=0,...  21.6 us
    all_to_all x2, starting transfers between devices, exchanged(): lax.all_to_all(shard.reshape(devices, slots, width), AXES, split_axis=0,...  10.9 us
    unnamed x32, local copies, waits for them, and re-layouts  8.64 us
    ppermute x6, starting transfers between devices, swapped(): lax.ppermute(piece, axis, [(i, i ^ k * step) for i in range(count)])  7.95 us
    ppermute x6, waiting for transfers between devices, swapped(): lax.ppermute(piece, axis, [(i, i ^ k * step) for i in range(count)])  5.52 us
    ppermute x2, starting transfers between devices, passed_along(): return lax.ppermute(shard, 'seq', pairs)  3.24 us
    ppermute x1, waiting for transfers between devices, shards(): got = lax.ppermute(send, 'seq', [(i, i ^ 1) for i in range(seqs)])  2.63 us
  transfers between devices with their start and end apart: 11, of which 5 were waited for; matrix products, arithmetic and copies ran while one was open for 1% of the time, Pallas kernels for 15%

profile of v10, /device:TPU:0, one launch (start us, length us, event | category | flops | bytes accessed | tf_op | source)
XLA Modules:
  0.0 96.5 jit_solution(1430893545380363947)
XLA Ops:
  0.7 1.1 %copy-done.13 = bf16[512,512]{1,0:T(8,128)(2,1)S(1)} copy-done((bf16[512,512]{1,0:T(8,128)(2,1)S(1)}, bf16[512,512]{1,0:T(8,128)(2,1)}, u32[]{:S(2)}) %copy-start.13) | copy-done | bytes 524312
  2.5 1.6 %shard_map.113 = bf16[512,512]{1,0:T(8,128)(2,1)} custom-call(s32[1,512]{1,0:T(1,128)S(1)} %bitcast.28, bf16[512,512]{1,0:T(8,128)(2,1)S(1)} %copy-done.13), custom_call_target="tpu_custom_call" | custom-call | flops 268435456 | bytes 1050624 | tf_op jit(solution)/shard_map/pallas_call | solution.py:38
  4.0 7.3 %all-to-all-start = ((bf16[32,16,512]{2,1,0:T(8,128)(2,1)}), bf16[32,16,512]{2,1,0:T(8,128)(2,1)S(1)}, u32[]{:S(2)}, u32[]{:S(2)}) async-start(bf16[32,16,512]{2,1,0:T(8,128)(2,1)} %bitcast.4), calls=%async_computation | async-start | bytes 1048576 | tf_op jit(solution)/shard_map/all_to_all | solution.py:406
  14.0 13.7 %all-to-all-done = bf16[32,16,512]{2,1,0:T(8,128)(2,1)S(1)} async-done(((bf16[32,16,512]{2,1,0:T(8,128)(2,1)}), bf16[32,16,512]{2,1,0:T(8,128)(2,1)S(1)}, u32[]{:S(2)}, u32[]{:S(2)}) %all-to-all-start) | async-done | bytes 524320 | tf_op jit(solution)/shard_map/all_to_all | solution.py:406
  28.3 1.9 %collective-permute-start = (bf16[512,512]{1,0:T(8,128)(2,1)S(1)}, bf16[512,512]{1,0:T(8,128)(2,1)S(1)}, u32[]{:S(2)}, u32[]{:S(2)}) collective-permute-start(bf16[512,512]{1,0:T(8,128)(2,1)S(1)} %get-tuple-element.43.refs_0_), channel_id=1, source_target_pairs={{0,1},{1,2},{2,3},{3,4},{4,5},{5,6},{6,7},{8,9},{9,10},{10,11},{11... | collective-permute-start | bytes 1572872 | tf_op jit(solution)/shard_map/ppermute | solution.py:357
  31.0 1.0 %copy-done.1 = bf16[512,512]{1,0:T(8,128)(2,1)S(1)} copy-done((bf16[512,512]{1,0:T(8,128)(2,1)S(1)}, bf16[512,512]{1,0:T(8,128)(2,1)}, u32[]{:S(2)}) %copy-start.1) | copy-done | bytes 524312
  32.1 1.0 %copy-done.3 = bf16[512,512]{1,0:T(8,128)(2,1)S(1)} copy-done((bf16[512,512]{1,0:T(8,128)(2,1)S(1)}, bf16[512,512]{1,0:T(8,128)(2,1)}, u32[]{:S(2)}) %copy-start.3) | copy-done | bytes 524312
  34.1 1.9 %shard_map.115 = (bf16[512,512]{1,0:T(8,128)(2,1)S(1)}, bf16[512,512]{1,0:T(8,128)(2,1)S(1)}, bf16[512,512]{1,0:T(8,128)(2,1)S(1)}, bf16[512,512]{1,0:T(8,128)(2...) custom-call(bf16[512,512]{1,0:T(8,128)(2,1)S(1)} %get-tuple-element., ...), custom_call_target="tpu_custom_call" | custom-call | flops 805306368 | bytes 6291456 | tf_op jit(solution)/shard_map/pallas_call | solution.py:38
  36.1 11.5 %shard_map.116 = (bf16[16,640,256]{2,1,0:T(8,128)(2,1)S(1)}, bf16[16,640,256]{2,1,0:T(8,128)(2,1)S(1)}, f32[16,1,256]{2,1,0:T(1,128)S(1)}, bf16[512,512]{1,0:T(8...) custom-call(s32[3]{0:T(128)S(1)} %pad_add_fusion.refs_0_, ...), custom_call_target="tpu_custom_call" | custom-call | flops 3221225472 | bytes 19415052 | tf_op jit(solution)/shard_map/pallas_call | solution.py:38
  47.6 1.3 %collective-permute-start.1 = (bf16[512,512]{1,0:T(8,128)(2,1)S(1)}, bf16[512,512]{1,0:T(8,128)(2,1)S(1)}, u32[]{:S(2)}, u32[]{:S(2)}) collective-permute-start(bf16[512,512]{1,0:T(8,128)(2,1)S(1)} %get-tuple-element.66), channel_id=1, source_target_pairs={{1,0},{2,1},{3,2},{4,3},{5,4},{6,5},{7,6},{9,8},{10,9},{11,10},{12... | collective-permute-start | bytes 1572872 | tf_op jit(solution)/shard_map/ppermute | solution.py:357
  49.0 7.6 %shard_map.117 = (bf16[256,2048]{1,0:T(8,128)(2,1)S(1)}, bf16[256,2048]{1,0:T(8,128)(2,1)}, bf16[512,512]{1,0:T(8,128)(2,1)}, f32[512,512]{1,0:T(8,128)S(1)}) custom-call(s32[3]{0:T(128)S(1)} %pad_add_fusion.refs_0_, bf16[512,512]{1,0:T(8,128)(2,1)S(1)} %get-tuple-element.44.refs_1_, bf16[512,512]{1,0:T(8,128)(2,1)S(1)} %get-tuple-element.51.refs_2_, ...), custom_call_target="tpu_custom_call" | custom-call | flops 4831838208 | bytes 22036492 | tf_op jit(solution)/shard_map/pallas_call | solution.py:38
  57.4 2.6 %collective-permute-start.2 = (bf16[256,2048]{1,0:T(8,128)(2,1)}, bf16[256,2048]{1,0:T(8,128)(2,1)}, u32[]{:S(2)}, u32[]{:S(2)}) collective-permute-start(bf16[256,2048]{1,0:T(8,128)(2,1)} %get-tuple-element.72), channel_id=1, source_target_pairs={{0,1},{1,0},{2,3},{3,2},{4,5},{5,4},{6,7},{7,6},{8,9},{9,8},{10,11... | collective-permute-start | bytes 3145736 | tf_op jit(solution)/shard_map/ppermute | solution.py:475
  60.0 2.6 %collective-permute-done.2 = bf16[256,2048]{1,0:T(8,128)(2,1)} collective-permute-done((bf16[256,2048]{1,0:T(8,128)(2,1)}, bf16[256,2048]{1,0:T(8,128)(2,1)}, u32[]{:S(2)}, u32[]{:S(2)}) %collective-permute-start.2) | collective-permute-done | bytes 1048608 | tf_op jit(solution)/shard_map/ppermute | solution.py:475
  62.6 2.3 %shard_map.121 = (bf16[64,2048]{1,0:T(8,128)(2,1)S(1)}, bf16[64,2048]{1,0:T(8,128)(2,1)}, bf16[64,2048]{1,0:T(8,128)(2,1)}, bf16[64,2048]{1,0:T(8,128)(2,1)}) custom-call(s32[1]{0:T(128)} %bitcast.11.refs_0_, bf16[4,64,2048]{2,1,0:T(8,128)(2,1)S(1)} %bitcast.23, bf16[4,64,2048]{2,1,0:T(8,128)(2,1)} %bitcast.13.refs_2_), custom_call_target="tpu_custom_call" | custom-call | bytes 3145732 | tf_op jit(solution)/shard_map/pallas_call | solution.py:38
  66.3 2.1 %collective-permute-start.5 = (bf16[64,2048]{1,0:T(8,128)(2,1)}, bf16[64,2048]{1,0:T(8,128)(2,1)S(1)}, u32[]{:S(2)}, u32[]{:S(2)}) collective-permute-start(bf16[64,2048]{1,0:T(8,128)(2,1)} %get-tuple-element.76), channel_id=1, source_target_pairs={{0,24},{8,16},{16,8},{24,0},{1,25},{9,17},{17,9},{25,1},{2,26},{10... | collective-permute-start | bytes 786440 | tf_op jit(solution)/shard_map/ppermute | solution.py:381
  70.5 2.1 %shard_map.118 = bf16[512,512]{1,0:T(8,128)(2,1)} custom-call(bf16[512,512]{1,0:T(8,128)(2,1)S(1)} %get-tuple-element.52.refs_3_.refs_0_, f32[512,512]{1,0:T(8,128)S(1)} %get-tuple-element.64.refs_1_, bf16[512,512]{1,0:T(8,128)(2,1)S(1)} %copy-done.12, bf16[512,512]{1,0:T(8,128)(2,1)S(1)} %bitcast.20, bf16[512,512]{1,0:T(8,128)(2,1)S(1)} %copy-done.10), custom_call_target="tpu_custom_call" | custom-call | flops 268435456 | bytes 3670016 | tf_op jit(solution)/shard_map/pallas_call | solution.py:38
  72.6 3.6 %all-to-all-start.1 = ((bf16[32,16,512]{2,1,0:T(8,128)(2,1)}), bf16[32,16,512]{2,1,0:T(8,128)(2,1)S(1)}, u32[]{:S(2)}, u32[]{:S(2)}) async-start(bf16[32,16,512]{2,1,0:T(8,128)(2,1)} %bitcast.8), calls=%async_computation.1 | async-start | bytes 1048576 | tf_op jit(solution)/shard_map/all_to_all | solution.py:406
  76.1 3.8 %collective-permute-done.4 = bf16[64,2048]{1,0:T(8,128)(2,1)S(1)} collective-permute-done((bf16[64,2048]{1,0:T(8,128)(2,1)}, bf16[64,2048]{1,0:T(8,128)(2,1)S(1)}, u32[]{:S(2)}, u32[]{:S(2)}) %collective-permute-start.4) | collective-permute-done | bytes 262176 | tf_op jit(solution)/shard_map/ppermute | solution.py:381
  80.1 1.3 %collective-permute-start.6 = (bf16[16,2048]{1,0:T(8,128)(2,1)S(1)}, bf16[16,2048]{1,0:T(8,128)(2,1)S(1)}, u32[]{:S(2)}, u32[]{:S(2)}) collective-permute-start(bf16[16,2048]{1,0:T(8,128)(2,1)S(1)} %get-tuple-element.78), channel_id=1, source_target_pairs={{0,2},{1,3},{2,0},{3,1},{4,6},{5,7},{6,4},{7,5},{8,10},{9,11},{10,... | collective-permute-start | bytes 196616 | tf_op jit(solution)/shard_map/ppermute | solution.py:381
  81.4 1.2 %collective-permute-start.7 = (bf16[16,2048]{1,0:T(8,128)(2,1)S(1)}, bf16[16,2048]{1,0:T(8,128)(2,1)S(1)}, u32[]{:S(2)}, u32[]{:S(2)}) collective-permute-start(bf16[16,2048]{1,0:T(8,128)(2,1)S(1)} %get-tuple-element.79), channel_id=1, source_target_pairs={{0,4},{1,5},{2,6},{3,7},{4,0},{5,1},{6,2},{7,3},{8,12},{9,13},{10,... | collective-permute-start | bytes 196616 | tf_op jit(solution)/shard_map/ppermute | solution.py:381
  82.6 1.9 %collective-permute-start.8 = (bf16[16,2048]{1,0:T(8,128)(2,1)S(1)}, bf16[16,2048]{1,0:T(8,128)(2,1)S(1)}, u32[]{:S(2)}, u32[]{:S(2)}) collective-permute-start(bf16[16,2048]{1,0:T(8,128)(2,1)S(1)} %get-tuple-element.80), channel_id=1, source_target_pairs={{0,6},{1,7},{2,4},{3,5},{4,2},{5,3},{6,0},{7,1},{8,14},{9,15},{10,... | collective-permute-start | bytes 196616 | tf_op jit(solution)/shard_map/ppermute | solution.py:381
  85.0 7.9 %all-to-all-done.1 = bf16[32,16,512]{2,1,0:T(8,128)(2,1)S(1)} async-done(((bf16[32,16,512]{2,1,0:T(8,128)(2,1)}), bf16[32,16,512]{2,1,0:T(8,128)(2,1)S(1)}, u32[]{:S(2)}, u32[]{:S(2)}) %all-to-all-start.1) | async-done | bytes 524320 | tf_op jit(solution)/shard_map/all_to_all | solution.py:406
  92.9 1.2 %shard_map.120 = bf16[512,512]{1,0:T(8,128)(2,1)} custom-call(bf16[512,512]{1,0:T(8,128)(2,1)S(1)} %shard_map.119.refs_0_, bf16[512,512]{1,0:T(8,128)(2,1)S(1)} %bitcast.21), custom_call_target="tpu_custom_call" | custom-call | flops 268435456 | bytes 1572864 | tf_op jit(solution)/shard_map/pallas_call | solution.py:38
  94.1 1.7 %collective-permute-done.7 = bf16[16,2048]{1,0:T(8,128)(2,1)S(1)} collective-permute-done((bf16[16,2048]{1,0:T(8,128)(2,1)S(1)}, bf16[16,2048]{1,0:T(8,128)(2,1)S(1)}, u32[]{:S(2)}, u32[]{:S(2)}) %collective-permute-start.7) | collective-permute-done | bytes 65568 | tf_op jit(solution)/shard_map/ppermute | solution.py:381
  (44 shorter events, 10.7 us)
Async XLA Ops:
  0.6 35.4 %copy-start.7 = (bf16[512,512]{1,0:T(8,128)(2,1)S(1)}, bf16[512,512]{1,0:T(8,128)(2,1)}, u32[]{:S(2)}) copy-start(bf16[512,512]{1,0:T(8,128)(2,1)} %refs_8_.1) | copy-start | bytes 1572868
  0.6 35.4 %copy-start = (bf16[1,512,512]{2,1,0:T(8,128)(2,1)S(1)}, bf16[1,512,512]{2,1,0:T(8,128)(2,1)}, u32[]{:S(2)}) copy-start(bf16[1,512,512]{2,1,0:T(8,128)(2,1)} %param.17) | copy-start | bytes 1572868
  0.7 1.1 %copy-start.13 = (bf16[512,512]{1,0:T(8,128)(2,1)S(1)}, bf16[512,512]{1,0:T(8,128)(2,1)}, u32[]{:S(2)}) copy-start(bf16[512,512]{1,0:T(8,128)(2,1)} %refs_1_.2) | copy-start | bytes 1572868
  4.0 23.7 %all-to-all-start = ((bf16[32,16,512]{2,1,0:T(8,128)(2,1)}), bf16[32,16,512]{2,1,0:T(8,128)(2,1)S(1)}, u32[]{:S(2)}, u32[]{:S(2)}) async-start(bf16[32,16,512]{2,1,0:T(8,128)(2,1)} %bitcast.4), calls=%async_computation | async-start | bytes 1048576 | tf_op jit(solution)/shard_map/all_to_all | solution.py:406
  28.3 7.7 %collective-permute-start = (bf16[512,512]{1,0:T(8,128)(2,1)S(1)}, bf16[512,512]{1,0:T(8,128)(2,1)S(1)}, u32[]{:S(2)}, u32[]{:S(2)}) collective-permute-start(bf16[512,512]{1,0:T(8,128)(2,1)S(1)} %get-tuple-element.43.refs_0_), channel_id=1, source_target_pairs={{0,1},{1,2},{2,3},{3,4},{4,5},{5,6},{6,7},{8,9},{9,10},{10,11},{11... | collective-permute-start | bytes 1572872 | tf_op jit(solution)/shard_map/ppermute | solution.py:357
  31.0 1.0 %copy-start.1 = (bf16[512,512]{1,0:T(8,128)(2,1)S(1)}, bf16[512,512]{1,0:T(8,128)(2,1)}, u32[]{:S(2)}) copy-start(bf16[512,512]{1,0:T(8,128)(2,1)} %refs_5_.1) | copy-start | bytes 1572868
  32.1 1.0 %copy-start.3 = (bf16[512,512]{1,0:T(8,128)(2,1)S(1)}, bf16[512,512]{1,0:T(8,128)(2,1)}, u32[]{:S(2)}) copy-start(bf16[512,512]{1,0:T(8,128)(2,1)} %refs_6_.1) | copy-start | bytes 1572868
  33.1 1.0 %copy-start.5 = (bf16[512,512]{1,0:T(8,128)(2,1)S(1)}, bf16[512,512]{1,0:T(8,128)(2,1)}, u32[]{:S(2)}) copy-start(bf16[512,512]{1,0:T(8,128)(2,1)} %refs_7_.1) | copy-start | bytes 1572868
  36.0 12.9 %copy-start.2 = (bf16[512,512]{1,0:T(8,128)(2,1)S(1)}, bf16[512,512]{1,0:T(8,128)(2,1)}, u32[]{:S(2)}) copy-start(bf16[512,512]{1,0:T(8,128)(2,1)} %refs_5_.1) | copy-start | bytes 1572868
  36.1 12.9 %copy-start.4 = (bf16[512,512]{1,0:T(8,128)(2,1)S(1)}, bf16[512,512]{1,0:T(8,128)(2,1)}, u32[]{:S(2)}) copy-start(bf16[512,512]{1,0:T(8,128)(2,1)} %refs_6_.1) | copy-start | bytes 1572868
  36.1 12.9 %copy-start.6 = (bf16[512,512]{1,0:T(8,128)(2,1)S(1)}, bf16[512,512]{1,0:T(8,128)(2,1)}, u32[]{:S(2)}) copy-start(bf16[512,512]{1,0:T(8,128)(2,1)} %refs_7_.1) | copy-start | bytes 1572868
  36.1 12.9 %copy-start.8 = (bf16[512,512]{1,0:T(8,128)(2,1)S(1)}, bf16[512,512]{1,0:T(8,128)(2,1)}, u32[]{:S(2)}) copy-start(bf16[512,512]{1,0:T(8,128)(2,1)} %refs_8_.1) | copy-start | bytes 1572868
  47.6 9.0 %collective-permute-start.1 = (bf16[512,512]{1,0:T(8,128)(2,1)S(1)}, bf16[512,512]{1,0:T(8,128)(2,1)S(1)}, u32[]{:S(2)}, u32[]{:S(2)}) collective-permute-start(bf16[512,512]{1,0:T(8,128)(2,1)S(1)} %get-tuple-element.66), channel_id=1, source_target_pairs={{1,0},{2,1},{3,2},{4,3},{5,4},{6,5},{7,6},{9,8},{10,9},{11,10},{12... | collective-permute-start | bytes 1572872 | tf_op jit(solution)/shard_map/ppermute | solution.py:357
  56.6 28.0 %copy-start.15 = (s32[512]{0:T(512)S(1)}, s32[512]{0:T(512)}, u32[]{:S(2)}) copy-start(s32[512]{0:T(512)} %param.10) | copy-start | bytes 6148
  57.4 5.2 %collective-permute-start.2 = (bf16[256,2048]{1,0:T(8,128)(2,1)}, bf16[256,2048]{1,0:T(8,128)(2,1)}, u32[]{:S(2)}, u32[]{:S(2)}) collective-permute-start(bf16[256,2048]{1,0:T(8,128)(2,1)} %get-tuple-element.72), channel_id=1, source_target_pairs={{0,1},{1,0},{2,3},{3,2},{4,5},{5,4},{6,7},{7,6},{8,9},{9,8},{10,11... | collective-permute-start | bytes 3145736 | tf_op jit(solution)/shard_map/ppermute | solution.py:475
  64.9 11.3 %collective-permute-start.3 = (bf16[64,2048]{1,0:T(8,128)(2,1)}, bf16[64,2048]{1,0:T(8,128)(2,1)S(1)}, u32[]{:S(2)}, u32[]{:S(2)}) collective-permute-start(bf16[64,2048]{1,0:T(8,128)(2,1)} %get-tuple-element.74), channel_id=1, source_target_pairs={{0,8},{8,0},{16,24},{24,16},{1,9},{9,1},{17,25},{25,17},{2,10},{10... | collective-permute-start | bytes 786440 | tf_op jit(solution)/shard_map/ppermute | solution.py:381
  65.8 14.2 %collective-permute-start.4 = (bf16[64,2048]{1,0:T(8,128)(2,1)}, bf16[64,2048]{1,0:T(8,128)(2,1)S(1)}, u32[]{:S(2)}, u32[]{:S(2)}) collective-permute-start(bf16[64,2048]{1,0:T(8,128)(2,1)} %get-tuple-element.75), channel_id=1, source_target_pairs={{0,16},{8,24},{16,0},{24,8},{1,17},{9,25},{17,1},{25,9},{2,18},{10... | collective-permute-start | bytes 786440 | tf_op jit(solution)/shard_map/ppermute | solution.py:381
  66.3 13.7 %collective-permute-start.5 = (bf16[64,2048]{1,0:T(8,128)(2,1)}, bf16[64,2048]{1,0:T(8,128)(2,1)S(1)}, u32[]{:S(2)}, u32[]{:S(2)}) collective-permute-start(bf16[64,2048]{1,0:T(8,128)(2,1)} %get-tuple-element.76), channel_id=1, source_target_pairs={{0,24},{8,16},{16,8},{24,0},{1,25},{9,17},{17,9},{25,1},{2,26},{10... | collective-permute-start | bytes 786440 | tf_op jit(solution)/shard_map/ppermute | solution.py:381
  68.4 1.0 %copy-start.10 = (bf16[512,512]{1,0:T(8,128)(2,1)S(1)}, bf16[512,512]{1,0:T(8,128)(2,1)}, u32[]{:S(2)}) copy-start(bf16[512,512]{1,0:T(8,128)(2,1)} %copy-done.9) | copy-start | bytes 1572868
  69.4 1.0 %copy-start.12 = (bf16[512,512]{1,0:T(8,128)(2,1)S(1)}, bf16[512,512]{1,0:T(8,128)(2,1)}, u32[]{:S(2)}) copy-start(bf16[512,512]{1,0:T(8,128)(2,1)} %copy-done.11) | copy-start | bytes 1572868
  72.6 20.4 %all-to-all-start.1 = ((bf16[32,16,512]{2,1,0:T(8,128)(2,1)}), bf16[32,16,512]{2,1,0:T(8,128)(2,1)S(1)}, u32[]{:S(2)}, u32[]{:S(2)}) async-start(bf16[32,16,512]{2,1,0:T(8,128)(2,1)} %bitcast.8), calls=%async_computation.1 | async-start | bytes 1048576 | tf_op jit(solution)/shard_map/all_to_all | solution.py:406
  80.1 14.0 %collective-permute-start.6 = (bf16[16,2048]{1,0:T(8,128)(2,1)S(1)}, bf16[16,2048]{1,0:T(8,128)(2,1)S(1)}, u32[]{:S(2)}, u32[]{:S(2)}) collective-permute-start(bf16[16,2048]{1,0:T(8,128)(2,1)S(1)} %get-tuple-element.78), channel_id=1, source_target_pairs={{0,2},{1,3},{2,0},{3,1},{4,6},{5,7},{6,4},{7,5},{8,10},{9,11},{10,... | collective-permute-start | bytes 196616 | tf_op jit(solution)/shard_map/ppermute | solution.py:381
  81.4 14.4 %collective-permute-start.7 = (bf16[16,2048]{1,0:T(8,128)(2,1)S(1)}, bf16[16,2048]{1,0:T(8,128)(2,1)S(1)}, u32[]{:S(2)}, u32[]{:S(2)}) collective-permute-start(bf16[16,2048]{1,0:T(8,128)(2,1)S(1)} %get-tuple-element.79), channel_id=1, source_target_pairs={{0,4},{1,5},{2,6},{3,7},{4,0},{5,1},{6,2},{7,3},{8,12},{9,13},{10,... | collective-permute-start | bytes 196616 | tf_op jit(solution)/shard_map/ppermute | solution.py:381
  82.6 13.2 %collective-permute-start.8 = (bf16[16,2048]{1,0:T(8,128)(2,1)S(1)}, bf16[16,2048]{1,0:T(8,128)(2,1)S(1)}, u32[]{:S(2)}, u32[]{:S(2)}) collective-permute-start(bf16[16,2048]{1,0:T(8,128)(2,1)S(1)} %get-tuple-element.80), channel_id=1, source_target_pairs={{0,6},{1,7},{2,4},{3,5},{4,2},{5,3},{6,0},{7,1},{8,14},{9,15},{10,... | collective-permute-start | bytes 196616 | tf_op jit(solution)/shard_map/ppermute | solution.py:381
  (3 other events, 2.3 us)

commit v11 on v9

--- a/solution.py
+++ b/solution.py
@@ -335,15 +335,12 @@
 
 
 def returning_body(
-    frames_ref, slope_ref, extra_ref, cot_hbm, pick_t_hbm, out_ref, cot_ref, pick_t_ref, sems
+    frames_ref, slope_ref, extra_ref, cot_ref, pick_t_ref, out_ref
 ):
-    copies = fetch([cot_hbm, pick_t_hbm], [cot_ref, pick_t_ref], sems)
     _, inverse, normed32 = unit_frames(frames_ref[...])
     slope = slope_ref[...] + extra_ref[...].astype(F32)
     centre = jnp.mean(slope * normed32, axis=1, keepdims=True)
-    copies[0].wait()
     grad = inverse * (slope - normed32 * centre) + cot_ref[...].astype(F32)
-    copies[1].wait()
     out_ref[...] = mm(pick_t_ref[...], grad.astype(BF)).astype(BF)
 
 
@@ -464,7 +461,6 @@
         flops=18 * cube,
         limit=26,
     )
-    send, extra = lax.optimization_barrier((send, extra))
     if not in_kernel:
         sums = jnp.concatenate([keep, send], axis=0).reshape(-1, 2, rows, 4 * width)
         keep = lax.dynamic_index_in_dim(sums, core, 1, keepdims=False).reshape(half.shape)
@@ -477,9 +473,7 @@
         returning_body,
         [square],
         [frames, slope, extra, cot, pick_t],
-        hbm=(3, 4),
-        scratch=[whole, whole, pltpu.SemaphoreType.DMA((2,))],
-        flops=cube,
+        flops=40 * cube,
     )
     pieces = spread([keep, got], lax.axis_index("stream"), lax.axis_size("stream"), [returning])
     pieces = swapped(pieces, "stream", 1)

time: 94.3 us -> 98.7 us (1.047)
  Pallas kernels: 29.7 us -> 32.6 us
    pallas_call x11, Pallas kernels: 29.7 us -> 32.6 us  [vmem_call(): pl.pallas_call(body, out_shape=tuple(outs), in_specs=[pl.BlockSpec(memory...]
    ppermute x6, waiting for transfers between devices: 12.2 us -> 14.2 us  [swapped(): lax.ppermute(piece, axis, [(i, i ^ k * step) for i in range(count)])]
    all_to_all x2, waiting for transfers between devices: 15.2 us -> 13.7 us  [exchanged(): lax.all_to_all(shard.reshape(devices, slots, width), AXES, split_axis=0,...]
    ppermute x1, starting transfers between devices: 2.58 us -> 1.12 us  [shards(): got = lax.ppermute(send, 'seq', [(i, i ^ 1) for i in range(seqs)])]
    all_to_all x2, starting transfers between devices: 10.9 us -> 12.2 us  [exchanged(): lax.all_to_all(shard.reshape(devices, slots, width), AXES, split_axis=0,...]
    unnamed x32 -> x30, local copies, waits for them, and re-layouts: 8.64 us -> 8.97 us
  transfers between devices with their start and end apart: 11 -> 11, of which waited for: 7 -> 5; matrix products, arithmetic and copies ran while one was open for 1% -> 2% of each run, Pallas kernels for 15% -> 15%
where the time goes in v11:
time: 98.7 us; the launch traced here: 97.9 us
  Pallas kernels  32.6 us (33%)
  waiting for transfers between devices  27.9 us (28%)
  starting transfers between devices  25.4 us (26%)
  local copies, waits for them, and re-layouts  9.79 us (10%)
  between operations  1.51 us (2%)
    pallas_call x11, Pallas kernels, vmem_call(): pl.pallas_call(body, out_shape=tuple(outs), in_specs=[pl.BlockSpec(memory...  32.6 us
    ppermute x6, waiting for transfers between devices, swapped(): lax.ppermute(piece, axis, [(i, i ^ k * step) for i in range(count)])  14.2 us
    all_to_all x2, waiting for transfers between devices, exchanged(): lax.all_to_all(shard.reshape(devices, slots, width), AXES, split_axis=0,...  13.7 us
    all_to_all x2, starting transfers between devices, exchanged(): lax.all_to_all(shard.reshape(devices, slots, width), AXES, split_axis=0,...  12.2 us
    unnamed x30, local copies, waits for them, and re-layouts  8.97 us
    ppermute x6, starting transfers between devices, swapped(): lax.ppermute(piece, axis, [(i, i ^ k * step) for i in range(count)])  8.78 us
    ppermute x2, starting transfers between devices, passed_along(): return lax.ppermute(shard, 'seq', pairs)  3.23 us
  transfers between devices with their start and end apart: 11, of which 5 were waited for; matrix products, arithmetic and copies ran while one was open for 2% of the time, Pallas kernels for 15%

profile of v11, /device:TPU:0, one launch (start us, length us, event | category | flops | bytes accessed | tf_op | source)
XLA Modules:
  0.0 97.9 jit_solution(4360943660680500537)
XLA Ops:
  0.7 1.1 %copy-done.8 = bf16[512,512]{1,0:T(8,128)(2,1)S(1)} copy-done((bf16[512,512]{1,0:T(8,128)(2,1)S(1)}, bf16[512,512]{1,0:T(8,128)(2,1)}, u32[]{:S(2)}) %copy-start.8) | copy-done | bytes 524312
  2.5 1.6 %shard_map.113 = bf16[512,512]{1,0:T(8,128)(2,1)} custom-call(s32[1,512]{1,0:T(1,128)S(1)} %bitcast.29, bf16[512,512]{1,0:T(8,128)(2,1)S(1)} %copy-done.8), custom_call_target="tpu_custom_call" | custom-call | flops 268435456 | bytes 1050624 | tf_op jit(solution)/shard_map/pallas_call | solution.py:38
  4.0 7.3 %all-to-all-start = ((bf16[32,16,512]{2,1,0:T(8,128)(2,1)}), bf16[32,16,512]{2,1,0:T(8,128)(2,1)S(1)}, u32[]{:S(2)}, u32[]{:S(2)}) async-start(bf16[32,16,512]{2,1,0:T(8,128)(2,1)} %bitcast.4), calls=%async_computation | async-start | bytes 1048576 | tf_op jit(solution)/shard_map/all_to_all | solution.py:403
  14.0 13.7 %all-to-all-done = bf16[32,16,512]{2,1,0:T(8,128)(2,1)S(1)} async-done(((bf16[32,16,512]{2,1,0:T(8,128)(2,1)}), bf16[32,16,512]{2,1,0:T(8,128)(2,1)S(1)}, u32[]{:S(2)}, u32[]{:S(2)}) %all-to-all-start) | async-done | bytes 524320 | tf_op jit(solution)/shard_map/all_to_all | solution.py:403
  27.7 1.4 %shard_map.114 = (bf16[512,512]{1,0:T(8,128)(2,1)S(1)}, bf16[512,512]{1,0:T(8,128)(2,1)}) custom-call(bf16[512,512]{1,0:T(8,128)(2,1)S(1)} %get-tuple-element.40.refs_0_, bf16[512,512]{1,0:T(8,128)(2,1)S(1)} %bitcast.19), custom_call_target="tpu_custom_call" | custom-call | flops 268435456 | bytes 2097152 | tf_op jit(solution)/shard_map/pallas_call | solution.py:38
  29.1 1.9 %collective-permute-start = (bf16[512,512]{1,0:T(8,128)(2,1)}, bf16[512,512]{1,0:T(8,128)(2,1)S(1)}, u32[]{:S(2)}, u32[]{:S(2)}) collective-permute-start(bf16[512,512]{1,0:T(8,128)(2,1)} %get-tuple-element.41.refs_0_), channel_id=1, source_target_pairs={{0,1},{1,2},{2,3},{3,4},{4,5},{5,6},{6,7},{8,9},{9,10},{10,11},{11... | collective-permute-start | bytes 1572872 | tf_op jit(solution)/shard_map/ppermute | solution.py:354
  31.8 1.0 %copy-done = bf16[512,512]{1,0:T(8,128)(2,1)S(1)} copy-done((bf16[512,512]{1,0:T(8,128)(2,1)S(1)}, bf16[512,512]{1,0:T(8,128)(2,1)}, u32[]{:S(2)}) %copy-start) | copy-done | bytes 524312
  34.9 2.9 %shard_map.115 = (bf16[512,512]{1,0:T(8,128)(2,1)S(1)}, bf16[512,512]{1,0:T(8,128)(2,1)S(1)}, bf16[512,512]{1,0:T(8,128)(2,1)S(1)}, bf16[512,512]{1,0:T(8,128)(2...) custom-call(bf16[512,512]{1,0:T(8,128)(2,1)} %get-tuple-element.41.r, ...), custom_call_target="tpu_custom_call" | custom-call | flops 805306368 | bytes 6291456 | tf_op jit(solution)/shard_map/pallas_call | solution.py:38
  37.9 12.3 %shard_map.116 = (bf16[16,640,256]{2,1,0:T(8,128)(2,1)S(1)}, bf16[16,640,256]{2,1,0:T(8,128)(2,1)S(1)}, f32[16,1,256]{2,1,0:T(1,128)S(1)}, bf16[512,512]{1,0:T(8...) custom-call(s32[3]{0:T(128)S(1)} %pad_add_fusion.refs_0_, ...), custom_call_target="tpu_custom_call" | custom-call | flops 3221225472 | bytes 19415052 | tf_op jit(solution)/shard_map/pallas_call | solution.py:38
  50.2 1.3 %collective-permute-start.1 = (bf16[512,512]{1,0:T(8,128)(2,1)}, bf16[512,512]{1,0:T(8,128)(2,1)}, u32[]{:S(2)}, u32[]{:S(2)}) collective-permute-start(bf16[512,512]{1,0:T(8,128)(2,1)} %get-tuple-element.63), channel_id=1, source_target_pairs={{1,0},{2,1},{3,2},{4,3},{5,4},{6,5},{7,6},{9,8},{10,9},{11,10},{12... | collective-permute-start | bytes 1572872 | tf_op jit(solution)/shard_map/ppermute | solution.py:354
  51.6 7.6 %shard_map.117 = (bf16[256,2048]{1,0:T(8,128)(2,1)S(1)}, bf16[256,2048]{1,0:T(8,128)(2,1)}, bf16[512,512]{1,0:T(8,128)(2,1)}, f32[512,512]{1,0:T(8,128)S(1)}) custom-call(s32[3]{0:T(128)S(1)} %pad_add_fusion.refs_0_, bf16[512,512]{1,0:T(8,128)(2,1)S(1)} %get-tuple-element.42.refs_1_, bf16[512,512]{1,0:T(8,128)(2,1)S(1)} %get-tuple-element.49.refs_2_, ...), custom_call_target="tpu_custom_call" | custom-call | flops 4831838208 | bytes 22036492 | tf_op jit(solution)/shard_map/pallas_call | solution.py:38
  60.1 1.1 %collective-permute-start.2 = (bf16[256,2048]{1,0:T(8,128)(2,1)}, bf16[256,2048]{1,0:T(8,128)(2,1)S(1)}, u32[]{:S(2)}, u32[]{:S(2)}) collective-permute-start(bf16[256,2048]{1,0:T(8,128)(2,1)} %get-tuple-element.68), channel_id=1, source_target_pairs={{0,1},{1,0},{2,3},{3,2},{4,5},{5,4},{6,7},{7,6},{8,9},{9,8},{10,11... | collective-permute-start | bytes 3145736 | tf_op jit(solution)/shard_map/ppermute | solution.py:471
  61.3 1.2 %copy-done.12 = f32[512,512]{1,0:T(8,128)S(1)} copy-done((f32[512,512]{1,0:T(8,128)S(1)}, f32[512,512]{1,0:T(8,128)}, u32[]{:S(2)}) %copy-start.12) | copy-done | bytes 1048600
  62.5 1.0 %copy-done.14 = bf16[512,512]{1,0:T(8,128)(2,1)S(1)} copy-done((bf16[512,512]{1,0:T(8,128)(2,1)S(1)}, bf16[512,512]{1,0:T(8,128)(2,1)}, u32[]{:S(2)}) %copy-start.14) | copy-done | bytes 524312
  63.5 2.6 %shard_map.118.refs_3_ = bf16[512,512]{1,0:T(8,128)(2,1)} custom-call(bf16[512,512]{1,0:T(8,128)(2,1)S(1)} %get-tuple-element.50.refs_3_.refs_0_, f32[512,512]{1,0:T(8,128)S(1)} %copy-done.12, bf16[512,512]{1,0:T(8,128)(2,1)} %collective-permute-done.1.refs_2_, bf16[512,512]{1,0:T(8,128)(2,1)S(1)} %bitcast.24, bf16[512,512]{1,0:T(8,128)(2,1)S(1)} %copy-done.14), custom_call_target="tpu_custom_call" | custom-call | flops 10737418240 | bytes 3670016 | tf_op jit(solution)/shard_map/pallas_call | solution.py:38
  66.2 1.3 %shard_map.121 = (bf16[64,2048]{1,0:T(8,128)(2,1)S(1)}, bf16[64,2048]{1,0:T(8,128)(2,1)S(1)}, bf16[64,2048]{1,0:T(8,128)(2,1)S(1)}, bf16[64,2048]{1,0:T(8,128)(2,1)S(1)}) custom-call(s32[1]{0:T(128)} %bitcast.11.refs_0_, bf16[4,64,2048]{2,1,0:T(8,128)(2,1)S(1)} %bitcast.20, bf16[4,64,2048]{2,1,0:T(8,128)(2,1)S(1)} %bitcast.21, ...), custom_call_target="tpu_custom_call" | custom-call | bytes 3670020 | tf_op jit(solution)/shard_map/pallas_call | solution.py:38
  68.9 2.1 %collective-permute-start.5 = (bf16[64,2048]{1,0:T(8,128)(2,1)S(1)}, bf16[64,2048]{1,0:T(8,128)(2,1)S(1)}, u32[]{:S(2)}, u32[]{:S(2)}) collective-permute-start(bf16[64,2048]{1,0:T(8,128)(2,1)S(1)} %get-tuple-element.72), channel_id=1, source_target_pairs={{0,24},{8,16},{16,8},{24,0},{1,25},{9,17},{17,9},{25,1},{2,26},{10... | collective-permute-start | bytes 786440 | tf_op jit(solution)/shard_map/ppermute | solution.py:378
  71.0 4.9 %all-to-all-start.1 = ((bf16[32,16,512]{2,1,0:T(8,128)(2,1)}), bf16[32,16,512]{2,1,0:T(8,128)(2,1)S(1)}, u32[]{:S(2)}, u32[]{:S(2)}) async-start(bf16[32,16,512]{2,1,0:T(8,128)(2,1)} %bitcast.8), calls=%async_computation.1 | async-start | bytes 1048576 | tf_op jit(solution)/shard_map/all_to_all | solution.py:403
  76.7 7.8 %collective-permute-done.4 = bf16[64,2048]{1,0:T(8,128)(2,1)S(1)} collective-permute-done((bf16[64,2048]{1,0:T(8,128)(2,1)S(1)}, bf16[64,2048]{1,0:T(8,128)(2,1)S(1)}, u32[]{:S(2)}, u32[]{:S(2)}) %collective-permute-start.4) | collective-permute-done | bytes 262176 | tf_op jit(solution)/shard_map/ppermute | solution.py:378
  84.6 2.4 %collective-permute-start.6 = (bf16[16,2048]{1,0:T(8,128)(2,1)S(1)}, bf16[16,2048]{1,0:T(8,128)(2,1)S(1)}, u32[]{:S(2)}, u32[]{:S(2)}) collective-permute-start(bf16[16,2048]{1,0:T(8,128)(2,1)S(1)} %get-tuple-element.74), channel_id=1, source_target_pairs={{0,2},{1,3},{2,0},{3,1},{4,6},{5,7},{6,4},{7,5},{8,10},{9,11},{10,... | collective-permute-start | bytes 196616 | tf_op jit(solution)/shard_map/ppermute | solution.py:378
  87.0 2.8 %collective-permute-start.7 = (bf16[16,2048]{1,0:T(8,128)(2,1)S(1)}, bf16[16,2048]{1,0:T(8,128)(2,1)S(1)}, u32[]{:S(2)}, u32[]{:S(2)}) collective-permute-start(bf16[16,2048]{1,0:T(8,128)(2,1)S(1)} %get-tuple-element.75), channel_id=1, source_target_pairs={{0,4},{1,5},{2,6},{3,7},{4,0},{5,1},{6,2},{7,3},{8,12},{9,13},{10,... | collective-permute-start | bytes 196616 | tf_op jit(solution)/shard_map/ppermute | solution.py:378
  90.3 4.6 %collective-permute-done.7 = bf16[16,2048]{1,0:T(8,128)(2,1)S(1)} collective-permute-done((bf16[16,2048]{1,0:T(8,128)(2,1)S(1)}, bf16[16,2048]{1,0:T(8,128)(2,1)S(1)}, u32[]{:S(2)}, u32[]{:S(2)}) %collective-permute-start.7) | collective-permute-done | bytes 65568 | tf_op jit(solution)/shard_map/ppermute | solution.py:378
  94.9 1.1 %collective-permute-done.8 = bf16[16,2048]{1,0:T(8,128)(2,1)S(1)} collective-permute-done((bf16[16,2048]{1,0:T(8,128)(2,1)S(1)}, bf16[16,2048]{1,0:T(8,128)(2,1)S(1)}, u32[]{:S(2)}, u32[]{:S(2)}) %collective-permute-start.8) | collective-permute-done | bytes 65568 | tf_op jit(solution)/shard_map/ppermute | solution.py:378
  96.7 1.2 %shard_map.120 = bf16[512,512]{1,0:T(8,128)(2,1)} custom-call(bf16[512,512]{1,0:T(8,128)(2,1)S(1)} %shard_map.119.refs_0_, bf16[512,512]{1,0:T(8,128)(2,1)S(1)} %bitcast.18), custom_call_target="tpu_custom_call" | custom-call | flops 268435456 | bytes 1572864 | tf_op jit(solution)/shard_map/pallas_call | solution.py:38
  (42 shorter events, 9.9 us)
Async XLA Ops:
  0.6 37.2 %copy-start.6 = (bf16[512,512]{1,0:T(8,128)(2,1)S(1)}, bf16[512,512]{1,0:T(8,128)(2,1)}, u32[]{:S(2)}) copy-start(bf16[512,512]{1,0:T(8,128)(2,1)} %refs_8_.1) | copy-start | bytes 1572868
  0.6 37.2 %copy-start.7 = (bf16[1,512,512]{2,1,0:T(8,128)(2,1)S(1)}, bf16[1,512,512]{2,1,0:T(8,128)(2,1)}, u32[]{:S(2)}) copy-start(bf16[1,512,512]{2,1,0:T(8,128)(2,1)} %param.17) | copy-start | bytes 1572868
  0.7 1.1 %copy-start.8 = (bf16[512,512]{1,0:T(8,128)(2,1)S(1)}, bf16[512,512]{1,0:T(8,128)(2,1)}, u32[]{:S(2)}) copy-start(bf16[512,512]{1,0:T(8,128)(2,1)} %refs_1_.2) | copy-start | bytes 1572868
  4.0 23.7 %all-to-all-start = ((bf16[32,16,512]{2,1,0:T(8,128)(2,1)}), bf16[32,16,512]{2,1,0:T(8,128)(2,1)S(1)}, u32[]{:S(2)}, u32[]{:S(2)}) async-start(bf16[32,16,512]{2,1,0:T(8,128)(2,1)} %bitcast.4), calls=%async_computation | async-start | bytes 1048576 | tf_op jit(solution)/shard_map/all_to_all | solution.py:403
  29.1 8.7 %collective-permute-start = (bf16[512,512]{1,0:T(8,128)(2,1)}, bf16[512,512]{1,0:T(8,128)(2,1)S(1)}, u32[]{:S(2)}, u32[]{:S(2)}) collective-permute-start(bf16[512,512]{1,0:T(8,128)(2,1)} %get-tuple-element.41.refs_0_), channel_id=1, source_target_pairs={{0,1},{1,2},{2,3},{3,4},{4,5},{5,6},{6,7},{8,9},{9,10},{10,11},{11... | collective-permute-start | bytes 1572872 | tf_op jit(solution)/shard_map/ppermute | solution.py:354
  31.8 1.0 %copy-start = (bf16[512,512]{1,0:T(8,128)(2,1)S(1)}, bf16[512,512]{1,0:T(8,128)(2,1)}, u32[]{:S(2)}) copy-start(bf16[512,512]{1,0:T(8,128)(2,1)} %refs_5_.1) | copy-start | bytes 1572868
  32.8 1.0 %copy-start.2 = (bf16[512,512]{1,0:T(8,128)(2,1)S(1)}, bf16[512,512]{1,0:T(8,128)(2,1)}, u32[]{:S(2)}) copy-start(bf16[512,512]{1,0:T(8,128)(2,1)} %refs_6_.1) | copy-start | bytes 1572868
  33.9 1.0 %copy-start.4 = (bf16[512,512]{1,0:T(8,128)(2,1)S(1)}, bf16[512,512]{1,0:T(8,128)(2,1)}, u32[]{:S(2)}) copy-start(bf16[512,512]{1,0:T(8,128)(2,1)} %refs_7_.1) | copy-start | bytes 1572868
  37.9 13.7 %copy-start.1 = (bf16[512,512]{1,0:T(8,128)(2,1)S(1)}, bf16[512,512]{1,0:T(8,128)(2,1)}, u32[]{:S(2)}) copy-start(bf16[512,512]{1,0:T(8,128)(2,1)} %refs_5_.1) | copy-start | bytes 1572868
  37.9 13.7 %copy-start.3 = (bf16[512,512]{1,0:T(8,128)(2,1)S(1)}, bf16[512,512]{1,0:T(8,128)(2,1)}, u32[]{:S(2)}) copy-start(bf16[512,512]{1,0:T(8,128)(2,1)} %refs_6_.1) | copy-start | bytes 1572868
  37.9 13.7 %copy-start.5 = (bf16[512,512]{1,0:T(8,128)(2,1)S(1)}, bf16[512,512]{1,0:T(8,128)(2,1)}, u32[]{:S(2)}) copy-start(bf16[512,512]{1,0:T(8,128)(2,1)} %refs_7_.1) | copy-start | bytes 1572868
  50.2 11.0 %collective-permute-start.1 = (bf16[512,512]{1,0:T(8,128)(2,1)}, bf16[512,512]{1,0:T(8,128)(2,1)}, u32[]{:S(2)}, u32[]{:S(2)}) collective-permute-start(bf16[512,512]{1,0:T(8,128)(2,1)} %get-tuple-element.63), channel_id=1, source_target_pairs={{1,0},{2,1},{3,2},{4,3},{5,4},{6,5},{7,6},{9,8},{10,9},{11,10},{12... | collective-permute-start | bytes 1572872 | tf_op jit(solution)/shard_map/ppermute | solution.py:354
  59.2 1.0 copy-start.11
  60.1 6.0 %collective-permute-start.2 = (bf16[256,2048]{1,0:T(8,128)(2,1)}, bf16[256,2048]{1,0:T(8,128)(2,1)S(1)}, u32[]{:S(2)}, u32[]{:S(2)}) collective-permute-start(bf16[256,2048]{1,0:T(8,128)(2,1)} %get-tuple-element.68), channel_id=1, source_target_pairs={{0,1},{1,0},{2,3},{3,2},{4,5},{5,4},{6,7},{7,6},{8,9},{9,8},{10,11... | collective-permute-start | bytes 3145736 | tf_op jit(solution)/shard_map/ppermute | solution.py:471
  61.3 1.2 %copy-start.12 = (f32[512,512]{1,0:T(8,128)S(1)}, f32[512,512]{1,0:T(8,128)}, u32[]{:S(2)}) copy-start(f32[512,512]{1,0:T(8,128)} %copy-done.11) | copy-start | bytes 3145732
  62.5 1.0 %copy-start.14 = (bf16[512,512]{1,0:T(8,128)(2,1)S(1)}, bf16[512,512]{1,0:T(8,128)(2,1)}, u32[]{:S(2)}) copy-start(bf16[512,512]{1,0:T(8,128)(2,1)} %copy-done.13) | copy-start | bytes 1572868
  63.5 26.3 %copy-start.10 = (s32[512]{0:T(512)S(1)}, s32[512]{0:T(512)}, u32[]{:S(2)}) copy-start(s32[512]{0:T(512)} %param.10) | copy-start | bytes 6148
  67.5 9.2 %collective-permute-start.3 = (bf16[64,2048]{1,0:T(8,128)(2,1)S(1)}, bf16[64,2048]{1,0:T(8,128)(2,1)S(1)}, u32[]{:S(2)}, u32[]{:S(2)}) collective-permute-start(bf16[64,2048]{1,0:T(8,128)(2,1)S(1)} %get-tuple-element.70), channel_id=1, source_target_pairs={{0,8},{8,0},{16,24},{24,16},{1,9},{9,1},{17,25},{25,17},{2,10},{10... | collective-permute-start | bytes 786440 | tf_op jit(solution)/shard_map/ppermute | solution.py:378
  68.4 16.1 %collective-permute-start.4 = (bf16[64,2048]{1,0:T(8,128)(2,1)S(1)}, bf16[64,2048]{1,0:T(8,128)(2,1)S(1)}, u32[]{:S(2)}, u32[]{:S(2)}) collective-permute-start(bf16[64,2048]{1,0:T(8,128)(2,1)S(1)} %get-tuple-element.71), channel_id=1, source_target_pairs={{0,16},{8,24},{16,0},{24,8},{1,17},{9,25},{17,1},{25,9},{2,18},{10... | collective-permute-start | bytes 786440 | tf_op jit(solution)/shard_map/ppermute | solution.py:378
  68.9 15.6 %collective-permute-start.5 = (bf16[64,2048]{1,0:T(8,128)(2,1)S(1)}, bf16[64,2048]{1,0:T(8,128)(2,1)S(1)}, u32[]{:S(2)}, u32[]{:S(2)}) collective-permute-start(bf16[64,2048]{1,0:T(8,128)(2,1)S(1)} %get-tuple-element.72), channel_id=1, source_target_pairs={{0,24},{8,16},{16,8},{24,0},{1,25},{9,17},{17,9},{25,1},{2,26},{10... | collective-permute-start | bytes 786440 | tf_op jit(solution)/shard_map/ppermute | solution.py:378
  71.0 25.7 %all-to-all-start.1 = ((bf16[32,16,512]{2,1,0:T(8,128)(2,1)}), bf16[32,16,512]{2,1,0:T(8,128)(2,1)S(1)}, u32[]{:S(2)}, u32[]{:S(2)}) async-start(bf16[32,16,512]{2,1,0:T(8,128)(2,1)} %bitcast.8), calls=%async_computation.1 | async-start | bytes 1048576 | tf_op jit(solution)/shard_map/all_to_all | solution.py:403
  84.6 5.7 %collective-permute-start.6 = (bf16[16,2048]{1,0:T(8,128)(2,1)S(1)}, bf16[16,2048]{1,0:T(8,128)(2,1)S(1)}, u32[]{:S(2)}, u32[]{:S(2)}) collective-permute-start(bf16[16,2048]{1,0:T(8,128)(2,1)S(1)} %get-tuple-element.74), channel_id=1, source_target_pairs={{0,2},{1,3},{2,0},{3,1},{4,6},{5,7},{6,4},{7,5},{8,10},{9,11},{10,... | collective-permute-start | bytes 196616 | tf_op jit(solution)/shard_map/ppermute | solution.py:378
  87.0 7.9 %collective-permute-start.7 = (bf16[16,2048]{1,0:T(8,128)(2,1)S(1)}, bf16[16,2048]{1,0:T(8,128)(2,1)S(1)}, u32[]{:S(2)}, u32[]{:S(2)}) collective-permute-start(bf16[16,2048]{1,0:T(8,128)(2,1)S(1)} %get-tuple-element.75), channel_id=1, source_target_pairs={{0,4},{1,5},{2,6},{3,7},{4,0},{5,1},{6,2},{7,3},{8,12},{9,13},{10,... | collective-permute-start | bytes 196616 | tf_op jit(solution)/shard_map/ppermute | solution.py:378
  89.8 6.2 %collective-permute-start.8 = (bf16[16,2048]{1,0:T(8,128)(2,1)S(1)}, bf16[16,2048]{1,0:T(8,128)(2,1)S(1)}, u32[]{:S(2)}, u32[]{:S(2)}) collective-permute-start(bf16[16,2048]{1,0:T(8,128)(2,1)S(1)} %get-tuple-element.76), channel_id=1, source_target_pairs={{0,6},{1,7},{2,4},{3,5},{4,2},{5,3},{6,0},{7,1},{8,14},{9,15},{10,... | collective-permute-start | bytes 196616 | tf_op jit(solution)/shard_map/ppermute | solution.py:378
  (2 other events, 1.5 us)

commit v12 on v11

--- a/solution.py
+++ b/solution.py
@@ -461,6 +461,7 @@
         flops=18 * cube,
         limit=26,
     )
+    send, extra = lax.optimization_barrier((send, extra))
     if not in_kernel:
         sums = jnp.concatenate([keep, send], axis=0).reshape(-1, 2, rows, 4 * width)
         keep = lax.dynamic_index_in_dim(sums, core, 1, keepdims=False).reshape(half.shape)
@@ -473,7 +474,7 @@
         returning_body,
         [square],
         [frames, slope, extra, cot, pick_t],
-        flops=40 * cube,
+        flops=cube,
     )
     pieces = spread([keep, got], lax.axis_index("stream"), lax.axis_size("stream"), [returning])
     pieces = swapped(pieces, "stream", 1)

time: 98.7 us -> 93.8 us (0.950)
  Pallas kernels: 32.6 us -> 29.2 us
    pallas_call x11, Pallas kernels: 32.6 us -> 29.2 us  [vmem_call(): pl.pallas_call(body, out_shape=tuple(outs), in_specs=[pl.BlockSpec(memory...]
    ppermute x6, waiting for transfers between devices: 14.2 us -> 12.2 us  [swapped(): lax.ppermute(piece, axis, [(i, i ^ k * step) for i in range(count)])]
    all_to_all x2, waiting for transfers between devices: 13.7 us -> 15.2 us  [exchanged(): lax.all_to_all(shard.reshape(devices, slots, width), AXES, split_axis=0,...]
    ppermute x1, starting transfers between devices: 1.12 us -> 2.58 us  [shards(): got = lax.ppermute(send, 'seq', [(i, i ^ 1) for i in range(seqs)])]
    all_to_all x2, starting transfers between devices: 12.2 us -> 10.9 us  [exchanged(): lax.all_to_all(shard.reshape(devices, slots, width), AXES, split_axis=0,...]
    unnamed x30 -> x32, local copies, waits for them, and re-layouts: 8.97 us -> 8.64 us
  transfers between devices with their start and end apart: 11 -> 11, of which waited for: 5 -> 7; matrix products, arithmetic and copies ran while one was open for 2% -> 1% of each run, Pallas kernels for 15% -> 15%
where the time goes in v12:
time: 93.8 us; the launch traced here: 93.1 us
  Pallas kernels  29.2 us (31%)
  waiting for transfers between devices  27.5 us (29%)
  starting transfers between devices  24.7 us (26%)
  local copies, waits for them, and re-layouts  9.46 us (10%)
  between operations  1.54 us (2%)
    pallas_call x11, Pallas kernels, vmem_call(): pl.pallas_call(body, out_shape=tuple(outs), in_specs=[pl.BlockSpec(memory...  29.2 us
    all_to_all x2, waiting for transfers between devices, exchanged(): lax.all_to_all(shard.reshape(devices, slots, width), AXES, split_axis=0,...  15.2 us
    ppermute x6, waiting for transfers between devices, swapped(): lax.ppermute(piece, axis, [(i, i ^ k * step) for i in range(count)])  12.2 us
    all_to_all x2, starting transfers between devices, exchanged(): lax.all_to_all(shard.reshape(devices, slots, width), AXES, split_axis=0,...  10.9 us
    unnamed x32, local copies, waits for them, and re-layouts  8.64 us
    ppermute x6, starting transfers between devices, swapped(): lax.ppermute(piece, axis, [(i, i ^ k * step) for i in range(count)])  8.01 us
    ppermute x2, starting transfers between devices, passed_along(): return lax.ppermute(shard, 'seq', pairs)  3.24 us
    ppermute x1, starting transfers between devices, shards(): got = lax.ppermute(send, 'seq', [(i, i ^ 1) for i in range(seqs)])  2.58 us
  transfers between devices with their start and end apart: 11, of which 7 were waited for; matrix products, arithmetic and copies ran while one was open for 1% of the time, Pallas kernels for 15%

profile of v12, /device:TPU:0, one launch (start us, length us, event | category | flops | bytes accessed | tf_op | source)
XLA Modules:
  0.0 93.1 jit_solution(4510777526772349495)
XLA Ops:
  0.7 1.1 %copy-done.13 = bf16[512,512]{1,0:T(8,128)(2,1)S(1)} copy-done((bf16[512,512]{1,0:T(8,128)(2,1)S(1)}, bf16[512,512]{1,0:T(8,128)(2,1)}, u32[]{:S(2)}) %copy-start.13) | copy-done | bytes 524312
  2.5 1.6 %shard_map.113 = bf16[512,512]{1,0:T(8,128)(2,1)} custom-call(s32[1,512]{1,0:T(1,128)S(1)} %bitcast.28, bf16[512,512]{1,0:T(8,128)(2,1)S(1)} %copy-done.13), custom_call_target="tpu_custom_call" | custom-call | flops 268435456 | bytes 1050624 | tf_op jit(solution)/shard_map/pallas_call | solution.py:38
  4.0 7.3 %all-to-all-start = ((bf16[32,16,512]{2,1,0:T(8,128)(2,1)}), bf16[32,16,512]{2,1,0:T(8,128)(2,1)S(1)}, u32[]{:S(2)}, u32[]{:S(2)}) async-start(bf16[32,16,512]{2,1,0:T(8,128)(2,1)} %bitcast.4), calls=%async_computation | async-start | bytes 1048576 | tf_op jit(solution)/shard_map/all_to_all | solution.py:403
  14.0 13.7 %all-to-all-done = bf16[32,16,512]{2,1,0:T(8,128)(2,1)S(1)} async-done(((bf16[32,16,512]{2,1,0:T(8,128)(2,1)}), bf16[32,16,512]{2,1,0:T(8,128)(2,1)S(1)}, u32[]{:S(2)}, u32[]{:S(2)}) %all-to-all-start) | async-done | bytes 524320 | tf_op jit(solution)/shard_map/all_to_all | solution.py:403
  28.3 1.9 %collective-permute-start = (bf16[512,512]{1,0:T(8,128)(2,1)S(1)}, bf16[512,512]{1,0:T(8,128)(2,1)S(1)}, u32[]{:S(2)}, u32[]{:S(2)}) collective-permute-start(bf16[512,512]{1,0:T(8,128)(2,1)S(1)} %get-tuple-element.43.refs_0_), channel_id=1, source_target_pairs={{0,1},{1,2},{2,3},{3,4},{4,5},{5,6},{6,7},{8,9},{9,10},{10,11},{11... | collective-permute-start | bytes 1572872 | tf_op jit(solution)/shard_map/ppermute | solution.py:354
  31.0 1.0 %copy-done.1 = bf16[512,512]{1,0:T(8,128)(2,1)S(1)} copy-done((bf16[512,512]{1,0:T(8,128)(2,1)S(1)}, bf16[512,512]{1,0:T(8,128)(2,1)}, u32[]{:S(2)}) %copy-start.1) | copy-done | bytes 524312
  32.1 1.0 %copy-done.3 = bf16[512,512]{1,0:T(8,128)(2,1)S(1)} copy-done((bf16[512,512]{1,0:T(8,128)(2,1)S(1)}, bf16[512,512]{1,0:T(8,128)(2,1)}, u32[]{:S(2)}) %copy-start.3) | copy-done | bytes 524312
  34.1 1.9 %shard_map.115 = (bf16[512,512]{1,0:T(8,128)(2,1)S(1)}, bf16[512,512]{1,0:T(8,128)(2,1)S(1)}, bf16[512,512]{1,0:T(8,128)(2,1)S(1)}, bf16[512,512]{1,0:T(8,128)(2...) custom-call(bf16[512,512]{1,0:T(8,128)(2,1)S(1)} %get-tuple-element., ...), custom_call_target="tpu_custom_call" | custom-call | flops 805306368 | bytes 6291456 | tf_op jit(solution)/shard_map/pallas_call | solution.py:38
  36.1 11.5 %shard_map.116 = (bf16[16,640,256]{2,1,0:T(8,128)(2,1)S(1)}, bf16[16,640,256]{2,1,0:T(8,128)(2,1)S(1)}, f32[16,1,256]{2,1,0:T(1,128)S(1)}, bf16[512,512]{1,0:T(8...) custom-call(s32[3]{0:T(128)S(1)} %pad_add_fusion.refs_0_, ...), custom_call_target="tpu_custom_call" | custom-call | flops 3221225472 | bytes 19415052 | tf_op jit(solution)/shard_map/pallas_call | solution.py:38
  47.6 1.3 %collective-permute-start.1 = (bf16[512,512]{1,0:T(8,128)(2,1)S(1)}, bf16[512,512]{1,0:T(8,128)(2,1)S(1)}, u32[]{:S(2)}, u32[]{:S(2)}) collective-permute-start(bf16[512,512]{1,0:T(8,128)(2,1)S(1)} %get-tuple-element.66), channel_id=1, source_target_pairs={{1,0},{2,1},{3,2},{4,3},{5,4},{6,5},{7,6},{9,8},{10,9},{11,10},{12... | collective-permute-start | bytes 1572872 | tf_op jit(solution)/shard_map/ppermute | solution.py:354
  49.0 7.6 %shard_map.117 = (bf16[256,2048]{1,0:T(8,128)(2,1)S(1)}, bf16[256,2048]{1,0:T(8,128)(2,1)}, bf16[512,512]{1,0:T(8,128)(2,1)}, f32[512,512]{1,0:T(8,128)S(1)}) custom-call(s32[3]{0:T(128)S(1)} %pad_add_fusion.refs_0_, bf16[512,512]{1,0:T(8,128)(2,1)S(1)} %get-tuple-element.44.refs_1_, bf16[512,512]{1,0:T(8,128)(2,1)S(1)} %get-tuple-element.51.refs_2_, ...), custom_call_target="tpu_custom_call" | custom-call | flops 4831838208 | bytes 22036492 | tf_op jit(solution)/shard_map/pallas_call | solution.py:38
  57.4 2.6 %collective-permute-start.2 = (bf16[256,2048]{1,0:T(8,128)(2,1)}, bf16[256,2048]{1,0:T(8,128)(2,1)}, u32[]{:S(2)}, u32[]{:S(2)}) collective-permute-start(bf16[256,2048]{1,0:T(8,128)(2,1)} %get-tuple-element.72), channel_id=1, source_target_pairs={{0,1},{1,0},{2,3},{3,2},{4,5},{5,4},{6,7},{7,6},{8,9},{9,8},{10,11... | collective-permute-start | bytes 3145736 | tf_op jit(solution)/shard_map/ppermute | solution.py:472
  62.1 1.6 %shard_map.118.refs_3_ = bf16[512,512]{1,0:T(8,128)(2,1)} custom-call(bf16[512,512]{1,0:T(8,128)(2,1)S(1)} %get-tuple-element.52.refs_3_.refs_0_, f32[512,512]{1,0:T(8,128)S(1)} %get-tuple-element.64.refs_1_, bf16[512,512]{1,0:T(8,128)(2,1)S(1)} %copy-done.12, bf16[512,512]{1,0:T(8,128)(2,1)S(1)} %bitcast.20, bf16[512,512]{1,0:T(8,128)(2,1)S(1)} %copy-done.10), custom_call_target="tpu_custom_call" | custom-call | flops 268435456 | bytes 3670016 | tf_op jit(solution)/shard_map/pallas_call | solution.py:38
  63.7 1.6 %shard_map.121 = (bf16[64,2048]{1,0:T(8,128)(2,1)S(1)}, bf16[64,2048]{1,0:T(8,128)(2,1)S(1)}, bf16[64,2048]{1,0:T(8,128)(2,1)S(1)}, bf16[64,2048]{1,0:T(8,128)(2,1)S(1)}) custom-call(s32[1]{0:T(128)} %bitcast.11.refs_0_, bf16[4,64,2048]{2,1,0:T(8,128)(2,1)S(1)} %bitcast.23, bf16[4,64,2048]{2,1,0:T(8,128)(2,1)} %bitcast.13.refs_2_, ...), custom_call_target="tpu_custom_call" | custom-call | bytes 3670020 | tf_op jit(solution)/shard_map/pallas_call | solution.py:38
  66.7 2.1 %collective-permute-start.5 = (bf16[64,2048]{1,0:T(8,128)(2,1)S(1)}, bf16[64,2048]{1,0:T(8,128)(2,1)S(1)}, u32[]{:S(2)}, u32[]{:S(2)}) collective-permute-start(bf16[64,2048]{1,0:T(8,128)(2,1)S(1)} %get-tuple-element.76), channel_id=1, source_target_pairs={{0,24},{8,16},{16,8},{24,0},{1,25},{9,17},{17,9},{25,1},{2,26},{10... | collective-permute-start | bytes 786440 | tf_op jit(solution)/shard_map/ppermute | solution.py:378
  68.8 3.6 %all-to-all-start.1 = ((bf16[32,16,512]{2,1,0:T(8,128)(2,1)}), bf16[32,16,512]{2,1,0:T(8,128)(2,1)S(1)}, u32[]{:S(2)}, u32[]{:S(2)}) async-start(bf16[32,16,512]{2,1,0:T(8,128)(2,1)} %bitcast.8), calls=%async_computation.1 | async-start | bytes 1048576 | tf_op jit(solution)/shard_map/all_to_all | solution.py:403
  72.4 2.1 %collective-permute-done.3 = bf16[64,2048]{1,0:T(8,128)(2,1)S(1)} collective-permute-done((bf16[64,2048]{1,0:T(8,128)(2,1)S(1)}, bf16[64,2048]{1,0:T(8,128)(2,1)S(1)}, u32[]{:S(2)}, u32[]{:S(2)}) %collective-permute-start.3) | collective-permute-done | bytes 262176 | tf_op jit(solution)/shard_map/ppermute | solution.py:378
  74.5 7.5 %collective-permute-done.4 = bf16[64,2048]{1,0:T(8,128)(2,1)S(1)} collective-permute-done((bf16[64,2048]{1,0:T(8,128)(2,1)S(1)}, bf16[64,2048]{1,0:T(8,128)(2,1)S(1)}, u32[]{:S(2)}, u32[]{:S(2)}) %collective-permute-start.4) | collective-permute-done | bytes 262176 | tf_op jit(solution)/shard_map/ppermute | solution.py:378
  83.0 1.7 %collective-permute-start.6 = (bf16[16,2048]{1,0:T(8,128)(2,1)S(1)}, bf16[16,2048]{1,0:T(8,128)(2,1)S(1)}, u32[]{:S(2)}, u32[]{:S(2)}) collective-permute-start(bf16[16,2048]{1,0:T(8,128)(2,1)S(1)} %get-tuple-element.78), channel_id=1, source_target_pairs={{0,2},{1,3},{2,0},{3,1},{4,6},{5,7},{6,4},{7,5},{8,10},{9,11},{10,... | collective-permute-start | bytes 196616 | tf_op jit(solution)/shard_map/ppermute | solution.py:378
  84.7 1.6 %collective-permute-start.7 = (bf16[16,2048]{1,0:T(8,128)(2,1)S(1)}, bf16[16,2048]{1,0:T(8,128)(2,1)S(1)}, u32[]{:S(2)}, u32[]{:S(2)}) collective-permute-start(bf16[16,2048]{1,0:T(8,128)(2,1)S(1)} %get-tuple-element.79), channel_id=1, source_target_pairs={{0,4},{1,5},{2,6},{3,7},{4,0},{5,1},{6,2},{7,3},{8,12},{9,13},{10,... | collective-permute-start | bytes 196616 | tf_op jit(solution)/shard_map/ppermute | solution.py:378
  86.3 1.2 %collective-permute-start.8 = (bf16[16,2048]{1,0:T(8,128)(2,1)S(1)}, bf16[16,2048]{1,0:T(8,128)(2,1)S(1)}, u32[]{:S(2)}, u32[]{:S(2)}) collective-permute-start(bf16[16,2048]{1,0:T(8,128)(2,1)S(1)} %get-tuple-element.80), channel_id=1, source_target_pairs={{0,6},{1,7},{2,4},{3,5},{4,2},{5,3},{6,0},{7,1},{8,14},{9,15},{10,... | collective-permute-start | bytes 196616 | tf_op jit(solution)/shard_map/ppermute | solution.py:378
  87.9 1.5 %all-to-all-done.1 = bf16[32,16,512]{2,1,0:T(8,128)(2,1)S(1)} async-done(((bf16[32,16,512]{2,1,0:T(8,128)(2,1)}), bf16[32,16,512]{2,1,0:T(8,128)(2,1)S(1)}, u32[]{:S(2)}, u32[]{:S(2)}) %all-to-all-start.1) | async-done | bytes 524320 | tf_op jit(solution)/shard_map/all_to_all | solution.py:403
  89.5 1.2 %shard_map.120 = bf16[512,512]{1,0:T(8,128)(2,1)} custom-call(bf16[512,512]{1,0:T(8,128)(2,1)S(1)} %shard_map.119.refs_0_, bf16[512,512]{1,0:T(8,128)(2,1)S(1)} %bitcast.21), custom_call_target="tpu_custom_call" | custom-call | flops 268435456 | bytes 1572864 | tf_op jit(solution)/shard_map/pallas_call | solution.py:38
  91.4 1.1 %collective-permute-done.8 = bf16[16,2048]{1,0:T(8,128)(2,1)S(1)} collective-permute-done((bf16[16,2048]{1,0:T(8,128)(2,1)S(1)}, bf16[16,2048]{1,0:T(8,128)(2,1)S(1)}, u32[]{:S(2)}, u32[]{:S(2)}) %collective-permute-start.8) | collective-permute-done | bytes 65568 | tf_op jit(solution)/shard_map/ppermute | solution.py:378
  (44 shorter events, 12.3 us)
Async XLA Ops:
  0.6 35.4 %copy-start.7 = (bf16[512,512]{1,0:T(8,128)(2,1)S(1)}, bf16[512,512]{1,0:T(8,128)(2,1)}, u32[]{:S(2)}) copy-start(bf16[512,512]{1,0:T(8,128)(2,1)} %refs_8_.1) | copy-start | bytes 1572868
  0.6 35.4 %copy-start = (bf16[1,512,512]{2,1,0:T(8,128)(2,1)S(1)}, bf16[1,512,512]{2,1,0:T(8,128)(2,1)}, u32[]{:S(2)}) copy-start(bf16[1,512,512]{2,1,0:T(8,128)(2,1)} %param.17) | copy-start | bytes 1572868
  0.7 1.1 %copy-start.13 = (bf16[512,512]{1,0:T(8,128)(2,1)S(1)}, bf16[512,512]{1,0:T(8,128)(2,1)}, u32[]{:S(2)}) copy-start(bf16[512,512]{1,0:T(8,128)(2,1)} %refs_1_.2) | copy-start | bytes 1572868
  4.0 23.7 %all-to-all-start = ((bf16[32,16,512]{2,1,0:T(8,128)(2,1)}), bf16[32,16,512]{2,1,0:T(8,128)(2,1)S(1)}, u32[]{:S(2)}, u32[]{:S(2)}) async-start(bf16[32,16,512]{2,1,0:T(8,128)(2,1)} %bitcast.4), calls=%async_computation | async-start | bytes 1048576 | tf_op jit(solution)/shard_map/all_to_all | solution.py:403
  28.3 7.7 %collective-permute-start = (bf16[512,512]{1,0:T(8,128)(2,1)S(1)}, bf16[512,512]{1,0:T(8,128)(2,1)S(1)}, u32[]{:S(2)}, u32[]{:S(2)}) collective-permute-start(bf16[512,512]{1,0:T(8,128)(2,1)S(1)} %get-tuple-element.43.refs_0_), channel_id=1, source_target_pairs={{0,1},{1,2},{2,3},{3,4},{4,5},{5,6},{6,7},{8,9},{9,10},{10,11},{11... | collective-permute-start | bytes 1572872 | tf_op jit(solution)/shard_map/ppermute | solution.py:354
  31.0 1.0 %copy-start.1 = (bf16[512,512]{1,0:T(8,128)(2,1)S(1)}, bf16[512,512]{1,0:T(8,128)(2,1)}, u32[]{:S(2)}) copy-start(bf16[512,512]{1,0:T(8,128)(2,1)} %refs_5_.1) | copy-start | bytes 1572868
  32.1 1.0 %copy-start.3 = (bf16[512,512]{1,0:T(8,128)(2,1)S(1)}, bf16[512,512]{1,0:T(8,128)(2,1)}, u32[]{:S(2)}) copy-start(bf16[512,512]{1,0:T(8,128)(2,1)} %refs_6_.1) | copy-start | bytes 1572868
  33.1 1.0 %copy-start.5 = (bf16[512,512]{1,0:T(8,128)(2,1)S(1)}, bf16[512,512]{1,0:T(8,128)(2,1)}, u32[]{:S(2)}) copy-start(bf16[512,512]{1,0:T(8,128)(2,1)} %refs_7_.1) | copy-start | bytes 1572868
  36.0 12.9 %copy-start.2 = (bf16[512,512]{1,0:T(8,128)(2,1)S(1)}, bf16[512,512]{1,0:T(8,128)(2,1)}, u32[]{:S(2)}) copy-start(bf16[512,512]{1,0:T(8,128)(2,1)} %refs_5_.1) | copy-start | bytes 1572868
  36.1 12.9 %copy-start.4 = (bf16[512,512]{1,0:T(8,128)(2,1)S(1)}, bf16[512,512]{1,0:T(8,128)(2,1)}, u32[]{:S(2)}) copy-start(bf16[512,512]{1,0:T(8,128)(2,1)} %refs_6_.1) | copy-start | bytes 1572868
  36.1 12.9 %copy-start.6 = (bf16[512,512]{1,0:T(8,128)(2,1)S(1)}, bf16[512,512]{1,0:T(8,128)(2,1)}, u32[]{:S(2)}) copy-start(bf16[512,512]{1,0:T(8,128)(2,1)} %refs_7_.1) | copy-start | bytes 1572868
  36.1 12.9 %copy-start.8 = (bf16[512,512]{1,0:T(8,128)(2,1)S(1)}, bf16[512,512]{1,0:T(8,128)(2,1)}, u32[]{:S(2)}) copy-start(bf16[512,512]{1,0:T(8,128)(2,1)} %refs_8_.1) | copy-start | bytes 1572868
  47.6 9.0 %collective-permute-start.1 = (bf16[512,512]{1,0:T(8,128)(2,1)S(1)}, bf16[512,512]{1,0:T(8,128)(2,1)S(1)}, u32[]{:S(2)}, u32[]{:S(2)}) collective-permute-start(bf16[512,512]{1,0:T(8,128)(2,1)S(1)} %get-tuple-element.66), channel_id=1, source_target_pairs={{1,0},{2,1},{3,2},{4,3},{5,4},{6,5},{7,6},{9,8},{10,9},{11,10},{12... | collective-permute-start | bytes 1572872 | tf_op jit(solution)/shard_map/ppermute | solution.py:354
  56.6 30.9 %copy-start.15 = (s32[512]{0:T(512)S(1)}, s32[512]{0:T(512)}, u32[]{:S(2)}) copy-start(s32[512]{0:T(512)} %param.10) | copy-start | bytes 6148
  57.4 6.2 %collective-permute-start.2 = (bf16[256,2048]{1,0:T(8,128)(2,1)}, bf16[256,2048]{1,0:T(8,128)(2,1)}, u32[]{:S(2)}, u32[]{:S(2)}) collective-permute-start(bf16[256,2048]{1,0:T(8,128)(2,1)} %get-tuple-element.72), channel_id=1, source_target_pairs={{0,1},{1,0},{2,3},{3,2},{4,5},{5,4},{6,7},{7,6},{8,9},{9,8},{10,11... | collective-permute-start | bytes 3145736 | tf_op jit(solution)/shard_map/ppermute | solution.py:472
  60.0 1.0 %copy-start.10 = (bf16[512,512]{1,0:T(8,128)(2,1)S(1)}, bf16[512,512]{1,0:T(8,128)(2,1)}, u32[]{:S(2)}) copy-start(bf16[512,512]{1,0:T(8,128)(2,1)} %copy-done.9) | copy-start | bytes 1572868
  61.0 1.0 %copy-start.12 = (bf16[512,512]{1,0:T(8,128)(2,1)S(1)}, bf16[512,512]{1,0:T(8,128)(2,1)}, u32[]{:S(2)}) copy-start(bf16[512,512]{1,0:T(8,128)(2,1)} %copy-done.11) | copy-start | bytes 1572868
  65.3 9.2 %collective-permute-start.3 = (bf16[64,2048]{1,0:T(8,128)(2,1)S(1)}, bf16[64,2048]{1,0:T(8,128)(2,1)S(1)}, u32[]{:S(2)}, u32[]{:S(2)}) collective-permute-start(bf16[64,2048]{1,0:T(8,128)(2,1)S(1)} %get-tuple-element.74), channel_id=1, source_target_pairs={{0,8},{8,0},{16,24},{24,16},{1,9},{9,1},{17,25},{25,17},{2,10},{10... | collective-permute-start | bytes 786440 | tf_op jit(solution)/shard_map/ppermute | solution.py:378
  66.2 15.8 %collective-permute-start.4 = (bf16[64,2048]{1,0:T(8,128)(2,1)S(1)}, bf16[64,2048]{1,0:T(8,128)(2,1)S(1)}, u32[]{:S(2)}, u32[]{:S(2)}) collective-permute-start(bf16[64,2048]{1,0:T(8,128)(2,1)S(1)} %get-tuple-element.75), channel_id=1, source_target_pairs={{0,16},{8,24},{16,0},{24,8},{1,17},{9,25},{17,1},{25,9},{2,18},{10... | collective-permute-start | bytes 786440 | tf_op jit(solution)/shard_map/ppermute | solution.py:378
  66.7 16.1 %collective-permute-start.5 = (bf16[64,2048]{1,0:T(8,128)(2,1)S(1)}, bf16[64,2048]{1,0:T(8,128)(2,1)S(1)}, u32[]{:S(2)}, u32[]{:S(2)}) collective-permute-start(bf16[64,2048]{1,0:T(8,128)(2,1)S(1)} %get-tuple-element.76), channel_id=1, source_target_pairs={{0,24},{8,16},{16,8},{24,0},{1,25},{9,17},{17,9},{25,1},{2,26},{10... | collective-permute-start | bytes 786440 | tf_op jit(solution)/shard_map/ppermute | solution.py:378
  68.8 20.6 %all-to-all-start.1 = ((bf16[32,16,512]{2,1,0:T(8,128)(2,1)}), bf16[32,16,512]{2,1,0:T(8,128)(2,1)S(1)}, u32[]{:S(2)}, u32[]{:S(2)}) async-start(bf16[32,16,512]{2,1,0:T(8,128)(2,1)} %bitcast.8), calls=%async_computation.1 | async-start | bytes 1048576 | tf_op jit(solution)/shard_map/all_to_all | solution.py:403
  83.0 7.7 %collective-permute-start.6 = (bf16[16,2048]{1,0:T(8,128)(2,1)S(1)}, bf16[16,2048]{1,0:T(8,128)(2,1)S(1)}, u32[]{:S(2)}, u32[]{:S(2)}) collective-permute-start(bf16[16,2048]{1,0:T(8,128)(2,1)S(1)} %get-tuple-element.78), channel_id=1, source_target_pairs={{0,2},{1,3},{2,0},{3,1},{4,6},{5,7},{6,4},{7,5},{8,10},{9,11},{10,... | collective-permute-start | bytes 196616 | tf_op jit(solution)/shard_map/ppermute | solution.py:378
  84.7 6.7 %collective-permute-start.7 = (bf16[16,2048]{1,0:T(8,128)(2,1)S(1)}, bf16[16,2048]{1,0:T(8,128)(2,1)S(1)}, u32[]{:S(2)}, u32[]{:S(2)}) collective-permute-start(bf16[16,2048]{1,0:T(8,128)(2,1)S(1)} %get-tuple-element.79), channel_id=1, source_target_pairs={{0,4},{1,5},{2,6},{3,7},{4,0},{5,1},{6,2},{7,3},{8,12},{9,13},{10,... | collective-permute-start | bytes 196616 | tf_op jit(solution)/shard_map/ppermute | solution.py:378
  86.3 6.2 %collective-permute-start.8 = (bf16[16,2048]{1,0:T(8,128)(2,1)S(1)}, bf16[16,2048]{1,0:T(8,128)(2,1)S(1)}, u32[]{:S(2)}, u32[]{:S(2)}) collective-permute-start(bf16[16,2048]{1,0:T(8,128)(2,1)S(1)} %get-tuple-element.80), channel_id=1, source_target_pairs={{0,6},{1,7},{2,4},{3,5},{4,2},{5,3},{6,0},{7,1},{8,14},{9,15},{10,... | collective-permute-start | bytes 196616 | tf_op jit(solution)/shard_map/ppermute | solution.py:378
  (3 other events, 2.3 us)

commit v13 on v12

--- a/solution.py
+++ b/solution.py
@@ -260,7 +260,7 @@
     for copy in copies:
         copy.wait()
     dot_ref[...] = mm(cot_ref[...], wo_ref[...], NT).astype(BF).T
-    lax.fori_loop(0, width // pair, one_pair, 0)
+    lax.fori_loop(0, width // pair, one_pair, 0, unroll=2)
     back_ref[...] = (mm(dkh_ref[...], wk_ref[...], NT) + mm(dvh_ref[...], wv_ref[...], NT)).astype(BF)
 
 
@@ -306,7 +306,7 @@
                 out[j * TILE : (j + 1) * TILE, cols] = (total * factor).astype(BF)
         return carry
 
-    lax.fori_loop(0, width // pair, one_pair, 0)
+    lax.fori_loop(0, width // pair, one_pair, 0, unroll=2)
 
     for copy in copies:
         copy.wait()

time: 93.8 us -> 93.1 us (level)
  no operation moved by 1% of the time
where the time goes in v13:
time: 93.1 us; the launch traced here: 92.5 us
  Pallas kernels  28.4 us (31%)
  waiting for transfers between devices  27.5 us (30%)
  starting transfers between devices  24.9 us (27%)
  local copies, waits for them, and re-layouts  9.46 us (10%)
  between operations  1.54 us (2%)
    pallas_call x11, Pallas kernels, vmem_call(): pl.pallas_call(body, out_shape=tuple(outs), in_specs=[pl.BlockSpec(memory...  28.4 us
    all_to_all x2, waiting for transfers between devices, exchanged(): lax.all_to_all(shard.reshape(devices, slots, width), AXES, split_axis=0,...  15 us
    ppermute x6, waiting for transfers between devices, swapped(): lax.ppermute(piece, axis, [(i, i ^ k * step) for i in range(count)])  12.5 us
    all_to_all x2, starting transfers between devices, exchanged(): lax.all_to_all(shard.reshape(devices, slots, width), AXES, split_axis=0,...  10.7 us
    unnamed x32, local copies, waits for them, and re-layouts  8.64 us
    ppermute x6, starting transfers between devices, swapped(): lax.ppermute(piece, axis, [(i, i ^ k * step) for i in range(count)])  8.01 us
    ppermute x2, starting transfers between devices, passed_along(): return lax.ppermute(shard, 'seq', pairs)  3.42 us
    ppermute x1, starting transfers between devices, shards(): got = lax.ppermute(send, 'seq', [(i, i ^ 1) for i in range(seqs)])  2.74 us
  transfers between devices with their start and end apart: 11, of which 7 were waited for; matrix products, arithmetic and copies ran while one was open for 1% of the time, Pallas kernels for 15%

profile of v13, /device:TPU:0, one launch (start us, length us, event | category | flops | bytes accessed | tf_op | source)
XLA Modules:
  0.0 92.5 jit_solution(1733108517299473018)
XLA Ops:
  0.7 1.1 %copy-done.13 = bf16[512,512]{1,0:T(8,128)(2,1)S(1)} copy-done((bf16[512,512]{1,0:T(8,128)(2,1)S(1)}, bf16[512,512]{1,0:T(8,128)(2,1)}, u32[]{:S(2)}) %copy-start.13) | copy-done | bytes 524312
  2.5 1.6 %shard_map.113 = bf16[512,512]{1,0:T(8,128)(2,1)} custom-call(s32[1,512]{1,0:T(1,128)S(1)} %bitcast.28, bf16[512,512]{1,0:T(8,128)(2,1)S(1)} %copy-done.13), custom_call_target="tpu_custom_call" | custom-call | flops 268435456 | bytes 1050624 | tf_op jit(solution)/shard_map/pallas_call | solution.py:38
  4.0 7.3 %all-to-all-start = ((bf16[32,16,512]{2,1,0:T(8,128)(2,1)}), bf16[32,16,512]{2,1,0:T(8,128)(2,1)S(1)}, u32[]{:S(2)}, u32[]{:S(2)}) async-start(bf16[32,16,512]{2,1,0:T(8,128)(2,1)} %bitcast.4), calls=%async_computation | async-start | bytes 1048576 | tf_op jit(solution)/shard_map/all_to_all | solution.py:403
  14.0 13.7 %all-to-all-done = bf16[32,16,512]{2,1,0:T(8,128)(2,1)S(1)} async-done(((bf16[32,16,512]{2,1,0:T(8,128)(2,1)}), bf16[32,16,512]{2,1,0:T(8,128)(2,1)S(1)}, u32[]{:S(2)}, u32[]{:S(2)}) %all-to-all-start) | async-done | bytes 524320 | tf_op jit(solution)/shard_map/all_to_all | solution.py:403
  28.3 1.9 %collective-permute-start = (bf16[512,512]{1,0:T(8,128)(2,1)S(1)}, bf16[512,512]{1,0:T(8,128)(2,1)S(1)}, u32[]{:S(2)}, u32[]{:S(2)}) collective-permute-start(bf16[512,512]{1,0:T(8,128)(2,1)S(1)} %get-tuple-element.43.refs_0_), channel_id=1, source_target_pairs={{0,1},{1,2},{2,3},{3,4},{4,5},{5,6},{6,7},{8,9},{9,10},{10,11},{11... | collective-permute-start | bytes 1572872 | tf_op jit(solution)/shard_map/ppermute | solution.py:354
  31.0 1.0 %copy-done.1 = bf16[512,512]{1,0:T(8,128)(2,1)S(1)} copy-done((bf16[512,512]{1,0:T(8,128)(2,1)S(1)}, bf16[512,512]{1,0:T(8,128)(2,1)}, u32[]{:S(2)}) %copy-start.1) | copy-done | bytes 524312
  34.1 1.9 %shard_map.115 = (bf16[512,512]{1,0:T(8,128)(2,1)S(1)}, bf16[512,512]{1,0:T(8,128)(2,1)S(1)}, bf16[512,512]{1,0:T(8,128)(2,1)S(1)}, bf16[512,512]{1,0:T(8,128)(2...) custom-call(bf16[512,512]{1,0:T(8,128)(2,1)S(1)} %get-tuple-element., ...), custom_call_target="tpu_custom_call" | custom-call | flops 805306368 | bytes 6291456 | tf_op jit(solution)/shard_map/pallas_call | solution.py:38
  36.1 11.0 %shard_map.116 = (bf16[16,640,256]{2,1,0:T(8,128)(2,1)S(1)}, bf16[16,640,256]{2,1,0:T(8,128)(2,1)S(1)}, f32[16,1,256]{2,1,0:T(1,128)S(1)}, bf16[512,512]{1,0:T(8...) custom-call(s32[3]{0:T(128)S(1)} %pad_add_fusion.refs_0_, ...), custom_call_target="tpu_custom_call" | custom-call | flops 3221225472 | bytes 19415052 | tf_op jit(solution)/shard_map/pallas_call | solution.py:38
  47.1 1.5 %collective-permute-start.1 = (bf16[512,512]{1,0:T(8,128)(2,1)S(1)}, bf16[512,512]{1,0:T(8,128)(2,1)S(1)}, u32[]{:S(2)}, u32[]{:S(2)}) collective-permute-start(bf16[512,512]{1,0:T(8,128)(2,1)S(1)} %get-tuple-element.66), channel_id=1, source_target_pairs={{1,0},{2,1},{3,2},{4,3},{5,4},{6,5},{7,6},{9,8},{10,9},{11,10},{12... | collective-permute-start | bytes 1572872 | tf_op jit(solution)/shard_map/ppermute | solution.py:354
  48.6 7.3 %shard_map.117 = (bf16[256,2048]{1,0:T(8,128)(2,1)S(1)}, bf16[256,2048]{1,0:T(8,128)(2,1)}, bf16[512,512]{1,0:T(8,128)(2,1)}, f32[512,512]{1,0:T(8,128)S(1)}) custom-call(s32[3]{0:T(128)S(1)} %pad_add_fusion.refs_0_, bf16[512,512]{1,0:T(8,128)(2,1)S(1)} %get-tuple-element.44.refs_1_, bf16[512,512]{1,0:T(8,128)(2,1)S(1)} %get-tuple-element.51.refs_2_, ...), custom_call_target="tpu_custom_call" | custom-call | flops 4831838208 | bytes 22036492 | tf_op jit(solution)/shard_map/pallas_call | solution.py:38
  56.8 2.7 %collective-permute-start.2 = (bf16[256,2048]{1,0:T(8,128)(2,1)}, bf16[256,2048]{1,0:T(8,128)(2,1)}, u32[]{:S(2)}, u32[]{:S(2)}) collective-permute-start(bf16[256,2048]{1,0:T(8,128)(2,1)} %get-tuple-element.72), channel_id=1, source_target_pairs={{0,1},{1,0},{2,3},{3,2},{4,5},{5,4},{6,7},{7,6},{8,9},{9,8},{10,11... | collective-permute-start | bytes 3145736 | tf_op jit(solution)/shard_map/ppermute | solution.py:472
  61.6 1.6 %shard_map.118.refs_3_ = bf16[512,512]{1,0:T(8,128)(2,1)} custom-call(bf16[512,512]{1,0:T(8,128)(2,1)S(1)} %get-tuple-element.52.refs_3_.refs_0_, f32[512,512]{1,0:T(8,128)S(1)} %get-tuple-element.64.refs_1_, bf16[512,512]{1,0:T(8,128)(2,1)S(1)} %copy-done.12, bf16[512,512]{1,0:T(8,128)(2,1)S(1)} %bitcast.20, bf16[512,512]{1,0:T(8,128)(2,1)S(1)} %copy-done.10), custom_call_target="tpu_custom_call" | custom-call | flops 268435456 | bytes 3670016 | tf_op jit(solution)/shard_map/pallas_call | solution.py:38
  63.2 1.6 %shard_map.121 = (bf16[64,2048]{1,0:T(8,128)(2,1)S(1)}, bf16[64,2048]{1,0:T(8,128)(2,1)S(1)}, bf16[64,2048]{1,0:T(8,128)(2,1)S(1)}, bf16[64,2048]{1,0:T(8,128)(2,1)S(1)}) custom-call(s32[1]{0:T(128)} %bitcast.11.refs_0_, bf16[4,64,2048]{2,1,0:T(8,128)(2,1)S(1)} %bitcast.23, bf16[4,64,2048]{2,1,0:T(8,128)(2,1)} %bitcast.13.refs_2_, ...), custom_call_target="tpu_custom_call" | custom-call | bytes 3670020 | tf_op jit(solution)/shard_map/pallas_call | solution.py:38
  66.2 2.1 %collective-permute-start.5 = (bf16[64,2048]{1,0:T(8,128)(2,1)S(1)}, bf16[64,2048]{1,0:T(8,128)(2,1)S(1)}, u32[]{:S(2)}, u32[]{:S(2)}) collective-permute-start(bf16[64,2048]{1,0:T(8,128)(2,1)S(1)} %get-tuple-element.76), channel_id=1, source_target_pairs={{0,24},{8,16},{16,8},{24,0},{1,25},{9,17},{17,9},{25,1},{2,26},{10... | collective-permute-start | bytes 786440 | tf_op jit(solution)/shard_map/ppermute | solution.py:378
  68.3 3.4 %all-to-all-start.1 = ((bf16[32,16,512]{2,1,0:T(8,128)(2,1)}), bf16[32,16,512]{2,1,0:T(8,128)(2,1)S(1)}, u32[]{:S(2)}, u32[]{:S(2)}) async-start(bf16[32,16,512]{2,1,0:T(8,128)(2,1)} %bitcast.8), calls=%async_computation.1 | async-start | bytes 1048576 | tf_op jit(solution)/shard_map/all_to_all | solution.py:403
  71.7 2.3 %collective-permute-done.3 = bf16[64,2048]{1,0:T(8,128)(2,1)S(1)} collective-permute-done((bf16[64,2048]{1,0:T(8,128)(2,1)S(1)}, bf16[64,2048]{1,0:T(8,128)(2,1)S(1)}, u32[]{:S(2)}, u32[]{:S(2)}) %collective-permute-start.3) | collective-permute-done | bytes 262176 | tf_op jit(solution)/shard_map/ppermute | solution.py:378
  74.0 7.3 %collective-permute-done.4 = bf16[64,2048]{1,0:T(8,128)(2,1)S(1)} collective-permute-done((bf16[64,2048]{1,0:T(8,128)(2,1)S(1)}, bf16[64,2048]{1,0:T(8,128)(2,1)S(1)}, u32[]{:S(2)}, u32[]{:S(2)}) %collective-permute-start.4) | collective-permute-done | bytes 262176 | tf_op jit(solution)/shard_map/ppermute | solution.py:378
  81.4 1.1 %collective-permute-done.5 = bf16[64,2048]{1,0:T(8,128)(2,1)S(1)} collective-permute-done((bf16[64,2048]{1,0:T(8,128)(2,1)S(1)}, bf16[64,2048]{1,0:T(8,128)(2,1)S(1)}, u32[]{:S(2)}, u32[]{:S(2)}) %collective-permute-start.5) | collective-permute-done | bytes 262176 | tf_op jit(solution)/shard_map/ppermute | solution.py:378
  82.6 1.5 %collective-permute-start.6 = (bf16[16,2048]{1,0:T(8,128)(2,1)S(1)}, bf16[16,2048]{1,0:T(8,128)(2,1)S(1)}, u32[]{:S(2)}, u32[]{:S(2)}) collective-permute-start(bf16[16,2048]{1,0:T(8,128)(2,1)S(1)} %get-tuple-element.78), channel_id=1, source_target_pairs={{0,2},{1,3},{2,0},{3,1},{4,6},{5,7},{6,4},{7,5},{8,10},{9,11},{10,... | collective-permute-start | bytes 196616 | tf_op jit(solution)/shard_map/ppermute | solution.py:378
  84.1 1.6 %collective-permute-start.7 = (bf16[16,2048]{1,0:T(8,128)(2,1)S(1)}, bf16[16,2048]{1,0:T(8,128)(2,1)S(1)}, u32[]{:S(2)}, u32[]{:S(2)}) collective-permute-start(bf16[16,2048]{1,0:T(8,128)(2,1)S(1)} %get-tuple-element.79), channel_id=1, source_target_pairs={{0,4},{1,5},{2,6},{3,7},{4,0},{5,1},{6,2},{7,3},{8,12},{9,13},{10,... | collective-permute-start | bytes 196616 | tf_op jit(solution)/shard_map/ppermute | solution.py:378
  85.6 1.4 %collective-permute-start.8 = (bf16[16,2048]{1,0:T(8,128)(2,1)S(1)}, bf16[16,2048]{1,0:T(8,128)(2,1)S(1)}, u32[]{:S(2)}, u32[]{:S(2)}) collective-permute-start(bf16[16,2048]{1,0:T(8,128)(2,1)S(1)} %get-tuple-element.80), channel_id=1, source_target_pairs={{0,6},{1,7},{2,4},{3,5},{4,2},{5,3},{6,0},{7,1},{8,14},{9,15},{10,... | collective-permute-start | bytes 196616 | tf_op jit(solution)/shard_map/ppermute | solution.py:378
  87.5 1.3 %all-to-all-done.1 = bf16[32,16,512]{2,1,0:T(8,128)(2,1)S(1)} async-done(((bf16[32,16,512]{2,1,0:T(8,128)(2,1)}), bf16[32,16,512]{2,1,0:T(8,128)(2,1)S(1)}, u32[]{:S(2)}, u32[]{:S(2)}) %all-to-all-start.1) | async-done | bytes 524320 | tf_op jit(solution)/shard_map/all_to_all | solution.py:403
  88.8 1.2 %shard_map.120 = bf16[512,512]{1,0:T(8,128)(2,1)} custom-call(bf16[512,512]{1,0:T(8,128)(2,1)S(1)} %shard_map.119.refs_0_, bf16[512,512]{1,0:T(8,128)(2,1)S(1)} %bitcast.21), custom_call_target="tpu_custom_call" | custom-call | flops 268435456 | bytes 1572864 | tf_op jit(solution)/shard_map/pallas_call | solution.py:38
  90.7 1.1 %collective-permute-done.8 = bf16[16,2048]{1,0:T(8,128)(2,1)S(1)} collective-permute-done((bf16[16,2048]{1,0:T(8,128)(2,1)S(1)}, bf16[16,2048]{1,0:T(8,128)(2,1)S(1)}, u32[]{:S(2)}, u32[]{:S(2)}) %collective-permute-start.8) | collective-permute-done | bytes 65568 | tf_op jit(solution)/shard_map/ppermute | solution.py:378
  (44 shorter events, 12.5 us)
Async XLA Ops:
  0.6 35.4 %copy-start.7 = (bf16[512,512]{1,0:T(8,128)(2,1)S(1)}, bf16[512,512]{1,0:T(8,128)(2,1)}, u32[]{:S(2)}) copy-start(bf16[512,512]{1,0:T(8,128)(2,1)} %refs_8_.1) | copy-start | bytes 1572868
  0.6 35.4 %copy-start = (bf16[1,512,512]{2,1,0:T(8,128)(2,1)S(1)}, bf16[1,512,512]{2,1,0:T(8,128)(2,1)}, u32[]{:S(2)}) copy-start(bf16[1,512,512]{2,1,0:T(8,128)(2,1)} %param.17) | copy-start | bytes 1572868
  0.7 1.1 %copy-start.13 = (bf16[512,512]{1,0:T(8,128)(2,1)S(1)}, bf16[512,512]{1,0:T(8,128)(2,1)}, u32[]{:S(2)}) copy-start(bf16[512,512]{1,0:T(8,128)(2,1)} %refs_1_.2) | copy-start | bytes 1572868
  4.0 23.7 %all-to-all-start = ((bf16[32,16,512]{2,1,0:T(8,128)(2,1)}), bf16[32,16,512]{2,1,0:T(8,128)(2,1)S(1)}, u32[]{:S(2)}, u32[]{:S(2)}) async-start(bf16[32,16,512]{2,1,0:T(8,128)(2,1)} %bitcast.4), calls=%async_computation | async-start | bytes 1048576 | tf_op jit(solution)/shard_map/all_to_all | solution.py:403
  28.3 7.7 %collective-permute-start = (bf16[512,512]{1,0:T(8,128)(2,1)S(1)}, bf16[512,512]{1,0:T(8,128)(2,1)S(1)}, u32[]{:S(2)}, u32[]{:S(2)}) collective-permute-start(bf16[512,512]{1,0:T(8,128)(2,1)S(1)} %get-tuple-element.43.refs_0_), channel_id=1, source_target_pairs={{0,1},{1,2},{2,3},{3,4},{4,5},{5,6},{6,7},{8,9},{9,10},{10,11},{11... | collective-permute-start | bytes 1572872 | tf_op jit(solution)/shard_map/ppermute | solution.py:354
  31.0 1.0 %copy-start.1 = (bf16[512,512]{1,0:T(8,128)(2,1)S(1)}, bf16[512,512]{1,0:T(8,128)(2,1)}, u32[]{:S(2)}) copy-start(bf16[512,512]{1,0:T(8,128)(2,1)} %refs_5_.1) | copy-start | bytes 1572868
  32.1 1.0 %copy-start.3 = (bf16[512,512]{1,0:T(8,128)(2,1)S(1)}, bf16[512,512]{1,0:T(8,128)(2,1)}, u32[]{:S(2)}) copy-start(bf16[512,512]{1,0:T(8,128)(2,1)} %refs_6_.1) | copy-start | bytes 1572868
  33.1 1.0 %copy-start.5 = (bf16[512,512]{1,0:T(8,128)(2,1)S(1)}, bf16[512,512]{1,0:T(8,128)(2,1)}, u32[]{:S(2)}) copy-start(bf16[512,512]{1,0:T(8,128)(2,1)} %refs_7_.1) | copy-start | bytes 1572868
  36.0 12.6 %copy-start.2 = (bf16[512,512]{1,0:T(8,128)(2,1)S(1)}, bf16[512,512]{1,0:T(8,128)(2,1)}, u32[]{:S(2)}) copy-start(bf16[512,512]{1,0:T(8,128)(2,1)} %refs_5_.1) | copy-start | bytes 1572868
  36.1 12.6 %copy-start.4 = (bf16[512,512]{1,0:T(8,128)(2,1)S(1)}, bf16[512,512]{1,0:T(8,128)(2,1)}, u32[]{:S(2)}) copy-start(bf16[512,512]{1,0:T(8,128)(2,1)} %refs_6_.1) | copy-start | bytes 1572868
  36.1 12.6 %copy-start.6 = (bf16[512,512]{1,0:T(8,128)(2,1)S(1)}, bf16[512,512]{1,0:T(8,128)(2,1)}, u32[]{:S(2)}) copy-start(bf16[512,512]{1,0:T(8,128)(2,1)} %refs_7_.1) | copy-start | bytes 1572868
  36.1 12.6 %copy-start.8 = (bf16[512,512]{1,0:T(8,128)(2,1)S(1)}, bf16[512,512]{1,0:T(8,128)(2,1)}, u32[]{:S(2)}) copy-start(bf16[512,512]{1,0:T(8,128)(2,1)} %refs_8_.1) | copy-start | bytes 1572868
  47.1 8.8 %collective-permute-start.1 = (bf16[512,512]{1,0:T(8,128)(2,1)S(1)}, bf16[512,512]{1,0:T(8,128)(2,1)S(1)}, u32[]{:S(2)}, u32[]{:S(2)}) collective-permute-start(bf16[512,512]{1,0:T(8,128)(2,1)S(1)} %get-tuple-element.66), channel_id=1, source_target_pairs={{1,0},{2,1},{3,2},{4,3},{5,4},{6,5},{7,6},{9,8},{10,9},{11,10},{12... | collective-permute-start | bytes 1572872 | tf_op jit(solution)/shard_map/ppermute | solution.py:354
  55.9 31.1 %copy-start.15 = (s32[512]{0:T(512)S(1)}, s32[512]{0:T(512)}, u32[]{:S(2)}) copy-start(s32[512]{0:T(512)} %param.10) | copy-start | bytes 6148
  56.8 6.4 %collective-permute-start.2 = (bf16[256,2048]{1,0:T(8,128)(2,1)}, bf16[256,2048]{1,0:T(8,128)(2,1)}, u32[]{:S(2)}, u32[]{:S(2)}) collective-permute-start(bf16[256,2048]{1,0:T(8,128)(2,1)} %get-tuple-element.72), channel_id=1, source_target_pairs={{0,1},{1,0},{2,3},{3,2},{4,5},{5,4},{6,7},{7,6},{8,9},{9,8},{10,11... | collective-permute-start | bytes 3145736 | tf_op jit(solution)/shard_map/ppermute | solution.py:472
  59.5 1.0 %copy-start.10 = (bf16[512,512]{1,0:T(8,128)(2,1)S(1)}, bf16[512,512]{1,0:T(8,128)(2,1)}, u32[]{:S(2)}) copy-start(bf16[512,512]{1,0:T(8,128)(2,1)} %copy-done.9) | copy-start | bytes 1572868
  60.5 1.0 %copy-start.12 = (bf16[512,512]{1,0:T(8,128)(2,1)S(1)}, bf16[512,512]{1,0:T(8,128)(2,1)}, u32[]{:S(2)}) copy-start(bf16[512,512]{1,0:T(8,128)(2,1)} %copy-done.11) | copy-start | bytes 1572868
  64.8 9.2 %collective-permute-start.3 = (bf16[64,2048]{1,0:T(8,128)(2,1)S(1)}, bf16[64,2048]{1,0:T(8,128)(2,1)S(1)}, u32[]{:S(2)}, u32[]{:S(2)}) collective-permute-start(bf16[64,2048]{1,0:T(8,128)(2,1)S(1)} %get-tuple-element.74), channel_id=1, source_target_pairs={{0,8},{8,0},{16,24},{24,16},{1,9},{9,1},{17,25},{25,17},{2,10},{10... | collective-permute-start | bytes 786440 | tf_op jit(solution)/shard_map/ppermute | solution.py:378
  65.7 15.7 %collective-permute-start.4 = (bf16[64,2048]{1,0:T(8,128)(2,1)S(1)}, bf16[64,2048]{1,0:T(8,128)(2,1)S(1)}, u32[]{:S(2)}, u32[]{:S(2)}) collective-permute-start(bf16[64,2048]{1,0:T(8,128)(2,1)S(1)} %get-tuple-element.75), channel_id=1, source_target_pairs={{0,16},{8,24},{16,0},{24,8},{1,17},{9,25},{17,1},{25,9},{2,18},{10... | collective-permute-start | bytes 786440 | tf_op jit(solution)/shard_map/ppermute | solution.py:378
  66.2 16.2 %collective-permute-start.5 = (bf16[64,2048]{1,0:T(8,128)(2,1)S(1)}, bf16[64,2048]{1,0:T(8,128)(2,1)S(1)}, u32[]{:S(2)}, u32[]{:S(2)}) collective-permute-start(bf16[64,2048]{1,0:T(8,128)(2,1)S(1)} %get-tuple-element.76), channel_id=1, source_target_pairs={{0,24},{8,16},{16,8},{24,0},{1,25},{9,17},{17,9},{25,1},{2,26},{10... | collective-permute-start | bytes 786440 | tf_op jit(solution)/shard_map/ppermute | solution.py:378
  68.3 20.5 %all-to-all-start.1 = ((bf16[32,16,512]{2,1,0:T(8,128)(2,1)}), bf16[32,16,512]{2,1,0:T(8,128)(2,1)S(1)}, u32[]{:S(2)}, u32[]{:S(2)}) async-start(bf16[32,16,512]{2,1,0:T(8,128)(2,1)} %bitcast.8), calls=%async_computation.1 | async-start | bytes 1048576 | tf_op jit(solution)/shard_map/all_to_all | solution.py:403
  82.6 7.5 %collective-permute-start.6 = (bf16[16,2048]{1,0:T(8,128)(2,1)S(1)}, bf16[16,2048]{1,0:T(8,128)(2,1)S(1)}, u32[]{:S(2)}, u32[]{:S(2)}) collective-permute-start(bf16[16,2048]{1,0:T(8,128)(2,1)S(1)} %get-tuple-element.78), channel_id=1, source_target_pairs={{0,2},{1,3},{2,0},{3,1},{4,6},{5,7},{6,4},{7,5},{8,10},{9,11},{10,... | collective-permute-start | bytes 196616 | tf_op jit(solution)/shard_map/ppermute | solution.py:378
  84.1 6.7 %collective-permute-start.7 = (bf16[16,2048]{1,0:T(8,128)(2,1)S(1)}, bf16[16,2048]{1,0:T(8,128)(2,1)S(1)}, u32[]{:S(2)}, u32[]{:S(2)}) collective-permute-start(bf16[16,2048]{1,0:T(8,128)(2,1)S(1)} %get-tuple-element.79), channel_id=1, source_target_pairs={{0,4},{1,5},{2,6},{3,7},{4,0},{5,1},{6,2},{7,3},{8,12},{9,13},{10,... | collective-permute-start | bytes 196616 | tf_op jit(solution)/shard_map/ppermute | solution.py:378
  85.6 6.2 %collective-permute-start.8 = (bf16[16,2048]{1,0:T(8,128)(2,1)S(1)}, bf16[16,2048]{1,0:T(8,128)(2,1)S(1)}, u32[]{:S(2)}, u32[]{:S(2)}) collective-permute-start(bf16[16,2048]{1,0:T(8,128)(2,1)S(1)} %get-tuple-element.80), channel_id=1, source_target_pairs={{0,6},{1,7},{2,4},{3,5},{4,2},{5,3},{6,0},{7,1},{8,14},{9,15},{10,... | collective-permute-start | bytes 196616 | tf_op jit(solution)/shard_map/ppermute | solution.py:378
  (3 other events, 2.3 us)

commit v14 on v13

--- a/solution.py
+++ b/solution.py
@@ -260,7 +260,7 @@
     for copy in copies:
         copy.wait()
     dot_ref[...] = mm(cot_ref[...], wo_ref[...], NT).astype(BF).T
-    lax.fori_loop(0, width // pair, one_pair, 0, unroll=2)
+    lax.fori_loop(0, width // pair, one_pair, 0, unroll=4)
     back_ref[...] = (mm(dkh_ref[...], wk_ref[...], NT) + mm(dvh_ref[...], wv_ref[...], NT)).astype(BF)
 
 
@@ -306,7 +306,7 @@
                 out[j * TILE : (j + 1) * TILE, cols] = (total * factor).astype(BF)
         return carry
 
-    lax.fori_loop(0, width // pair, one_pair, 0, unroll=2)
+    lax.fori_loop(0, width // pair, one_pair, 0, unroll=4)
 
     for copy in copies:
         copy.wait()

time: 93.1 us -> 92.3 us (level)
  transfers between devices with their start and end apart: 11 -> 11, of which waited for: 7 -> 7; matrix products, arithmetic and copies ran while one was open for 1% -> 1% of each run, Pallas kernels for 15% -> 14%
where the time goes in v14:
time: 92.3 us; the launch traced here: 91.7 us
  Pallas kernels  27.5 us (30%)
  waiting for transfers between devices  27.5 us (30%)
  starting transfers between devices  24.9 us (27%)
  local copies, waits for them, and re-layouts  9.46 us (10%)
  between operations  1.54 us (2%)
    pallas_call x11, Pallas kernels, vmem_call(): pl.pallas_call(body, out_shape=tuple(outs), in_specs=[pl.BlockSpec(memory...  27.5 us
    all_to_all x2, waiting for transfers between devices, exchanged(): lax.all_to_all(shard.reshape(devices, slots, width), AXES, split_axis=0,...  14.6 us
    ppermute x6, waiting for transfers between devices, swapped(): lax.ppermute(piece, axis, [(i, i ^ k * step) for i in range(count)])  12.9 us
    all_to_all x2, starting transfers between devices, exchanged(): lax.all_to_all(shard.reshape(devices, slots, width), AXES, split_axis=0,...  10.4 us
    unnamed x32, local copies, waits for them, and re-layouts  8.64 us
    ppermute x6, starting transfers between devices, swapped(): lax.ppermute(piece, axis, [(i, i ^ k * step) for i in range(count)])  8.01 us
    ppermute x2, starting transfers between devices, passed_along(): return lax.ppermute(shard, 'seq', pairs)  3.42 us
    ppermute x1, starting transfers between devices, shards(): got = lax.ppermute(send, 'seq', [(i, i ^ 1) for i in range(seqs)])  3.01 us
  transfers between devices with their start and end apart: 11, of which 7 were waited for; matrix products, arithmetic and copies ran while one was open for 1% of the time, Pallas kernels for 14%

profile of v14, /device:TPU:0, one launch (start us, length us, event | category | flops | bytes accessed | tf_op | source)
XLA Modules:
  0.0 91.7 jit_solution(9006944062358321839)
XLA Ops:
  0.7 1.1 %copy-done.13 = bf16[512,512]{1,0:T(8,128)(2,1)S(1)} copy-done((bf16[512,512]{1,0:T(8,128)(2,1)S(1)}, bf16[512,512]{1,0:T(8,128)(2,1)}, u32[]{:S(2)}) %copy-start.13) | copy-done | bytes 524312
  2.5 1.6 %shard_map.113 = bf16[512,512]{1,0:T(8,128)(2,1)} custom-call(s32[1,512]{1,0:T(1,128)S(1)} %bitcast.28, bf16[512,512]{1,0:T(8,128)(2,1)S(1)} %copy-done.13), custom_call_target="tpu_custom_call" | custom-call | flops 268435456 | bytes 1050624 | tf_op jit(solution)/shard_map/pallas_call | solution.py:38
  4.0 7.3 %all-to-all-start = ((bf16[32,16,512]{2,1,0:T(8,128)(2,1)}), bf16[32,16,512]{2,1,0:T(8,128)(2,1)S(1)}, u32[]{:S(2)}, u32[]{:S(2)}) async-start(bf16[32,16,512]{2,1,0:T(8,128)(2,1)} %bitcast.4), calls=%async_computation | async-start | bytes 1048576 | tf_op jit(solution)/shard_map/all_to_all | solution.py:403
  14.0 13.7 %all-to-all-done = bf16[32,16,512]{2,1,0:T(8,128)(2,1)S(1)} async-done(((bf16[32,16,512]{2,1,0:T(8,128)(2,1)}), bf16[32,16,512]{2,1,0:T(8,128)(2,1)S(1)}, u32[]{:S(2)}, u32[]{:S(2)}) %all-to-all-start) | async-done | bytes 524320 | tf_op jit(solution)/shard_map/all_to_all | solution.py:403
  28.3 1.9 %collective-permute-start = (bf16[512,512]{1,0:T(8,128)(2,1)S(1)}, bf16[512,512]{1,0:T(8,128)(2,1)S(1)}, u32[]{:S(2)}, u32[]{:S(2)}) collective-permute-start(bf16[512,512]{1,0:T(8,128)(2,1)S(1)} %get-tuple-element.43.refs_0_), channel_id=1, source_target_pairs={{0,1},{1,2},{2,3},{3,4},{4,5},{5,6},{6,7},{8,9},{9,10},{10,11},{11... | collective-permute-start | bytes 1572872 | tf_op jit(solution)/shard_map/ppermute | solution.py:354
  31.0 1.0 %copy-done.1 = bf16[512,512]{1,0:T(8,128)(2,1)S(1)} copy-done((bf16[512,512]{1,0:T(8,128)(2,1)S(1)}, bf16[512,512]{1,0:T(8,128)(2,1)}, u32[]{:S(2)}) %copy-start.1) | copy-done | bytes 524312
  32.1 1.0 %copy-done.3 = bf16[512,512]{1,0:T(8,128)(2,1)S(1)} copy-done((bf16[512,512]{1,0:T(8,128)(2,1)S(1)}, bf16[512,512]{1,0:T(8,128)(2,1)}, u32[]{:S(2)}) %copy-start.3) | copy-done | bytes 524312
  34.1 1.9 %shard_map.115 = (bf16[512,512]{1,0:T(8,128)(2,1)S(1)}, bf16[512,512]{1,0:T(8,128)(2,1)S(1)}, bf16[512,512]{1,0:T(8,128)(2,1)S(1)}, bf16[512,512]{1,0:T(8,128)(2...) custom-call(bf16[512,512]{1,0:T(8,128)(2,1)S(1)} %get-tuple-element., ...), custom_call_target="tpu_custom_call" | custom-call | flops 805306368 | bytes 6291456 | tf_op jit(solution)/shard_map/pallas_call | solution.py:38
  36.1 10.5 %shard_map.116 = (bf16[16,640,256]{2,1,0:T(8,128)(2,1)S(1)}, bf16[16,640,256]{2,1,0:T(8,128)(2,1)S(1)}, f32[16,1,256]{2,1,0:T(1,128)S(1)}, bf16[512,512]{1,0:T(8...) custom-call(s32[3]{0:T(128)S(1)} %pad_add_fusion.refs_0_, ...), custom_call_target="tpu_custom_call" | custom-call | flops 3221225472 | bytes 19415052 | tf_op jit(solution)/shard_map/pallas_call | solution.py:38
  46.6 1.5 %collective-permute-start.1 = (bf16[512,512]{1,0:T(8,128)(2,1)S(1)}, bf16[512,512]{1,0:T(8,128)(2,1)S(1)}, u32[]{:S(2)}, u32[]{:S(2)}) collective-permute-start(bf16[512,512]{1,0:T(8,128)(2,1)S(1)} %get-tuple-element.66), channel_id=1, source_target_pairs={{1,0},{2,1},{3,2},{4,3},{5,4},{6,5},{7,6},{9,8},{10,9},{11,10},{12... | collective-permute-start | bytes 1572872 | tf_op jit(solution)/shard_map/ppermute | solution.py:354
  48.1 7.0 %shard_map.117 = (bf16[256,2048]{1,0:T(8,128)(2,1)S(1)}, bf16[256,2048]{1,0:T(8,128)(2,1)}, bf16[512,512]{1,0:T(8,128)(2,1)}, f32[512,512]{1,0:T(8,128)S(1)}) custom-call(s32[3]{0:T(128)S(1)} %pad_add_fusion.refs_0_, bf16[512,512]{1,0:T(8,128)(2,1)S(1)} %get-tuple-element.44.refs_1_, bf16[512,512]{1,0:T(8,128)(2,1)S(1)} %get-tuple-element.51.refs_2_, ...), custom_call_target="tpu_custom_call" | custom-call | flops 4831838208 | bytes 22036492 | tf_op jit(solution)/shard_map/pallas_call | solution.py:38
  55.9 3.0 %collective-permute-start.2 = (bf16[256,2048]{1,0:T(8,128)(2,1)}, bf16[256,2048]{1,0:T(8,128)(2,1)}, u32[]{:S(2)}, u32[]{:S(2)}) collective-permute-start(bf16[256,2048]{1,0:T(8,128)(2,1)} %get-tuple-element.72), channel_id=1, source_target_pairs={{0,1},{1,0},{2,3},{3,2},{4,5},{5,4},{6,7},{7,6},{8,9},{9,8},{10,11... | collective-permute-start | bytes 3145736 | tf_op jit(solution)/shard_map/ppermute | solution.py:472
  58.9 1.0 %copy-done.10 = bf16[512,512]{1,0:T(8,128)(2,1)S(1)} copy-done((bf16[512,512]{1,0:T(8,128)(2,1)S(1)}, bf16[512,512]{1,0:T(8,128)(2,1)}, u32[]{:S(2)}) %copy-start.10) | copy-done | bytes 524312
  61.0 1.6 %shard_map.118.refs_3_ = bf16[512,512]{1,0:T(8,128)(2,1)} custom-call(bf16[512,512]{1,0:T(8,128)(2,1)S(1)} %get-tuple-element.52.refs_3_.refs_0_, f32[512,512]{1,0:T(8,128)S(1)} %get-tuple-element.64.refs_1_, bf16[512,512]{1,0:T(8,128)(2,1)S(1)} %copy-done.12, bf16[512,512]{1,0:T(8,128)(2,1)S(1)} %bitcast.20, bf16[512,512]{1,0:T(8,128)(2,1)S(1)} %copy-done.10), custom_call_target="tpu_custom_call" | custom-call | flops 268435456 | bytes 3670016 | tf_op jit(solution)/shard_map/pallas_call | solution.py:38
  62.6 1.6 %shard_map.121 = (bf16[64,2048]{1,0:T(8,128)(2,1)S(1)}, bf16[64,2048]{1,0:T(8,128)(2,1)S(1)}, bf16[64,2048]{1,0:T(8,128)(2,1)S(1)}, bf16[64,2048]{1,0:T(8,128)(2,1)S(1)}) custom-call(s32[1]{0:T(128)} %bitcast.11.refs_0_, bf16[4,64,2048]{2,1,0:T(8,128)(2,1)S(1)} %bitcast.23, bf16[4,64,2048]{2,1,0:T(8,128)(2,1)} %bitcast.13.refs_2_, ...), custom_call_target="tpu_custom_call" | custom-call | bytes 3670020 | tf_op jit(solution)/shard_map/pallas_call | solution.py:38
  65.7 2.1 %collective-permute-start.5 = (bf16[64,2048]{1,0:T(8,128)(2,1)S(1)}, bf16[64,2048]{1,0:T(8,128)(2,1)S(1)}, u32[]{:S(2)}, u32[]{:S(2)}) collective-permute-start(bf16[64,2048]{1,0:T(8,128)(2,1)S(1)} %get-tuple-element.76), channel_id=1, source_target_pairs={{0,24},{8,16},{16,8},{24,0},{1,25},{9,17},{17,9},{25,1},{2,26},{10... | collective-permute-start | bytes 786440 | tf_op jit(solution)/shard_map/ppermute | solution.py:378
  67.8 3.1 %all-to-all-start.1 = ((bf16[32,16,512]{2,1,0:T(8,128)(2,1)}), bf16[32,16,512]{2,1,0:T(8,128)(2,1)S(1)}, u32[]{:S(2)}, u32[]{:S(2)}) async-start(bf16[32,16,512]{2,1,0:T(8,128)(2,1)} %bitcast.8), calls=%async_computation.1 | async-start | bytes 1048576 | tf_op jit(solution)/shard_map/all_to_all | solution.py:403
  70.9 2.5 %collective-permute-done.3 = bf16[64,2048]{1,0:T(8,128)(2,1)S(1)} collective-permute-done((bf16[64,2048]{1,0:T(8,128)(2,1)S(1)}, bf16[64,2048]{1,0:T(8,128)(2,1)S(1)}, u32[]{:S(2)}, u32[]{:S(2)}) %collective-permute-start.3) | collective-permute-done | bytes 262176 | tf_op jit(solution)/shard_map/ppermute | solution.py:378
  73.4 7.6 %collective-permute-done.4 = bf16[64,2048]{1,0:T(8,128)(2,1)S(1)} collective-permute-done((bf16[64,2048]{1,0:T(8,128)(2,1)S(1)}, bf16[64,2048]{1,0:T(8,128)(2,1)S(1)}, u32[]{:S(2)}, u32[]{:S(2)}) %collective-permute-start.4) | collective-permute-done | bytes 262176 | tf_op jit(solution)/shard_map/ppermute | solution.py:378
  82.1 1.1 %collective-permute-start.6 = (bf16[16,2048]{1,0:T(8,128)(2,1)S(1)}, bf16[16,2048]{1,0:T(8,128)(2,1)S(1)}, u32[]{:S(2)}, u32[]{:S(2)}) collective-permute-start(bf16[16,2048]{1,0:T(8,128)(2,1)S(1)} %get-tuple-element.78), channel_id=1, source_target_pairs={{0,2},{1,3},{2,0},{3,1},{4,6},{5,7},{6,4},{7,5},{8,10},{9,11},{10,... | collective-permute-start | bytes 196616 | tf_op jit(solution)/shard_map/ppermute | solution.py:378
  83.2 1.6 %collective-permute-start.7 = (bf16[16,2048]{1,0:T(8,128)(2,1)S(1)}, bf16[16,2048]{1,0:T(8,128)(2,1)S(1)}, u32[]{:S(2)}, u32[]{:S(2)}) collective-permute-start(bf16[16,2048]{1,0:T(8,128)(2,1)S(1)} %get-tuple-element.79), channel_id=1, source_target_pairs={{0,4},{1,5},{2,6},{3,7},{4,0},{5,1},{6,2},{7,3},{8,12},{9,13},{10,... | collective-permute-start | bytes 196616 | tf_op jit(solution)/shard_map/ppermute | solution.py:378
  84.8 1.8 %collective-permute-start.8 = (bf16[16,2048]{1,0:T(8,128)(2,1)S(1)}, bf16[16,2048]{1,0:T(8,128)(2,1)S(1)}, u32[]{:S(2)}, u32[]{:S(2)}) collective-permute-start(bf16[16,2048]{1,0:T(8,128)(2,1)S(1)} %get-tuple-element.80), channel_id=1, source_target_pairs={{0,6},{1,7},{2,4},{3,5},{4,2},{5,3},{6,0},{7,1},{8,14},{9,15},{10,... | collective-permute-start | bytes 196616 | tf_op jit(solution)/shard_map/ppermute | solution.py:378
  88.0 1.2 %shard_map.120 = bf16[512,512]{1,0:T(8,128)(2,1)} custom-call(bf16[512,512]{1,0:T(8,128)(2,1)S(1)} %shard_map.119.refs_0_, bf16[512,512]{1,0:T(8,128)(2,1)S(1)} %bitcast.21), custom_call_target="tpu_custom_call" | custom-call | flops 268435456 | bytes 1572864 | tf_op jit(solution)/shard_map/pallas_call | solution.py:38
  89.9 1.1 %collective-permute-done.8 = bf16[16,2048]{1,0:T(8,128)(2,1)S(1)} collective-permute-done((bf16[16,2048]{1,0:T(8,128)(2,1)S(1)}, bf16[16,2048]{1,0:T(8,128)(2,1)S(1)}, u32[]{:S(2)}, u32[]{:S(2)}) %collective-permute-start.8) | collective-permute-done | bytes 65568 | tf_op jit(solution)/shard_map/ppermute | solution.py:378
  (44 shorter events, 12.2 us)
Async XLA Ops:
  0.6 35.4 %copy-start.7 = (bf16[512,512]{1,0:T(8,128)(2,1)S(1)}, bf16[512,512]{1,0:T(8,128)(2,1)}, u32[]{:S(2)}) copy-start(bf16[512,512]{1,0:T(8,128)(2,1)} %refs_8_.1) | copy-start | bytes 1572868
  0.6 35.4 %copy-start = (bf16[1,512,512]{2,1,0:T(8,128)(2,1)S(1)}, bf16[1,512,512]{2,1,0:T(8,128)(2,1)}, u32[]{:S(2)}) copy-start(bf16[1,512,512]{2,1,0:T(8,128)(2,1)} %param.17) | copy-start | bytes 1572868
  0.7 1.1 %copy-start.13 = (bf16[512,512]{1,0:T(8,128)(2,1)S(1)}, bf16[512,512]{1,0:T(8,128)(2,1)}, u32[]{:S(2)}) copy-start(bf16[512,512]{1,0:T(8,128)(2,1)} %refs_1_.2) | copy-start | bytes 1572868
  4.0 23.7 %all-to-all-start = ((bf16[32,16,512]{2,1,0:T(8,128)(2,1)}), bf16[32,16,512]{2,1,0:T(8,128)(2,1)S(1)}, u32[]{:S(2)}, u32[]{:S(2)}) async-start(bf16[32,16,512]{2,1,0:T(8,128)(2,1)} %bitcast.4), calls=%async_computation | async-start | bytes 1048576 | tf_op jit(solution)/shard_map/all_to_all | solution.py:403
  28.3 7.7 %collective-permute-start = (bf16[512,512]{1,0:T(8,128)(2,1)S(1)}, bf16[512,512]{1,0:T(8,128)(2,1)S(1)}, u32[]{:S(2)}, u32[]{:S(2)}) collective-permute-start(bf16[512,512]{1,0:T(8,128)(2,1)S(1)} %get-tuple-element.43.refs_0_), channel_id=1, source_target_pairs={{0,1},{1,2},{2,3},{3,4},{4,5},{5,6},{6,7},{8,9},{9,10},{10,11},{11... | collective-permute-start | bytes 1572872 | tf_op jit(solution)/shard_map/ppermute | solution.py:354
  31.0 1.0 %copy-start.1 = (bf16[512,512]{1,0:T(8,128)(2,1)S(1)}, bf16[512,512]{1,0:T(8,128)(2,1)}, u32[]{:S(2)}) copy-start(bf16[512,512]{1,0:T(8,128)(2,1)} %refs_5_.1) | copy-start | bytes 1572868
  32.1 1.0 %copy-start.3 = (bf16[512,512]{1,0:T(8,128)(2,1)S(1)}, bf16[512,512]{1,0:T(8,128)(2,1)}, u32[]{:S(2)}) copy-start(bf16[512,512]{1,0:T(8,128)(2,1)} %refs_6_.1) | copy-start | bytes 1572868
  33.1 1.0 %copy-start.5 = (bf16[512,512]{1,0:T(8,128)(2,1)S(1)}, bf16[512,512]{1,0:T(8,128)(2,1)}, u32[]{:S(2)}) copy-start(bf16[512,512]{1,0:T(8,128)(2,1)} %refs_7_.1) | copy-start | bytes 1572868
  36.0 12.0 %copy-start.2 = (bf16[512,512]{1,0:T(8,128)(2,1)S(1)}, bf16[512,512]{1,0:T(8,128)(2,1)}, u32[]{:S(2)}) copy-start(bf16[512,512]{1,0:T(8,128)(2,1)} %refs_5_.1) | copy-start | bytes 1572868
  36.1 12.0 %copy-start.4 = (bf16[512,512]{1,0:T(8,128)(2,1)S(1)}, bf16[512,512]{1,0:T(8,128)(2,1)}, u32[]{:S(2)}) copy-start(bf16[512,512]{1,0:T(8,128)(2,1)} %refs_6_.1) | copy-start | bytes 1572868
  36.1 12.0 %copy-start.6 = (bf16[512,512]{1,0:T(8,128)(2,1)S(1)}, bf16[512,512]{1,0:T(8,128)(2,1)}, u32[]{:S(2)}) copy-start(bf16[512,512]{1,0:T(8,128)(2,1)} %refs_7_.1) | copy-start | bytes 1572868
  36.1 12.0 %copy-start.8 = (bf16[512,512]{1,0:T(8,128)(2,1)S(1)}, bf16[512,512]{1,0:T(8,128)(2,1)}, u32[]{:S(2)}) copy-start(bf16[512,512]{1,0:T(8,128)(2,1)} %refs_8_.1) | copy-start | bytes 1572868
  46.6 8.5 %collective-permute-start.1 = (bf16[512,512]{1,0:T(8,128)(2,1)S(1)}, bf16[512,512]{1,0:T(8,128)(2,1)S(1)}, u32[]{:S(2)}, u32[]{:S(2)}) collective-permute-start(bf16[512,512]{1,0:T(8,128)(2,1)S(1)} %get-tuple-element.66), channel_id=1, source_target_pairs={{1,0},{2,1},{3,2},{4,3},{5,4},{6,5},{7,6},{9,8},{10,9},{11,10},{12... | collective-permute-start | bytes 1572872 | tf_op jit(solution)/shard_map/ppermute | solution.py:354
  55.1 31.5 %copy-start.15 = (s32[512]{0:T(512)S(1)}, s32[512]{0:T(512)}, u32[]{:S(2)}) copy-start(s32[512]{0:T(512)} %param.10) | copy-start | bytes 6148
  55.9 6.7 %collective-permute-start.2 = (bf16[256,2048]{1,0:T(8,128)(2,1)}, bf16[256,2048]{1,0:T(8,128)(2,1)}, u32[]{:S(2)}, u32[]{:S(2)}) collective-permute-start(bf16[256,2048]{1,0:T(8,128)(2,1)} %get-tuple-element.72), channel_id=1, source_target_pairs={{0,1},{1,0},{2,3},{3,2},{4,5},{5,4},{6,7},{7,6},{8,9},{9,8},{10,11... | collective-permute-start | bytes 3145736 | tf_op jit(solution)/shard_map/ppermute | solution.py:472
  58.9 1.0 %copy-start.10 = (bf16[512,512]{1,0:T(8,128)(2,1)S(1)}, bf16[512,512]{1,0:T(8,128)(2,1)}, u32[]{:S(2)}) copy-start(bf16[512,512]{1,0:T(8,128)(2,1)} %copy-done.9) | copy-start | bytes 1572868
  60.0 1.0 %copy-start.12 = (bf16[512,512]{1,0:T(8,128)(2,1)S(1)}, bf16[512,512]{1,0:T(8,128)(2,1)}, u32[]{:S(2)}) copy-start(bf16[512,512]{1,0:T(8,128)(2,1)} %copy-done.11) | copy-start | bytes 1572868
  64.2 9.2 %collective-permute-start.3 = (bf16[64,2048]{1,0:T(8,128)(2,1)S(1)}, bf16[64,2048]{1,0:T(8,128)(2,1)S(1)}, u32[]{:S(2)}, u32[]{:S(2)}) collective-permute-start(bf16[64,2048]{1,0:T(8,128)(2,1)S(1)} %get-tuple-element.74), channel_id=1, source_target_pairs={{0,8},{8,0},{16,24},{24,16},{1,9},{9,1},{17,25},{25,17},{2,10},{10... | collective-permute-start | bytes 786440 | tf_op jit(solution)/shard_map/ppermute | solution.py:378
  65.1 16.0 %collective-permute-start.4 = (bf16[64,2048]{1,0:T(8,128)(2,1)S(1)}, bf16[64,2048]{1,0:T(8,128)(2,1)S(1)}, u32[]{:S(2)}, u32[]{:S(2)}) collective-permute-start(bf16[64,2048]{1,0:T(8,128)(2,1)S(1)} %get-tuple-element.75), channel_id=1, source_target_pairs={{0,16},{8,24},{16,0},{24,8},{1,17},{9,25},{17,1},{25,9},{2,18},{10... | collective-permute-start | bytes 786440 | tf_op jit(solution)/shard_map/ppermute | solution.py:378
  65.7 16.3 %collective-permute-start.5 = (bf16[64,2048]{1,0:T(8,128)(2,1)S(1)}, bf16[64,2048]{1,0:T(8,128)(2,1)S(1)}, u32[]{:S(2)}, u32[]{:S(2)}) collective-permute-start(bf16[64,2048]{1,0:T(8,128)(2,1)S(1)} %get-tuple-element.76), channel_id=1, source_target_pairs={{0,24},{8,16},{16,8},{24,0},{1,25},{9,17},{17,9},{25,1},{2,26},{10... | collective-permute-start | bytes 786440 | tf_op jit(solution)/shard_map/ppermute | solution.py:378
  67.8 20.2 %all-to-all-start.1 = ((bf16[32,16,512]{2,1,0:T(8,128)(2,1)}), bf16[32,16,512]{2,1,0:T(8,128)(2,1)S(1)}, u32[]{:S(2)}, u32[]{:S(2)}) async-start(bf16[32,16,512]{2,1,0:T(8,128)(2,1)} %bitcast.8), calls=%async_computation.1 | async-start | bytes 1048576 | tf_op jit(solution)/shard_map/all_to_all | solution.py:403
  82.1 7.1 %collective-permute-start.6 = (bf16[16,2048]{1,0:T(8,128)(2,1)S(1)}, bf16[16,2048]{1,0:T(8,128)(2,1)S(1)}, u32[]{:S(2)}, u32[]{:S(2)}) collective-permute-start(bf16[16,2048]{1,0:T(8,128)(2,1)S(1)} %get-tuple-element.78), channel_id=1, source_target_pairs={{0,2},{1,3},{2,0},{3,1},{4,6},{5,7},{6,4},{7,5},{8,10},{9,11},{10,... | collective-permute-start | bytes 196616 | tf_op jit(solution)/shard_map/ppermute | solution.py:378
  83.2 6.7 %collective-permute-start.7 = (bf16[16,2048]{1,0:T(8,128)(2,1)S(1)}, bf16[16,2048]{1,0:T(8,128)(2,1)S(1)}, u32[]{:S(2)}, u32[]{:S(2)}) collective-permute-start(bf16[16,2048]{1,0:T(8,128)(2,1)S(1)} %get-tuple-element.79), channel_id=1, source_target_pairs={{0,4},{1,5},{2,6},{3,7},{4,0},{5,1},{6,2},{7,3},{8,12},{9,13},{10,... | collective-permute-start | bytes 196616 | tf_op jit(solution)/shard_map/ppermute | solution.py:378
  84.8 6.2 %collective-permute-start.8 = (bf16[16,2048]{1,0:T(8,128)(2,1)S(1)}, bf16[16,2048]{1,0:T(8,128)(2,1)S(1)}, u32[]{:S(2)}, u32[]{:S(2)}) collective-permute-start(bf16[16,2048]{1,0:T(8,128)(2,1)S(1)} %get-tuple-element.80), channel_id=1, source_target_pairs={{0,6},{1,7},{2,4},{3,5},{4,2},{5,3},{6,0},{7,1},{8,14},{9,15},{10,... | collective-permute-start | bytes 196616 | tf_op jit(solution)/shard_map/ppermute | solution.py:378
  (3 other events, 2.3 us)

commit v15 on v14

--- a/solution.py
+++ b/solution.py
@@ -241,9 +241,9 @@
         waiting = None
         for a in range(tiles):
             ahead = multiply(a + 1) if a + 1 < tiles else None
-            mixed = raise_and_mix(a, scores)
             if waiting is not None:
                 finish(*waiting)
+            mixed = raise_and_mix(a, scores)
             waiting = (a, slopes, *mixed)
             if ahead is not None:
                 scores, slopes = ahead

time: 92.3 us -> 93.5 us (1.013)
  Pallas kernels: 27.5 us -> 28.8 us
    pallas_call x11, Pallas kernels: 27.5 us -> 28.8 us  [vmem_call(): pl.pallas_call(body, out_shape=tuple(outs), in_specs=[pl.BlockSpec(memory...]
where the time goes in v15:
time: 93.5 us; the launch traced here: 92.9 us
  Pallas kernels  28.8 us (31%)
  waiting for transfers between devices  27.5 us (29%)
  starting transfers between devices  24.9 us (27%)
  local copies, waits for them, and re-layouts  9.46 us (10%)
  between operations  1.54 us (2%)
    pallas_call x11, Pallas kernels, vmem_call(): pl.pallas_call(body, out_shape=tuple(outs), in_specs=[pl.BlockSpec(memory...  28.8 us
    all_to_all x2, waiting for transfers between devices, exchanged(): lax.all_to_all(shard.reshape(devices, slots, width), AXES, split_axis=0,...  14.6 us
    ppermute x6, waiting for transfers between devices, swapped(): lax.ppermute(piece, axis, [(i, i ^ k * step) for i in range(count)])  12.9 us
    all_to_all x2, starting transfers between devices, exchanged(): lax.all_to_all(shard.reshape(devices, slots, width), AXES, split_axis=0,...  10.4 us
    unnamed x32, local copies, waits for them, and re-layouts  8.64 us
    ppermute x6, starting transfers between devices, swapped(): lax.ppermute(piece, axis, [(i, i ^ k * step) for i in range(count)])  8.01 us
    ppermute x2, starting transfers between devices, passed_along(): return lax.ppermute(shard, 'seq', pairs)  3.42 us
    ppermute x1, starting transfers between devices, shards(): got = lax.ppermute(send, 'seq', [(i, i ^ 1) for i in range(seqs)])  3.01 us
  transfers between devices with their start and end apart: 11, of which 7 were waited for; matrix products, arithmetic and copies ran while one was open for 1% of the time, Pallas kernels for 14%

profile of v15, /device:TPU:0, one launch (start us, length us, event | category | flops | bytes accessed | tf_op | source)
XLA Modules:
  0.0 92.9 jit_solution(626275358658342113)
XLA Ops:
  0.7 1.1 %copy-done.13 = bf16[512,512]{1,0:T(8,128)(2,1)S(1)} copy-done((bf16[512,512]{1,0:T(8,128)(2,1)S(1)}, bf16[512,512]{1,0:T(8,128)(2,1)}, u32[]{:S(2)}) %copy-start.13) | copy-done | bytes 524312
  2.5 1.6 %shard_map.113 = bf16[512,512]{1,0:T(8,128)(2,1)} custom-call(s32[1,512]{1,0:T(1,128)S(1)} %bitcast.28, bf16[512,512]{1,0:T(8,128)(2,1)S(1)} %copy-done.13), custom_call_target="tpu_custom_call" | custom-call | flops 268435456 | bytes 1050624 | tf_op jit(solution)/shard_map/pallas_call | solution.py:38
  4.0 7.3 %all-to-all-start = ((bf16[32,16,512]{2,1,0:T(8,128)(2,1)}), bf16[32,16,512]{2,1,0:T(8,128)(2,1)S(1)}, u32[]{:S(2)}, u32[]{:S(2)}) async-start(bf16[32,16,512]{2,1,0:T(8,128)(2,1)} %bitcast.4), calls=%async_computation | async-start | bytes 1048576 | tf_op jit(solution)/shard_map/all_to_all | solution.py:403
  14.0 13.7 %all-to-all-done = bf16[32,16,512]{2,1,0:T(8,128)(2,1)S(1)} async-done(((bf16[32,16,512]{2,1,0:T(8,128)(2,1)}), bf16[32,16,512]{2,1,0:T(8,128)(2,1)S(1)}, u32[]{:S(2)}, u32[]{:S(2)}) %all-to-all-start) | async-done | bytes 524320 | tf_op jit(solution)/shard_map/all_to_all | solution.py:403
  28.3 1.9 %collective-permute-start = (bf16[512,512]{1,0:T(8,128)(2,1)S(1)}, bf16[512,512]{1,0:T(8,128)(2,1)S(1)}, u32[]{:S(2)}, u32[]{:S(2)}) collective-permute-start(bf16[512,512]{1,0:T(8,128)(2,1)S(1)} %get-tuple-element.43.refs_0_), channel_id=1, source_target_pairs={{0,1},{1,2},{2,3},{3,4},{4,5},{5,6},{6,7},{8,9},{9,10},{10,11},{11... | collective-permute-start | bytes 1572872 | tf_op jit(solution)/shard_map/ppermute | solution.py:354
  31.0 1.0 %copy-done.1 = bf16[512,512]{1,0:T(8,128)(2,1)S(1)} copy-done((bf16[512,512]{1,0:T(8,128)(2,1)S(1)}, bf16[512,512]{1,0:T(8,128)(2,1)}, u32[]{:S(2)}) %copy-start.1) | copy-done | bytes 524312
  32.1 1.0 %copy-done.3 = bf16[512,512]{1,0:T(8,128)(2,1)S(1)} copy-done((bf16[512,512]{1,0:T(8,128)(2,1)S(1)}, bf16[512,512]{1,0:T(8,128)(2,1)}, u32[]{:S(2)}) %copy-start.3) | copy-done | bytes 524312
  34.1 1.9 %shard_map.115 = (bf16[512,512]{1,0:T(8,128)(2,1)S(1)}, bf16[512,512]{1,0:T(8,128)(2,1)S(1)}, bf16[512,512]{1,0:T(8,128)(2,1)S(1)}, bf16[512,512]{1,0:T(8,128)(2...) custom-call(bf16[512,512]{1,0:T(8,128)(2,1)S(1)} %get-tuple-element., ...), custom_call_target="tpu_custom_call" | custom-call | flops 805306368 | bytes 6291456 | tf_op jit(solution)/shard_map/pallas_call | solution.py:38
  36.1 11.7 %shard_map.116 = (bf16[16,640,256]{2,1,0:T(8,128)(2,1)S(1)}, bf16[16,640,256]{2,1,0:T(8,128)(2,1)S(1)}, f32[16,1,256]{2,1,0:T(1,128)S(1)}, bf16[512,512]{1,0:T(8...) custom-call(s32[3]{0:T(128)S(1)} %pad_add_fusion.refs_0_, ...), custom_call_target="tpu_custom_call" | custom-call | flops 3221225472 | bytes 19415052 | tf_op jit(solution)/shard_map/pallas_call | solution.py:38
  47.8 1.5 %collective-permute-start.1 = (bf16[512,512]{1,0:T(8,128)(2,1)S(1)}, bf16[512,512]{1,0:T(8,128)(2,1)S(1)}, u32[]{:S(2)}, u32[]{:S(2)}) collective-permute-start(bf16[512,512]{1,0:T(8,128)(2,1)S(1)} %get-tuple-element.66), channel_id=1, source_target_pairs={{1,0},{2,1},{3,2},{4,3},{5,4},{6,5},{7,6},{9,8},{10,9},{11,10},{12... | collective-permute-start | bytes 1572872 | tf_op jit(solution)/shard_map/ppermute | solution.py:354
  49.3 7.0 %shard_map.117 = (bf16[256,2048]{1,0:T(8,128)(2,1)S(1)}, bf16[256,2048]{1,0:T(8,128)(2,1)}, bf16[512,512]{1,0:T(8,128)(2,1)}, f32[512,512]{1,0:T(8,128)S(1)}) custom-call(s32[3]{0:T(128)S(1)} %pad_add_fusion.refs_0_, bf16[512,512]{1,0:T(8,128)(2,1)S(1)} %get-tuple-element.44.refs_1_, bf16[512,512]{1,0:T(8,128)(2,1)S(1)} %get-tuple-element.51.refs_2_, ...), custom_call_target="tpu_custom_call" | custom-call | flops 4831838208 | bytes 22036492 | tf_op jit(solution)/shard_map/pallas_call | solution.py:38
  57.1 3.0 %collective-permute-start.2 = (bf16[256,2048]{1,0:T(8,128)(2,1)}, bf16[256,2048]{1,0:T(8,128)(2,1)}, u32[]{:S(2)}, u32[]{:S(2)}) collective-permute-start(bf16[256,2048]{1,0:T(8,128)(2,1)} %get-tuple-element.72), channel_id=1, source_target_pairs={{0,1},{1,0},{2,3},{3,2},{4,5},{5,4},{6,7},{7,6},{8,9},{9,8},{10,11... | collective-permute-start | bytes 3145736 | tf_op jit(solution)/shard_map/ppermute | solution.py:472
  60.2 1.0 %copy-done.10 = bf16[512,512]{1,0:T(8,128)(2,1)S(1)} copy-done((bf16[512,512]{1,0:T(8,128)(2,1)S(1)}, bf16[512,512]{1,0:T(8,128)(2,1)}, u32[]{:S(2)}) %copy-start.10) | copy-done | bytes 524312
  62.2 1.6 %shard_map.118.refs_3_ = bf16[512,512]{1,0:T(8,128)(2,1)} custom-call(bf16[512,512]{1,0:T(8,128)(2,1)S(1)} %get-tuple-element.52.refs_3_.refs_0_, f32[512,512]{1,0:T(8,128)S(1)} %get-tuple-element.64.refs_1_, bf16[512,512]{1,0:T(8,128)(2,1)S(1)} %copy-done.12, bf16[512,512]{1,0:T(8,128)(2,1)S(1)} %bitcast.20, bf16[512,512]{1,0:T(8,128)(2,1)S(1)} %copy-done.10), custom_call_target="tpu_custom_call" | custom-call | flops 268435456 | bytes 3670016 | tf_op jit(solution)/shard_map/pallas_call | solution.py:38
  63.8 1.6 %shard_map.121 = (bf16[64,2048]{1,0:T(8,128)(2,1)S(1)}, bf16[64,2048]{1,0:T(8,128)(2,1)S(1)}, bf16[64,2048]{1,0:T(8,128)(2,1)S(1)}, bf16[64,2048]{1,0:T(8,128)(2,1)S(1)}) custom-call(s32[1]{0:T(128)} %bitcast.11.refs_0_, bf16[4,64,2048]{2,1,0:T(8,128)(2,1)S(1)} %bitcast.23, bf16[4,64,2048]{2,1,0:T(8,128)(2,1)} %bitcast.13.refs_2_, ...), custom_call_target="tpu_custom_call" | custom-call | bytes 3670020 | tf_op jit(solution)/shard_map/pallas_call | solution.py:38
  66.9 2.1 %collective-permute-start.5 = (bf16[64,2048]{1,0:T(8,128)(2,1)S(1)}, bf16[64,2048]{1,0:T(8,128)(2,1)S(1)}, u32[]{:S(2)}, u32[]{:S(2)}) collective-permute-start(bf16[64,2048]{1,0:T(8,128)(2,1)S(1)} %get-tuple-element.76), channel_id=1, source_target_pairs={{0,24},{8,16},{16,8},{24,0},{1,25},{9,17},{17,9},{25,1},{2,26},{10... | collective-permute-start | bytes 786440 | tf_op jit(solution)/shard_map/ppermute | solution.py:378
  69.0 3.1 %all-to-all-start.1 = ((bf16[32,16,512]{2,1,0:T(8,128)(2,1)}), bf16[32,16,512]{2,1,0:T(8,128)(2,1)S(1)}, u32[]{:S(2)}, u32[]{:S(2)}) async-start(bf16[32,16,512]{2,1,0:T(8,128)(2,1)} %bitcast.8), calls=%async_computation.1 | async-start | bytes 1048576 | tf_op jit(solution)/shard_map/all_to_all | solution.py:403
  72.1 2.5 %collective-permute-done.3 = bf16[64,2048]{1,0:T(8,128)(2,1)S(1)} collective-permute-done((bf16[64,2048]{1,0:T(8,128)(2,1)S(1)}, bf16[64,2048]{1,0:T(8,128)(2,1)S(1)}, u32[]{:S(2)}, u32[]{:S(2)}) %collective-permute-start.3) | collective-permute-done | bytes 262176 | tf_op jit(solution)/shard_map/ppermute | solution.py:378
  74.7 7.7 %collective-permute-done.4 = bf16[64,2048]{1,0:T(8,128)(2,1)S(1)} collective-permute-done((bf16[64,2048]{1,0:T(8,128)(2,1)S(1)}, bf16[64,2048]{1,0:T(8,128)(2,1)S(1)}, u32[]{:S(2)}, u32[]{:S(2)}) %collective-permute-start.4) | collective-permute-done | bytes 262176 | tf_op jit(solution)/shard_map/ppermute | solution.py:378
  83.3 1.1 %collective-permute-start.6 = (bf16[16,2048]{1,0:T(8,128)(2,1)S(1)}, bf16[16,2048]{1,0:T(8,128)(2,1)S(1)}, u32[]{:S(2)}, u32[]{:S(2)}) collective-permute-start(bf16[16,2048]{1,0:T(8,128)(2,1)S(1)} %get-tuple-element.78), channel_id=1, source_target_pairs={{0,2},{1,3},{2,0},{3,1},{4,6},{5,7},{6,4},{7,5},{8,10},{9,11},{10,... | collective-permute-start | bytes 196616 | tf_op jit(solution)/shard_map/ppermute | solution.py:378
  84.5 1.6 %collective-permute-start.7 = (bf16[16,2048]{1,0:T(8,128)(2,1)S(1)}, bf16[16,2048]{1,0:T(8,128)(2,1)S(1)}, u32[]{:S(2)}, u32[]{:S(2)}) collective-permute-start(bf16[16,2048]{1,0:T(8,128)(2,1)S(1)} %get-tuple-element.79), channel_id=1, source_target_pairs={{0,4},{1,5},{2,6},{3,7},{4,0},{5,1},{6,2},{7,3},{8,12},{9,13},{10,... | collective-permute-start | bytes 196616 | tf_op jit(solution)/shard_map/ppermute | solution.py:378
  86.0 1.8 %collective-permute-start.8 = (bf16[16,2048]{1,0:T(8,128)(2,1)S(1)}, bf16[16,2048]{1,0:T(8,128)(2,1)S(1)}, u32[]{:S(2)}, u32[]{:S(2)}) collective-permute-start(bf16[16,2048]{1,0:T(8,128)(2,1)S(1)} %get-tuple-element.80), channel_id=1, source_target_pairs={{0,6},{1,7},{2,4},{3,5},{4,2},{5,3},{6,0},{7,1},{8,14},{9,15},{10,... | collective-permute-start | bytes 196616 | tf_op jit(solution)/shard_map/ppermute | solution.py:378
  89.2 1.2 %shard_map.120 = bf16[512,512]{1,0:T(8,128)(2,1)} custom-call(bf16[512,512]{1,0:T(8,128)(2,1)S(1)} %shard_map.119.refs_0_, bf16[512,512]{1,0:T(8,128)(2,1)S(1)} %bitcast.21), custom_call_target="tpu_custom_call" | custom-call | flops 268435456 | bytes 1572864 | tf_op jit(solution)/shard_map/pallas_call | solution.py:38
  91.1 1.1 %collective-permute-done.8 = bf16[16,2048]{1,0:T(8,128)(2,1)S(1)} collective-permute-done((bf16[16,2048]{1,0:T(8,128)(2,1)S(1)}, bf16[16,2048]{1,0:T(8,128)(2,1)S(1)}, u32[]{:S(2)}, u32[]{:S(2)}) %collective-permute-start.8) | collective-permute-done | bytes 65568 | tf_op jit(solution)/shard_map/ppermute | solution.py:378
  (44 shorter events, 12.2 us)
Async XLA Ops:
  0.6 35.4 %copy-start.7 = (bf16[512,512]{1,0:T(8,128)(2,1)S(1)}, bf16[512,512]{1,0:T(8,128)(2,1)}, u32[]{:S(2)}) copy-start(bf16[512,512]{1,0:T(8,128)(2,1)} %refs_8_.1) | copy-start | bytes 1572868
  0.6 35.4 %copy-start = (bf16[1,512,512]{2,1,0:T(8,128)(2,1)S(1)}, bf16[1,512,512]{2,1,0:T(8,128)(2,1)}, u32[]{:S(2)}) copy-start(bf16[1,512,512]{2,1,0:T(8,128)(2,1)} %param.17) | copy-start | bytes 1572868
  0.7 1.1 %copy-start.13 = (bf16[512,512]{1,0:T(8,128)(2,1)S(1)}, bf16[512,512]{1,0:T(8,128)(2,1)}, u32[]{:S(2)}) copy-start(bf16[512,512]{1,0:T(8,128)(2,1)} %refs_1_.2) | copy-start | bytes 1572868
  4.0 23.7 %all-to-all-start = ((bf16[32,16,512]{2,1,0:T(8,128)(2,1)}), bf16[32,16,512]{2,1,0:T(8,128)(2,1)S(1)}, u32[]{:S(2)}, u32[]{:S(2)}) async-start(bf16[32,16,512]{2,1,0:T(8,128)(2,1)} %bitcast.4), calls=%async_computation | async-start | bytes 1048576 | tf_op jit(solution)/shard_map/all_to_all | solution.py:403
  28.3 7.7 %collective-permute-start = (bf16[512,512]{1,0:T(8,128)(2,1)S(1)}, bf16[512,512]{1,0:T(8,128)(2,1)S(1)}, u32[]{:S(2)}, u32[]{:S(2)}) collective-permute-start(bf16[512,512]{1,0:T(8,128)(2,1)S(1)} %get-tuple-element.43.refs_0_), channel_id=1, source_target_pairs={{0,1},{1,2},{2,3},{3,4},{4,5},{5,6},{6,7},{8,9},{9,10},{10,11},{11... | collective-permute-start | bytes 1572872 | tf_op jit(solution)/shard_map/ppermute | solution.py:354
  31.0 1.0 %copy-start.1 = (bf16[512,512]{1,0:T(8,128)(2,1)S(1)}, bf16[512,512]{1,0:T(8,128)(2,1)}, u32[]{:S(2)}) copy-start(bf16[512,512]{1,0:T(8,128)(2,1)} %refs_5_.1) | copy-start | bytes 1572868
  32.1 1.0 %copy-start.3 = (bf16[512,512]{1,0:T(8,128)(2,1)S(1)}, bf16[512,512]{1,0:T(8,128)(2,1)}, u32[]{:S(2)}) copy-start(bf16[512,512]{1,0:T(8,128)(2,1)} %refs_6_.1) | copy-start | bytes 1572868
  33.1 1.0 %copy-start.5 = (bf16[512,512]{1,0:T(8,128)(2,1)S(1)}, bf16[512,512]{1,0:T(8,128)(2,1)}, u32[]{:S(2)}) copy-start(bf16[512,512]{1,0:T(8,128)(2,1)} %refs_7_.1) | copy-start | bytes 1572868
  36.0 13.2 %copy-start.2 = (bf16[512,512]{1,0:T(8,128)(2,1)S(1)}, bf16[512,512]{1,0:T(8,128)(2,1)}, u32[]{:S(2)}) copy-start(bf16[512,512]{1,0:T(8,128)(2,1)} %refs_5_.1) | copy-start | bytes 1572868
  36.1 13.2 %copy-start.4 = (bf16[512,512]{1,0:T(8,128)(2,1)S(1)}, bf16[512,512]{1,0:T(8,128)(2,1)}, u32[]{:S(2)}) copy-start(bf16[512,512]{1,0:T(8,128)(2,1)} %refs_6_.1) | copy-start | bytes 1572868
  36.1 13.2 %copy-start.6 = (bf16[512,512]{1,0:T(8,128)(2,1)S(1)}, bf16[512,512]{1,0:T(8,128)(2,1)}, u32[]{:S(2)}) copy-start(bf16[512,512]{1,0:T(8,128)(2,1)} %refs_7_.1) | copy-start | bytes 1572868
  36.1 13.2 %copy-start.8 = (bf16[512,512]{1,0:T(8,128)(2,1)S(1)}, bf16[512,512]{1,0:T(8,128)(2,1)}, u32[]{:S(2)}) copy-start(bf16[512,512]{1,0:T(8,128)(2,1)} %refs_8_.1) | copy-start | bytes 1572868
  47.8 8.5 %collective-permute-start.1 = (bf16[512,512]{1,0:T(8,128)(2,1)S(1)}, bf16[512,512]{1,0:T(8,128)(2,1)S(1)}, u32[]{:S(2)}, u32[]{:S(2)}) collective-permute-start(bf16[512,512]{1,0:T(8,128)(2,1)S(1)} %get-tuple-element.66), channel_id=1, source_target_pairs={{1,0},{2,1},{3,2},{4,3},{5,4},{6,5},{7,6},{9,8},{10,9},{11,10},{12... | collective-permute-start | bytes 1572872 | tf_op jit(solution)/shard_map/ppermute | solution.py:354
  56.3 31.5 %copy-start.15 = (s32[512]{0:T(512)S(1)}, s32[512]{0:T(512)}, u32[]{:S(2)}) copy-start(s32[512]{0:T(512)} %param.10) | copy-start | bytes 6148
  57.1 6.7 %collective-permute-start.2 = (bf16[256,2048]{1,0:T(8,128)(2,1)}, bf16[256,2048]{1,0:T(8,128)(2,1)}, u32[]{:S(2)}, u32[]{:S(2)}) collective-permute-start(bf16[256,2048]{1,0:T(8,128)(2,1)} %get-tuple-element.72), channel_id=1, source_target_pairs={{0,1},{1,0},{2,3},{3,2},{4,5},{5,4},{6,7},{7,6},{8,9},{9,8},{10,11... | collective-permute-start | bytes 3145736 | tf_op jit(solution)/shard_map/ppermute | solution.py:472
  60.2 1.0 %copy-start.10 = (bf16[512,512]{1,0:T(8,128)(2,1)S(1)}, bf16[512,512]{1,0:T(8,128)(2,1)}, u32[]{:S(2)}) copy-start(bf16[512,512]{1,0:T(8,128)(2,1)} %copy-done.9) | copy-start | bytes 1572868
  61.2 1.0 %copy-start.12 = (bf16[512,512]{1,0:T(8,128)(2,1)S(1)}, bf16[512,512]{1,0:T(8,128)(2,1)}, u32[]{:S(2)}) copy-start(bf16[512,512]{1,0:T(8,128)(2,1)} %copy-done.11) | copy-start | bytes 1572868
  65.4 9.2 %collective-permute-start.3 = (bf16[64,2048]{1,0:T(8,128)(2,1)S(1)}, bf16[64,2048]{1,0:T(8,128)(2,1)S(1)}, u32[]{:S(2)}, u32[]{:S(2)}) collective-permute-start(bf16[64,2048]{1,0:T(8,128)(2,1)S(1)} %get-tuple-element.74), channel_id=1, source_target_pairs={{0,8},{8,0},{16,24},{24,16},{1,9},{9,1},{17,25},{25,17},{2,10},{10... | collective-permute-start | bytes 786440 | tf_op jit(solution)/shard_map/ppermute | solution.py:378
  66.3 16.0 %collective-permute-start.4 = (bf16[64,2048]{1,0:T(8,128)(2,1)S(1)}, bf16[64,2048]{1,0:T(8,128)(2,1)S(1)}, u32[]{:S(2)}, u32[]{:S(2)}) collective-permute-start(bf16[64,2048]{1,0:T(8,128)(2,1)S(1)} %get-tuple-element.75), channel_id=1, source_target_pairs={{0,16},{8,24},{16,0},{24,8},{1,17},{9,25},{17,1},{25,9},{2,18},{10... | collective-permute-start | bytes 786440 | tf_op jit(solution)/shard_map/ppermute | solution.py:378
  66.9 16.3 %collective-permute-start.5 = (bf16[64,2048]{1,0:T(8,128)(2,1)S(1)}, bf16[64,2048]{1,0:T(8,128)(2,1)S(1)}, u32[]{:S(2)}, u32[]{:S(2)}) collective-permute-start(bf16[64,2048]{1,0:T(8,128)(2,1)S(1)} %get-tuple-element.76), channel_id=1, source_target_pairs={{0,24},{8,16},{16,8},{24,0},{1,25},{9,17},{17,9},{25,1},{2,26},{10... | collective-permute-start | bytes 786440 | tf_op jit(solution)/shard_map/ppermute | solution.py:378
  69.0 20.2 %all-to-all-start.1 = ((bf16[32,16,512]{2,1,0:T(8,128)(2,1)}), bf16[32,16,512]{2,1,0:T(8,128)(2,1)S(1)}, u32[]{:S(2)}, u32[]{:S(2)}) async-start(bf16[32,16,512]{2,1,0:T(8,128)(2,1)} %bitcast.8), calls=%async_computation.1 | async-start | bytes 1048576 | tf_op jit(solution)/shard_map/all_to_all | solution.py:403
  83.3 7.1 %collective-permute-start.6 = (bf16[16,2048]{1,0:T(8,128)(2,1)S(1)}, bf16[16,2048]{1,0:T(8,128)(2,1)S(1)}, u32[]{:S(2)}, u32[]{:S(2)}) collective-permute-start(bf16[16,2048]{1,0:T(8,128)(2,1)S(1)} %get-tuple-element.78), channel_id=1, source_target_pairs={{0,2},{1,3},{2,0},{3,1},{4,6},{5,7},{6,4},{7,5},{8,10},{9,11},{10,... | collective-permute-start | bytes 196616 | tf_op jit(solution)/shard_map/ppermute | solution.py:378
  84.5 6.6 %collective-permute-start.7 = (bf16[16,2048]{1,0:T(8,128)(2,1)S(1)}, bf16[16,2048]{1,0:T(8,128)(2,1)S(1)}, u32[]{:S(2)}, u32[]{:S(2)}) collective-permute-start(bf16[16,2048]{1,0:T(8,128)(2,1)S(1)} %get-tuple-element.79), channel_id=1, source_target_pairs={{0,4},{1,5},{2,6},{3,7},{4,0},{5,1},{6,2},{7,3},{8,12},{9,13},{10,... | collective-permute-start | bytes 196616 | tf_op jit(solution)/shard_map/ppermute | solution.py:378
  86.0 6.2 %collective-permute-start.8 = (bf16[16,2048]{1,0:T(8,128)(2,1)S(1)}, bf16[16,2048]{1,0:T(8,128)(2,1)S(1)}, u32[]{:S(2)}, u32[]{:S(2)}) collective-permute-start(bf16[16,2048]{1,0:T(8,128)(2,1)S(1)} %get-tuple-element.80), channel_id=1, source_target_pairs={{0,6},{1,7},{2,4},{3,5},{4,2},{5,3},{6,0},{7,1},{8,14},{9,15},{10,... | collective-permute-start | bytes 196616 | tf_op jit(solution)/shard_map/ppermute | solution.py:378
  (3 other events, 2.3 us)
